TPU v7x, 32 devices: a whole 2x2x4 slice. The times are simulated.
32 devices in a mesh: groups: 2 (over x), blk: 4 (over y, core), sub: 4 (over z).
Axes of the slice: x: 2, y: 2, z: 4, core: 2. Of those that a mesh axis runs over, the one named last changes fastest.
Arguments:
- teacher: bfloat16 [4096, 1024], P(('groups', 'blk', 'sub')), parts along dimension 0, may hold values from -8 to 8
- student: bfloat16 [4096, 384], P(('groups', 'blk', 'sub')), parts along dimension 0, may hold values from -0.25 to 0.25
Outputs:
- student_grad: float32 [4096, 384], P(('groups', 'blk', 'sub')), parts along dimension 0
- distill_loss: float32 [2], P('groups'), parts along dimension 0
There are 2 independent parts, one for each index of `groups`. A program takes and returns all parts, laid end to end along the dimension named above; each array names one. Nothing has to cross between parts.
All inputs are finite; a program needn't handle non-finite values.
Results may differ from a plain program's by a relative error of at most 0.00085.
Values may be sent and summed in bfloat16 or wider, within the bound.
No kernel may reach another device: no remote copies, remote signals or barrier semaphores. Data moves between devices by JAX's collectives and lax.ppermute only.
A program may use at most 64 MiB of HBM per device.

v0:
```python
import jax
import jax.numpy as jnp
from jax import lax
from jax.sharding import PartitionSpec as P

FLOOR = 0.01
EPSILON = 1e-06


def passed_along(block, axis, distance):
    devices = range(lax.axis_size(axis))
    route = [((i - distance) % len(devices), i) for i in devices]
    return lax.ppermute(block, axis, route)


def local_moments(part_teacher, part_student):
    float_teacher = part_teacher.astype(jnp.float32)
    float_student = part_student.astype(jnp.float32)
    return (
        jnp.sum(float_teacher * float_teacher),
        jnp.sum(float_teacher, axis=0),
        jnp.sum(float_student * float_student),
        jnp.sum(float_student, axis=0),
    )


def spread_of(square_sum, column_sum, total_float):
    centre = column_sum / total_float
    return (centre, 2.0 * (square_sum / total_float - jnp.sum(centre * centre)) + EPSILON)


def accumulate(running, extra):
    return tuple((first + second for first, second in zip(running, extra)))


def per_device(teacher, student):
    tile_rows = teacher.shape[0]
    blk_count = lax.axis_size("blk")
    sub_count = lax.axis_size("sub")
    block_rows = tile_rows * sub_count
    total_rows = block_rows * blk_count
    blk_index = lax.axis_index("blk")
    sub_index = lax.axis_index("sub")
    home_teacher, home_student = (
        lax.all_gather(teacher, "sub", axis=0, tiled=True),
        lax.all_gather(student, "sub", axis=0, tiled=True),
    )
    square_t, column_t, square_s, column_s = local_moments(teacher, student)
    square_t, column_t, square_s, column_s = lax.psum(
        (square_t, column_t, square_s, column_s), ("blk", "sub")
    )
    centre_teacher, spread_teacher = spread_of(square_t, column_t, float(total_rows))
    centre_student, spread_student = spread_of(square_s, column_s, float(total_rows))
    float_home_teacher = home_teacher.astype(jnp.float32)
    float_home_student = home_student.astype(jnp.float32)
    norms_home_teacher = jnp.sum(float_home_teacher * float_home_teacher, axis=1)
    norms_home_student = jnp.sum(float_home_student * float_home_student, axis=1)
    home_index = blk_index * block_rows + jnp.arange(block_rows, dtype=jnp.int32)
    contract_last = (((1,), (1,)), ((), ()))

    def score_pair(visit_teacher, visit_student, visit_block):
        visit_index = (
            visit_block * block_rows
            + sub_index * tile_rows
            + jnp.arange(tile_rows, dtype=jnp.int32)
        )
        float_visit_teacher = visit_teacher.astype(jnp.float32)
        float_visit_student = visit_student.astype(jnp.float32)
        norms_visit_teacher = jnp.sum(float_visit_teacher * float_visit_teacher, axis=1)
        norms_visit_student = jnp.sum(float_visit_student * float_visit_student, axis=1)
        gram_teacher = lax.dot_general(
            home_teacher, visit_teacher, contract_last, preferred_element_type=jnp.float32
        )
        gram_student = lax.dot_general(
            home_student, visit_student, contract_last, preferred_element_type=jnp.float32
        )
        square_teacher = jnp.maximum(
            norms_home_teacher[:, None] + norms_visit_teacher[None, :] - 2.0 * gram_teacher, 0.0
        )
        square_student = jnp.maximum(
            norms_home_student[:, None] + norms_visit_student[None, :] - 2.0 * gram_student, 0.0
        )
        scaled_teacher = jnp.sqrt(square_teacher / spread_teacher + FLOOR)
        scaled_student = jnp.sqrt(square_student / spread_student + FLOOR)
        residue = scaled_student - scaled_teacher
        magnitude = jnp.abs(residue)
        huber_value = jnp.where(magnitude < 1.0, 0.5 * residue * residue, magnitude - 0.5)
        slope = jnp.clip(residue, -1.0, 1.0)
        pair_mask = (home_index[:, None] != visit_index[None, :]).astype(jnp.float32)
        factor = 1.0
        loss_part = factor * jnp.sum(huber_value * pair_mask)
        spread_part = -factor * jnp.sum(slope * square_student / scaled_student * pair_mask)
        weights = (slope / (spread_student * scaled_student) * pair_mask).astype(jnp.bfloat16)
        float_weights = weights.astype(jnp.float32)
        row_weight = jnp.sum(float_weights, axis=1)
        cross_term = jnp.dot(weights, visit_student, preferred_element_type=jnp.float32)
        partner = None
        return ((loss_part, spread_part, row_weight, cross_term), partner)

    running, unused = score_pair(teacher, student, blk_index)

    def cycle_step(distance, loop_state):
        visit_teacher, visit_student, inner = loop_state
        visit_teacher, visit_student = passed_along((visit_teacher, visit_student), "blk", 1)
        fresh_terms, unused_part = score_pair(
            visit_teacher, visit_student, (blk_index - distance) % blk_count
        )
        return (visit_teacher, visit_student, accumulate(inner, fresh_terms))

    unused_teacher, unused_student, running = lax.fori_loop(
        1, blk_count, cycle_step, (teacher, student, running)
    )
    loss_sum, spread_sum, row_weight, cross_sum = running
    home_grad = float_home_student * row_weight[:, None] - cross_sum
    own_rows = lax.psum_scatter(home_grad, "sub", scatter_dimension=0, tiled=True)
    loss_total, spread_total = lax.psum((loss_sum, spread_sum), ("blk", "sub"))
    pair_count = float(total_rows) * float(total_rows - 1)
    correction = 2.0 * spread_total / (pair_count * spread_student * spread_student)
    student_grad = 2.0 / float(total_rows - 1) * own_rows + correction * (
        student.astype(jnp.float32) - centre_student[None, :]
    )
    return (student_grad, (loss_total / pair_count).reshape(1))


def solution(mesh):
    placed = (P(("groups", "blk", "sub"), None), P(("groups", "blk", "sub"), None))
    return jax.shard_map(
        per_device,
        mesh=mesh,
        in_specs=placed,
        out_specs=(P(("groups", "blk", "sub"), None), P("groups")),
        check_vma=False,
    )
```

profile of v0, /device:TPU:0, one launch (start us, length us, event | category | flops | bytes accessed | tf_op | source)
XLA Modules:
  0.0 150.7 jit_solution(7076193937142985488)
XLA Ops:
  7.2 1.7 %copy.26 = bf16[128,1024]{1,0:T(8,128)(2,1)} copy(bf16[128,1024]{1,0:T(8,128)(2,1)} %param.4) | data formatting | bytes 524288
  9.0 1.6 %convert_reduce_fusion.2 = (f32[384]{0:T(512)S(1)}, f32[]{:T(128)}, f32[128]{0:T(128)S(1)}) fusion(bf16[128,384]{1,0:T(8,128)(2,1)} %param.5), kind=kLoop, calls=%fused_computation.44 | loop fusion | flops 245247 | bytes 100356 | tf_op jit(solution)/shard_map/reduce_sum | solution.py:23
  10.6 1.7 %fusion.17 = (f32[128]{0:T(128)S(1)}, f32[]{:T(128)}, f32[1024]{0:T(1024)S(1)}) fusion(bf16[128,1024]{1,0:T(8,128)(2,1)} %copy.26), kind=kLoop, calls=%fused_computation.38 | loop fusion | flops 654207 | bytes 266756 | tf_op jit(solution)/shard_map/reduce_sum | solution.py:69
  12.3 37.9 %all-reduce.1 = (f32[]{:T(128)}, f32[1024]{0:T(1024)S(1)}, f32[]{:T(128)}, f32[384]{0:T(512)S(1)}) all-reduce(f32[]{:T(128)} %get-tuple-element.427, f32[1024]{0:T(1024)S(1)} %get-tuple-element.428, f32[]{:T(128)} %get-tuple-element.430, f32[384]{0:T(512)S(1)} %get-tuple-element.429), channel_id=1, replica_groups=mesh['groups'=2,'blk'=4,'sub'=4] {'blk','sub'}, use_global_device_ids=true, to_apply=%region_10.0 | all-reduce | flops 1410 | bytes 11280 | tf_op jit(solution)/shard_map/psum | solution.py:49
  51.5 0.6 broadcast_multiply_fusion
  52.8 0.6 multiply_reduce_fusion.3
  54.1 14.2 %all_gather.6 = bf16[512,384]{1,0:T(8,128)(2,1)S(1)} all-gather(bf16[128,384]{1,0:T(8,128)(2,1)S(1)} %copy-done), channel_id=1, replica_groups=mesh['groups'=2,'blk'=4,'sub'=4] {'sub'}, dimensions={0}, use_global_device_ids=true | all-gather | bytes 491520 | tf_op jit(solution)/shard_map/all_gather | solution.py:46
  68.5 0.3 fusion.7
  68.8 1.6 %multiply_reduce_fusion.2 = f32[512]{0:T(512)S(1)} fusion(bf16[512,1024]{1,0:T(8,128)(2,1)} %all-gather.2.cloned.1.call-done), kind=kLoop, calls=%fused_computation.20 | loop fusion | flops 1572352 | bytes 1050624 | tf_op jit(solution)/shard_map/reduce_sum | solution.py:56
  70.4 1.6 %convert_reduce_fusion.3 = (f32[512]{0:T(512)S(1)}, bf16[512,128]{0,1:T(8,128)(2,1)S(1)}, f32[]{:T(128)}, f32[]{:T(128)}) fusion(f32[512,128]{0,1:T(8,128)S(1)} %fusion.7, f32[]{:T(128)} %add.297, s32[128]{0:T(128)S(1)} %iota_add_fusion.3, s32[512]{0:T(512)S(1)} %iota_add_fusion.2, f32[]{:T(128)} %add.302, bf16[512,1024]{1,0:T(8,128)(2,1)S(1)} %copy-done.3, ...), kind=kOutput, calls=%fused_computation.50 | convolution fusion | flops 136117760 | bytes 1711120 | tf_op jit(solution)/shard_map/dot_general | solution.py:71
  72.0 0.3 fusion.28
  72.8 34.2 %while.26 = (s32[]{:T(128)}, bf16[128,1024]{1,0:T(8,128)(2,1)S(1)}, bf16[128,384]{1,0:T(8,128)(2,1)S(1)}, f32[]{:T(128)}, f32[]{:T(128)}, /*index=5*/f32[512]{0:...) while((s32[]{:T(128)}, bf16[128,1024]{1,0:T(8,128)(2,1)S(1)}, ...), condition=%wide.region_23.24_spmd.clone, body=%wide.region_17.23_spmd.clone.sunk | while | flops 237781376 | bytes 6802914 | solution.py:110
  72.9 1.1 collective-permute-start
  74.0 2.9 %collective-permute-done.1 = bf16[128,384]{1,0:T(8,128)(2,1)S(1)} collective-permute-done((bf16[128,384]{1,0:T(8,128)(2,1)S(1)}, bf16[128,384]{1,0:T(8,128)(2,1)S(1)}, u32[]{:S(2)}, u32[]{:S(2)}) %collective-permute-start.1) | collective-permute-done | bytes 98336 | tf_op jit(solution)/shard_map/while/body/eval_jaxpr/ppermute | solution.py:13
  77.3 2.4 %collective-permute-done = bf16[128,1024]{1,0:T(8,128)(2,1)S(1)} collective-permute-done((bf16[128,1024]{1,0:T(8,128)(2,1)S(1)}, bf16[128,1024]{1,0:T(8,128)(2,1)S(1)}, u32[]{:S(2)}, u32[]{:S(2)}) %collective-permute-start) | collective-permute-done | bytes 262176 | tf_op jit(solution)/shard_map/while/body/eval_jaxpr/ppermute | solution.py:13
  79.9 1.6 %convert_reduce_fusion.5 = (f32[512]{0:T(512)S(1)}, bf16[512,128]{0,1:T(8,128)(2,1)S(1)}, f32[]{:T(128)}, f32[]{:T(128)}) fusion(f32[512,128]{0,1:T(8,128)S(1)} %convolution_multiply_fusion.5, f32[128]{0:T(128)S(1)} %multiply_reduce_fusion.7, f32[512]{0:T(512)S(1)} %get-tuple-element.638, f32[]{:T(128)} %get-tuple-element.640, ...), kind=kOutput, calls=%fused_computation.13.clone.1 | convolution fusion | flops 136314368 | bytes 1713680 | tf_op jit(solution)/shard_map/while/body/eval_jaxpr/dot_general | solution.py:71
  83.4 0.3 convolution_add_fusion.2
  84.3 1.1 collective-permute-start
  85.4 2.9 %collective-permute-done.1 = bf16[128,384]{1,0:T(8,128)(2,1)S(1)} collective-permute-done((bf16[128,384]{1,0:T(8,128)(2,1)S(1)}, bf16[128,384]{1,0:T(8,128)(2,1)S(1)}, u32[]{:S(2)}, u32[]{:S(2)}) %collective-permute-start.1) | collective-permute-done | bytes 98336 | tf_op jit(solution)/shard_map/while/body/eval_jaxpr/ppermute | solution.py:13
  88.5 0.3 convolution_multiply_fusion.5
  88.7 2.4 %collective-permute-done = bf16[128,1024]{1,0:T(8,128)(2,1)S(1)} collective-permute-done((bf16[128,1024]{1,0:T(8,128)(2,1)S(1)}, bf16[128,1024]{1,0:T(8,128)(2,1)S(1)}, u32[]{:S(2)}, u32[]{:S(2)}) %collective-permute-start) | collective-permute-done | bytes 262176 | tf_op jit(solution)/shard_map/while/body/eval_jaxpr/ppermute | solution.py:13
  91.3 1.6 %convert_reduce_fusion.5 = (f32[512]{0:T(512)S(1)}, bf16[512,128]{0,1:T(8,128)(2,1)S(1)}, f32[]{:T(128)}, f32[]{:T(128)}) fusion(f32[512,128]{0,1:T(8,128)S(1)} %convolution_multiply_fusion.5, f32[128]{0:T(128)S(1)} %multiply_reduce_fusion.7, f32[512]{0:T(512)S(1)} %get-tuple-element.638, f32[]{:T(128)} %get-tuple-element.640, ...), kind=kOutput, calls=%fused_computation.13.clone.1 | convolution fusion | flops 136314368 | bytes 1713680 | tf_op jit(solution)/shard_map/while/body/eval_jaxpr/dot_general | solution.py:71
  94.8 0.3 convolution_add_fusion.2
  95.7 1.1 collective-permute-start
  96.8 2.9 %collective-permute-done.1 = bf16[128,384]{1,0:T(8,128)(2,1)S(1)} collective-permute-done((bf16[128,384]{1,0:T(8,128)(2,1)S(1)}, bf16[128,384]{1,0:T(8,128)(2,1)S(1)}, u32[]{:S(2)}, u32[]{:S(2)}) %collective-permute-start.1) | collective-permute-done | bytes 98336 | tf_op jit(solution)/shard_map/while/body/eval_jaxpr/ppermute | solution.py:13
  99.9 0.3 convolution_multiply_fusion.5
  100.1 2.4 %collective-permute-done = bf16[128,1024]{1,0:T(8,128)(2,1)S(1)} collective-permute-done((bf16[128,1024]{1,0:T(8,128)(2,1)S(1)}, bf16[128,1024]{1,0:T(8,128)(2,1)S(1)}, u32[]{:S(2)}, u32[]{:S(2)}) %collective-permute-start) | collective-permute-done | bytes 262176 | tf_op jit(solution)/shard_map/while/body/eval_jaxpr/ppermute | solution.py:13
  102.7 1.6 %convert_reduce_fusion.5 = (f32[512]{0:T(512)S(1)}, bf16[512,128]{0,1:T(8,128)(2,1)S(1)}, f32[]{:T(128)}, f32[]{:T(128)}) fusion(f32[512,128]{0,1:T(8,128)S(1)} %convolution_multiply_fusion.5, f32[128]{0:T(128)S(1)} %multiply_reduce_fusion.7, f32[512]{0:T(512)S(1)} %get-tuple-element.638, f32[]{:T(128)} %get-tuple-element.640, ...), kind=kOutput, calls=%fused_computation.13.clone.1 | convolution fusion | flops 136314368 | bytes 1713680 | tf_op jit(solution)/shard_map/while/body/eval_jaxpr/dot_general | solution.py:71
  106.2 0.3 convolution_add_fusion.2
  107.1 1.0 fusion.15
  108.1 31.6 %all-reduce = (f32[]{:T(128)}, f32[]{:T(128)}) all-reduce(f32[]{:T(128)} %get-tuple-element.385, f32[]{:T(128)} %get-tuple-element.386), channel_id=1, replica_groups=mesh['groups'=2,'blk'=4,'sub'=4] {'blk','sub'}, use_global_device_ids=true, to_apply=%region_25.26 | all-reduce | flops 2 | bytes 16 | tf_op jit(solution)/shard_map/psum | solution.py:116
  141.1 1.6 %fusion.25 = f32[128,384]{1,0:T(8,128)} fusion(bf16[128,384]{1,0:T(8,128)(2,1)S(1)} %copy-done, f32[128,384]{1,0:T(8,128)} %reduce-scatter.2.cloned.1.call-done, f32[384]{0:T(512)S(1)} %get-tuple-element.478, f32[]{:T(128)S(6)} %div.114), kind=kLoop, calls=%fused_computation.55 | loop fusion | flops 245760 | bytes 493060 | tf_op jit(solution)/shard_map/add | solution.py:119
  (42 shorter events, 1.5 us)
Async XLA Ops:
  7.2 46.9 %copy-start = (bf16[128,384]{1,0:T(8,128)(2,1)S(1)}, bf16[128,384]{1,0:T(8,128)(2,1)}, u32[]{:S(2)}) copy-start(bf16[128,384]{1,0:T(8,128)(2,1)} %param.5) | copy-start | bytes 294916
  7.2 61.6 %all-gather.2.cloned.1.call-start = ((), (), s32[]{:S(2)}) async-start(), calls=%async_computation.1 | async-start | bytes 1310720 | tf_op jit(solution)/shard_map/all_gather | solution.py:45
  8.9 132.1 %reduce-scatter.2.cloned.1.call-start = ((), (), s32[]{:S(2)}) async-start(), calls=%async_computation.2 | async-start | bytes 983040 | tf_op jit(solution)/shard_map/reduce_scatter | solution.py:115
  68.3 2.1 %copy-start.2 = (bf16[128,1024]{1,0:T(8,128)(2,1)S(1)}, bf16[128,1024]{1,0:T(8,128)(2,1)}, u32[]{:S(2)}) copy-start(bf16[128,1024]{1,0:T(8,128)(2,1)} %copy.26) | copy-start | bytes 786436
  68.8 1.6 %copy-start.3 = (bf16[512,1024]{1,0:T(8,128)(2,1)S(1)}, bf16[512,1024]{1,0:T(8,128)(2,1)}, u32[]{:S(2)}) copy-start(bf16[512,1024]{1,0:T(8,128)(2,1)} %all-gather.2.cloned.1.call-done) | copy-start | bytes 3145732
  70.4 2.4 %copy-start.1 = (bf16[128,384]{1,0:T(8,128)(2,1)S(1)}, bf16[128,384]{1,0:T(8,128)(2,1)}, u32[]{:S(2)}) copy-start(bf16[128,384]{1,0:T(8,128)(2,1)} %param.5) | copy-start | bytes 294916
  72.8 4.1 %collective-permute-start.1 = (bf16[128,384]{1,0:T(8,128)(2,1)S(1)}, bf16[128,384]{1,0:T(8,128)(2,1)S(1)}, u32[]{:S(2)}, u32[]{:S(2)}) collective-permute-start(bf16[128,384]{1,0:T(8,128)(2,1)S(1)} %get-tuple-element.609), channel_id=1, source_target_pairs={{12,0},{0,4},{4,8},{8,12},{13,1},{1,5},{5,9},{9,13},{14,2},{2,6},{... | collective-permute-start | bytes 294920 | tf_op jit(solution)/shard_map/while/body/eval_jaxpr/ppermute | solution.py:13
  72.9 6.8 %collective-permute-start = (bf16[128,1024]{1,0:T(8,128)(2,1)S(1)}, bf16[128,1024]{1,0:T(8,128)(2,1)S(1)}, u32[]{:S(2)}, u32[]{:S(2)}) collective-permute-start(bf16[128,1024]{1,0:T(8,128)(2,1)S(1)} %get-tuple-element.608), channel_id=1, source_target_pairs={{12,0},{0,4},{4,8},{8,12},{13,1},{1,5},{5,9},{9,13},{14,2},{2,6},{... | collective-permute-start | bytes 786440 | tf_op jit(solution)/shard_map/while/body/eval_jaxpr/ppermute | solution.py:13
  84.3 4.0 %collective-permute-start.1 = (bf16[128,384]{1,0:T(8,128)(2,1)S(1)}, bf16[128,384]{1,0:T(8,128)(2,1)S(1)}, u32[]{:S(2)}, u32[]{:S(2)}) collective-permute-start(bf16[128,384]{1,0:T(8,128)(2,1)S(1)} %get-tuple-element.609), channel_id=1, source_target_pairs={{12,0},{0,4},{4,8},{8,12},{13,1},{1,5},{5,9},{9,13},{14,2},{2,6},{... | collective-permute-start | bytes 294920 | tf_op jit(solution)/shard_map/while/body/eval_jaxpr/ppermute | solution.py:13
  84.3 6.8 %collective-permute-start = (bf16[128,1024]{1,0:T(8,128)(2,1)S(1)}, bf16[128,1024]{1,0:T(8,128)(2,1)S(1)}, u32[]{:S(2)}, u32[]{:S(2)}) collective-permute-start(bf16[128,1024]{1,0:T(8,128)(2,1)S(1)} %get-tuple-element.608), channel_id=1, source_target_pairs={{12,0},{0,4},{4,8},{8,12},{13,1},{1,5},{5,9},{9,13},{14,2},{2,6},{... | collective-permute-start | bytes 786440 | tf_op jit(solution)/shard_map/while/body/eval_jaxpr/ppermute | solution.py:13
  95.7 4.0 %collective-permute-start.1 = (bf16[128,384]{1,0:T(8,128)(2,1)S(1)}, bf16[128,384]{1,0:T(8,128)(2,1)S(1)}, u32[]{:S(2)}, u32[]{:S(2)}) collective-permute-start(bf16[128,384]{1,0:T(8,128)(2,1)S(1)} %get-tuple-element.609), channel_id=1, source_target_pairs={{12,0},{0,4},{4,8},{8,12},{13,1},{1,5},{5,9},{9,13},{14,2},{2,6},{... | collective-permute-start | bytes 294920 | tf_op jit(solution)/shard_map/while/body/eval_jaxpr/ppermute | solution.py:13
  95.7 6.8 %collective-permute-start = (bf16[128,1024]{1,0:T(8,128)(2,1)S(1)}, bf16[128,1024]{1,0:T(8,128)(2,1)S(1)}, u32[]{:S(2)}, u32[]{:S(2)}) collective-permute-start(bf16[128,1024]{1,0:T(8,128)(2,1)S(1)} %get-tuple-element.608), channel_id=1, source_target_pairs={{12,0},{0,4},{4,8},{8,12},{13,1},{1,5},{5,9},{9,13},{14,2},{2,6},{... | collective-permute-start | bytes 786440 | tf_op jit(solution)/shard_map/while/body/eval_jaxpr/ppermute | solution.py:13
Sparse Core Ops, SparseCore 0:
  9.6 32.0 all-gather.1
  108.2 21.7 reduce-scatter.1
where the time goes:
time: 151 us
  blocking collectives  83.7 us (55%)
  between operations  19.8 us (13%)
  waiting for transfers between devices  16 us (11%)
  other arithmetic  9.7 us (6%)
  matrix products  8.49 us (6%)
  loops' own time  7.65 us (5%)
  starting transfers between devices  3.49 us (2%)
  local copies, waits for them, and re-layouts  1.81 us (1%)
    psum x1, blocking collectives, per_device(): lax.psum((square_t, column_t, square_s, column_s), ('blk', 'sub'))  37.9 us
    psum x1, blocking collectives, per_device(): loss_total, spread_total = lax.psum((loss_sum, spread_sum), ('blk', 'sub'))  31.6 us
    ppermute x6, waiting for transfers between devices, passed_along(): return lax.ppermute(block, axis, route)  16 us
    all_gather x1, blocking collectives, per_device(): lax.all_gather(student, 'sub', axis=0, tiled=True)  14.2 us
    another operation x1, loops' own time, per_device(): lax.fori_loop(1, blk_count, cycle_step, (teacher, student, running))  7.65 us
    dot_general x4, matrix products, score_pair(): lax.dot_general(home_teacher, visit_teacher, contract_last, preferred_ele...  6.26 us
    ppermute x6, starting transfers between devices, passed_along(): return lax.ppermute(block, axis, route)  3.41 us
  transfers between devices with their start and end apart: 8, of which 6 were waited for; matrix products, arithmetic and copies ran while one was open for 4% of the time, Pallas kernels for 0%

commit v1 on v0

v1 whole, which is shorter than its diff:
```python
import functools

import jax
import jax.numpy as jnp
from jax import lax
from jax.experimental import pallas as pl
from jax.experimental.pallas import tpu as pltpu
from jax.sharding import PartitionSpec as P

FLOOR = 0.01
EPSILON = 1e-06
LANES = 128
WHOLE = pl.BlockSpec(memory_space=pltpu.VMEM)


def exchange(value, axis, distance):
    size = lax.axis_size(axis)
    return lax.ppermute(value, axis, [(i, i ^ distance) for i in range(size)])


def shifted(value, axis, distance):
    size = lax.axis_size(axis)
    return lax.ppermute(value, axis, [(i, (i + distance) % size) for i in range(size)])


def stats_kernel(t_ref, s_ref, out_ref):
    t = t_ref[...].astype(jnp.float32)
    s = s_ref[...].astype(jnp.float32)
    t_width, s_width = t.shape[1], s.shape[1]
    out_ref[:, :t_width] = jnp.sum(t, axis=0, keepdims=True)
    out_ref[:, t_width : t_width + s_width] = jnp.sum(s, axis=0, keepdims=True)
    square_t = jnp.sum(jnp.sum(t * t, axis=0, keepdims=True), axis=1, keepdims=True)
    square_s = jnp.sum(jnp.sum(s * s, axis=0, keepdims=True), axis=1, keepdims=True)
    lane = lax.broadcasted_iota(jnp.int32, (1, LANES), 1)
    out_ref[:, t_width + s_width :] = jnp.where(
        lane == 0, square_t, jnp.where(lane == 1, square_s, 0.0)
    )


def spreads_of(stats, t_width, s_width, total_rows):
    centre_t = stats[:, :t_width] / total_rows
    centre_s = stats[:, t_width : t_width + s_width] / total_rows
    square_t = stats[:, t_width + s_width : t_width + s_width + 1]
    square_s = stats[:, t_width + s_width + 1 : t_width + s_width + 2]
    spread_t = (
        2.0 * (square_t / total_rows - jnp.sum(centre_t * centre_t, axis=1, keepdims=True)) + EPSILON
    )
    spread_s = (
        2.0 * (square_s / total_rows - jnp.sum(centre_s * centre_s, axis=1, keepdims=True)) + EPSILON
    )
    return spread_t, spread_s, centre_s


def column_norms(ref):
    value = ref[...].astype(jnp.float32)
    return jnp.sum(value * value, axis=1, keepdims=True)


def diagonal(rows):
    return lax.broadcasted_iota(jnp.int32, (rows, rows), 0) == lax.broadcasted_iota(
        jnp.int32, (rows, rows), 1
    )


def as_row(column):
    return jnp.sum(jnp.where(diagonal(column.shape[0]), column, 0.0), axis=0, keepdims=True)


def with_ones(ref):
    return jnp.concatenate([ref[...], jnp.ones((ref.shape[0], LANES), ref.dtype)], axis=1)


def pair_tile(v, c, inv_t, inv_s, own):
    (vt, vs, nvt, nvs), (ct, cs, nct, ncs) = v, c
    last = (((1,), (1,)), ((), ()))
    gram_t = lax.dot_general(vt[...], ct[...], last, preferred_element_type=jnp.float32)
    gram_s = lax.dot_general(vs[...], cs[...], last, preferred_element_type=jnp.float32)
    square_t = jnp.maximum(nvt + nct - 2.0 * gram_t, 0.0)
    square_s = jnp.maximum(nvs + ncs - 2.0 * gram_s, 0.0)
    under_t = square_t * inv_t + FLOOR
    under_s = square_s * inv_s + FLOOR
    inverse_s = lax.rsqrt(under_s)
    residue = under_s * inverse_s - under_t * lax.rsqrt(under_t)
    slope = jnp.clip(residue, -1.0, 1.0)
    huber = slope * (residue - 0.5 * slope)
    pull = slope * inverse_s
    if own:
        diag = diagonal(pull.shape[0])
        pull = jnp.where(diag, 0.0, pull)
        huber = jnp.where(diag, 0.0, huber)
    weights = (pull * inv_s).astype(jnp.bfloat16)
    return (
        weights,
        jnp.sum(huber, axis=0, keepdims=True),
        jnp.sum(pull * square_s, axis=0, keepdims=True),
    )


def direct_of(ref, summed):
    width = ref.shape[1]
    row_weight = summed[:, width:]
    spread_out = jnp.concatenate([row_weight] * (width // LANES), axis=1)
    return ref[...].astype(jnp.float32) * spread_out - summed[:, :width]


def early_kernel(n_blk, steps, total_rows, *refs):
    refs = list(refs)
    plane = [(refs.pop(0), refs.pop(0)) for _ in range(n_blk)]
    line = [plane[0]] + [(refs.pop(0), refs.pop(0)) for _ in range(steps - 1)]
    stats_refs = refs.pop(0), refs.pop(0)
    n_sub_stats = stats_refs[1].shape[0]
    own_ref = refs.pop(0)
    back_refs = [refs.pop(0) for _ in range(steps - 1)]
    acc_ref, norm_ref, total_ref, sums_ref = refs
    t_width, s_width = plane[0][0].shape[1], plane[0][1].shape[1]
    stats = stats_refs[0][...]
    for i in range(n_sub_stats):
        stats = stats + stats_refs[1][i]
    total_ref[...] = stats
    spread_t, spread_s, _ = spreads_of(stats, t_width, s_width, total_rows)
    inv_t, inv_s = 1.0 / spread_t, 1.0 / spread_s
    cols = []
    for d, (t, s) in enumerate(plane):
        nt, ns = as_row(column_norms(t)), as_row(column_norms(s))
        norm_ref[d : d + 1, :LANES] = nt
        norm_ref[d : d + 1, LANES:] = ns
        cols.append((t, s, nt, ns))
    loss = jnp.zeros((1, LANES), jnp.float32)
    spread = jnp.zeros((1, LANES), jnp.float32)
    for k, (t, s) in enumerate(line):
        v = (t, s, column_norms(t), column_norms(s))
        summed = None
        for d in range(n_blk):
            weights, loss_part, spread_part = pair_tile(v, cols[d], inv_t, inv_s, k == 0 and d == 0)
            factor = 1.0 if k == 0 else 2.0
            loss = loss + factor * loss_part
            spread = spread + factor * spread_part
            term = jnp.dot(weights, with_ones(cols[d][1]), preferred_element_type=jnp.float32)
            summed = term if summed is None else summed + term
            if k > 0:
                back = lax.dot_general(
                    weights,
                    with_ones(s),
                    (((0,), (0,)), ((), ())),
                    preferred_element_type=jnp.float32,
                )
                acc_ref[d] = back if k == 1 else acc_ref[d] + back
        if k == 0:
            own_ref[...] = direct_of(s, summed)
        else:
            back_refs[k - 1][...] = direct_of(s, summed)
    if steps == 1:
        acc_ref[...] = jnp.zeros_like(acc_ref)
    sums_ref[0:1, :] = loss
    sums_ref[1:2, :] = spread


def late_kernel(n_blk, total_rows, *refs):
    refs = list(refs)
    plane = [(refs.pop(0), refs.pop(0)) for _ in range(n_blk)]
    t, s, stats_ref, acc_ref, norm_ref, early_sums = (refs.pop(0) for _ in range(6))
    out_refs = [refs.pop(0) for _ in range(n_blk)]
    (sums_ref,) = refs
    t_width, s_width = t.shape[1], s.shape[1]
    spread_t, spread_s, _ = spreads_of(stats_ref[...], t_width, s_width, total_rows)
    inv_t, inv_s = 1.0 / spread_t, 1.0 / spread_s
    v = (t, s, column_norms(t), column_norms(s))
    loss = early_sums[0:1, :]
    spread = early_sums[1:2, :]
    for d in range(n_blk):
        ct, cs = plane[d]
        c = (ct, cs, norm_ref[d : d + 1, :LANES], norm_ref[d : d + 1, LANES:])
        weights, loss_part, spread_part = pair_tile(v, c, inv_t, inv_s, False)
        loss = loss + loss_part
        spread = spread + spread_part
        back = lax.dot_general(
            weights, with_ones(s), (((0,), (0,)), ((), ())), preferred_element_type=jnp.float32
        )
        out_refs[d][...] = direct_of(cs, acc_ref[d] + back)
    sums_ref[0:1, :] = loss
    sums_ref[1:2, :] = spread


def final_kernel(n_parts, n_sums, total_rows, *refs):
    refs = list(refs)
    student_ref, stats_ref = refs.pop(0), refs.pop(0)
    parts = [refs.pop(0) for _ in range(n_parts)]
    sums = [refs.pop(0) for _ in range(n_sums)]
    grad_ref, loss_ref = refs
    s_width = student_ref.shape[1]
    t_width = stats_ref.shape[1] - s_width - LANES
    direct = parts[0][...]
    for part in parts[1:]:
        direct = direct + part[...]
    both = sums[0][...]
    for one in sums[1:]:
        both = both + one[...]
    both = jnp.sum(both, axis=1, keepdims=True)
    loss_total, spread_total = both[0:1, :], -both[1:2, :]
    _, spread_s, centre = spreads_of(stats_ref[...], t_width, s_width, total_rows)
    pairs = total_rows * (total_rows - 1.0)
    correction = 2.0 * spread_total / (pairs * spread_s * spread_s)
    grad_ref[...] = (2.0 / (total_rows - 1.0)) * direct + correction * (
        student_ref[...].astype(jnp.float32) - centre
    )
    loss_ref[...] = jnp.broadcast_to(loss_total / pairs, loss_ref.shape)


def call(kernel, out_shape, operands, flops):
    nbytes = sum(x.size * x.dtype.itemsize for x in operands)
    return pl.pallas_call(
        kernel,
        out_shape=out_shape,
        in_specs=[WHOLE] * len(operands),
        out_specs=jax.tree.map(lambda _: WHOLE, out_shape),
        compiler_params=pltpu.CompilerParams(vmem_limit_bytes=48 * 1024 * 1024),
        cost_estimate=pl.CostEstimate(flops=flops, bytes_accessed=nbytes, transcendentals=0),
    )(*operands)


def per_device(teacher, student):
    rows, t_width = teacher.shape
    s_width = student.shape[1]
    n_blk = lax.axis_size("blk")
    n_sub = lax.axis_size("sub")
    total_rows = float(rows * n_blk * n_sub)
    half = n_sub // 2
    f32 = functools.partial(jax.ShapeDtypeStruct, dtype=jnp.float32)

    line = [(teacher, student)]
    for _ in range(half):
        line.append(tuple(shifted(x, "sub", 1) for x in line[-1]))
    plane = [(teacher, student)]
    for d in range(1, n_blk):
        plane.append(tuple(exchange(x, "blk", d) for x in (teacher, student)))

    stats = call(
        stats_kernel, f32((1, t_width + s_width + LANES)), (teacher, student), 4 * teacher.size
    )
    for_plane = stats
    for d in range(1, n_blk):
        for_plane = for_plane + exchange(stats, "blk", d)
    others = [exchange(for_plane, "sub", d) for d in range(1, n_sub)]

    pair_flops = 2 * rows * rows * n_blk * (t_width + 3 * s_width)
    flat_plane = [x for pair in plane for x in pair]
    flat_line = [x for pair in line[1:half] for x in pair]
    out_shape = (
        [f32((rows, s_width))] * half
        + [f32((n_blk, rows, s_width + LANES)), f32((n_blk, 2 * LANES))]
        + [f32(stats.shape), f32((2, LANES))]
    )
    *tiles, acc, norms, totals, early_sums = call(
        functools.partial(early_kernel, n_blk, half, total_rows),
        out_shape,
        flat_plane + flat_line + [for_plane, jnp.stack(others)],
        half * pair_flops,
    )
    own, backs = tiles[0], tiles[1:]
    returned = [shifted(x, "sub", -k) for k, x in enumerate(backs, 1)]
    *shares, sums = call(
        functools.partial(late_kernel, n_blk, total_rows),
        [f32((rows, s_width))] * n_blk + [f32((2, LANES))],
        flat_plane + list(line[half]) + [totals, acc, norms, early_sums],
        pair_flops,
    )
    plane_sums = sums
    for d in range(1, n_blk):
        plane_sums = plane_sums + exchange(sums, "blk", d)
    all_sums = [plane_sums] + [exchange(plane_sums, "sub", d) for d in range(1, n_sub)]
    received = [exchange(shares[d], "blk", d) for d in range(1, n_blk)]
    parts = [own, shares[0]] + returned + received
    grad, loss = call(
        functools.partial(final_kernel, len(parts), len(all_sums), total_rows),
        [f32((rows, s_width)), f32((1, LANES))],
        [student, totals] + parts + all_sums,
        8 * student.size,
    )
    return grad, loss[0, :1]


def solution(mesh):
    placed = P(("groups", "blk", "sub"), None)
    return jax.shard_map(
        per_device,
        mesh=mesh,
        in_specs=(placed, placed),
        out_specs=(placed, P("groups")),
        check_vma=False,
    )
```

time: 151 us -> 62.4 us (0.41)
  blocking collectives: 83.7 us -> 0 us
  starting transfers between devices: 3.49 us -> 24.6 us
  between operations: 19.8 us -> 0.71 us
  waiting for transfers between devices: 16 us -> 29.4 us
  other arithmetic: 9.7 us -> 0.04 us
  matrix products: 8.49 us -> 0 us
  loops' own time: 7.65 us -> 0 us
  Pallas kernels: 0 us -> 5.66 us
    psum x2 -> x0, blocking collectives: 69.5 us -> none  [the longest x1 37.9 us: per_device(): lax.psum((square_t, column_t, square_s, column_s), ('blk', 'sub'))]
    ppermute x6 -> x26, starting transfers between devices: 3.41 us -> 24.6 us  [the longest x21 18.2 us: exchange(): return lax.ppermute(value, axis, [(i, i ^ distance) for i in range(size)])]
    all_gather x1 -> x0, blocking collectives: 14.2 us -> none  [per_device(): lax.all_gather(student, 'sub', axis=0, tiled=True)]
    ppermute x6 -> x26, waiting for transfers between devices: 16 us -> 29.4 us  [the longest x21 26.6 us: exchange(): return lax.ppermute(value, axis, [(i, i ^ distance) for i in range(size)])]
    dot_general x12 -> x0, matrix products: 8.49 us -> none  [the longest x4 6.26 us: score_pair(): lax.dot_general(home_teacher, visit_teacher, contract_last, preferred_ele...]
    another operation x1 -> x0, loops' own time: 7.65 us -> none  [per_device(): lax.fori_loop(1, blk_count, cycle_step, (teacher, student, running))]
    reduce_sum x11 -> x0, other arithmetic: 6.38 us -> none  [the longest x4 2.12 us: score_pair(): jnp.sum(float_visit_teacher * float_visit_teacher, axis=1)]
    pallas_call x0 -> x4, Pallas kernels: none -> 5.66 us  [call(): pl.pallas_call(kernel, out_shape=out_shape, in_specs=[WHOLE] * len(operan...]
  transfers between devices with their start and end apart: 8 -> 26, of which waited for: 6 -> 10; matrix products, arithmetic and copies ran while one was open for 4% -> 0% of each run, Pallas kernels for 0% -> 5%
where the time goes in v1:
time: 62.4 us; the launch traced here: 62.2 us
  waiting for transfers between devices  29.4 us (47%)
  starting transfers between devices  24.6 us (39%)
  Pallas kernels  5.66 us (9%)
  local copies, waits for them, and re-layouts  1.84 us (3%)
  between operations  0.71 us (1%)
    ppermute x21, waiting for transfers between devices, exchange(): return lax.ppermute(value, axis, [(i, i ^ distance) for i in range(size)])  26.6 us
    ppermute x21, starting transfers between devices, exchange(): return lax.ppermute(value, axis, [(i, i ^ distance) for i in range(size)])  18.2 us
    ppermute x5, starting transfers between devices, shifted(): lax.ppermute(value, axis, [(i, (i + distance) % size) for i in range(size)])  6.37 us
    pallas_call x4, Pallas kernels, call(): pl.pallas_call(kernel, out_shape=out_shape, in_specs=[WHOLE] * len(operan...  5.66 us
    ppermute x5, waiting for transfers between devices, shifted(): lax.ppermute(value, axis, [(i, (i + distance) % size) for i in range(size)])  2.75 us
    unnamed x6, local copies, waits for them, and re-layouts  1.84 us
  transfers between devices with their start and end apart: 26, of which 10 were waited for; matrix products, arithmetic and copies ran while one was open for 0% of the time, Pallas kernels for 5%

profile of v1, /device:TPU:0, one launch (start us, length us, event | category | flops | bytes accessed | tf_op | source)
XLA Modules:
  0.0 62.2 jit_solution(10217755051592735301)
XLA Ops:
  0.6 0.9 %copy-done = bf16[128,1024]{1,0:T(8,128)(2,1)S(1)} copy-done((bf16[128,1024]{1,0:T(8,128)(2,1)S(1)}, bf16[128,1024]{1,0:T(8,128)(2,1)}, u32[]{:S(2)}) %copy-start) | copy-done | bytes 262168
  1.6 0.9 %copy-done.1 = bf16[128,384]{1,0:T(8,128)(2,1)S(1)} copy-done((bf16[128,384]{1,0:T(8,128)(2,1)S(1)}, bf16[128,384]{1,0:T(8,128)(2,1)}, u32[]{:S(2)}) %copy-start.1) | copy-done | bytes 98328
  2.6 2.4 %collective-permute-start.10 = (f32[1,1536]{1,0:T(1,128)S(1)}, f32[1,1536]{1,0:T(1,128)S(1)}, u32[]{:S(2)}, u32[]{:S(2)}) collective-permute-start(f32[1,1536]{1,0:T(1,128)S(1)} %shard_map.41), channel_id=1, source_target_pairs={{0,12},{4,8},{8,4},{12,0},{1,13},{5,9},{9,5},{13,1},{2,14},{6,10},... | collective-permute-start | bytes 18440 | tf_op jit(solution)/shard_map/ppermute | solution.py:18
  5.0 0.6 %collective-permute-start.9 = (f32[1,1536]{1,0:T(1,128)S(1)}, f32[1,1536]{1,0:T(1,128)S(1)}, u32[]{:S(2)}, u32[]{:S(2)}) collective-permute-start(f32[1,1536]{1,0:T(1,128)S(1)} %shard_map.41), channel_id=1, source_target_pairs={{0,8},{4,12},{8,0},{12,4},{1,9},{5,13},{9,1},{13,5},{2,10},{6,14},... | collective-permute-start | bytes 18440 | tf_op jit(solution)/shard_map/ppermute | solution.py:18
  5.7 1.8 %collective-permute-start.7 = (bf16[128,384]{1,0:T(8,128)(2,1)S(1)}, bf16[128,384]{1,0:T(8,128)(2,1)S(1)}, u32[]{:S(2)}, u32[]{:S(2)}) collective-permute-start(bf16[128,384]{1,0:T(8,128)(2,1)S(1)} %copy-done.1), channel_id=1, source_target_pairs={{0,1},{1,2},{2,3},{3,0},{4,5},{5,6},{6,7},{7,4},{8,9},{9,10},{10,1... | collective-permute-start | bytes 294920 | tf_op jit(solution)/shard_map/ppermute | solution.py:23
  7.5 1.0 %collective-permute-start.5 = (bf16[128,384]{1,0:T(8,128)(2,1)S(1)}, bf16[128,384]{1,0:T(8,128)(2,1)S(1)}, u32[]{:S(2)}, u32[]{:S(2)}) collective-permute-start(bf16[128,384]{1,0:T(8,128)(2,1)S(1)} %copy-done.1), channel_id=1, source_target_pairs={{0,12},{4,8},{8,4},{12,0},{1,13},{5,9},{9,5},{13,1},{2,14},{6,10},... | collective-permute-start | bytes 294920 | tf_op jit(solution)/shard_map/ppermute | solution.py:18
  8.5 0.6 %collective-permute-start.3 = (bf16[128,384]{1,0:T(8,128)(2,1)S(1)}, bf16[128,384]{1,0:T(8,128)(2,1)S(1)}, u32[]{:S(2)}, u32[]{:S(2)}) collective-permute-start(bf16[128,384]{1,0:T(8,128)(2,1)S(1)} %copy-done.1), channel_id=1, source_target_pairs={{0,8},{4,12},{8,0},{12,4},{1,9},{5,13},{9,1},{13,5},{2,10},{6,14},... | collective-permute-start | bytes 294920 | tf_op jit(solution)/shard_map/ppermute | solution.py:18
  9.1 1.6 %collective-permute-start.6 = (bf16[128,1024]{1,0:T(8,128)(2,1)S(1)}, bf16[128,1024]{1,0:T(8,128)(2,1)S(1)}, u32[]{:S(2)}, u32[]{:S(2)}) collective-permute-start(bf16[128,1024]{1,0:T(8,128)(2,1)S(1)} %copy-done), channel_id=1, source_target_pairs={{0,1},{1,2},{2,3},{3,0},{4,5},{5,6},{6,7},{7,4},{8,9},{9,10},{10,1... | collective-permute-start | bytes 786440 | tf_op jit(solution)/shard_map/ppermute | solution.py:23
  10.7 2.3 %collective-permute-start.13 = (f32[1,1536]{1,0:T(1,128)S(1)}, f32[1,1536]{1,0:T(1,128)S(1)}, u32[]{:S(2)}, u32[]{:S(2)}) collective-permute-start(f32[1,1536]{1,0:T(1,128)S(1)} %add_add_fusion.refs_10_), channel_id=1, source_target_pairs={{0,3},{1,2},{2,1},{3,0},{4,7},{5,6},{6,5},{7,4},{8,11},{9,10},{10,... | collective-permute-start | bytes 18440 | tf_op jit(solution)/shard_map/ppermute | solution.py:18
  13.0 6.6 %collective-permute-done.13 = f32[1,1536]{1,0:T(1,128)S(1)} collective-permute-done((f32[1,1536]{1,0:T(1,128)S(1)}, f32[1,1536]{1,0:T(1,128)S(1)}, u32[]{:S(2)}, u32[]{:S(2)}) %collective-permute-start.13) | collective-permute-done | bytes 6176 | tf_op jit(solution)/shard_map/ppermute | solution.py:18
  19.6 0.8 %collective-permute-start.12 = (f32[1,1536]{1,0:T(1,128)S(1)}, f32[1,1536]{1,0:T(1,128)S(1)}, u32[]{:S(2)}, u32[]{:S(2)}) collective-permute-start(f32[1,1536]{1,0:T(1,128)S(1)} %add_add_fusion.refs_10_), channel_id=1, source_target_pairs={{0,2},{1,3},{2,0},{3,1},{4,6},{5,7},{6,4},{7,5},{8,10},{9,11},{10,... | collective-permute-start | bytes 18440 | tf_op jit(solution)/shard_map/ppermute | solution.py:18
  20.5 3.7 %collective-permute-done.12 = f32[1,1536]{1,0:T(1,128)S(1)} collective-permute-done((f32[1,1536]{1,0:T(1,128)S(1)}, f32[1,1536]{1,0:T(1,128)S(1)}, u32[]{:S(2)}, u32[]{:S(2)}) %collective-permute-start.12) | collective-permute-done | bytes 6176 | tf_op jit(solution)/shard_map/ppermute | solution.py:18
  24.2 0.6 collective-permute-start.11
  24.8 3.0 %collective-permute-done.11 = f32[1,1536]{1,0:T(1,128)S(1)} collective-permute-done((f32[1,1536]{1,0:T(1,128)S(1)}, f32[1,1536]{1,0:T(1,128)S(1)}, u32[]{:S(2)}, u32[]{:S(2)}) %collective-permute-start.11) | collective-permute-done | bytes 6176 | tf_op jit(solution)/shard_map/ppermute | solution.py:18
  27.8 1.7 %collective-permute-start.4 = (bf16[128,1024]{1,0:T(8,128)(2,1)S(1)}, bf16[128,1024]{1,0:T(8,128)(2,1)S(1)}, u32[]{:S(2)}, u32[]{:S(2)}) collective-permute-start(bf16[128,1024]{1,0:T(8,128)(2,1)S(1)} %copy-done), channel_id=1, source_target_pairs={{0,12},{4,8},{8,4},{12,0},{1,13},{5,9},{9,5},{13,1},{2,14},{6,10},... | collective-permute-start | bytes 786440 | tf_op jit(solution)/shard_map/ppermute | solution.py:18
  30.0 0.7 %collective-permute-start.15 = (bf16[128,384]{1,0:T(8,128)(2,1)S(1)}, bf16[128,384]{1,0:T(8,128)(2,1)S(1)}, u32[]{:S(2)}, u32[]{:S(2)}) collective-permute-start(bf16[128,384]{1,0:T(8,128)(2,1)S(1)} %collective-permute-done.7.refs_9_), channel_id=1, source_target_pairs={{0,1},{1,2},{2,3},{3,0},{4,5},{5,6},{6,7},{7,4},{8,9},{9,10},{10,1... | collective-permute-start | bytes 294920 | tf_op jit(solution)/shard_map/ppermute | solution.py:23
  30.6 0.8 %collective-permute-start.14 = (bf16[128,1024]{1,0:T(8,128)(2,1)S(1)}, bf16[128,1024]{1,0:T(8,128)(2,1)S(1)}, u32[]{:S(2)}, u32[]{:S(2)}) collective-permute-start(bf16[128,1024]{1,0:T(8,128)(2,1)S(1)} %collective-permute-done.6.refs_8_), channel_id=1, source_target_pairs={{0,1},{1,2},{2,3},{3,0},{4,5},{5,6},{6,7},{7,4},{8,9},{9,10},{10,1... | collective-permute-start | bytes 786440 | tf_op jit(solution)/shard_map/ppermute | solution.py:23
  31.4 4.7 %collective-permute-done.4.refs_6_ = bf16[128,1024]{1,0:T(8,128)(2,1)S(1)} collective-permute-done((bf16[128,1024]{1,0:T(8,128)(2,1)S(1)}, bf16[128,1024]{1,0:T(8,128)(2,1)S(1)}, u32[]{:S(2)}, u32[]{:S(2)}) %collective-permute-start.4) | collective-permute-done | bytes 262176 | tf_op jit(solution)/shard_map/ppermute | solution.py:18
  36.1 5.9 %collective-permute-done.2.refs_4_ = bf16[128,1024]{1,0:T(8,128)(2,1)S(1)} collective-permute-done((bf16[128,1024]{1,0:T(8,128)(2,1)S(1)}, bf16[128,1024]{1,0:T(8,128)(2,1)S(1)}, u32[]{:S(2)}, u32[]{:S(2)}) %collective-permute-start.2) | collective-permute-done | bytes 262176 | tf_op jit(solution)/shard_map/ppermute | solution.py:18
  42.0 2.9 %shard_map.42 = (f32[128,384]{1,0:T(8,128)S(1)}, f32[128,384]{1,0:T(8,128)S(1)}, f32[4,128,512]{2,1,0:T(8,128)S(1)}, f32[4,256]{1,0:T(4,128)S(1)}, f32[1,1536]{1,0:T(1,128)S(1)}, /*index=5*/f32[2,128]{1,0:T(2,128)S(1)}) custom-call(bf16[128,1024]{1,0:T(8,128)(2,1)S(1)} %copy-done, bf16[128,384]{1,0:T(8,128)(2,1)S(1)} %copy-done.1, ...), custom_call_target="tpu_custom_call" | custom-call | flops 570425344 | bytes 1826816 | tf_op jit(solution)/shard_map/pallas_call | solution.py:211
  45.0 1.8 %shard_map.43 = (f32[128,384]{1,0:T(8,128)S(1)}, f32[128,384]{1,0:T(8,128)S(1)}, f32[128,384]{1,0:T(8,128)S(1)}, f32[128,384]{1,0:T(8,128)S(1)}, f32[2,128]{1,0:T(2,128)S(1)}) custom-call(bf16[128,1024]{1,0:T(8,128)(2,1)S(1)} %copy-done, bf16[128,384]{1,0:T(8,128)(2,1)S(1)} %copy-done.1, bf16[128,1024]{1,0:T(8,128)(2,1)S(1)} %collective-permute-done.refs_2_, ...), custom_call_target="tpu_custom_call" | custom-call | flops 285212672 | bytes 2862080 | tf_op jit(solution)/shard_map/pallas_call | solution.py:211
  46.7 0.7 %collective-permute-start.22 = (f32[2,128]{1,0:T(2,128)S(1)}, f32[2,128]{1,0:T(2,128)S(1)}, u32[]{:S(2)}, u32[]{:S(2)}) collective-permute-start(f32[2,128]{1,0:T(2,128)S(1)} %get-tuple-element.25), channel_id=1, source_target_pairs={{0,12},{4,8},{8,4},{12,0},{1,13},{5,9},{9,5},{13,1},{2,14},{6,10},... | collective-permute-start | bytes 3080 | tf_op jit(solution)/shard_map/ppermute | solution.py:18
  47.4 1.0 %collective-permute-start.21 = (f32[2,128]{1,0:T(2,128)S(1)}, f32[2,128]{1,0:T(2,128)S(1)}, u32[]{:S(2)}, u32[]{:S(2)}) collective-permute-start(f32[2,128]{1,0:T(2,128)S(1)} %get-tuple-element.25), channel_id=1, source_target_pairs={{0,8},{4,12},{8,0},{12,4},{1,9},{5,13},{9,1},{13,5},{2,10},{6,14},... | collective-permute-start | bytes 3080 | tf_op jit(solution)/shard_map/ppermute | solution.py:18
  48.7 1.6 %collective-permute-start.16 = (f32[128,384]{1,0:T(8,128)S(1)}, f32[128,384]{1,0:T(8,128)S(1)}, u32[]{:S(2)}, u32[]{:S(2)}) collective-permute-start(f32[128,384]{1,0:T(8,128)S(1)} %get-tuple-element.21), channel_id=1, source_target_pairs={{0,3},{1,0},{2,1},{3,2},{4,7},{5,4},{6,5},{7,6},{8,11},{9,8},{10,9... | collective-permute-start | bytes 589832 | tf_op jit(solution)/shard_map/ppermute | solution.py:23
  50.2 1.6 %collective-permute-start.18 = (f32[128,384]{1,0:T(8,128)S(1)}, f32[128,384]{1,0:T(8,128)S(1)}, u32[]{:S(2)}, u32[]{:S(2)}) collective-permute-start(f32[128,384]{1,0:T(8,128)S(1)} %get-tuple-element.23), channel_id=1, source_target_pairs={{0,8},{4,12},{8,0},{12,4},{1,9},{5,13},{9,1},{13,5},{2,10},{6,14},... | collective-permute-start | bytes 589832 | tf_op jit(solution)/shard_map/ppermute | solution.py:18
  52.1 0.9 %collective-permute-start.25 = (f32[2,128]{1,0:T(2,128)S(1)}, f32[2,128]{1,0:T(2,128)S(1)}, u32[]{:S(2)}, u32[]{:S(2)}) collective-permute-start(f32[2,128]{1,0:T(2,128)S(1)} %add_add_fusion.1.refs_8_), channel_id=1, source_target_pairs={{0,3},{1,2},{2,1},{3,0},{4,7},{5,6},{6,5},{7,4},{8,11},{9,10},{10,... | collective-permute-start | bytes 3080 | tf_op jit(solution)/shard_map/ppermute | solution.py:18
  53.0 2.7 %collective-permute-done.16.refs_4_ = f32[128,384]{1,0:T(8,128)S(1)} collective-permute-done((f32[128,384]{1,0:T(8,128)S(1)}, f32[128,384]{1,0:T(8,128)S(1)}, u32[]{:S(2)}, u32[]{:S(2)}) %collective-permute-start.16) | collective-permute-done | bytes 196640 | tf_op jit(solution)/shard_map/ppermute | solution.py:23
  55.7 0.8 %collective-permute-start.24 = (f32[2,128]{1,0:T(2,128)S(1)}, f32[2,128]{1,0:T(2,128)S(1)}, u32[]{:S(2)}, u32[]{:S(2)}) collective-permute-start(f32[2,128]{1,0:T(2,128)S(1)} %add_add_fusion.1.refs_8_), channel_id=1, source_target_pairs={{0,2},{1,3},{2,0},{3,1},{4,6},{5,7},{6,4},{7,5},{8,10},{9,11},{10,... | collective-permute-start | bytes 3080 | tf_op jit(solution)/shard_map/ppermute | solution.py:18
  56.6 1.0 %collective-permute-done.25.refs_11_ = f32[2,128]{1,0:T(2,128)S(1)} collective-permute-done((f32[2,128]{1,0:T(2,128)S(1)}, f32[2,128]{1,0:T(2,128)S(1)}, u32[]{:S(2)}, u32[]{:S(2)}) %collective-permute-start.25) | collective-permute-done | bytes 1056 | tf_op jit(solution)/shard_map/ppermute | solution.py:18
  57.5 2.2 %collective-permute-start.23 = (f32[2,128]{1,0:T(2,128)S(1)}, f32[2,128]{1,0:T(2,128)S(1)}, u32[]{:S(2)}, u32[]{:S(2)}) collective-permute-start(f32[2,128]{1,0:T(2,128)S(1)} %add_add_fusion.1.refs_8_), channel_id=1, source_target_pairs={{0,1},{1,0},{2,3},{3,2},{4,5},{5,4},{6,7},{7,6},{8,9},{9,8},{10,11... | collective-permute-start | bytes 3080 | tf_op jit(solution)/shard_map/ppermute | solution.py:18
  60.2 1.0 %collective-permute-done.23.refs_9_ = f32[2,128]{1,0:T(2,128)S(1)} collective-permute-done((f32[2,128]{1,0:T(2,128)S(1)}, f32[2,128]{1,0:T(2,128)S(1)}, u32[]{:S(2)}, u32[]{:S(2)}) %collective-permute-start.23) | collective-permute-done | bytes 1056 | tf_op jit(solution)/shard_map/ppermute | solution.py:18
  61.4 0.8 %shard_map.44 = (f32[128,384]{1,0:T(8,128)}, f32[1,128]{1,0:T(1,128)}) custom-call(bf16[128,384]{1,0:T(8,128)(2,1)S(1)} %copy-done.2, f32[1,1536]{1,0:T(1,128)S(1)} %get-tuple-element.15.refs_10_.refs_1_, f32[128,384]{1,0:T(8,128)S(1)} %get-tuple-element.16.refs_2_, f32[128,384]{1,0:T(8,128)S(1)} %get-tuple-element.20.refs_3_, ...), custom_call_target="tpu_custom_call" | custom-call | flops 393216 | bytes 1288192 | tf_op jit(solution)/shard_map/pallas_call | solution.py:211
  (33 shorter events, 1.9 us)
Async XLA Ops:
  0.6 1.0 %copy-start = (bf16[128,1024]{1,0:T(8,128)(2,1)S(1)}, bf16[128,1024]{1,0:T(8,128)(2,1)}, u32[]{:S(2)}) copy-start(bf16[128,1024]{1,0:T(8,128)(2,1)} %refs_0_.4) | copy-start | bytes 786436
  1.6 0.9 %copy-start.1 = (bf16[128,384]{1,0:T(8,128)(2,1)S(1)}, bf16[128,384]{1,0:T(8,128)(2,1)}, u32[]{:S(2)}) copy-start(bf16[128,384]{1,0:T(8,128)(2,1)} %refs_0_.5) | copy-start | bytes 294916
  2.6 5.8 %collective-permute-start.10 = (f32[1,1536]{1,0:T(1,128)S(1)}, f32[1,1536]{1,0:T(1,128)S(1)}, u32[]{:S(2)}, u32[]{:S(2)}) collective-permute-start(f32[1,1536]{1,0:T(1,128)S(1)} %shard_map.41), channel_id=1, source_target_pairs={{0,12},{4,8},{8,4},{12,0},{1,13},{5,9},{9,5},{13,1},{2,14},{6,10},... | collective-permute-start | bytes 18440 | tf_op jit(solution)/shard_map/ppermute | solution.py:18
  5.0 4.1 %collective-permute-start.9 = (f32[1,1536]{1,0:T(1,128)S(1)}, f32[1,1536]{1,0:T(1,128)S(1)}, u32[]{:S(2)}, u32[]{:S(2)}) collective-permute-start(f32[1,1536]{1,0:T(1,128)S(1)} %shard_map.41), channel_id=1, source_target_pairs={{0,8},{4,12},{8,0},{12,4},{1,9},{5,13},{9,1},{13,5},{2,10},{6,14},... | collective-permute-start | bytes 18440 | tf_op jit(solution)/shard_map/ppermute | solution.py:18
  5.7 5.0 %collective-permute-start.8 = (f32[1,1536]{1,0:T(1,128)S(1)}, f32[1,1536]{1,0:T(1,128)S(1)}, u32[]{:S(2)}, u32[]{:S(2)}) collective-permute-start(f32[1,1536]{1,0:T(1,128)S(1)} %shard_map.41), channel_id=1, source_target_pairs={{0,4},{4,0},{8,12},{12,8},{1,5},{5,1},{9,13},{13,9},{2,6},{6,2},{1... | collective-permute-start | bytes 18440 | tf_op jit(solution)/shard_map/ppermute | solution.py:18
  5.7 22.1 %collective-permute-start.7 = (bf16[128,384]{1,0:T(8,128)(2,1)S(1)}, bf16[128,384]{1,0:T(8,128)(2,1)S(1)}, u32[]{:S(2)}, u32[]{:S(2)}) collective-permute-start(bf16[128,384]{1,0:T(8,128)(2,1)S(1)} %copy-done.1), channel_id=1, source_target_pairs={{0,1},{1,2},{2,3},{3,0},{4,5},{5,6},{6,7},{7,4},{8,9},{9,10},{10,1... | collective-permute-start | bytes 294920 | tf_op jit(solution)/shard_map/ppermute | solution.py:23
  7.5 22.0 %collective-permute-start.5 = (bf16[128,384]{1,0:T(8,128)(2,1)S(1)}, bf16[128,384]{1,0:T(8,128)(2,1)S(1)}, u32[]{:S(2)}, u32[]{:S(2)}) collective-permute-start(bf16[128,384]{1,0:T(8,128)(2,1)S(1)} %copy-done.1), channel_id=1, source_target_pairs={{0,12},{4,8},{8,4},{12,0},{1,13},{5,9},{9,5},{13,1},{2,14},{6,10},... | collective-permute-start | bytes 294920 | tf_op jit(solution)/shard_map/ppermute | solution.py:18
  8.5 21.5 %collective-permute-start.3 = (bf16[128,384]{1,0:T(8,128)(2,1)S(1)}, bf16[128,384]{1,0:T(8,128)(2,1)S(1)}, u32[]{:S(2)}, u32[]{:S(2)}) collective-permute-start(bf16[128,384]{1,0:T(8,128)(2,1)S(1)} %copy-done.1), channel_id=1, source_target_pairs={{0,8},{4,12},{8,0},{12,4},{1,9},{5,13},{9,1},{13,5},{2,10},{6,14},... | collective-permute-start | bytes 294920 | tf_op jit(solution)/shard_map/ppermute | solution.py:18
  9.1 21.5 %collective-permute-start.6 = (bf16[128,1024]{1,0:T(8,128)(2,1)S(1)}, bf16[128,1024]{1,0:T(8,128)(2,1)S(1)}, u32[]{:S(2)}, u32[]{:S(2)}) collective-permute-start(bf16[128,1024]{1,0:T(8,128)(2,1)S(1)} %copy-done), channel_id=1, source_target_pairs={{0,1},{1,2},{2,3},{3,0},{4,5},{5,6},{6,7},{7,4},{8,9},{9,10},{10,1... | collective-permute-start | bytes 786440 | tf_op jit(solution)/shard_map/ppermute | solution.py:23
  10.7 8.9 %collective-permute-start.13 = (f32[1,1536]{1,0:T(1,128)S(1)}, f32[1,1536]{1,0:T(1,128)S(1)}, u32[]{:S(2)}, u32[]{:S(2)}) collective-permute-start(f32[1,1536]{1,0:T(1,128)S(1)} %add_add_fusion.refs_10_), channel_id=1, source_target_pairs={{0,3},{1,2},{2,1},{3,0},{4,7},{5,6},{6,5},{7,4},{8,11},{9,10},{10,... | collective-permute-start | bytes 18440 | tf_op jit(solution)/shard_map/ppermute | solution.py:18
  19.6 4.5 %collective-permute-start.12 = (f32[1,1536]{1,0:T(1,128)S(1)}, f32[1,1536]{1,0:T(1,128)S(1)}, u32[]{:S(2)}, u32[]{:S(2)}) collective-permute-start(f32[1,1536]{1,0:T(1,128)S(1)} %add_add_fusion.refs_10_), channel_id=1, source_target_pairs={{0,2},{1,3},{2,0},{3,1},{4,6},{5,7},{6,4},{7,5},{8,10},{9,11},{10,... | collective-permute-start | bytes 18440 | tf_op jit(solution)/shard_map/ppermute | solution.py:18
  24.2 3.6 %collective-permute-start.11 = (f32[1,1536]{1,0:T(1,128)S(1)}, f32[1,1536]{1,0:T(1,128)S(1)}, u32[]{:S(2)}, u32[]{:S(2)}) collective-permute-start(f32[1,1536]{1,0:T(1,128)S(1)} %add_add_fusion.refs_10_), channel_id=1, source_target_pairs={{0,1},{1,0},{2,3},{3,2},{4,5},{5,4},{6,7},{7,6},{8,9},{9,8},{10,11... | collective-permute-start | bytes 18440 | tf_op jit(solution)/shard_map/ppermute | solution.py:18
  27.8 2.2 %collective-permute-start.1 = (bf16[128,384]{1,0:T(8,128)(2,1)S(1)}, bf16[128,384]{1,0:T(8,128)(2,1)S(1)}, u32[]{:S(2)}, u32[]{:S(2)}) collective-permute-start(bf16[128,384]{1,0:T(8,128)(2,1)S(1)} %copy-done.1), channel_id=1, source_target_pairs={{0,4},{4,0},{8,12},{12,8},{1,5},{5,1},{9,13},{13,9},{2,6},{6,2},{1... | collective-permute-start | bytes 294920 | tf_op jit(solution)/shard_map/ppermute | solution.py:18
  27.8 8.3 %collective-permute-start.4 = (bf16[128,1024]{1,0:T(8,128)(2,1)S(1)}, bf16[128,1024]{1,0:T(8,128)(2,1)S(1)}, u32[]{:S(2)}, u32[]{:S(2)}) collective-permute-start(bf16[128,1024]{1,0:T(8,128)(2,1)S(1)} %copy-done), channel_id=1, source_target_pairs={{0,12},{4,8},{8,4},{12,0},{1,13},{5,9},{9,5},{13,1},{2,14},{6,10},... | collective-permute-start | bytes 786440 | tf_op jit(solution)/shard_map/ppermute | solution.py:18
  29.5 12.6 %collective-permute-start.2 = (bf16[128,1024]{1,0:T(8,128)(2,1)S(1)}, bf16[128,1024]{1,0:T(8,128)(2,1)S(1)}, u32[]{:S(2)}, u32[]{:S(2)}) collective-permute-start(bf16[128,1024]{1,0:T(8,128)(2,1)S(1)} %copy-done), channel_id=1, source_target_pairs={{0,8},{4,12},{8,0},{12,4},{1,9},{5,13},{9,1},{13,5},{2,10},{6,14},... | collective-permute-start | bytes 786440 | tf_op jit(solution)/shard_map/ppermute | solution.py:18
  30.0 12.1 %collective-permute-start = (bf16[128,1024]{1,0:T(8,128)(2,1)S(1)}, bf16[128,1024]{1,0:T(8,128)(2,1)S(1)}, u32[]{:S(2)}, u32[]{:S(2)}) collective-permute-start(bf16[128,1024]{1,0:T(8,128)(2,1)S(1)} %copy-done), channel_id=1, source_target_pairs={{0,4},{4,0},{8,12},{12,8},{1,5},{5,1},{9,13},{13,9},{2,6},{6,2},{1... | collective-permute-start | bytes 786440 | tf_op jit(solution)/shard_map/ppermute | solution.py:18
  30.0 15.0 %collective-permute-start.15 = (bf16[128,384]{1,0:T(8,128)(2,1)S(1)}, bf16[128,384]{1,0:T(8,128)(2,1)S(1)}, u32[]{:S(2)}, u32[]{:S(2)}) collective-permute-start(bf16[128,384]{1,0:T(8,128)(2,1)S(1)} %collective-permute-done.7.refs_9_), channel_id=1, source_target_pairs={{0,1},{1,2},{2,3},{3,0},{4,5},{5,6},{6,7},{7,4},{8,9},{9,10},{10,1... | collective-permute-start | bytes 294920 | tf_op jit(solution)/shard_map/ppermute | solution.py:23
  30.6 14.3 %collective-permute-start.14 = (bf16[128,1024]{1,0:T(8,128)(2,1)S(1)}, bf16[128,1024]{1,0:T(8,128)(2,1)S(1)}, u32[]{:S(2)}, u32[]{:S(2)}) collective-permute-start(bf16[128,1024]{1,0:T(8,128)(2,1)S(1)} %collective-permute-done.6.refs_8_), channel_id=1, source_target_pairs={{0,1},{1,2},{2,3},{3,0},{4,5},{5,6},{6,7},{7,4},{8,9},{9,10},{10,1... | collective-permute-start | bytes 786440 | tf_op jit(solution)/shard_map/ppermute | solution.py:23
  45.0 16.4 %copy-start.2 = (bf16[128,384]{1,0:T(8,128)(2,1)S(1)}, bf16[128,384]{1,0:T(8,128)(2,1)}, u32[]{:S(2)}) copy-start(bf16[128,384]{1,0:T(8,128)(2,1)} %refs_0_.5) | copy-start | bytes 294916
  46.7 3.5 %collective-permute-start.22 = (f32[2,128]{1,0:T(2,128)S(1)}, f32[2,128]{1,0:T(2,128)S(1)}, u32[]{:S(2)}, u32[]{:S(2)}) collective-permute-start(f32[2,128]{1,0:T(2,128)S(1)} %get-tuple-element.25), channel_id=1, source_target_pairs={{0,12},{4,8},{8,4},{12,0},{1,13},{5,9},{9,5},{13,1},{2,14},{6,10},... | collective-permute-start | bytes 3080 | tf_op jit(solution)/shard_map/ppermute | solution.py:18
  47.4 4.4 %collective-permute-start.21 = (f32[2,128]{1,0:T(2,128)S(1)}, f32[2,128]{1,0:T(2,128)S(1)}, u32[]{:S(2)}, u32[]{:S(2)}) collective-permute-start(f32[2,128]{1,0:T(2,128)S(1)} %get-tuple-element.25), channel_id=1, source_target_pairs={{0,8},{4,12},{8,0},{12,4},{1,9},{5,13},{9,1},{13,5},{2,10},{6,14},... | collective-permute-start | bytes 3080 | tf_op jit(solution)/shard_map/ppermute | solution.py:18
  48.4 3.7 %collective-permute-start.20 = (f32[2,128]{1,0:T(2,128)S(1)}, f32[2,128]{1,0:T(2,128)S(1)}, u32[]{:S(2)}, u32[]{:S(2)}) collective-permute-start(f32[2,128]{1,0:T(2,128)S(1)} %get-tuple-element.25), channel_id=1, source_target_pairs={{0,4},{4,0},{8,12},{12,8},{1,5},{5,1},{9,13},{13,9},{2,6},{6,2},{1... | collective-permute-start | bytes 3080 | tf_op jit(solution)/shard_map/ppermute | solution.py:18
  48.7 7.1 %collective-permute-start.16 = (f32[128,384]{1,0:T(8,128)S(1)}, f32[128,384]{1,0:T(8,128)S(1)}, u32[]{:S(2)}, u32[]{:S(2)}) collective-permute-start(f32[128,384]{1,0:T(8,128)S(1)} %get-tuple-element.21), channel_id=1, source_target_pairs={{0,3},{1,0},{2,1},{3,2},{4,7},{5,4},{6,5},{7,6},{8,11},{9,8},{10,9... | collective-permute-start | bytes 589832 | tf_op jit(solution)/shard_map/ppermute | solution.py:23
  50.2 11.0 %collective-permute-start.17 = (f32[128,384]{1,0:T(8,128)S(1)}, f32[128,384]{1,0:T(8,128)S(1)}, u32[]{:S(2)}, u32[]{:S(2)}) collective-permute-start(f32[128,384]{1,0:T(8,128)S(1)} %get-tuple-element.22), channel_id=1, source_target_pairs={{0,4},{4,0},{8,12},{12,8},{1,5},{5,1},{9,13},{13,9},{2,6},{6,2},{1... | collective-permute-start | bytes 589832 | tf_op jit(solution)/shard_map/ppermute | solution.py:18
  50.2 11.0 %collective-permute-start.18 = (f32[128,384]{1,0:T(8,128)S(1)}, f32[128,384]{1,0:T(8,128)S(1)}, u32[]{:S(2)}, u32[]{:S(2)}) collective-permute-start(f32[128,384]{1,0:T(8,128)S(1)} %get-tuple-element.23), channel_id=1, source_target_pairs={{0,8},{4,12},{8,0},{12,4},{1,9},{5,13},{9,1},{13,5},{2,10},{6,14},... | collective-permute-start | bytes 589832 | tf_op jit(solution)/shard_map/ppermute | solution.py:18
  51.8 9.6 %collective-permute-start.19 = (f32[128,384]{1,0:T(8,128)S(1)}, f32[128,384]{1,0:T(8,128)S(1)}, u32[]{:S(2)}, u32[]{:S(2)}) collective-permute-start(f32[128,384]{1,0:T(8,128)S(1)} %get-tuple-element.24), channel_id=1, source_target_pairs={{0,12},{4,8},{8,4},{12,0},{1,13},{5,9},{9,5},{13,1},{2,14},{6,10},... | collective-permute-start | bytes 589832 | tf_op jit(solution)/shard_map/ppermute | solution.py:18
  52.1 5.4 %collective-permute-start.25 = (f32[2,128]{1,0:T(2,128)S(1)}, f32[2,128]{1,0:T(2,128)S(1)}, u32[]{:S(2)}, u32[]{:S(2)}) collective-permute-start(f32[2,128]{1,0:T(2,128)S(1)} %add_add_fusion.1.refs_8_), channel_id=1, source_target_pairs={{0,3},{1,2},{2,1},{3,0},{4,7},{5,6},{6,5},{7,4},{8,11},{9,10},{10,... | collective-permute-start | bytes 3080 | tf_op jit(solution)/shard_map/ppermute | solution.py:18
  55.7 4.5 %collective-permute-start.24 = (f32[2,128]{1,0:T(2,128)S(1)}, f32[2,128]{1,0:T(2,128)S(1)}, u32[]{:S(2)}, u32[]{:S(2)}) collective-permute-start(f32[2,128]{1,0:T(2,128)S(1)} %add_add_fusion.1.refs_8_), channel_id=1, source_target_pairs={{0,2},{1,3},{2,0},{3,1},{4,6},{5,7},{6,4},{7,5},{8,10},{9,11},{10,... | collective-permute-start | bytes 3080 | tf_op jit(solution)/shard_map/ppermute | solution.py:18
  57.5 3.7 %collective-permute-start.23 = (f32[2,128]{1,0:T(2,128)S(1)}, f32[2,128]{1,0:T(2,128)S(1)}, u32[]{:S(2)}, u32[]{:S(2)}) collective-permute-start(f32[2,128]{1,0:T(2,128)S(1)} %add_add_fusion.1.refs_8_), channel_id=1, source_target_pairs={{0,1},{1,0},{2,3},{3,2},{4,5},{5,4},{6,7},{7,6},{8,9},{9,8},{10,11... | collective-permute-start | bytes 3080 | tf_op jit(solution)/shard_map/ppermute | solution.py:18

commit v2 on v1

--- a/solution.py
+++ b/solution.py
@@ -23,18 +23,24 @@
     return lax.ppermute(value, axis, [(i, (i + distance) % size) for i in range(size)])
 
 
-def stats_kernel(t_ref, s_ref, out_ref):
-    t = t_ref[...].astype(jnp.float32)
-    s = s_ref[...].astype(jnp.float32)
-    t_width, s_width = t.shape[1], s.shape[1]
-    out_ref[:, :t_width] = jnp.sum(t, axis=0, keepdims=True)
-    out_ref[:, t_width : t_width + s_width] = jnp.sum(s, axis=0, keepdims=True)
-    square_t = jnp.sum(jnp.sum(t * t, axis=0, keepdims=True), axis=1, keepdims=True)
-    square_s = jnp.sum(jnp.sum(s * s, axis=0, keepdims=True), axis=1, keepdims=True)
+def pack_kernel(t_hbm, s_hbm, packed_ref, stats_ref, sems):
+    t_width, s_width = t_hbm.shape[1], s_hbm.shape[1]
+    copies = [
+        pltpu.make_async_copy(t_hbm, packed_ref.at[:, :t_width], sems.at[0]),
+        pltpu.make_async_copy(s_hbm, packed_ref.at[:, t_width:], sems.at[1]),
+    ]
+    for copy in copies:
+        copy.start()
+    for copy in copies:
+        copy.wait()
+    value = packed_ref[...].astype(jnp.float32)
+    squares = jnp.sum(value * value, axis=0, keepdims=True)
+    square_t = jnp.sum(squares[:, :t_width], axis=1, keepdims=True)
+    square_s = jnp.sum(squares[:, t_width:], axis=1, keepdims=True)
     lane = lax.broadcasted_iota(jnp.int32, (1, LANES), 1)
-    out_ref[:, t_width + s_width :] = jnp.where(
-        lane == 0, square_t, jnp.where(lane == 1, square_s, 0.0)
-    )
+    last = jnp.where(lane == 0, square_t, jnp.where(lane == 1, square_s, 0.0))
+    row = jnp.concatenate([jnp.sum(value, axis=0, keepdims=True), last], axis=1)
+    stats_ref[...] = jnp.broadcast_to(row[None], stats_ref.shape)
 
 
 def spreads_of(stats, t_width, s_width, total_rows):
@@ -49,6 +55,10 @@
         2.0 * (square_s / total_rows - jnp.sum(centre_s * centre_s, axis=1, keepdims=True)) + EPSILON
     )
     return spread_t, spread_s, centre_s
+
+
+def halves(ref, t_width):
+    return ref.at[:, :t_width], ref.at[:, t_width:]
 
 
 def column_norms(ref):
@@ -103,19 +113,15 @@
     return ref[...].astype(jnp.float32) * spread_out - summed[:, :width]
 
 
-def early_kernel(n_blk, steps, total_rows, *refs):
+def early_kernel(n_blk, steps, t_width, total_rows, *refs):
     refs = list(refs)
-    plane = [(refs.pop(0), refs.pop(0)) for _ in range(n_blk)]
-    line = [plane[0]] + [(refs.pop(0), refs.pop(0)) for _ in range(steps - 1)]
-    stats_refs = refs.pop(0), refs.pop(0)
-    n_sub_stats = stats_refs[1].shape[0]
-    own_ref = refs.pop(0)
+    plane = [halves(refs.pop(0), t_width) for _ in range(n_blk)]
+    line = [plane[0]] + [halves(refs.pop(0), t_width) for _ in range(steps - 1)]
+    stats_ref, own_ref = refs.pop(0), refs.pop(0)
     back_refs = [refs.pop(0) for _ in range(steps - 1)]
     acc_ref, norm_ref, total_ref, sums_ref = refs
-    t_width, s_width = plane[0][0].shape[1], plane[0][1].shape[1]
-    stats = stats_refs[0][...]
-    for i in range(n_sub_stats):
-        stats = stats + stats_refs[1][i]
+    s_width = plane[0][1].shape[1]
+    stats = jnp.sum(stats_ref[...], axis=0)
     total_ref[...] = stats
     spread_t, spread_s, _ = spreads_of(stats, t_width, s_width, total_rows)
     inv_t, inv_s = 1.0 / spread_t, 1.0 / spread_s
@@ -155,13 +161,14 @@
     sums_ref[1:2, :] = spread
 
 
-def late_kernel(n_blk, total_rows, *refs):
+def late_kernel(n_blk, t_width, total_rows, *refs):
     refs = list(refs)
-    plane = [(refs.pop(0), refs.pop(0)) for _ in range(n_blk)]
-    t, s, stats_ref, acc_ref, norm_ref, early_sums = (refs.pop(0) for _ in range(6))
+    plane = [halves(refs.pop(0), t_width) for _ in range(n_blk)]
+    t, s = halves(refs.pop(0), t_width)
+    stats_ref, acc_ref, norm_ref, early_sums = (refs.pop(0) for _ in range(4))
     out_refs = [refs.pop(0) for _ in range(n_blk)]
     (sums_ref,) = refs
-    t_width, s_width = t.shape[1], s.shape[1]
+    s_width = s.shape[1]
     spread_t, spread_s, _ = spreads_of(stats_ref[...], t_width, s_width, total_rows)
     inv_t, inv_s = 1.0 / spread_t, 1.0 / spread_s
     v = (t, s, column_norms(t), column_norms(s))
@@ -177,25 +184,22 @@
             weights, with_ones(s), (((0,), (0,)), ((), ())), preferred_element_type=jnp.float32
         )
         out_refs[d][...] = direct_of(cs, acc_ref[d] + back)
-    sums_ref[0:1, :] = loss
-    sums_ref[1:2, :] = spread
-
-
-def final_kernel(n_parts, n_sums, total_rows, *refs):
+    for i in range(sums_ref.shape[0]):
+        sums_ref[i, 0:1, :] = loss
+        sums_ref[i, 1:2, :] = spread
+
+
+def final_kernel(n_parts, total_rows, *refs):
     refs = list(refs)
     student_ref, stats_ref = refs.pop(0), refs.pop(0)
     parts = [refs.pop(0) for _ in range(n_parts)]
-    sums = [refs.pop(0) for _ in range(n_sums)]
-    grad_ref, loss_ref = refs
+    sums_ref, grad_ref, loss_ref = refs
     s_width = student_ref.shape[1]
     t_width = stats_ref.shape[1] - s_width - LANES
     direct = parts[0][...]
     for part in parts[1:]:
         direct = direct + part[...]
-    both = sums[0][...]
-    for one in sums[1:]:
-        both = both + one[...]
-    both = jnp.sum(both, axis=1, keepdims=True)
+    both = jnp.sum(jnp.sum(sums_ref[...], axis=0), axis=1, keepdims=True)
     loss_total, spread_total = both[0:1, :], -both[1:2, :]
     _, spread_s, centre = spreads_of(stats_ref[...], t_width, s_width, total_rows)
     pairs = total_rows * (total_rows - 1.0)
@@ -206,16 +210,22 @@
     loss_ref[...] = jnp.broadcast_to(loss_total / pairs, loss_ref.shape)
 
 
-def call(kernel, out_shape, operands, flops):
+def call(kernel, out_shape, operands, flops, vmem=48, **more):
     nbytes = sum(x.size * x.dtype.itemsize for x in operands)
+    in_specs = more.pop("in_specs", [WHOLE] * len(operands))
     return pl.pallas_call(
         kernel,
         out_shape=out_shape,
-        in_specs=[WHOLE] * len(operands),
+        in_specs=in_specs,
         out_specs=jax.tree.map(lambda _: WHOLE, out_shape),
-        compiler_params=pltpu.CompilerParams(vmem_limit_bytes=48 * 1024 * 1024),
+        compiler_params=pltpu.CompilerParams(vmem_limit_bytes=vmem * 1024 * 1024),
         cost_estimate=pl.CostEstimate(flops=flops, bytes_accessed=nbytes, transcendentals=0),
+        **more,
     )(*operands)
+
+
+def to_all(value):
+    return lax.all_to_all(value, ("blk", "sub"), 0, 0, tiled=True)
 
 
 def per_device(teacher, student):
@@ -223,57 +233,65 @@
     s_width = student.shape[1]
     n_blk = lax.axis_size("blk")
     n_sub = lax.axis_size("sub")
-    total_rows = float(rows * n_blk * n_sub)
+    n_all = n_blk * n_sub
+    total_rows = float(rows * n_all)
     half = n_sub // 2
     f32 = functools.partial(jax.ShapeDtypeStruct, dtype=jnp.float32)
 
-    line = [(teacher, student)]
+    packed, stats = call(
+        pack_kernel,
+        [
+            jax.ShapeDtypeStruct((rows, t_width + s_width), teacher.dtype),
+            f32((n_all, 1, t_width + s_width + LANES)),
+        ],
+        (teacher, student),
+        4 * teacher.size,
+        vmem=62,
+        in_specs=[pl.BlockSpec(memory_space=pl.ANY)] * 2,
+        scratch_shapes=[pltpu.SemaphoreType.DMA((2,))],
+    )
+    line = [packed]
     for _ in range(half):
-        line.append(tuple(shifted(x, "sub", 1) for x in line[-1]))
-    plane = [(teacher, student)]
-    for d in range(1, n_blk):
-        plane.append(tuple(exchange(x, "blk", d) for x in (teacher, student)))
-
-    stats = call(
-        stats_kernel, f32((1, t_width + s_width + LANES)), (teacher, student), 4 * teacher.size
-    )
-    for_plane = stats
-    for d in range(1, n_blk):
-        for_plane = for_plane + exchange(stats, "blk", d)
-    others = [exchange(for_plane, "sub", d) for d in range(1, n_sub)]
+        line.append(shifted(line[-1], "sub", 1))
+    plane = [packed]
+    distance = n_blk // 2
+    while distance:
+        plane = plane + [exchange(x, "blk", distance) for x in plane]
+        distance //= 2
+    distances = [0]
+    distance = n_blk // 2
+    while distance:
+        distances = distances + [x ^ distance for x in distances]
+        distance //= 2
+    stats = to_all(stats)
 
     pair_flops = 2 * rows * rows * n_blk * (t_width + 3 * s_width)
-    flat_plane = [x for pair in plane for x in pair]
-    flat_line = [x for pair in line[1:half] for x in pair]
     out_shape = (
         [f32((rows, s_width))] * half
         + [f32((n_blk, rows, s_width + LANES)), f32((n_blk, 2 * LANES))]
-        + [f32(stats.shape), f32((2, LANES))]
+        + [f32(stats.shape[1:]), f32((2, LANES))]
     )
     *tiles, acc, norms, totals, early_sums = call(
-        functools.partial(early_kernel, n_blk, half, total_rows),
+        functools.partial(early_kernel, n_blk, half, t_width, total_rows),
         out_shape,
-        flat_plane + flat_line + [for_plane, jnp.stack(others)],
+        plane + line[1:half] + [stats],
         half * pair_flops,
     )
     own, backs = tiles[0], tiles[1:]
     returned = [shifted(x, "sub", -k) for k, x in enumerate(backs, 1)]
     *shares, sums = call(
-        functools.partial(late_kernel, n_blk, total_rows),
-        [f32((rows, s_width))] * n_blk + [f32((2, LANES))],
-        flat_plane + list(line[half]) + [totals, acc, norms, early_sums],
+        functools.partial(late_kernel, n_blk, t_width, total_rows),
+        [f32((rows, s_width))] * n_blk + [f32((n_all, 2, LANES))],
+        plane + [line[half], totals, acc, norms, early_sums],
         pair_flops,
     )
-    plane_sums = sums
-    for d in range(1, n_blk):
-        plane_sums = plane_sums + exchange(sums, "blk", d)
-    all_sums = [plane_sums] + [exchange(plane_sums, "sub", d) for d in range(1, n_sub)]
-    received = [exchange(shares[d], "blk", d) for d in range(1, n_blk)]
+    received = [exchange(share, "blk", d) for share, d in zip(shares[1:], distances[1:])]
+    all_sums = to_all(sums)
     parts = [own, shares[0]] + returned + received
     grad, loss = call(
-        functools.partial(final_kernel, len(parts), len(all_sums), total_rows),
+        functools.partial(final_kernel, len(parts), total_rows),
         [f32((rows, s_width)), f32((1, LANES))],
-        [student, totals] + parts + all_sums,
+        [student, totals] + parts + [all_sums],
         8 * student.size,
     )
     return grad, loss[0, :1]

time: 62.4 us -> 50 us (0.80)
  blocking collectives: 0 us -> 22.8 us
  waiting for transfers between devices: 29.4 us -> 10.4 us
  starting transfers between devices: 24.6 us -> 7.56 us
  Pallas kernels: 5.66 us -> 7.3 us
  local copies, waits for them, and re-layouts: 1.84 us -> 0.99 us
    all_to_all x0 -> x2, blocking collectives: none -> 22.8 us  [to_all(): return lax.all_to_all(value, ('blk', 'sub'), 0, 0, tiled=True)]
    ppermute x21 -> x6, waiting for transfers between devices: 26.6 us -> 7.06 us  [exchange(): return lax.ppermute(value, axis, [(i, i ^ distance) for i in range(size)])]
    ppermute x21 -> x6, starting transfers between devices: 18.2 us -> 5.24 us  [exchange(): return lax.ppermute(value, axis, [(i, i ^ distance) for i in range(size)])]
    ppermute x5 -> x3, starting transfers between devices: 6.37 us -> 2.31 us  [shifted(): lax.ppermute(value, axis, [(i, (i + distance) % size) for i in range(size)])]
    pallas_call x4, Pallas kernels: 5.66 us -> 7.3 us  [call(): pl.pallas_call(kernel, out_shape=out_shape, in_specs=in_specs, out_specs=...]
    unnamed x6 -> x4, local copies, waits for them, and re-layouts: 1.84 us -> 0.99 us
    ppermute x5 -> x3, waiting for transfers between devices: 2.75 us -> 3.35 us  [shifted(): lax.ppermute(value, axis, [(i, (i + distance) % size) for i in range(size)])]
  transfers between devices with their start and end apart: 26 -> 9, of which waited for: 10 -> 2; matrix products, arithmetic and copies ran while one was open for 0% -> 0% of each run, Pallas kernels for 5% -> 6%
where the time goes in v2:
time: 50 us; the launch traced here: 49.7 us
  blocking collectives  22.8 us (46%)
  waiting for transfers between devices  10.4 us (21%)
  starting transfers between devices  7.56 us (15%)
  Pallas kernels  7.3 us (15%)
  local copies, waits for them, and re-layouts  0.99 us (2%)
  between operations  0.69 us (1%)
    all_to_all x2, blocking collectives, to_all(): return lax.all_to_all(value, ('blk', 'sub'), 0, 0, tiled=True)  22.8 us
    pallas_call x4, Pallas kernels, call(): pl.pallas_call(kernel, out_shape=out_shape, in_specs=in_specs, out_specs=...  7.3 us
    ppermute x6, waiting for transfers between devices, exchange(): return lax.ppermute(value, axis, [(i, i ^ distance) for i in range(size)])  7.06 us
    ppermute x6, starting transfers between devices, exchange(): return lax.ppermute(value, axis, [(i, i ^ distance) for i in range(size)])  5.24 us
    ppermute x3, waiting for transfers between devices, shifted(): lax.ppermute(value, axis, [(i, (i + distance) % size) for i in range(size)])  3.35 us
    ppermute x3, starting transfers between devices, shifted(): lax.ppermute(value, axis, [(i, (i + distance) % size) for i in range(size)])  2.31 us
  transfers between devices with their start and end apart: 9, of which 2 were waited for; matrix products, arithmetic and copies ran while one was open for 0% of the time, Pallas kernels for 6%

profile of v2, /device:TPU:0, one launch (start us, length us, event | category | flops | bytes accessed | tf_op | source)
XLA Modules:
  0.0 49.7 jit_solution(4170410767463285150)
XLA Ops:
  0.6 1.8 %shard_map.41 = (bf16[128,1408]{1,0:T(8,128)(2,1)}, f32[16,1,1536]{2,1,0:T(1,128)}) custom-call(bf16[128,1024]{1,0:T(8,128)(2,1)} %t_hbm.1, bf16[128,384]{1,0:T(8,128)(2,1)} %refs_0_.1), custom_call_target="tpu_custom_call" | custom-call | flops 524288 | bytes 360448 | tf_op jit(solution)/shard_map/pallas_call | solution.py:216
  2.4 3.0 %collective-permute-start = (bf16[128,1408]{1,0:T(8,128)(2,1)}, bf16[128,1408]{1,0:T(8,128)(2,1)S(1)}, u32[]{:S(2)}, u32[]{:S(2)}) collective-permute-start(bf16[128,1408]{1,0:T(8,128)(2,1)} %get-tuple-element.17.refs_0_), channel_id=1, source_target_pairs={{0,8},{4,12},{8,0},{12,4},{1,9},{5,13},{9,1},{13,5},{2,10},{6,14},... | collective-permute-start | bytes 1081352 | tf_op jit(solution)/shard_map/ppermute | solution.py:18
  5.5 1.6 %collective-permute-start.3 = (bf16[128,1408]{1,0:T(8,128)(2,1)}, bf16[128,1408]{1,0:T(8,128)(2,1)S(1)}, u32[]{:S(2)}, u32[]{:S(2)}) collective-permute-start(bf16[128,1408]{1,0:T(8,128)(2,1)} %get-tuple-element.17.refs_0_), channel_id=1, source_target_pairs={{0,1},{1,2},{2,3},{3,0},{4,5},{5,6},{6,7},{7,4},{8,9},{9,10},{10,1... | collective-permute-start | bytes 1081352 | tf_op jit(solution)/shard_map/ppermute | solution.py:23
  7.0 0.0 collective-permute-start.1
  7.1 7.0 %collective-permute-done.refs_1_ = bf16[128,1408]{1,0:T(8,128)(2,1)S(1)} collective-permute-done((bf16[128,1408]{1,0:T(8,128)(2,1)}, bf16[128,1408]{1,0:T(8,128)(2,1)S(1)}, u32[]{:S(2)}, u32[]{:S(2)}) %collective-permute-start) | collective-permute-done | bytes 360480 | tf_op jit(solution)/shard_map/ppermute | solution.py:18
  14.1 0.0 collective-permute-start.2
  14.1 3.3 %collective-permute-done.3.refs_4_ = bf16[128,1408]{1,0:T(8,128)(2,1)S(1)} collective-permute-done((bf16[128,1408]{1,0:T(8,128)(2,1)}, bf16[128,1408]{1,0:T(8,128)(2,1)S(1)}, u32[]{:S(2)}, u32[]{:S(2)}) %collective-permute-start.3) | collective-permute-done | bytes 360480 | tf_op jit(solution)/shard_map/ppermute | solution.py:23
  17.4 0.0 collective-permute-start.4
  17.5 13.1 %all_to_all.10.refs_5_ = f32[16,1,1536]{2,1,0:T(1,128)S(1)} all-to-all(f32[16,1,1536]{2,1,0:T(1,128)} %get-tuple-element.18), channel_id=1, replica_groups=mesh['groups'=2,'blk'=4,'sub'=4] {'blk','sub'}, dimensions={0} | all-to-all | bytes 196608 | tf_op jit(solution)/shard_map/all_to_all | solution.py:228
  30.6 0.0 collective-permute-done.1.refs_2_
  30.6 0.0 collective-permute-done.2.refs_3_
  30.6 0.0 copy-start.1
  30.6 1.0 %copy-done.1 = bf16[128,1408]{1,0:T(8,128)(2,1)S(1)} copy-done((bf16[128,1408]{1,0:T(8,128)(2,1)S(1)}, bf16[128,1408]{1,0:T(8,128)(2,1)}, u32[]{:S(2)}) %copy-start.1) | copy-done | bytes 360472
  31.6 2.9 %shard_map.42 = (f32[128,384]{1,0:T(8,128)S(1)}, f32[128,384]{1,0:T(8,128)S(1)}, f32[4,128,512]{2,1,0:T(8,128)S(1)}, f32[4,256]{1,0:T(4,128)S(1)}, f32[1,1536]{1,0:T(1,128)S(1)}, /*index=5*/f32[2,128]{1,0:T(2,128)S(1)}) custom-call(bf16[128,1408]{1,0:T(8,128)(2,1)S(1)} %copy-done.1, bf16[128,1408]{1,0:T(8,128)(2,1)S(1)} %collective-permute-done.refs_1_, ...), custom_call_target="tpu_custom_call" | custom-call | flops 570425344 | bytes 1900544 | tf_op jit(solution)/shard_map/pallas_call | solution.py:216
  34.5 0.0 collective-permute-done.4.refs_4_
  34.5 0.0 copy-start
  34.5 1.7 %shard_map.43 = (f32[128,384]{1,0:T(8,128)S(1)}, f32[128,384]{1,0:T(8,128)S(1)}, f32[128,384]{1,0:T(8,128)S(1)}, f32[128,384]{1,0:T(8,128)S(1)}, f32[16,2,128]{2,1,0:T(2,128)S(1)}) custom-call(bf16[128,1408]{1,0:T(8,128)(2,1)S(1)} %copy-done.1, bf16[128,1408]{1,0:T(8,128)(2,1)S(1)} %collective-permute-done.refs_1_, ...), custom_call_target="tpu_custom_call" | custom-call | flops 285212672 | bytes 2862080 | tf_op jit(solution)/shard_map/pallas_call | solution.py:216
  36.2 1.4 %collective-permute-start.6 = (f32[128,384]{1,0:T(8,128)S(1)}, f32[128,384]{1,0:T(8,128)S(1)}, u32[]{:S(2)}, u32[]{:S(2)}) collective-permute-start(f32[128,384]{1,0:T(8,128)S(1)} %get-tuple-element.26), channel_id=1, source_target_pairs={{0,8},{4,12},{8,0},{12,4},{1,9},{5,13},{9,1},{13,5},{2,10},{6,14},... | collective-permute-start | bytes 589832 | tf_op jit(solution)/shard_map/ppermute | solution.py:18
  37.6 0.0 collective-permute-start.7
  37.6 0.8 %collective-permute-start.8 = (f32[128,384]{1,0:T(8,128)S(1)}, f32[128,384]{1,0:T(8,128)S(1)}, u32[]{:S(2)}, u32[]{:S(2)}) collective-permute-start(f32[128,384]{1,0:T(8,128)S(1)} %get-tuple-element.28), channel_id=1, source_target_pairs={{0,12},{4,8},{8,4},{12,0},{1,13},{5,9},{9,5},{13,1},{2,14},{6,10},... | collective-permute-start | bytes 589832 | tf_op jit(solution)/shard_map/ppermute | solution.py:18
  38.4 0.7 %collective-permute-start.5 = (f32[128,384]{1,0:T(8,128)S(1)}, f32[128,384]{1,0:T(8,128)S(1)}, u32[]{:S(2)}, u32[]{:S(2)}) collective-permute-start(f32[128,384]{1,0:T(8,128)S(1)} %get-tuple-element.25), channel_id=1, source_target_pairs={{0,3},{1,0},{2,1},{3,2},{4,7},{5,4},{6,5},{7,6},{8,11},{9,8},{10,9... | collective-permute-start | bytes 589832 | tf_op jit(solution)/shard_map/ppermute | solution.py:23
  39.2 9.6 %all_to_all.11.refs_8_ = f32[16,2,128]{2,1,0:T(2,128)S(1)} all-to-all(f32[16,2,128]{2,1,0:T(2,128)S(1)} %get-tuple-element.29), channel_id=1, replica_groups=mesh['groups'=2,'blk'=4,'sub'=4] {'blk','sub'}, dimensions={0} | all-to-all | bytes 32768 | tf_op jit(solution)/shard_map/all_to_all | solution.py:228
  48.8 0.0 collective-permute-done.6.refs_5_
  48.8 0.0 collective-permute-done.7.refs_6_
  48.8 0.0 collective-permute-done.8.refs_7_
  48.8 0.0 collective-permute-done.5.refs_4_
  48.8 0.0 copy-done
  48.8 0.9 %shard_map.44 = (f32[128,384]{1,0:T(8,128)}, f32[1,128]{1,0:T(1,128)}) custom-call(bf16[128,384]{1,0:T(8,128)(2,1)S(1)} %copy-done, f32[1,1536]{1,0:T(1,128)S(1)} %get-tuple-element.19.refs_5_.refs_1_, f32[128,384]{1,0:T(8,128)S(1)} %get-tuple-element.20.refs_2_, f32[128,384]{1,0:T(8,128)S(1)} %get-tuple-element.24.refs_3_, ...), custom_call_target="tpu_custom_call" | custom-call | flops 393216 | bytes 1300480 | tf_op jit(solution)/shard_map/pallas_call | solution.py:216
Async XLA Ops:
  2.4 11.7 %collective-permute-start = (bf16[128,1408]{1,0:T(8,128)(2,1)}, bf16[128,1408]{1,0:T(8,128)(2,1)S(1)}, u32[]{:S(2)}, u32[]{:S(2)}) collective-permute-start(bf16[128,1408]{1,0:T(8,128)(2,1)} %get-tuple-element.17.refs_0_), channel_id=1, source_target_pairs={{0,8},{4,12},{8,0},{12,4},{1,9},{5,13},{9,1},{13,5},{2,10},{6,14},... | collective-permute-start | bytes 1081352 | tf_op jit(solution)/shard_map/ppermute | solution.py:18
  5.5 12.0 %collective-permute-start.3 = (bf16[128,1408]{1,0:T(8,128)(2,1)}, bf16[128,1408]{1,0:T(8,128)(2,1)S(1)}, u32[]{:S(2)}, u32[]{:S(2)}) collective-permute-start(bf16[128,1408]{1,0:T(8,128)(2,1)} %get-tuple-element.17.refs_0_), channel_id=1, source_target_pairs={{0,1},{1,2},{2,3},{3,0},{4,5},{5,6},{6,7},{7,4},{8,9},{9,10},{10,1... | collective-permute-start | bytes 1081352 | tf_op jit(solution)/shard_map/ppermute | solution.py:23
  7.0 23.5 %collective-permute-start.1 = (bf16[128,1408]{1,0:T(8,128)(2,1)}, bf16[128,1408]{1,0:T(8,128)(2,1)S(1)}, u32[]{:S(2)}, u32[]{:S(2)}) collective-permute-start(bf16[128,1408]{1,0:T(8,128)(2,1)} %get-tuple-element.17.refs_0_), channel_id=1, source_target_pairs={{0,4},{4,0},{8,12},{12,8},{1,5},{5,1},{9,13},{13,9},{2,6},{6,2},{1... | collective-permute-start | bytes 1081352 | tf_op jit(solution)/shard_map/ppermute | solution.py:18
  14.1 16.5 %collective-permute-start.2 = (bf16[128,1408]{1,0:T(8,128)(2,1)S(1)}, bf16[128,1408]{1,0:T(8,128)(2,1)S(1)}, u32[]{:S(2)}, u32[]{:S(2)}) collective-permute-start(bf16[128,1408]{1,0:T(8,128)(2,1)S(1)} %collective-permute-done.refs_1_), channel_id=1, source_target_pairs={{0,4},{4,0},{8,12},{12,8},{1,5},{5,1},{9,13},{13,9},{2,6},{6,2},{1... | collective-permute-start | bytes 1081352 | tf_op jit(solution)/shard_map/ppermute | solution.py:18
  17.4 17.0 %collective-permute-start.4 = (bf16[128,1408]{1,0:T(8,128)(2,1)S(1)}, bf16[128,1408]{1,0:T(8,128)(2,1)S(1)}, u32[]{:S(2)}, u32[]{:S(2)}) collective-permute-start(bf16[128,1408]{1,0:T(8,128)(2,1)S(1)} %collective-permute-done.3.refs_4_), channel_id=1, source_target_pairs={{0,1},{1,2},{2,3},{3,0},{4,5},{5,6},{6,7},{7,4},{8,9},{9,10},{10,1... | collective-permute-start | bytes 1081352 | tf_op jit(solution)/shard_map/ppermute | solution.py:23
  30.6 1.0 %copy-start.1 = (bf16[128,1408]{1,0:T(8,128)(2,1)S(1)}, bf16[128,1408]{1,0:T(8,128)(2,1)}, u32[]{:S(2)}) copy-start(bf16[128,1408]{1,0:T(8,128)(2,1)} %get-tuple-element.17.refs_0_) | copy-start | bytes 1081348
  34.5 14.3 %copy-start = (bf16[128,384]{1,0:T(8,128)(2,1)S(1)}, bf16[128,384]{1,0:T(8,128)(2,1)}, u32[]{:S(2)}) copy-start(bf16[128,384]{1,0:T(8,128)(2,1)} %refs_0_.1) | copy-start | bytes 294916
  36.2 12.6 %collective-permute-start.6 = (f32[128,384]{1,0:T(8,128)S(1)}, f32[128,384]{1,0:T(8,128)S(1)}, u32[]{:S(2)}, u32[]{:S(2)}) collective-permute-start(f32[128,384]{1,0:T(8,128)S(1)} %get-tuple-element.26), channel_id=1, source_target_pairs={{0,8},{4,12},{8,0},{12,4},{1,9},{5,13},{9,1},{13,5},{2,10},{6,14},... | collective-permute-start | bytes 589832 | tf_op jit(solution)/shard_map/ppermute | solution.py:18
  37.6 11.2 %collective-permute-start.7 = (f32[128,384]{1,0:T(8,128)S(1)}, f32[128,384]{1,0:T(8,128)S(1)}, u32[]{:S(2)}, u32[]{:S(2)}) collective-permute-start(f32[128,384]{1,0:T(8,128)S(1)} %get-tuple-element.27), channel_id=1, source_target_pairs={{0,4},{4,0},{8,12},{12,8},{1,5},{5,1},{9,13},{13,9},{2,6},{6,2},{1... | collective-permute-start | bytes 589832 | tf_op jit(solution)/shard_map/ppermute | solution.py:18
  37.6 11.2 %collective-permute-start.8 = (f32[128,384]{1,0:T(8,128)S(1)}, f32[128,384]{1,0:T(8,128)S(1)}, u32[]{:S(2)}, u32[]{:S(2)}) collective-permute-start(f32[128,384]{1,0:T(8,128)S(1)} %get-tuple-element.28), channel_id=1, source_target_pairs={{0,12},{4,8},{8,4},{12,0},{1,13},{5,9},{9,5},{13,1},{2,14},{6,10},... | collective-permute-start | bytes 589832 | tf_op jit(solution)/shard_map/ppermute | solution.py:18
  38.4 10.4 %collective-permute-start.5 = (f32[128,384]{1,0:T(8,128)S(1)}, f32[128,384]{1,0:T(8,128)S(1)}, u32[]{:S(2)}, u32[]{:S(2)}) collective-permute-start(f32[128,384]{1,0:T(8,128)S(1)} %get-tuple-element.25), channel_id=1, source_target_pairs={{0,3},{1,0},{2,1},{3,2},{4,7},{5,4},{6,5},{7,6},{8,11},{9,8},{10,9... | collective-permute-start | bytes 589832 | tf_op jit(solution)/shard_map/ppermute | solution.py:23

commit v3 on v2

--- a/solution.py
+++ b/solution.py
@@ -23,8 +23,8 @@
     return lax.ppermute(value, axis, [(i, (i + distance) % size) for i in range(size)])
 
 
-def pack_kernel(t_hbm, s_hbm, packed_ref, stats_ref, sems):
-    t_width, s_width = t_hbm.shape[1], s_hbm.shape[1]
+def pack_kernel(t_hbm, s_hbm, packed_ref, sems):
+    t_width = t_hbm.shape[1]
     copies = [
         pltpu.make_async_copy(t_hbm, packed_ref.at[:, :t_width], sems.at[0]),
         pltpu.make_async_copy(s_hbm, packed_ref.at[:, t_width:], sems.at[1]),
@@ -33,14 +33,17 @@
         copy.start()
     for copy in copies:
         copy.wait()
+
+
+def stats_kernel(t_width, packed_ref, stats_ref):
     value = packed_ref[...].astype(jnp.float32)
     squares = jnp.sum(value * value, axis=0, keepdims=True)
     square_t = jnp.sum(squares[:, :t_width], axis=1, keepdims=True)
     square_s = jnp.sum(squares[:, t_width:], axis=1, keepdims=True)
     lane = lax.broadcasted_iota(jnp.int32, (1, LANES), 1)
-    last = jnp.where(lane == 0, square_t, jnp.where(lane == 1, square_s, 0.0))
-    row = jnp.concatenate([jnp.sum(value, axis=0, keepdims=True), last], axis=1)
-    stats_ref[...] = jnp.broadcast_to(row[None], stats_ref.shape)
+    width = value.shape[1]
+    stats_ref[:, :width] = jnp.sum(value, axis=0, keepdims=True)
+    stats_ref[:, width:] = jnp.where(lane == 0, square_t, jnp.where(lane == 1, square_s, 0.0))
 
 
 def spreads_of(stats, t_width, s_width, total_rows):
@@ -117,11 +120,12 @@
     refs = list(refs)
     plane = [halves(refs.pop(0), t_width) for _ in range(n_blk)]
     line = [plane[0]] + [halves(refs.pop(0), t_width) for _ in range(steps - 1)]
-    stats_ref, own_ref = refs.pop(0), refs.pop(0)
+    stats_refs = refs.pop(0), refs.pop(0)
+    own_ref = refs.pop(0)
     back_refs = [refs.pop(0) for _ in range(steps - 1)]
     acc_ref, norm_ref, total_ref, sums_ref = refs
     s_width = plane[0][1].shape[1]
-    stats = jnp.sum(stats_ref[...], axis=0)
+    stats = stats_refs[0][...] + stats_refs[1][...]
     total_ref[...] = stats
     spread_t, spread_s, _ = spreads_of(stats, t_width, s_width, total_rows)
     inv_t, inv_s = 1.0 / spread_t, 1.0 / spread_s
@@ -184,22 +188,24 @@
             weights, with_ones(s), (((0,), (0,)), ((), ())), preferred_element_type=jnp.float32
         )
         out_refs[d][...] = direct_of(cs, acc_ref[d] + back)
-    for i in range(sums_ref.shape[0]):
-        sums_ref[i, 0:1, :] = loss
-        sums_ref[i, 1:2, :] = spread
-
-
-def final_kernel(n_parts, total_rows, *refs):
+    sums_ref[0:1, :] = loss
+    sums_ref[1:2, :] = spread
+
+
+def final_kernel(n_parts, t_width, total_rows, *refs):
     refs = list(refs)
-    student_ref, stats_ref = refs.pop(0), refs.pop(0)
+    packed_ref, stats_ref = refs.pop(0), refs.pop(0)
     parts = [refs.pop(0) for _ in range(n_parts)]
-    sums_ref, grad_ref, loss_ref = refs
+    *sums, grad_ref, loss_ref = refs
+    student_ref = packed_ref.at[:, t_width:]
     s_width = student_ref.shape[1]
-    t_width = stats_ref.shape[1] - s_width - LANES
     direct = parts[0][...]
     for part in parts[1:]:
         direct = direct + part[...]
-    both = jnp.sum(jnp.sum(sums_ref[...], axis=0), axis=1, keepdims=True)
+    both = sums[0][...]
+    for one in sums[1:]:
+        both = both + one[...]
+    both = jnp.sum(both, axis=1, keepdims=True)
     loss_total, spread_total = both[0:1, :], -both[1:2, :]
     _, spread_s, centre = spreads_of(stats_ref[...], t_width, s_width, total_rows)
     pairs = total_rows * (total_rows - 1.0)
@@ -224,8 +230,13 @@
     )(*operands)
 
 
-def to_all(value):
-    return lax.all_to_all(value, ("blk", "sub"), 0, 0, tiled=True)
+def gathered(value, axis):
+    return [value] + [exchange(value, axis, d) for d in range(1, lax.axis_size(axis))]
+
+
+def halvings(axis):
+    size = lax.axis_size(axis)
+    return [size >> i for i in range(1, size.bit_length())]
 
 
 def per_device(teacher, student):
@@ -238,14 +249,11 @@
     half = n_sub // 2
     f32 = functools.partial(jax.ShapeDtypeStruct, dtype=jnp.float32)
 
-    packed, stats = call(
+    packed = call(
         pack_kernel,
-        [
-            jax.ShapeDtypeStruct((rows, t_width + s_width), teacher.dtype),
-            f32((n_all, 1, t_width + s_width + LANES)),
-        ],
+        jax.ShapeDtypeStruct((rows, t_width + s_width), teacher.dtype),
         (teacher, student),
-        4 * teacher.size,
+        0,
         vmem=62,
         in_specs=[pl.BlockSpec(memory_space=pl.ANY)] * 2,
         scratch_shapes=[pltpu.SemaphoreType.DMA((2,))],
@@ -253,45 +261,52 @@
     line = [packed]
     for _ in range(half):
         line.append(shifted(line[-1], "sub", 1))
-    plane = [packed]
-    distance = n_blk // 2
-    while distance:
+    plane, distances = [packed], [0]
+    for distance in halvings("blk"):
         plane = plane + [exchange(x, "blk", distance) for x in plane]
-        distance //= 2
-    distances = [0]
-    distance = n_blk // 2
-    while distance:
         distances = distances + [x ^ distance for x in distances]
-        distance //= 2
-    stats = to_all(stats)
+    stats = call(
+        functools.partial(stats_kernel, t_width),
+        f32((1, t_width + s_width + LANES)),
+        (packed,),
+        4 * packed.size,
+    )
+    stats = functools.reduce(jnp.add, gathered(stats, "sub"))
+    for distance in halvings("blk")[:-1]:
+        stats = stats + exchange(stats, "blk", distance)
+    stats_other = exchange(stats, "blk", 1)
 
     pair_flops = 2 * rows * rows * n_blk * (t_width + 3 * s_width)
     out_shape = (
         [f32((rows, s_width))] * half
         + [f32((n_blk, rows, s_width + LANES)), f32((n_blk, 2 * LANES))]
-        + [f32(stats.shape[1:]), f32((2, LANES))]
+        + [f32(stats.shape), f32((2, LANES))]
     )
     *tiles, acc, norms, totals, early_sums = call(
         functools.partial(early_kernel, n_blk, half, t_width, total_rows),
         out_shape,
-        plane + line[1:half] + [stats],
+        plane + line[1:half] + [stats, stats_other],
         half * pair_flops,
     )
     own, backs = tiles[0], tiles[1:]
     returned = [shifted(x, "sub", -k) for k, x in enumerate(backs, 1)]
     *shares, sums = call(
         functools.partial(late_kernel, n_blk, t_width, total_rows),
-        [f32((rows, s_width))] * n_blk + [f32((n_all, 2, LANES))],
+        [f32((rows, s_width))] * n_blk + [f32((2, LANES))],
         plane + [line[half], totals, acc, norms, early_sums],
         pair_flops,
     )
     received = [exchange(share, "blk", d) for share, d in zip(shares[1:], distances[1:])]
-    all_sums = to_all(sums)
+    sums, returned = lax.optimization_barrier((sums, returned))
+    sums = functools.reduce(jnp.add, gathered(sums, "sub"))
+    for distance in halvings("blk")[:-1]:
+        sums = sums + exchange(sums, "blk", distance)
+    all_sums = [sums, exchange(sums, "blk", 1)]
     parts = [own, shares[0]] + returned + received
     grad, loss = call(
-        functools.partial(final_kernel, len(parts), total_rows),
+        functools.partial(final_kernel, len(parts), t_width, total_rows),
         [f32((rows, s_width)), f32((1, LANES))],
-        [student, totals] + parts + [all_sums],
+        [packed, totals] + parts + all_sums,
         8 * student.size,
     )
     return grad, loss[0, :1]

time: 50 us -> 50 us (level)
  blocking collectives: 22.8 us -> 0 us
  starting transfers between devices: 7.56 us -> 23 us
  waiting for transfers between devices: 10.4 us -> 17.8 us
    all_to_all x2 -> x0, blocking collectives: 22.8 us -> none  [to_all(): return lax.all_to_all(value, ('blk', 'sub'), 0, 0, tiled=True)]
    ppermute x6 -> x16, starting transfers between devices: 5.24 us -> 16 us  [exchange(): return lax.ppermute(value, axis, [(i, i ^ distance) for i in range(size)])]
    ppermute x6 -> x16, waiting for transfers between devices: 7.06 us -> 14.7 us  [exchange(): return lax.ppermute(value, axis, [(i, i ^ distance) for i in range(size)])]
    ppermute x3, starting transfers between devices: 2.31 us -> 6.95 us  [shifted(): lax.ppermute(value, axis, [(i, (i + distance) % size) for i in range(size)])]
    pallas_call x4 -> x5, Pallas kernels: 7.3 us -> 7.37 us  [call(): pl.pallas_call(kernel, out_shape=out_shape, in_specs=in_specs, out_specs=...]
  transfers between devices with their start and end apart: 9 -> 19, of which waited for: 2 -> 8; matrix products, arithmetic and copies ran while one was open for 0% -> 0% of each run, Pallas kernels for 6% -> 10%
where the time goes in v3:
time: 50 us; the launch traced here: 49.9 us
  starting transfers between devices  23 us (46%)
  waiting for transfers between devices  17.8 us (36%)
  Pallas kernels  7.37 us (15%)
  local copies, waits for them, and re-layouts  1.02 us (2%)
  between operations  0.71 us (1%)
    ppermute x16, starting transfers between devices, exchange(): return lax.ppermute(value, axis, [(i, i ^ distance) for i in range(size)])  16 us
    ppermute x16, waiting for transfers between devices, exchange(): return lax.ppermute(value, axis, [(i, i ^ distance) for i in range(size)])  14.7 us
    pallas_call x5, Pallas kernels, call(): pl.pallas_call(kernel, out_shape=out_shape, in_specs=in_specs, out_specs=...  7.37 us
    ppermute x3, starting transfers between devices, shifted(): lax.ppermute(value, axis, [(i, (i + distance) % size) for i in range(size)])  6.95 us
    ppermute x3, waiting for transfers between devices, shifted(): lax.ppermute(value, axis, [(i, (i + distance) % size) for i in range(size)])  3.1 us
    unnamed x4, local copies, waits for them, and re-layouts  1.02 us
  transfers between devices with their start and end apart: 19, of which 8 were waited for; matrix products, arithmetic and copies ran while one was open for 0% of the time, Pallas kernels for 10%

profile of v3, /device:TPU:0, one launch (start us, length us, event | category | flops | bytes accessed | tf_op | source)
XLA Modules:
  0.0 49.9 jit_solution(10837429703864904799)
XLA Ops:
  0.6 1.7 %shard_map.41.packed_ref.refs_0_ = bf16[128,1408]{1,0:T(8,128)(2,1)} custom-call(bf16[128,1024]{1,0:T(8,128)(2,1)} %t_hbm.1, bf16[128,384]{1,0:T(8,128)(2,1)} %s_hbm.1), custom_call_target="tpu_custom_call" | custom-call | bytes 360448 | tf_op jit(solution)/shard_map/pallas_call | solution.py:222
  2.4 3.1 %collective-permute-start.3 = (bf16[128,1408]{1,0:T(8,128)(2,1)}, bf16[128,1408]{1,0:T(8,128)(2,1)S(1)}, u32[]{:S(2)}, u32[]{:S(2)}) collective-permute-start(bf16[128,1408]{1,0:T(8,128)(2,1)} %shard_map.41.packed_ref.refs_0_), channel_id=1, source_target_pairs={{0,1},{1,2},{2,3},{3,0},{4,5},{5,6},{6,7},{7,4},{8,9},{9,10},{10,1... | collective-permute-start | bytes 1081352 | tf_op jit(solution)/shard_map/ppermute | solution.py:23
  5.4 1.5 %collective-permute-start = (bf16[128,1408]{1,0:T(8,128)(2,1)}, bf16[128,1408]{1,0:T(8,128)(2,1)S(1)}, u32[]{:S(2)}, u32[]{:S(2)}) collective-permute-start(bf16[128,1408]{1,0:T(8,128)(2,1)} %shard_map.41.packed_ref.refs_0_), channel_id=1, source_target_pairs={{0,8},{4,12},{8,0},{12,4},{1,9},{5,13},{9,1},{13,5},{2,10},{6,14},... | collective-permute-start | bytes 1081352 | tf_op jit(solution)/shard_map/ppermute | solution.py:18
  7.0 1.0 %copy-done = bf16[128,1408]{1,0:T(8,128)(2,1)S(1)} copy-done((bf16[128,1408]{1,0:T(8,128)(2,1)S(1)}, bf16[128,1408]{1,0:T(8,128)(2,1)}, u32[]{:S(2)}) %copy-start) | copy-done | bytes 360472
  8.0 0.2 shard_map.42
  8.1 2.2 %collective-permute-start.6 = (f32[1,1536]{1,0:T(1,128)S(1)}, f32[1,1536]{1,0:T(1,128)S(1)}, u32[]{:S(2)}, u32[]{:S(2)}) collective-permute-start(f32[1,1536]{1,0:T(1,128)S(1)} %shard_map.42), channel_id=1, source_target_pairs={{0,3},{1,2},{2,1},{3,0},{4,7},{5,6},{6,5},{7,4},{8,11},{9,10},{10,... | collective-permute-start | bytes 18440 | tf_op jit(solution)/shard_map/ppermute | solution.py:18
  10.4 0.8 %collective-permute-start.5 = (f32[1,1536]{1,0:T(1,128)S(1)}, f32[1,1536]{1,0:T(1,128)S(1)}, u32[]{:S(2)}, u32[]{:S(2)}) collective-permute-start(f32[1,1536]{1,0:T(1,128)S(1)} %shard_map.42), channel_id=1, source_target_pairs={{0,2},{1,3},{2,0},{3,1},{4,6},{5,7},{6,4},{7,5},{8,10},{9,11},{10,... | collective-permute-start | bytes 18440 | tf_op jit(solution)/shard_map/ppermute | solution.py:18
  11.2 1.3 %collective-permute-start.4 = (f32[1,1536]{1,0:T(1,128)S(1)}, f32[1,1536]{1,0:T(1,128)S(1)}, u32[]{:S(2)}, u32[]{:S(2)}) collective-permute-start(f32[1,1536]{1,0:T(1,128)S(1)} %shard_map.42), channel_id=1, source_target_pairs={{0,1},{1,0},{2,3},{3,2},{4,5},{5,4},{6,7},{7,6},{8,9},{9,8},{10,11... | collective-permute-start | bytes 18440 | tf_op jit(solution)/shard_map/ppermute | solution.py:18
  12.5 3.9 %collective-permute-done.6 = f32[1,1536]{1,0:T(1,128)S(1)} collective-permute-done((f32[1,1536]{1,0:T(1,128)S(1)}, f32[1,1536]{1,0:T(1,128)S(1)}, u32[]{:S(2)}, u32[]{:S(2)}) %collective-permute-start.6) | collective-permute-done | bytes 6176 | tf_op jit(solution)/shard_map/ppermute | solution.py:18
  16.4 0.7 %collective-permute-start.9 = (bf16[128,1408]{1,0:T(8,128)(2,1)S(1)}, bf16[128,1408]{1,0:T(8,128)(2,1)S(1)}, u32[]{:S(2)}, u32[]{:S(2)}) collective-permute-start(bf16[128,1408]{1,0:T(8,128)(2,1)S(1)} %collective-permute-done.3.refs_4_), channel_id=1, source_target_pairs={{0,1},{1,2},{2,3},{3,0},{4,5},{5,6},{6,7},{7,4},{8,9},{9,10},{10,1... | collective-permute-start | bytes 1081352 | tf_op jit(solution)/shard_map/ppermute | solution.py:23
  17.1 0.0 collective-permute-done.refs_1_
  17.1 0.2 collective-permute-start.2
  17.3 0.0 collective-permute-done.5
  17.3 0.0 collective-permute-done.4
  17.3 1.6 %collective-permute-start.7 = (f32[1,1536]{1,0:T(1,128)S(1)}, f32[1,1536]{1,0:T(1,128)S(1)}, u32[]{:S(2)}, u32[]{:S(2)}) collective-permute-start(f32[1,1536]{1,0:T(1,128)S(1)} %add_add_fusion), channel_id=1, source_target_pairs={{0,8},{4,12},{8,0},{12,4},{1,9},{5,13},{9,1},{13,5},{2,10},{6,14},... | collective-permute-start | bytes 18440 | tf_op jit(solution)/shard_map/ppermute | solution.py:18
  18.9 2.1 %collective-permute-done.7 = f32[1,1536]{1,0:T(1,128)S(1)} collective-permute-done((f32[1,1536]{1,0:T(1,128)S(1)}, f32[1,1536]{1,0:T(1,128)S(1)}, u32[]{:S(2)}, u32[]{:S(2)}) %collective-permute-start.7) | collective-permute-done | bytes 6176 | tf_op jit(solution)/shard_map/ppermute | solution.py:18
  21.0 0.1 collective-permute-start.8
  21.1 1.2 %collective-permute-done.8.refs_6_ = f32[1,1536]{1,0:T(1,128)S(1)} collective-permute-done((f32[1,1536]{1,0:T(1,128)S(1)}, f32[1,1536]{1,0:T(1,128)S(1)}, u32[]{:S(2)}, u32[]{:S(2)}) %collective-permute-start.8) | collective-permute-done | bytes 6176 | tf_op jit(solution)/shard_map/ppermute | solution.py:18
  22.3 2.9 %shard_map.43 = (f32[128,384]{1,0:T(8,128)S(1)}, f32[128,384]{1,0:T(8,128)S(1)}, f32[4,128,512]{2,1,0:T(8,128)S(1)}, f32[4,256]{1,0:T(4,128)S(1)}, f32[1,1536]{1,0:T(1,128)S(1)}, /*index=5*/f32[2,128]{1,0:T(2,128)S(1)}) custom-call(bf16[128,1408]{1,0:T(8,128)(2,1)S(1)} %copy-done.1, bf16[128,1408]{1,0:T(8,128)(2,1)S(1)} %collective-permute-done.refs_1_, ...), custom_call_target="tpu_custom_call" | custom-call | flops 570425344 | bytes 1814528 | tf_op jit(solution)/shard_map/pallas_call | solution.py:222
  25.2 3.2 %collective-permute-start.10 = (f32[128,384]{1,0:T(8,128)S(1)}, f32[128,384]{1,0:T(8,128)S(1)}, u32[]{:S(2)}, u32[]{:S(2)}) collective-permute-start(f32[128,384]{1,0:T(8,128)S(1)} %get-tuple-element.24), channel_id=1, source_target_pairs={{0,3},{1,0},{2,1},{3,2},{4,7},{5,4},{6,5},{7,6},{8,11},{9,8},{10,9... | collective-permute-start | bytes 589832 | tf_op jit(solution)/shard_map/ppermute | solution.py:23
  28.4 0.7 %collective-permute-done.9.refs_4_ = bf16[128,1408]{1,0:T(8,128)(2,1)S(1)} collective-permute-done((bf16[128,1408]{1,0:T(8,128)(2,1)S(1)}, bf16[128,1408]{1,0:T(8,128)(2,1)S(1)}, u32[]{:S(2)}, u32[]{:S(2)}) %collective-permute-start.9) | collective-permute-done | bytes 360480 | tf_op jit(solution)/shard_map/ppermute | solution.py:23
  29.2 1.7 %shard_map.44 = (f32[128,384]{1,0:T(8,128)S(1)}, f32[128,384]{1,0:T(8,128)S(1)}, f32[128,384]{1,0:T(8,128)S(1)}, f32[128,384]{1,0:T(8,128)S(1)}, f32[2,128]{1,0:T(2,128)S(1)}) custom-call(bf16[128,1408]{1,0:T(8,128)(2,1)S(1)} %copy-done.1, bf16[128,1408]{1,0:T(8,128)(2,1)S(1)} %collective-permute-done.refs_1_, ...), custom_call_target="tpu_custom_call" | custom-call | flops 285212672 | bytes 2862080 | tf_op jit(solution)/shard_map/pallas_call | solution.py:222
  30.9 2.4 %collective-permute-done.10.refs_4_ = f32[128,384]{1,0:T(8,128)S(1)} collective-permute-done((f32[128,384]{1,0:T(8,128)S(1)}, f32[128,384]{1,0:T(8,128)S(1)}, u32[]{:S(2)}, u32[]{:S(2)}) %collective-permute-start.10) | collective-permute-done | bytes 196640 | tf_op jit(solution)/shard_map/ppermute | solution.py:23
  33.3 3.9 %collective-permute-start.16 = (f32[2,128]{1,0:T(2,128)S(1)}, f32[2,128]{1,0:T(2,128)S(1)}, u32[]{:S(2)}, u32[]{:S(2)}) collective-permute-start(f32[2,128]{1,0:T(2,128)S(1)} %get-tuple-element.29), channel_id=1, source_target_pairs={{0,3},{1,2},{2,1},{3,0},{4,7},{5,6},{6,5},{7,4},{8,11},{9,10},{10,... | collective-permute-start | bytes 3080 | tf_op jit(solution)/shard_map/ppermute | solution.py:18
  37.2 0.6 %collective-permute-start.14 = (f32[2,128]{1,0:T(2,128)S(1)}, f32[2,128]{1,0:T(2,128)S(1)}, u32[]{:S(2)}, u32[]{:S(2)}) collective-permute-start(f32[2,128]{1,0:T(2,128)S(1)} %get-tuple-element.29), channel_id=1, source_target_pairs={{0,1},{1,0},{2,3},{3,2},{4,5},{5,4},{6,7},{7,6},{8,9},{9,8},{10,11... | collective-permute-start | bytes 3080 | tf_op jit(solution)/shard_map/ppermute | solution.py:18
  37.8 1.5 %collective-permute-start.11 = (f32[128,384]{1,0:T(8,128)S(1)}, f32[128,384]{1,0:T(8,128)S(1)}, u32[]{:S(2)}, u32[]{:S(2)}) collective-permute-start(f32[128,384]{1,0:T(8,128)S(1)} %get-tuple-element.26), channel_id=1, source_target_pairs={{0,8},{4,12},{8,0},{12,4},{1,9},{5,13},{9,1},{13,5},{2,10},{6,14},... | collective-permute-start | bytes 589832 | tf_op jit(solution)/shard_map/ppermute | solution.py:18
  39.3 0.6 %collective-permute-start.13 = (f32[128,384]{1,0:T(8,128)S(1)}, f32[128,384]{1,0:T(8,128)S(1)}, u32[]{:S(2)}, u32[]{:S(2)}) collective-permute-start(f32[128,384]{1,0:T(8,128)S(1)} %get-tuple-element.28), channel_id=1, source_target_pairs={{0,12},{4,8},{8,4},{12,0},{1,13},{5,9},{9,5},{13,1},{2,14},{6,10},... | collective-permute-start | bytes 589832 | tf_op jit(solution)/shard_map/ppermute | solution.py:18
  39.9 1.8 %collective-permute-done.15 = f32[2,128]{1,0:T(2,128)S(1)} collective-permute-done((f32[2,128]{1,0:T(2,128)S(1)}, f32[2,128]{1,0:T(2,128)S(1)}, u32[]{:S(2)}, u32[]{:S(2)}) %collective-permute-start.15) | collective-permute-done | bytes 1056 | tf_op jit(solution)/shard_map/ppermute | solution.py:18
  41.7 1.6 %collective-permute-start.17 = (f32[2,128]{1,0:T(2,128)S(1)}, f32[2,128]{1,0:T(2,128)S(1)}, u32[]{:S(2)}, u32[]{:S(2)}) collective-permute-start(f32[2,128]{1,0:T(2,128)S(1)} %add_add_fusion.1), channel_id=1, source_target_pairs={{0,8},{4,12},{8,0},{12,4},{1,9},{5,13},{9,1},{13,5},{2,10},{6,14},... | collective-permute-start | bytes 3080 | tf_op jit(solution)/shard_map/ppermute | solution.py:18
  43.2 4.6 %collective-permute-done.17 = f32[2,128]{1,0:T(2,128)S(1)} collective-permute-done((f32[2,128]{1,0:T(2,128)S(1)}, f32[2,128]{1,0:T(2,128)S(1)}, u32[]{:S(2)}, u32[]{:S(2)}) %collective-permute-start.17) | collective-permute-done | bytes 1056 | tf_op jit(solution)/shard_map/ppermute | solution.py:18
  47.9 1.1 %collective-permute-done.18.refs_9_ = f32[2,128]{1,0:T(2,128)S(1)} collective-permute-done((f32[2,128]{1,0:T(2,128)S(1)}, f32[2,128]{1,0:T(2,128)S(1)}, u32[]{:S(2)}, u32[]{:S(2)}) %collective-permute-start.18) | collective-permute-done | bytes 1056 | tf_op jit(solution)/shard_map/ppermute | solution.py:18
  49.0 0.8 %shard_map.45 = (f32[128,384]{1,0:T(8,128)}, f32[1,128]{1,0:T(1,128)}) custom-call(bf16[128,1408]{1,0:T(8,128)(2,1)S(1)} %copy-done.1, f32[1,1536]{1,0:T(1,128)S(1)} %get-tuple-element.17.refs_5_.refs_1_, f32[128,384]{1,0:T(8,128)S(1)} %get-tuple-element.18.refs_2_, f32[128,384]{1,0:T(8,128)S(1)} %get-tuple-element.22.refs_3_, ...), custom_call_target="tpu_custom_call" | custom-call | flops 393216 | bytes 1548288 | tf_op jit(solution)/shard_map/pallas_call | solution.py:222
  (19 shorter events, 0.1 us)
Async XLA Ops:
  2.4 14.1 %collective-permute-start.3 = (bf16[128,1408]{1,0:T(8,128)(2,1)}, bf16[128,1408]{1,0:T(8,128)(2,1)S(1)}, u32[]{:S(2)}, u32[]{:S(2)}) collective-permute-start(bf16[128,1408]{1,0:T(8,128)(2,1)} %shard_map.41.packed_ref.refs_0_), channel_id=1, source_target_pairs={{0,1},{1,2},{2,3},{3,0},{4,5},{5,6},{6,7},{7,4},{8,9},{9,10},{10,1... | collective-permute-start | bytes 1081352 | tf_op jit(solution)/shard_map/ppermute | solution.py:23
  5.4 11.7 %collective-permute-start = (bf16[128,1408]{1,0:T(8,128)(2,1)}, bf16[128,1408]{1,0:T(8,128)(2,1)S(1)}, u32[]{:S(2)}, u32[]{:S(2)}) collective-permute-start(bf16[128,1408]{1,0:T(8,128)(2,1)} %shard_map.41.packed_ref.refs_0_), channel_id=1, source_target_pairs={{0,8},{4,12},{8,0},{12,4},{1,9},{5,13},{9,1},{13,5},{2,10},{6,14},... | collective-permute-start | bytes 1081352 | tf_op jit(solution)/shard_map/ppermute | solution.py:18
  7.0 1.0 %copy-start = (bf16[128,1408]{1,0:T(8,128)(2,1)S(1)}, bf16[128,1408]{1,0:T(8,128)(2,1)}, u32[]{:S(2)}) copy-start(bf16[128,1408]{1,0:T(8,128)(2,1)} %shard_map.41.packed_ref.refs_0_) | copy-start | bytes 1081348
  8.0 14.3 %copy-start.1 = (bf16[128,1408]{1,0:T(8,128)(2,1)S(1)}, bf16[128,1408]{1,0:T(8,128)(2,1)}, u32[]{:S(2)}) copy-start(bf16[128,1408]{1,0:T(8,128)(2,1)} %shard_map.41.packed_ref.refs_0_) | copy-start | bytes 1081348
  8.1 8.3 %collective-permute-start.6 = (f32[1,1536]{1,0:T(1,128)S(1)}, f32[1,1536]{1,0:T(1,128)S(1)}, u32[]{:S(2)}, u32[]{:S(2)}) collective-permute-start(f32[1,1536]{1,0:T(1,128)S(1)} %shard_map.42), channel_id=1, source_target_pairs={{0,3},{1,2},{2,1},{3,0},{4,7},{5,6},{6,5},{7,4},{8,11},{9,10},{10,... | collective-permute-start | bytes 18440 | tf_op jit(solution)/shard_map/ppermute | solution.py:18
  10.4 6.9 %collective-permute-start.5 = (f32[1,1536]{1,0:T(1,128)S(1)}, f32[1,1536]{1,0:T(1,128)S(1)}, u32[]{:S(2)}, u32[]{:S(2)}) collective-permute-start(f32[1,1536]{1,0:T(1,128)S(1)} %shard_map.42), channel_id=1, source_target_pairs={{0,2},{1,3},{2,0},{3,1},{4,6},{5,7},{6,4},{7,5},{8,10},{9,11},{10,... | collective-permute-start | bytes 18440 | tf_op jit(solution)/shard_map/ppermute | solution.py:18
  11.2 6.1 %collective-permute-start.4 = (f32[1,1536]{1,0:T(1,128)S(1)}, f32[1,1536]{1,0:T(1,128)S(1)}, u32[]{:S(2)}, u32[]{:S(2)}) collective-permute-start(f32[1,1536]{1,0:T(1,128)S(1)} %shard_map.42), channel_id=1, source_target_pairs={{0,1},{1,0},{2,3},{3,2},{4,5},{5,4},{6,7},{7,6},{8,9},{9,8},{10,11... | collective-permute-start | bytes 18440 | tf_op jit(solution)/shard_map/ppermute | solution.py:18
  16.4 5.9 %collective-permute-start.1 = (bf16[128,1408]{1,0:T(8,128)(2,1)S(1)}, bf16[128,1408]{1,0:T(8,128)(2,1)S(1)}, u32[]{:S(2)}, u32[]{:S(2)}) collective-permute-start(bf16[128,1408]{1,0:T(8,128)(2,1)S(1)} %copy-done), channel_id=1, source_target_pairs={{0,4},{4,0},{8,12},{12,8},{1,5},{5,1},{9,13},{13,9},{2,6},{6,2},{1... | collective-permute-start | bytes 1081352 | tf_op jit(solution)/shard_map/ppermute | solution.py:18
  16.4 12.7 %collective-permute-start.9 = (bf16[128,1408]{1,0:T(8,128)(2,1)S(1)}, bf16[128,1408]{1,0:T(8,128)(2,1)S(1)}, u32[]{:S(2)}, u32[]{:S(2)}) collective-permute-start(bf16[128,1408]{1,0:T(8,128)(2,1)S(1)} %collective-permute-done.3.refs_4_), channel_id=1, source_target_pairs={{0,1},{1,2},{2,3},{3,0},{4,5},{5,6},{6,7},{7,4},{8,9},{9,10},{10,1... | collective-permute-start | bytes 1081352 | tf_op jit(solution)/shard_map/ppermute | solution.py:23
  17.1 5.2 %collective-permute-start.2 = (bf16[128,1408]{1,0:T(8,128)(2,1)S(1)}, bf16[128,1408]{1,0:T(8,128)(2,1)S(1)}, u32[]{:S(2)}, u32[]{:S(2)}) collective-permute-start(bf16[128,1408]{1,0:T(8,128)(2,1)S(1)} %collective-permute-done.refs_1_), channel_id=1, source_target_pairs={{0,4},{4,0},{8,12},{12,8},{1,5},{5,1},{9,13},{13,9},{2,6},{6,2},{1... | collective-permute-start | bytes 1081352 | tf_op jit(solution)/shard_map/ppermute | solution.py:18
  17.3 3.7 %collective-permute-start.7 = (f32[1,1536]{1,0:T(1,128)S(1)}, f32[1,1536]{1,0:T(1,128)S(1)}, u32[]{:S(2)}, u32[]{:S(2)}) collective-permute-start(f32[1,1536]{1,0:T(1,128)S(1)} %add_add_fusion), channel_id=1, source_target_pairs={{0,8},{4,12},{8,0},{12,4},{1,9},{5,13},{9,1},{13,5},{2,10},{6,14},... | collective-permute-start | bytes 18440 | tf_op jit(solution)/shard_map/ppermute | solution.py:18
  21.0 1.2 %collective-permute-start.8 = (f32[1,1536]{1,0:T(1,128)S(1)}, f32[1,1536]{1,0:T(1,128)S(1)}, u32[]{:S(2)}, u32[]{:S(2)}) collective-permute-start(f32[1,1536]{1,0:T(1,128)S(1)} %add.27.refs_5_), channel_id=1, source_target_pairs={{0,4},{4,0},{8,12},{12,8},{1,5},{5,1},{9,13},{13,9},{2,6},{6,2},{1... | collective-permute-start | bytes 18440 | tf_op jit(solution)/shard_map/ppermute | solution.py:18
  25.2 8.1 %collective-permute-start.10 = (f32[128,384]{1,0:T(8,128)S(1)}, f32[128,384]{1,0:T(8,128)S(1)}, u32[]{:S(2)}, u32[]{:S(2)}) collective-permute-start(f32[128,384]{1,0:T(8,128)S(1)} %get-tuple-element.24), channel_id=1, source_target_pairs={{0,3},{1,0},{2,1},{3,2},{4,7},{5,4},{6,5},{7,6},{8,11},{9,8},{10,9... | collective-permute-start | bytes 589832 | tf_op jit(solution)/shard_map/ppermute | solution.py:23
  33.3 6.0 %collective-permute-start.16 = (f32[2,128]{1,0:T(2,128)S(1)}, f32[2,128]{1,0:T(2,128)S(1)}, u32[]{:S(2)}, u32[]{:S(2)}) collective-permute-start(f32[2,128]{1,0:T(2,128)S(1)} %get-tuple-element.29), channel_id=1, source_target_pairs={{0,3},{1,2},{2,1},{3,0},{4,7},{5,6},{6,5},{7,4},{8,11},{9,10},{10,... | collective-permute-start | bytes 3080 | tf_op jit(solution)/shard_map/ppermute | solution.py:18
  37.2 4.5 %collective-permute-start.15 = (f32[2,128]{1,0:T(2,128)S(1)}, f32[2,128]{1,0:T(2,128)S(1)}, u32[]{:S(2)}, u32[]{:S(2)}) collective-permute-start(f32[2,128]{1,0:T(2,128)S(1)} %get-tuple-element.29), channel_id=1, source_target_pairs={{0,2},{1,3},{2,0},{3,1},{4,6},{5,7},{6,4},{7,5},{8,10},{9,11},{10,... | collective-permute-start | bytes 3080 | tf_op jit(solution)/shard_map/ppermute | solution.py:18
  37.2 4.5 %collective-permute-start.14 = (f32[2,128]{1,0:T(2,128)S(1)}, f32[2,128]{1,0:T(2,128)S(1)}, u32[]{:S(2)}, u32[]{:S(2)}) collective-permute-start(f32[2,128]{1,0:T(2,128)S(1)} %get-tuple-element.29), channel_id=1, source_target_pairs={{0,1},{1,0},{2,3},{3,2},{4,5},{5,4},{6,7},{7,6},{8,9},{9,8},{10,11... | collective-permute-start | bytes 3080 | tf_op jit(solution)/shard_map/ppermute | solution.py:18
  37.8 10.1 %collective-permute-start.11 = (f32[128,384]{1,0:T(8,128)S(1)}, f32[128,384]{1,0:T(8,128)S(1)}, u32[]{:S(2)}, u32[]{:S(2)}) collective-permute-start(f32[128,384]{1,0:T(8,128)S(1)} %get-tuple-element.26), channel_id=1, source_target_pairs={{0,8},{4,12},{8,0},{12,4},{1,9},{5,13},{9,1},{13,5},{2,10},{6,14},... | collective-permute-start | bytes 589832 | tf_op jit(solution)/shard_map/ppermute | solution.py:18
  39.3 8.6 %collective-permute-start.12 = (f32[128,384]{1,0:T(8,128)S(1)}, f32[128,384]{1,0:T(8,128)S(1)}, u32[]{:S(2)}, u32[]{:S(2)}) collective-permute-start(f32[128,384]{1,0:T(8,128)S(1)} %get-tuple-element.27), channel_id=1, source_target_pairs={{0,4},{4,0},{8,12},{12,8},{1,5},{5,1},{9,13},{13,9},{2,6},{6,2},{1... | collective-permute-start | bytes 589832 | tf_op jit(solution)/shard_map/ppermute | solution.py:18
  39.3 8.6 %collective-permute-start.13 = (f32[128,384]{1,0:T(8,128)S(1)}, f32[128,384]{1,0:T(8,128)S(1)}, u32[]{:S(2)}, u32[]{:S(2)}) collective-permute-start(f32[128,384]{1,0:T(8,128)S(1)} %get-tuple-element.28), channel_id=1, source_target_pairs={{0,12},{4,8},{8,4},{12,0},{1,13},{5,9},{9,5},{13,1},{2,14},{6,10},... | collective-permute-start | bytes 589832 | tf_op jit(solution)/shard_map/ppermute | solution.py:18
  41.7 6.2 %collective-permute-start.17 = (f32[2,128]{1,0:T(2,128)S(1)}, f32[2,128]{1,0:T(2,128)S(1)}, u32[]{:S(2)}, u32[]{:S(2)}) collective-permute-start(f32[2,128]{1,0:T(2,128)S(1)} %add_add_fusion.1), channel_id=1, source_target_pairs={{0,8},{4,12},{8,0},{12,4},{1,9},{5,13},{9,1},{13,5},{2,10},{6,14},... | collective-permute-start | bytes 3080 | tf_op jit(solution)/shard_map/ppermute | solution.py:18
  47.9 1.1 %collective-permute-start.18 = (f32[2,128]{1,0:T(2,128)S(1)}, f32[2,128]{1,0:T(2,128)S(1)}, u32[]{:S(2)}, u32[]{:S(2)}) collective-permute-start(f32[2,128]{1,0:T(2,128)S(1)} %add.31.refs_8_), channel_id=1, source_target_pairs={{0,4},{4,0},{8,12},{12,8},{1,5},{5,1},{9,13},{13,9},{2,6},{6,2},{1... | collective-permute-start | bytes 3080 | tf_op jit(solution)/shard_map/ppermute | solution.py:18

commit v4 on v3

--- a/solution.py
+++ b/solution.py
@@ -10,6 +10,8 @@
 FLOOR = 0.01
 EPSILON = 1e-06
 LANES = 128
+SUBLANES = 8
+PARTS = 2
 WHOLE = pl.BlockSpec(memory_space=pltpu.VMEM)
 
 
@@ -23,12 +25,21 @@
     return lax.ppermute(value, axis, [(i, (i + distance) % size) for i in range(size)])
 
 
-def pack_kernel(t_hbm, s_hbm, packed_ref, sems):
+def pack_kernel(t_hbm, s_hbm, packed_hbm, *rest):
+    *part_refs, sems = rest
     t_width = t_hbm.shape[1]
-    copies = [
-        pltpu.make_async_copy(t_hbm, packed_ref.at[:, :t_width], sems.at[0]),
-        pltpu.make_async_copy(s_hbm, packed_ref.at[:, t_width:], sems.at[1]),
-    ]
+    rows = part_refs[0].shape[0]
+    copies = []
+    for i, ref in enumerate([*part_refs, packed_hbm]):
+        start = i * rows if ref is not packed_hbm else 0
+        for j, (source, column) in enumerate(((t_hbm, 0), (s_hbm, t_width))):
+            copies.append(
+                pltpu.make_async_copy(
+                    source.at[start : start + ref.shape[0], :],
+                    ref.at[:, column : column + source.shape[1]],
+                    sems.at[2 * i + j],
+                )
+            )
     for copy in copies:
         copy.start()
     for copy in copies:
@@ -81,6 +92,12 @@
 
 def with_ones(ref):
     return jnp.concatenate([ref[...], jnp.ones((ref.shape[0], LANES), ref.dtype)], axis=1)
+
+
+def dot_rows(weights, value):
+    return lax.dot_general(
+        weights, value, (((0,), (0,)), ((), ())), preferred_element_type=jnp.float32
+    )
 
 
 def pair_tile(v, c, inv_t, inv_s, own):
@@ -119,7 +136,9 @@
 def early_kernel(n_blk, steps, t_width, total_rows, *refs):
     refs = list(refs)
     plane = [halves(refs.pop(0), t_width) for _ in range(n_blk)]
-    line = [plane[0]] + [halves(refs.pop(0), t_width) for _ in range(steps - 1)]
+    line = [[plane[0]]]
+    for _ in range(steps - 1):
+        line.append([halves(refs.pop(0), t_width) for _ in range(PARTS)])
     stats_refs = refs.pop(0), refs.pop(0)
     own_ref = refs.pop(0)
     back_refs = [refs.pop(0) for _ in range(steps - 1)]
@@ -137,30 +156,28 @@
         cols.append((t, s, nt, ns))
     loss = jnp.zeros((1, LANES), jnp.float32)
     spread = jnp.zeros((1, LANES), jnp.float32)
-    for k, (t, s) in enumerate(line):
-        v = (t, s, column_norms(t), column_norms(s))
-        summed = None
-        for d in range(n_blk):
-            weights, loss_part, spread_part = pair_tile(v, cols[d], inv_t, inv_s, k == 0 and d == 0)
-            factor = 1.0 if k == 0 else 2.0
-            loss = loss + factor * loss_part
-            spread = spread + factor * spread_part
-            term = jnp.dot(weights, with_ones(cols[d][1]), preferred_element_type=jnp.float32)
-            summed = term if summed is None else summed + term
-            if k > 0:
-                back = lax.dot_general(
-                    weights,
-                    with_ones(s),
-                    (((0,), (0,)), ((), ())),
-                    preferred_element_type=jnp.float32,
-                )
-                acc_ref[d] = back if k == 1 else acc_ref[d] + back
-        if k == 0:
-            own_ref[...] = direct_of(s, summed)
-        else:
-            back_refs[k - 1][...] = direct_of(s, summed)
     if steps == 1:
         acc_ref[...] = jnp.zeros_like(acc_ref)
+    for k, parts in enumerate(line):
+        for p, (t, s) in enumerate(parts):
+            v = (t, s, column_norms(t), column_norms(s))
+            summed = None
+            for d in range(n_blk):
+                own = k == 0 and d == 0
+                weights, loss_part, spread_part = pair_tile(v, cols[d], inv_t, inv_s, own)
+                factor = 1.0 if k == 0 else 2.0
+                loss = loss + factor * loss_part
+                spread = spread + factor * spread_part
+                term = jnp.dot(weights, with_ones(cols[d][1]), preferred_element_type=jnp.float32)
+                summed = term if summed is None else summed + term
+                if k > 0:
+                    back = dot_rows(weights, with_ones(s))
+                    acc_ref[d] = back if k == 1 and p == 0 else acc_ref[d] + back
+            if k == 0:
+                own_ref[...] = direct_of(s, summed)
+            else:
+                start = p * s.shape[0]
+                back_refs[k - 1][start : start + s.shape[0], :] = direct_of(s, summed)
     sums_ref[0:1, :] = loss
     sums_ref[1:2, :] = spread
 
@@ -168,28 +185,37 @@
 def late_kernel(n_blk, t_width, total_rows, *refs):
     refs = list(refs)
     plane = [halves(refs.pop(0), t_width) for _ in range(n_blk)]
-    t, s = halves(refs.pop(0), t_width)
-    stats_ref, acc_ref, norm_ref, early_sums = (refs.pop(0) for _ in range(4))
-    out_refs = [refs.pop(0) for _ in range(n_blk)]
-    (sums_ref,) = refs
-    s_width = s.shape[1]
+    parts = [halves(refs.pop(0), t_width) for _ in range(PARTS)]
+    stats_ref, acc_ref, norm_ref, early_sums, keep_ref, give_ref = refs
+    rows, s_width = plane[0][1].shape
     spread_t, spread_s, _ = spreads_of(stats_ref[...], t_width, s_width, total_rows)
     inv_t, inv_s = 1.0 / spread_t, 1.0 / spread_s
-    v = (t, s, column_norms(t), column_norms(s))
     loss = early_sums[0:1, :]
     spread = early_sums[1:2, :]
+    visits = [(t, s, column_norms(t), column_norms(s)) for t, s in parts]
     for d in range(n_blk):
         ct, cs = plane[d]
         c = (ct, cs, norm_ref[d : d + 1, :LANES], norm_ref[d : d + 1, LANES:])
-        weights, loss_part, spread_part = pair_tile(v, c, inv_t, inv_s, False)
-        loss = loss + loss_part
-        spread = spread + spread_part
-        back = lax.dot_general(
-            weights, with_ones(s), (((0,), (0,)), ((), ())), preferred_element_type=jnp.float32
-        )
-        out_refs[d][...] = direct_of(cs, acc_ref[d] + back)
-    sums_ref[0:1, :] = loss
-    sums_ref[1:2, :] = spread
+        summed = acc_ref[d]
+        for v in visits:
+            weights, loss_part, spread_part = pair_tile(v, c, inv_t, inv_s, False)
+            loss = loss + loss_part
+            spread = spread + spread_part
+            summed = summed + dot_rows(weights, with_ones(v[1]))
+        to_ref = keep_ref if d < n_blk // 2 else give_ref
+        start = d % (n_blk // 2) * rows
+        to_ref[start : start + rows, :] = direct_of(cs, summed)
+    for ref in (keep_ref, give_ref):
+        ref[-SUBLANES:, :] = jnp.zeros((SUBLANES, s_width), jnp.float32)
+        ref[-SUBLANES : 1 - SUBLANES, :LANES] = loss
+        ref[1 - SUBLANES : 2 - SUBLANES, :LANES] = spread
+
+
+def halve_kernel(rows, keep_ref, got_ref, *out_refs):
+    if len(out_refs) == 3:
+        out_refs[2][...] = keep_ref[-SUBLANES:, :LANES] + got_ref[-SUBLANES:, :LANES]
+    out_refs[0][...] = keep_ref[:rows, :] + got_ref[:rows, :]
+    out_refs[1][...] = keep_ref[rows : 2 * rows, :] + got_ref[rows : 2 * rows, :]
 
 
 def final_kernel(n_parts, t_width, total_rows, *refs):
@@ -219,11 +245,12 @@
 def call(kernel, out_shape, operands, flops, vmem=48, **more):
     nbytes = sum(x.size * x.dtype.itemsize for x in operands)
     in_specs = more.pop("in_specs", [WHOLE] * len(operands))
+    out_specs = more.pop("out_specs", jax.tree.map(lambda _: WHOLE, out_shape))
     return pl.pallas_call(
         kernel,
         out_shape=out_shape,
         in_specs=in_specs,
-        out_specs=jax.tree.map(lambda _: WHOLE, out_shape),
+        out_specs=out_specs,
         compiler_params=pltpu.CompilerParams(vmem_limit_bytes=vmem * 1024 * 1024),
         cost_estimate=pl.CostEstimate(flops=flops, bytes_accessed=nbytes, transcendentals=0),
         **more,
@@ -249,28 +276,32 @@
     half = n_sub // 2
     f32 = functools.partial(jax.ShapeDtypeStruct, dtype=jnp.float32)
 
-    packed = call(
+    whole = pl.BlockSpec(memory_space=pl.ANY)
+    shapes = [(rows, t_width + s_width)] + [(rows // PARTS, t_width + s_width)] * PARTS
+    packed, *parts = call(
         pack_kernel,
-        jax.ShapeDtypeStruct((rows, t_width + s_width), teacher.dtype),
+        [jax.ShapeDtypeStruct(shape, teacher.dtype) for shape in shapes],
         (teacher, student),
         0,
         vmem=62,
-        in_specs=[pl.BlockSpec(memory_space=pl.ANY)] * 2,
-        scratch_shapes=[pltpu.SemaphoreType.DMA((2,))],
-    )
-    line = [packed]
+        in_specs=[whole] * 2,
+        out_specs=[whole] * len(shapes),
+        scratch_shapes=[pltpu.SemaphoreType.DMA((2 * len(shapes),))],
+    )
+    line = [parts]
     for _ in range(half):
-        line.append(shifted(line[-1], "sub", 1))
-    plane, distances = [packed], [0]
-    for distance in halvings("blk"):
-        plane = plane + [exchange(x, "blk", distance) for x in plane]
-        distances = distances + [x ^ distance for x in distances]
+        line.append([shifted(x, "sub", 1) for x in line[-1]])
     stats = call(
         functools.partial(stats_kernel, t_width),
         f32((1, t_width + s_width + LANES)),
         (packed,),
         4 * packed.size,
     )
+    plane = [packed]
+    for distance in halvings("blk"):
+        if distance == 1:
+            plane = list(lax.optimization_barrier(tuple(plane)))
+        plane = plane + [exchange(x, "blk", distance) for x in plane]
     stats = functools.reduce(jnp.add, gathered(stats, "sub"))
     for distance in halvings("blk")[:-1]:
         stats = stats + exchange(stats, "blk", distance)
@@ -285,24 +316,37 @@
     *tiles, acc, norms, totals, early_sums = call(
         functools.partial(early_kernel, n_blk, half, t_width, total_rows),
         out_shape,
-        plane + line[1:half] + [stats, stats_other],
+        plane + [x for pair in line[1:half] for x in pair] + [stats, stats_other],
         half * pair_flops,
     )
     own, backs = tiles[0], tiles[1:]
     returned = [shifted(x, "sub", -k) for k, x in enumerate(backs, 1)]
-    *shares, sums = call(
+    mine = f32((rows * n_blk // 2 + SUBLANES, s_width))
+    keep, give = call(
         functools.partial(late_kernel, n_blk, t_width, total_rows),
-        [f32((rows, s_width))] * n_blk + [f32((2, LANES))],
-        plane + [line[half], totals, acc, norms, early_sums],
+        [mine, mine],
+        plane + line[half] + [totals, acc, norms, early_sums],
         pair_flops,
     )
-    received = [exchange(share, "blk", d) for share, d in zip(shares[1:], distances[1:])]
-    sums, returned = lax.optimization_barrier((sums, returned))
-    sums = functools.reduce(jnp.add, gathered(sums, "sub"))
+    got = exchange(give, "blk", 1)
+    tiles, distance = n_blk // 2, 2
+    while tiles > 1:
+        tiles //= 2
+        out_shape = [f32((rows * tiles, s_width))] * 2
+        if distance == 2:
+            out_shape = out_shape + [f32((SUBLANES, LANES))]
+        keep, give, *rest = call(
+            functools.partial(halve_kernel, rows * tiles), out_shape, (keep, got), 2 * keep.size
+        )
+        got = exchange(give, "blk", distance)
+        if distance == 2:
+            sums = functools.reduce(jnp.add, gathered(rest[0], "sub"))
+        distance *= 2
+    all_sums = [sums]
     for distance in halvings("blk")[:-1]:
-        sums = sums + exchange(sums, "blk", distance)
-    all_sums = [sums, exchange(sums, "blk", 1)]
-    parts = [own, shares[0]] + returned + received
+        all_sums = [sum(all_sums[1:], all_sums[0])]
+        all_sums.append(exchange(all_sums[0], "blk", distance))
+    parts = [own, keep, got] + returned
     grad, loss = call(
         functools.partial(final_kernel, len(parts), t_width, total_rows),
         [f32((rows, s_width)), f32((1, LANES))],

time: 50 us -> 68.7 us (1.37)
  Pallas kernels: 7.37 us -> 31.2 us
  waiting for transfers between devices: 17.8 us -> 14.5 us
  starting transfers between devices: 23 us -> 21.1 us
    pallas_call x5 -> x6, Pallas kernels: 7.37 us -> 31.2 us  [call(): pl.pallas_call(kernel, out_shape=out_shape, in_specs=in_specs, out_specs=...]
    ppermute x16 -> x14, waiting for transfers between devices: 14.7 us -> 8.04 us  [exchange(): return lax.ppermute(value, axis, [(i, i ^ distance) for i in range(size)])]
    ppermute x3 -> x5, waiting for transfers between devices: 3.1 us -> 6.48 us  [shifted(): lax.ppermute(value, axis, [(i, (i + distance) % size) for i in range(size)])]
    ppermute x16 -> x14, starting transfers between devices: 16 us -> 14 us  [exchange(): return lax.ppermute(value, axis, [(i, i ^ distance) for i in range(size)])]
    ppermute x3 -> x5, starting transfers between devices: 6.95 us -> 7.06 us  [shifted(): lax.ppermute(value, axis, [(i, (i + distance) % size) for i in range(size)])]
  transfers between devices with their start and end apart: 19 -> 19, of which waited for: 8 -> 7; matrix products, arithmetic and copies ran while one was open for 0% -> 0% of each run, Pallas kernels for 10% -> 6%
where the time goes in v4:
time: 68.7 us; the launch traced here: 68.6 us
  Pallas kernels  31.2 us (45%)
  starting transfers between devices  21.1 us (31%)
  waiting for transfers between devices  14.5 us (21%)
  local copies, waits for them, and re-layouts  0.99 us (1%)
  between operations  0.71 us (1%)
    pallas_call x6, Pallas kernels, call(): pl.pallas_call(kernel, out_shape=out_shape, in_specs=in_specs, out_specs=...  31.2 us
    ppermute x14, starting transfers between devices, exchange(): return lax.ppermute(value, axis, [(i, i ^ distance) for i in range(size)])  14 us
    ppermute x14, waiting for transfers between devices, exchange(): return lax.ppermute(value, axis, [(i, i ^ distance) for i in range(size)])  8.04 us
    ppermute x5, starting transfers between devices, shifted(): lax.ppermute(value, axis, [(i, (i + distance) % size) for i in range(size)])  7.06 us
    ppermute x5, waiting for transfers between devices, shifted(): lax.ppermute(value, axis, [(i, (i + distance) % size) for i in range(size)])  6.48 us
  transfers between devices with their start and end apart: 19, of which 7 were waited for; matrix products, arithmetic and copies ran while one was open for 0% of the time, Pallas kernels for 6%

profile of v4, /device:TPU:0, one launch (start us, length us, event | category | flops | bytes accessed | tf_op | source)
XLA Modules:
  0.0 68.6 jit_solution(4907389104607655843)
XLA Ops:
  0.6 23.0 %shard_map.41 = (bf16[128,1408]{1,0:T(8,128)(2,1)}, bf16[64,1408]{1,0:T(8,128)(2,1)}, bf16[64,1408]{1,0:T(8,128)(2,1)}) custom-call(bf16[128,1024]{1,0:T(8,128)(2,1)} %t_hbm.1, bf16[128,384]{1,0:T(8,128)(2,1)} %s_hbm.1), custom_call_target="tpu_custom_call" | custom-call | bytes 360448 | tf_op jit(solution)/shard_map/pallas_call | solution.py:249
  23.6 3.0 %collective-permute-start = (bf16[128,1408]{1,0:T(8,128)(2,1)}, bf16[128,1408]{1,0:T(8,128)(2,1)S(1)}, u32[]{:S(2)}, u32[]{:S(2)}) collective-permute-start(bf16[128,1408]{1,0:T(8,128)(2,1)} %get-tuple-element.21.packed_ref.refs_0_), channel_id=1, source_target_pairs={{0,8},{4,12},{8,0},{12,4},{1,9},{5,13},{9,1},{13,5},{2,10},{6,14},... | collective-permute-start | bytes 1081352 | tf_op jit(solution)/shard_map/ppermute | solution.py:20
  26.7 1.6 %collective-permute-start.3 = (bf16[64,1408]{1,0:T(8,128)(2,1)}, bf16[64,1408]{1,0:T(8,128)(2,1)S(1)}, u32[]{:S(2)}, u32[]{:S(2)}) collective-permute-start(bf16[64,1408]{1,0:T(8,128)(2,1)} %get-tuple-element.23), channel_id=1, source_target_pairs={{0,1},{1,2},{2,3},{3,0},{4,5},{5,6},{6,7},{7,4},{8,9},{9,10},{10,1... | collective-permute-start | bytes 540680 | tf_op jit(solution)/shard_map/ppermute | solution.py:25
  28.2 1.6 %collective-permute-start.4 = (bf16[64,1408]{1,0:T(8,128)(2,1)}, bf16[64,1408]{1,0:T(8,128)(2,1)S(1)}, u32[]{:S(2)}, u32[]{:S(2)}) collective-permute-start(bf16[64,1408]{1,0:T(8,128)(2,1)} %get-tuple-element.24), channel_id=1, source_target_pairs={{0,1},{1,2},{2,3},{3,0},{4,5},{5,6},{6,7},{7,4},{8,9},{9,10},{10,1... | collective-permute-start | bytes 540680 | tf_op jit(solution)/shard_map/ppermute | solution.py:25
  29.8 1.0 %copy-done = bf16[128,1408]{1,0:T(8,128)(2,1)S(1)} copy-done((bf16[128,1408]{1,0:T(8,128)(2,1)S(1)}, bf16[128,1408]{1,0:T(8,128)(2,1)}, u32[]{:S(2)}) %copy-start) | copy-done | bytes 360472
  30.8 0.2 shard_map.42
  31.0 2.2 %collective-permute-start.7 = (f32[1,1536]{1,0:T(1,128)S(1)}, f32[1,1536]{1,0:T(1,128)S(1)}, u32[]{:S(2)}, u32[]{:S(2)}) collective-permute-start(f32[1,1536]{1,0:T(1,128)S(1)} %shard_map.42), channel_id=1, source_target_pairs={{0,3},{1,2},{2,1},{3,0},{4,7},{5,6},{6,5},{7,4},{8,11},{9,10},{10,... | collective-permute-start | bytes 18440 | tf_op jit(solution)/shard_map/ppermute | solution.py:20
  33.2 0.8 %collective-permute-start.6 = (f32[1,1536]{1,0:T(1,128)S(1)}, f32[1,1536]{1,0:T(1,128)S(1)}, u32[]{:S(2)}, u32[]{:S(2)}) collective-permute-start(f32[1,1536]{1,0:T(1,128)S(1)} %shard_map.42), channel_id=1, source_target_pairs={{0,2},{1,3},{2,0},{3,1},{4,6},{5,7},{6,4},{7,5},{8,10},{9,11},{10,... | collective-permute-start | bytes 18440 | tf_op jit(solution)/shard_map/ppermute | solution.py:20
  34.0 2.2 %collective-permute-done.3.refs_4_ = bf16[64,1408]{1,0:T(8,128)(2,1)S(1)} collective-permute-done((bf16[64,1408]{1,0:T(8,128)(2,1)}, bf16[64,1408]{1,0:T(8,128)(2,1)S(1)}, u32[]{:S(2)}, u32[]{:S(2)}) %collective-permute-start.3) | collective-permute-done | bytes 180256 | tf_op jit(solution)/shard_map/ppermute | solution.py:25
  36.3 0.0 collective-permute-start.5
  36.3 2.6 %collective-permute-done.4.refs_5_ = bf16[64,1408]{1,0:T(8,128)(2,1)S(1)} collective-permute-done((bf16[64,1408]{1,0:T(8,128)(2,1)}, bf16[64,1408]{1,0:T(8,128)(2,1)S(1)}, u32[]{:S(2)}, u32[]{:S(2)}) %collective-permute-start.4) | collective-permute-done | bytes 180256 | tf_op jit(solution)/shard_map/ppermute | solution.py:25
  38.8 0.0 collective-permute-start.10
  38.8 0.0 collective-permute-done.refs_1_
  38.9 1.4 %collective-permute-start.11 = (bf16[64,1408]{1,0:T(8,128)(2,1)S(1)}, bf16[64,1408]{1,0:T(8,128)(2,1)S(1)}, u32[]{:S(2)}, u32[]{:S(2)}) collective-permute-start(bf16[64,1408]{1,0:T(8,128)(2,1)S(1)} %collective-permute-done.4.refs_5_), channel_id=1, source_target_pairs={{0,1},{1,2},{2,3},{3,0},{4,5},{5,6},{6,7},{7,4},{8,9},{9,10},{10,1... | collective-permute-start | bytes 540680 | tf_op jit(solution)/shard_map/ppermute | solution.py:25
  40.3 0.5 collective-permute-start.2
  40.8 0.6 collective-permute-start.8
  41.4 3.1 %collective-permute-done.8 = f32[1,1536]{1,0:T(1,128)S(1)} collective-permute-done((f32[1,1536]{1,0:T(1,128)S(1)}, f32[1,1536]{1,0:T(1,128)S(1)}, u32[]{:S(2)}, u32[]{:S(2)}) %collective-permute-start.8) | collective-permute-done | bytes 6176 | tf_op jit(solution)/shard_map/ppermute | solution.py:20
  44.5 0.1 collective-permute-start.9
  44.6 1.2 %collective-permute-done.9.refs_7_ = f32[1,1536]{1,0:T(1,128)S(1)} collective-permute-done((f32[1,1536]{1,0:T(1,128)S(1)}, f32[1,1536]{1,0:T(1,128)S(1)}, u32[]{:S(2)}, u32[]{:S(2)}) %collective-permute-start.9) | collective-permute-done | bytes 6176 | tf_op jit(solution)/shard_map/ppermute | solution.py:20
  45.8 4.2 %shard_map.43 = (f32[128,384]{1,0:T(8,128)S(1)}, f32[128,384]{1,0:T(8,128)S(1)}, f32[4,128,512]{2,1,0:T(8,128)S(1)}, f32[4,256]{1,0:T(4,128)S(1)}, f32[1,1536]{1,0:T(1,128)S(1)}, /*index=5*/f32[2,128]{1,0:T(2,128)S(1)}) custom-call(bf16[128,1408]{1,0:T(8,128)(2,1)S(1)} %copy-done, bf16[128,1408]{1,0:T(8,128)(2,1)S(1)} %collective-permute-done.refs_1_, ...), custom_call_target="tpu_custom_call" | custom-call | flops 570425344 | bytes 1814528 | tf_op jit(solution)/shard_map/pallas_call | solution.py:249
  50.0 3.0 %shard_map.44 = (f32[264,384]{1,0:T(8,128)S(1)}, f32[264,384]{1,0:T(8,128)S(1)}) custom-call(bf16[128,1408]{1,0:T(8,128)(2,1)S(1)} %copy-done, bf16[128,1408]{1,0:T(8,128)(2,1)S(1)} %collective-permute-done.refs_1_, bf16[128,1408]{1,0:T(8,128)(2,1)S(1)} %collective-permute-done.1.refs_2_, bf16[128,1408]{1,0:T(8,128)(2,1)S(1)} %collective-permute-done.2.refs_3_, ...), custom_call_target="tpu_custom_call" | custom-call | flops 285212672 | bytes 2862080 | tf_op jit(solution)/shard_map/pallas_call | solution.py:249
  53.0 0.2 collective-permute-start.12
  53.2 1.6 %collective-permute-done.12.got_ref = f32[264,384]{1,0:T(8,128)S(1)} collective-permute-done((f32[264,384]{1,0:T(8,128)S(1)}, f32[264,384]{1,0:T(8,128)S(1)}, u32[]{:S(2)}, u32[]{:S(2)}) %collective-permute-start.12) | collective-permute-done | bytes 405536 | tf_op jit(solution)/shard_map/ppermute | solution.py:20
  54.9 2.5 %collective-permute-start.17 = (f32[8,128]{1,0:T(8,128)S(1)}, f32[8,128]{1,0:T(8,128)S(1)}, u32[]{:S(2)}, u32[]{:S(2)}) collective-permute-start(f32[8,128]{1,0:T(8,128)S(1)} %get-tuple-element.35), channel_id=1, source_target_pairs={{0,3},{1,2},{2,1},{3,0},{4,7},{5,6},{6,5},{7,4},{8,11},{9,10},{10,... | collective-permute-start | bytes 12296 | tf_op jit(solution)/shard_map/ppermute | solution.py:20
  57.4 0.6 collective-permute-start.16
  57.9 1.4 %collective-permute-start.15 = (f32[8,128]{1,0:T(8,128)S(1)}, f32[8,128]{1,0:T(8,128)S(1)}, u32[]{:S(2)}, u32[]{:S(2)}) collective-permute-start(f32[8,128]{1,0:T(8,128)S(1)} %get-tuple-element.35), channel_id=1, source_target_pairs={{0,1},{1,0},{2,3},{3,2},{4,5},{5,4},{6,7},{7,6},{8,9},{9,8},{10,11... | collective-permute-start | bytes 12296 | tf_op jit(solution)/shard_map/ppermute | solution.py:20
  59.3 2.5 %collective-permute-start.14 = (f32[128,384]{1,0:T(8,128)S(1)}, f32[128,384]{1,0:T(8,128)S(1)}, u32[]{:S(2)}, u32[]{:S(2)}) collective-permute-start(f32[128,384]{1,0:T(8,128)S(1)} %get-tuple-element.34), channel_id=1, source_target_pairs={{0,3},{1,0},{2,1},{3,2},{4,7},{5,4},{6,5},{7,6},{8,11},{9,8},{10,9... | collective-permute-start | bytes 589832 | tf_op jit(solution)/shard_map/ppermute | solution.py:25
  61.8 0.5 collective-permute-start.13
  62.3 1.6 %collective-permute-start.18 = (f32[8,128]{1,0:T(8,128)S(1)}, f32[8,128]{1,0:T(8,128)S(1)}, u32[]{:S(2)}, u32[]{:S(2)}) collective-permute-start(f32[8,128]{1,0:T(8,128)S(1)} %add_add_fusion.1.refs_6_), channel_id=1, source_target_pairs={{0,8},{4,12},{8,0},{12,4},{1,9},{5,13},{9,1},{13,5},{2,10},{6,14},... | collective-permute-start | bytes 12296 | tf_op jit(solution)/shard_map/ppermute | solution.py:20
  63.9 1.6 %collective-permute-done.14.refs_5_ = f32[128,384]{1,0:T(8,128)S(1)} collective-permute-done((f32[128,384]{1,0:T(8,128)S(1)}, f32[128,384]{1,0:T(8,128)S(1)}, u32[]{:S(2)}, u32[]{:S(2)}) %collective-permute-start.14) | collective-permute-done | bytes 196640 | tf_op jit(solution)/shard_map/ppermute | solution.py:25
  65.5 2.2 %collective-permute-done.18.refs_7_ = f32[8,128]{1,0:T(8,128)S(1)} collective-permute-done((f32[8,128]{1,0:T(8,128)S(1)}, f32[8,128]{1,0:T(8,128)S(1)}, u32[]{:S(2)}, u32[]{:S(2)}) %collective-permute-start.18) | collective-permute-done | bytes 4128 | tf_op jit(solution)/shard_map/ppermute | solution.py:20
  67.7 0.9 %shard_map.46 = (f32[128,384]{1,0:T(8,128)}, f32[1,128]{1,0:T(1,128)}) custom-call(bf16[128,1408]{1,0:T(8,128)(2,1)S(1)} %copy-done.1, f32[1,1536]{1,0:T(1,128)S(1)} %get-tuple-element.25.refs_6_.refs_1_, f32[128,384]{1,0:T(8,128)S(1)} %get-tuple-element.26.refs_2_, f32[128,384]{1,0:T(8,128)S(1)} %get-tuple-element.32.refs_3_, ...), custom_call_target="tpu_custom_call" | custom-call | flops 393216 | bytes 1161216 | tf_op jit(solution)/shard_map/pallas_call | solution.py:249
  (19 shorter events, 0.1 us)
Async XLA Ops:
  23.6 15.2 %collective-permute-start = (bf16[128,1408]{1,0:T(8,128)(2,1)}, bf16[128,1408]{1,0:T(8,128)(2,1)S(1)}, u32[]{:S(2)}, u32[]{:S(2)}) collective-permute-start(bf16[128,1408]{1,0:T(8,128)(2,1)} %get-tuple-element.21.packed_ref.refs_0_), channel_id=1, source_target_pairs={{0,8},{4,12},{8,0},{12,4},{1,9},{5,13},{9,1},{13,5},{2,10},{6,14},... | collective-permute-start | bytes 1081352 | tf_op jit(solution)/shard_map/ppermute | solution.py:20
  26.7 9.6 %collective-permute-start.3 = (bf16[64,1408]{1,0:T(8,128)(2,1)}, bf16[64,1408]{1,0:T(8,128)(2,1)S(1)}, u32[]{:S(2)}, u32[]{:S(2)}) collective-permute-start(bf16[64,1408]{1,0:T(8,128)(2,1)} %get-tuple-element.23), channel_id=1, source_target_pairs={{0,1},{1,2},{2,3},{3,0},{4,5},{5,6},{6,7},{7,4},{8,9},{9,10},{10,1... | collective-permute-start | bytes 540680 | tf_op jit(solution)/shard_map/ppermute | solution.py:25
  28.2 10.6 %collective-permute-start.4 = (bf16[64,1408]{1,0:T(8,128)(2,1)}, bf16[64,1408]{1,0:T(8,128)(2,1)S(1)}, u32[]{:S(2)}, u32[]{:S(2)}) collective-permute-start(bf16[64,1408]{1,0:T(8,128)(2,1)} %get-tuple-element.24), channel_id=1, source_target_pairs={{0,1},{1,2},{2,3},{3,0},{4,5},{5,6},{6,7},{7,4},{8,9},{9,10},{10,1... | collective-permute-start | bytes 540680 | tf_op jit(solution)/shard_map/ppermute | solution.py:25
  29.8 1.0 %copy-start = (bf16[128,1408]{1,0:T(8,128)(2,1)S(1)}, bf16[128,1408]{1,0:T(8,128)(2,1)}, u32[]{:S(2)}) copy-start(bf16[128,1408]{1,0:T(8,128)(2,1)} %get-tuple-element.21.packed_ref.refs_0_) | copy-start | bytes 1081348
  31.0 9.3 %collective-permute-start.7 = (f32[1,1536]{1,0:T(1,128)S(1)}, f32[1,1536]{1,0:T(1,128)S(1)}, u32[]{:S(2)}, u32[]{:S(2)}) collective-permute-start(f32[1,1536]{1,0:T(1,128)S(1)} %shard_map.42), channel_id=1, source_target_pairs={{0,3},{1,2},{2,1},{3,0},{4,7},{5,6},{6,5},{7,4},{8,11},{9,10},{10,... | collective-permute-start | bytes 18440 | tf_op jit(solution)/shard_map/ppermute | solution.py:20
  33.2 7.1 %collective-permute-start.6 = (f32[1,1536]{1,0:T(1,128)S(1)}, f32[1,1536]{1,0:T(1,128)S(1)}, u32[]{:S(2)}, u32[]{:S(2)}) collective-permute-start(f32[1,1536]{1,0:T(1,128)S(1)} %shard_map.42), channel_id=1, source_target_pairs={{0,2},{1,3},{2,0},{3,1},{4,6},{5,7},{6,4},{7,5},{8,10},{9,11},{10,... | collective-permute-start | bytes 18440 | tf_op jit(solution)/shard_map/ppermute | solution.py:20
  36.3 4.6 %collective-permute-start.5 = (f32[1,1536]{1,0:T(1,128)S(1)}, f32[1,1536]{1,0:T(1,128)S(1)}, u32[]{:S(2)}, u32[]{:S(2)}) collective-permute-start(f32[1,1536]{1,0:T(1,128)S(1)} %shard_map.42), channel_id=1, source_target_pairs={{0,1},{1,0},{2,3},{3,2},{4,5},{5,4},{6,7},{7,6},{8,9},{9,8},{10,11... | collective-permute-start | bytes 18440 | tf_op jit(solution)/shard_map/ppermute | solution.py:20
  38.8 11.1 %collective-permute-start.10 = (bf16[64,1408]{1,0:T(8,128)(2,1)S(1)}, bf16[64,1408]{1,0:T(8,128)(2,1)S(1)}, u32[]{:S(2)}, u32[]{:S(2)}) collective-permute-start(bf16[64,1408]{1,0:T(8,128)(2,1)S(1)} %collective-permute-done.3.refs_4_), channel_id=1, source_target_pairs={{0,1},{1,2},{2,3},{3,0},{4,5},{5,6},{6,7},{7,4},{8,9},{9,10},{10,1... | collective-permute-start | bytes 540680 | tf_op jit(solution)/shard_map/ppermute | solution.py:25
  38.9 11.1 %collective-permute-start.11 = (bf16[64,1408]{1,0:T(8,128)(2,1)S(1)}, bf16[64,1408]{1,0:T(8,128)(2,1)S(1)}, u32[]{:S(2)}, u32[]{:S(2)}) collective-permute-start(bf16[64,1408]{1,0:T(8,128)(2,1)S(1)} %collective-permute-done.4.refs_5_), channel_id=1, source_target_pairs={{0,1},{1,2},{2,3},{3,0},{4,5},{5,6},{6,7},{7,4},{8,9},{9,10},{10,1... | collective-permute-start | bytes 540680 | tf_op jit(solution)/shard_map/ppermute | solution.py:25
  40.3 5.5 %collective-permute-start.1 = (bf16[128,1408]{1,0:T(8,128)(2,1)S(1)}, bf16[128,1408]{1,0:T(8,128)(2,1)S(1)}, u32[]{:S(2)}, u32[]{:S(2)}) collective-permute-start(bf16[128,1408]{1,0:T(8,128)(2,1)S(1)} %copy-done), channel_id=1, source_target_pairs={{0,4},{4,0},{8,12},{12,8},{1,5},{5,1},{9,13},{13,9},{2,6},{6,2},{1... | collective-permute-start | bytes 1081352 | tf_op jit(solution)/shard_map/ppermute | solution.py:20
  40.3 5.5 %collective-permute-start.2 = (bf16[128,1408]{1,0:T(8,128)(2,1)S(1)}, bf16[128,1408]{1,0:T(8,128)(2,1)S(1)}, u32[]{:S(2)}, u32[]{:S(2)}) collective-permute-start(bf16[128,1408]{1,0:T(8,128)(2,1)S(1)} %collective-permute-done.refs_1_), channel_id=1, source_target_pairs={{0,4},{4,0},{8,12},{12,8},{1,5},{5,1},{9,13},{13,9},{2,6},{6,2},{1... | collective-permute-start | bytes 1081352 | tf_op jit(solution)/shard_map/ppermute | solution.py:20
  40.8 3.7 %collective-permute-start.8 = (f32[1,1536]{1,0:T(1,128)S(1)}, f32[1,1536]{1,0:T(1,128)S(1)}, u32[]{:S(2)}, u32[]{:S(2)}) collective-permute-start(f32[1,1536]{1,0:T(1,128)S(1)} %add_add_fusion), channel_id=1, source_target_pairs={{0,8},{4,12},{8,0},{12,4},{1,9},{5,13},{9,1},{13,5},{2,10},{6,14},... | collective-permute-start | bytes 18440 | tf_op jit(solution)/shard_map/ppermute | solution.py:20
  44.5 1.2 %collective-permute-start.9 = (f32[1,1536]{1,0:T(1,128)S(1)}, f32[1,1536]{1,0:T(1,128)S(1)}, u32[]{:S(2)}, u32[]{:S(2)}) collective-permute-start(f32[1,1536]{1,0:T(1,128)S(1)} %add.24.refs_6_), channel_id=1, source_target_pairs={{0,4},{4,0},{8,12},{12,8},{1,5},{5,1},{9,13},{13,9},{2,6},{6,2},{1... | collective-permute-start | bytes 18440 | tf_op jit(solution)/shard_map/ppermute | solution.py:20
  53.0 1.8 %collective-permute-start.12 = (f32[264,384]{1,0:T(8,128)S(1)}, f32[264,384]{1,0:T(8,128)S(1)}, u32[]{:S(2)}, u32[]{:S(2)}) collective-permute-start(f32[264,384]{1,0:T(8,128)S(1)} %get-tuple-element.31), channel_id=1, source_target_pairs={{0,4},{4,0},{8,12},{12,8},{1,5},{5,1},{9,13},{13,9},{2,6},{6,2},{1... | collective-permute-start | bytes 1216520 | tf_op jit(solution)/shard_map/ppermute | solution.py:20
  54.8 12.9 %copy-start.1 = (bf16[128,1408]{1,0:T(8,128)(2,1)S(1)}, bf16[128,1408]{1,0:T(8,128)(2,1)}, u32[]{:S(2)}) copy-start(bf16[128,1408]{1,0:T(8,128)(2,1)} %get-tuple-element.21.packed_ref.refs_0_) | copy-start | bytes 1081348
  54.9 7.4 %collective-permute-start.17 = (f32[8,128]{1,0:T(8,128)S(1)}, f32[8,128]{1,0:T(8,128)S(1)}, u32[]{:S(2)}, u32[]{:S(2)}) collective-permute-start(f32[8,128]{1,0:T(8,128)S(1)} %get-tuple-element.35), channel_id=1, source_target_pairs={{0,3},{1,2},{2,1},{3,0},{4,7},{5,6},{6,5},{7,4},{8,11},{9,10},{10,... | collective-permute-start | bytes 12296 | tf_op jit(solution)/shard_map/ppermute | solution.py:20
  57.4 4.9 %collective-permute-start.16 = (f32[8,128]{1,0:T(8,128)S(1)}, f32[8,128]{1,0:T(8,128)S(1)}, u32[]{:S(2)}, u32[]{:S(2)}) collective-permute-start(f32[8,128]{1,0:T(8,128)S(1)} %get-tuple-element.35), channel_id=1, source_target_pairs={{0,2},{1,3},{2,0},{3,1},{4,6},{5,7},{6,4},{7,5},{8,10},{9,11},{10,... | collective-permute-start | bytes 12296 | tf_op jit(solution)/shard_map/ppermute | solution.py:20
  57.9 4.4 %collective-permute-start.15 = (f32[8,128]{1,0:T(8,128)S(1)}, f32[8,128]{1,0:T(8,128)S(1)}, u32[]{:S(2)}, u32[]{:S(2)}) collective-permute-start(f32[8,128]{1,0:T(8,128)S(1)} %get-tuple-element.35), channel_id=1, source_target_pairs={{0,1},{1,0},{2,3},{3,2},{4,5},{5,4},{6,7},{7,6},{8,9},{9,8},{10,11... | collective-permute-start | bytes 12296 | tf_op jit(solution)/shard_map/ppermute | solution.py:20
  59.3 6.2 %collective-permute-start.14 = (f32[128,384]{1,0:T(8,128)S(1)}, f32[128,384]{1,0:T(8,128)S(1)}, u32[]{:S(2)}, u32[]{:S(2)}) collective-permute-start(f32[128,384]{1,0:T(8,128)S(1)} %get-tuple-element.34), channel_id=1, source_target_pairs={{0,3},{1,0},{2,1},{3,2},{4,7},{5,4},{6,5},{7,6},{8,11},{9,8},{10,9... | collective-permute-start | bytes 589832 | tf_op jit(solution)/shard_map/ppermute | solution.py:25
  61.8 5.9 %collective-permute-start.13 = (f32[128,384]{1,0:T(8,128)S(1)}, f32[128,384]{1,0:T(8,128)S(1)}, u32[]{:S(2)}, u32[]{:S(2)}) collective-permute-start(f32[128,384]{1,0:T(8,128)S(1)} %get-tuple-element.33), channel_id=1, source_target_pairs={{0,8},{4,12},{8,0},{12,4},{1,9},{5,13},{9,1},{13,5},{2,10},{6,14},... | collective-permute-start | bytes 589832 | tf_op jit(solution)/shard_map/ppermute | solution.py:20
  62.3 5.4 %collective-permute-start.18 = (f32[8,128]{1,0:T(8,128)S(1)}, f32[8,128]{1,0:T(8,128)S(1)}, u32[]{:S(2)}, u32[]{:S(2)}) collective-permute-start(f32[8,128]{1,0:T(8,128)S(1)} %add_add_fusion.1.refs_6_), channel_id=1, source_target_pairs={{0,8},{4,12},{8,0},{12,4},{1,9},{5,13},{9,1},{13,5},{2,10},{6,14},... | collective-permute-start | bytes 12296 | tf_op jit(solution)/shard_map/ppermute | solution.py:20

commit v5 on v3

v5 whole, which is shorter than its diff:
```python
import functools

import jax
import jax.numpy as jnp
from jax import lax
from jax.experimental import pallas as pl
from jax.experimental.pallas import tpu as pltpu
from jax.sharding import PartitionSpec as P

FLOOR = 0.01
EPSILON = 1e-06
LANES = 128
CHUNK = 256
WHOLE = pl.BlockSpec(memory_space=pltpu.VMEM)


def exchange(value, axis, distance):
    size = lax.axis_size(axis)
    return lax.ppermute(value, axis, [(i, i ^ distance) for i in range(size)])


def shifted(value, axis, distance):
    size = lax.axis_size(axis)
    return lax.ppermute(value, axis, [(i, (i + distance) % size) for i in range(size)])


def pack_kernel(t_hbm, s_hbm, packed_ref, stats_ref, sems):
    t_width = t_hbm.shape[1]
    copies = [
        pltpu.make_async_copy(t_hbm, packed_ref.at[:, :t_width], sems.at[0]),
        pltpu.make_async_copy(s_hbm, packed_ref.at[:, t_width:], sems.at[1]),
    ]
    for copy in copies:
        copy.start()
    for copy in copies:
        copy.wait()
    value = packed_ref[...].astype(jnp.float32)
    squares = jnp.sum(value * value, axis=0, keepdims=True)
    square_t = jnp.sum(squares[:, :t_width], axis=1, keepdims=True)
    square_s = jnp.sum(squares[:, t_width:], axis=1, keepdims=True)
    lane = lax.broadcasted_iota(jnp.int32, (1, LANES), 1)
    width = value.shape[1]
    stats_ref[:, :width] = jnp.sum(value, axis=0, keepdims=True)
    stats_ref[:, width:] = jnp.where(lane == 0, square_t, jnp.where(lane == 1, square_s, 0.0))


def spreads_of(stats, t_width, s_width, total_rows):
    centre_t = stats[:, :t_width] / total_rows
    centre_s = stats[:, t_width : t_width + s_width] / total_rows
    square_t = stats[:, t_width + s_width : t_width + s_width + 1]
    square_s = stats[:, t_width + s_width + 1 : t_width + s_width + 2]
    spread_t = (
        2.0 * (square_t / total_rows - jnp.sum(centre_t * centre_t, axis=1, keepdims=True)) + EPSILON
    )
    spread_s = (
        2.0 * (square_s / total_rows - jnp.sum(centre_s * centre_s, axis=1, keepdims=True)) + EPSILON
    )
    return spread_t, spread_s, centre_s


def norms_of(value):
    value = value.astype(jnp.float32)
    return jnp.sum(value * value, axis=1, keepdims=True)


def as_row(column):
    rows = column.shape[0]
    row = lax.broadcasted_iota(jnp.int32, (rows, rows), 0)
    same = row == lax.broadcasted_iota(jnp.int32, (rows, rows), 1)
    return jnp.sum(jnp.where(same, column, 0.0), axis=0, keepdims=True)


def with_ones(value):
    return jnp.concatenate([value, jnp.ones((value.shape[0], LANES), value.dtype)], axis=1)


def visiting(ref, t_width):
    t, s = ref[:, :t_width], ref[:, t_width:]
    return t, s, as_row(norms_of(t)), as_row(norms_of(s))


def pair_tile(c, v, inv_t, inv_s, own):
    (ct, cs, nct, ncs), (vt, vs, nvt, nvs) = c, v
    last = (((1,), (1,)), ((), ()))
    gram_t = lax.dot_general(ct, vt, last, preferred_element_type=jnp.float32)
    gram_s = lax.dot_general(cs, vs, last, preferred_element_type=jnp.float32)
    square_t = jnp.maximum(nct + nvt - 2.0 * gram_t, 0.0)
    square_s = jnp.maximum(ncs + nvs - 2.0 * gram_s, 0.0)
    under_t = square_t * inv_t + FLOOR
    under_s = square_s * inv_s + FLOOR
    inverse_s = lax.rsqrt(under_s)
    residue = under_s * inverse_s - under_t * lax.rsqrt(under_t)
    slope = jnp.clip(residue, -1.0, 1.0)
    huber = slope * (residue - 0.5 * slope)
    pull = slope * inverse_s
    if own:
        row = lax.broadcasted_iota(jnp.int32, pull.shape, 0)
        same = row == lax.broadcasted_iota(jnp.int32, pull.shape, 1)
        pull = jnp.where(same, 0.0, pull)
        huber = jnp.where(same, 0.0, huber)
    weights = (pull * inv_s).astype(jnp.bfloat16)
    return (
        weights,
        jnp.sum(huber, axis=0, keepdims=True),
        jnp.sum(pull * square_s, axis=0, keepdims=True),
    )


def direct_of(rows, summed):
    width = rows.shape[1]
    row_weight = jnp.concatenate([summed[:, width:]] * (width // LANES), axis=1)
    return rows.astype(jnp.float32) * row_weight - summed[:, :width]


def chunks_of(ref):
    for h in range(ref.shape[0]):
        for start in range(0, ref.shape[1], CHUNK):
            yield h, pl.ds(start, min(CHUNK, ref.shape[1] - start))


def early_kernel(n_blk, steps, t_width, total_rows, *refs):
    refs = list(refs)
    tiles = [refs.pop(0) for _ in range(n_blk)]
    line = [tiles[0]] + [refs.pop(0) for _ in range(steps - 1)]
    *stats_refs, own_ref = refs[: -4 - steps]
    back_refs = refs[-4 - steps : -5]
    acc_ref, norm_ref, total_ref, sums_ref, plane_ref = refs[-5:]
    rows = own_ref.shape[0]
    for d, ref in enumerate(tiles):
        start = d % (n_blk // 2) * rows
        plane_ref[d // (n_blk // 2), start : start + rows, :] = ref[...]
    s_width = own_ref.shape[1]
    stats = stats_refs[0][...]
    for ref in stats_refs[1:]:
        stats = stats + ref[...]
    total_ref[...] = stats
    spread_t, spread_s, _ = spreads_of(stats, t_width, s_width, total_rows)
    inv_t, inv_s = 1.0 / spread_t, 1.0 / spread_s
    loss = jnp.zeros((1, LANES), jnp.float32)
    spread = jnp.zeros((1, LANES), jnp.float32)
    if steps == 1:
        acc_ref[...] = jnp.zeros_like(acc_ref)
    for h, at in chunks_of(plane_ref):
        norm_ref[h, 0, at, :] = jnp.broadcast_to(norms_of(plane_ref[h, at, :t_width]), (at.size, LANES))
        norm_ref[h, 1, at, :] = jnp.broadcast_to(norms_of(plane_ref[h, at, t_width:]), (at.size, LANES))
    for k, ref in enumerate(line):
        v = visiting(ref, t_width)
        factor = 1.0 if k == 0 else 2.0
        summed = None
        for h, at in chunks_of(plane_ref):
            cs = plane_ref[h, at, t_width:]
            c = (plane_ref[h, at, :t_width], cs, norm_ref[h, 0, at, :], norm_ref[h, 1, at, :])
            own = k == 0 and h == 0 and at.start == 0
            weights, loss_part, spread_part = pair_tile(c, v, inv_t, inv_s, own)
            loss = loss + factor * loss_part
            spread = spread + factor * spread_part
            term = lax.dot_general(
                weights,
                with_ones(cs),
                (((0,), (0,)), ((), ())),
                preferred_element_type=jnp.float32,
            )
            summed = term if summed is None else summed + term
            if k > 0:
                back = jnp.dot(weights, with_ones(v[1]), preferred_element_type=jnp.float32)
                acc_ref[h, at, :] = back if k == 1 else acc_ref[h, at, :] + back
        to_ref = own_ref if k == 0 else back_refs[k - 1]
        to_ref[...] = direct_of(v[1], summed)
    sums_ref[0:1, :] = loss
    sums_ref[1:2, :] = spread


def late_kernel(t_width, total_rows, *refs):
    plane_ref, ref, stats_ref, acc_ref, norm_ref, early_sums, keep_ref, give_ref, sums_ref = refs
    s_width = keep_ref.shape[1]
    spread_t, spread_s, _ = spreads_of(stats_ref[...], t_width, s_width, total_rows)
    inv_t, inv_s = 1.0 / spread_t, 1.0 / spread_s
    loss = early_sums[0:1, :]
    spread = early_sums[1:2, :]
    v = visiting(ref, t_width)
    for h, at in chunks_of(plane_ref):
        cs = plane_ref[h, at, t_width:]
        c = (plane_ref[h, at, :t_width], cs, norm_ref[h, 0, at, :], norm_ref[h, 1, at, :])
        weights, loss_part, spread_part = pair_tile(c, v, inv_t, inv_s, False)
        loss = loss + loss_part
        spread = spread + spread_part
        back = jnp.dot(weights, with_ones(v[1]), preferred_element_type=jnp.float32)
        to_ref = (keep_ref, give_ref)[h]
        to_ref[at, :] = direct_of(cs, acc_ref[h, at, :] + back)
    sums_ref[0:1, :] = loss
    sums_ref[1:2, :] = spread


def halve_kernel(rows, keep_ref, got_ref, *out_refs):
    out_refs[0][...] = keep_ref[:rows, :] + got_ref[:rows, :]
    out_refs[1][...] = keep_ref[rows : 2 * rows, :] + got_ref[rows : 2 * rows, :]


def add_kernel(*refs):
    *parts, out_ref = refs
    total = parts[0][...]
    for part in parts[1:]:
        total = total + part[...]
    out_ref[...] = total


def final_kernel(t_width, total_rows, packed_ref, stats_ref, direct_ref, *refs):
    *sums, grad_ref, loss_ref = refs
    rows, s_width = direct_ref.shape
    both = sums[0][...]
    for one in sums[1:]:
        both = both + one[...]
    both = jnp.sum(both, axis=1, keepdims=True)
    loss_total, spread_total = both[0:1, :], -both[1:2, :]
    _, spread_s, centre = spreads_of(stats_ref[...], t_width, s_width, total_rows)
    pairs = total_rows * (total_rows - 1.0)
    correction = 2.0 * spread_total / (pairs * spread_s * spread_s)
    student = packed_ref[:, t_width:].astype(jnp.float32)
    grad_ref[...] = (2.0 / (total_rows - 1.0)) * direct_ref[...] + correction * (student - centre)
    loss_ref[...] = jnp.broadcast_to(loss_total / pairs, loss_ref.shape)


def call(kernel, out_shape, operands, flops, vmem=48, **more):
    nbytes = sum(x.size * x.dtype.itemsize for x in operands)
    in_specs = more.pop("in_specs", [WHOLE] * len(operands))
    out_specs = more.pop("out_specs", jax.tree.map(lambda _: WHOLE, out_shape))
    return pl.pallas_call(
        kernel,
        out_shape=out_shape,
        in_specs=in_specs,
        out_specs=out_specs,
        compiler_params=pltpu.CompilerParams(vmem_limit_bytes=vmem * 1024 * 1024),
        cost_estimate=pl.CostEstimate(flops=flops, bytes_accessed=nbytes, transcendentals=0),
        **more,
    )(*operands)


def gathered(value, axis):
    return [value] + [exchange(value, axis, d) for d in range(1, lax.axis_size(axis))]


def halvings(axis):
    size = lax.axis_size(axis)
    return [size >> i for i in range(1, size.bit_length())]


def per_device(teacher, student):
    rows, t_width = teacher.shape
    s_width = student.shape[1]
    n_blk = lax.axis_size("blk")
    n_sub = lax.axis_size("sub")
    total_rows = float(rows * n_blk * n_sub)
    half = n_sub // 2
    side = rows * n_blk // 2
    f32 = functools.partial(jax.ShapeDtypeStruct, dtype=jnp.float32)

    packed, stats = call(
        pack_kernel,
        [
            jax.ShapeDtypeStruct((rows, t_width + s_width), teacher.dtype),
            f32((1, t_width + s_width + LANES)),
        ],
        (teacher, student),
        4 * teacher.size,
        vmem=62,
        in_specs=[pl.BlockSpec(memory_space=pl.ANY)] * 2,
        scratch_shapes=[pltpu.SemaphoreType.DMA((2,))],
    )
    line = [packed, shifted(packed, "sub", 1)]
    tz = [exchange(stats, "sub", d) for d in range(1, n_sub)]
    line[1], *tz = lax.optimization_barrier((line[1], *tz))
    for _ in range(half - 1):
        line.append(shifted(line[-1], "sub", 1))
    stats = functools.reduce(jnp.add, [stats] + tz)
    tiles = [packed]
    for distance in halvings("blk"):
        if distance == 1:
            *tiles, line[1] = lax.optimization_barrier((*tiles, line[1]))
        else:
            stats = stats + exchange(stats, "blk", distance)
        tiles = tiles + [exchange(x, "blk", distance) for x in tiles]
    stats = [stats, exchange(stats, "blk", 1)]

    pair_flops = 2 * rows * rows * n_blk * (t_width + 3 * s_width)
    out_shape = (
        [f32((rows, s_width))] * half
        + [f32((2, side, s_width + LANES)), f32((2, 2, side, LANES))]
        + [f32(stats[0].shape), f32((2, LANES))]
        + [jax.ShapeDtypeStruct((2, side, t_width + s_width), packed.dtype)]
    )
    *tiles, acc, norms, totals, early_sums, plane = call(
        functools.partial(early_kernel, n_blk, half, t_width, total_rows),
        out_shape,
        tiles + line[1:half] + stats,
        half * pair_flops,
    )
    own, backs = tiles[0], tiles[1:]
    returned = [shifted(x, "sub", -k) for k, x in enumerate(backs, 1)]
    keep, give, sums = call(
        functools.partial(late_kernel, t_width, total_rows),
        [f32((side, s_width))] * 2 + [f32((2, LANES))],
        [plane, line[half], totals, acc, norms, early_sums],
        pair_flops,
    )
    give, returned = lax.optimization_barrier((give, returned))
    got = exchange(give, "blk", 1)
    for distance in halvings("blk")[:-1]:
        sums = sums + exchange(sums, "blk", distance)
    tiles, distance = n_blk // 2, 2
    while tiles > 1:
        tiles //= 2
        out_shape = [f32((rows * tiles, s_width))] * 2
        keep, give = call(
            functools.partial(halve_kernel, rows * tiles), out_shape, (keep, got), 2 * keep.size
        )
        if tiles == n_blk // 4:
            give, sums = lax.optimization_barrier((give, sums))
        got = exchange(give, "blk", distance)
        distance *= 2
    sums = gathered(sums, "sub")
    direct = call(add_kernel, f32((rows, s_width)), [own, keep, got] + returned, 4 * own.size)
    *sums, direct = lax.optimization_barrier((*sums, direct))
    sums = functools.reduce(jnp.add, sums)
    all_sums = [sums, exchange(sums, "blk", 1)]
    grad, loss = call(
        functools.partial(final_kernel, t_width, total_rows),
        [f32((rows, s_width)), f32((1, LANES))],
        [packed, totals, direct] + all_sums,
        8 * student.size,
    )
    return grad, loss[0, :1]


def solution(mesh):
    placed = P(("groups", "blk", "sub"), None)
    return jax.shard_map(
        per_device,
        mesh=mesh,
        in_specs=(placed, placed),
        out_specs=(placed, P("groups")),
        check_vma=False,
    )
```

time: 50 us -> 52 us (1.040)
  waiting for transfers between devices: 17.8 us -> 20.3 us
  Pallas kernels: 7.37 us -> 6.1 us
  other arithmetic: 0.03 us -> 0.72 us
    ppermute x16 -> x15, waiting for transfers between devices: 14.7 us -> 17.1 us  [exchange(): return lax.ppermute(value, axis, [(i, i ^ distance) for i in range(size)])]
    pallas_call x5 -> x6, Pallas kernels: 7.37 us -> 6.1 us  [call(): pl.pallas_call(kernel, out_shape=out_shape, in_specs=in_specs, out_specs=...]
    add x2, other arithmetic: 0.02 us -> 0.71 us  [the longest x1 0.7 us: per_device(): stats = functools.reduce(jnp.add, [stats] + tz)]
    ppermute x16 -> x15, starting transfers between devices: 16 us -> 15.9 us  [exchange(): return lax.ppermute(value, axis, [(i, i ^ distance) for i in range(size)])]
  transfers between devices with their start and end apart: 19 -> 18, of which waited for: 8 -> 9; matrix products, arithmetic and copies ran while one was open for 0% -> 1% of each run, Pallas kernels for 10% -> 7%
where the time goes in v5:
time: 52 us; the launch traced here: 51.8 us
  starting transfers between devices  22.9 us (44%)
  waiting for transfers between devices  20.3 us (39%)
  Pallas kernels  6.1 us (12%)
  local copies, waits for them, and re-layouts  0.99 us (2%)
  other arithmetic  0.72 us (1%)
  between operations  0.71 us (1%)
    ppermute x15, waiting for transfers between devices, exchange(): return lax.ppermute(value, axis, [(i, i ^ distance) for i in range(size)])  17.1 us
    ppermute x15, starting transfers between devices, exchange(): return lax.ppermute(value, axis, [(i, i ^ distance) for i in range(size)])  15.9 us
    ppermute x3, starting transfers between devices, shifted(): lax.ppermute(value, axis, [(i, (i + distance) % size) for i in range(size)])  6.95 us
    pallas_call x6, Pallas kernels, call(): pl.pallas_call(kernel, out_shape=out_shape, in_specs=in_specs, out_specs=...  6.1 us
    ppermute x3, waiting for transfers between devices, shifted(): lax.ppermute(value, axis, [(i, (i + distance) % size) for i in range(size)])  3.27 us
  transfers between devices with their start and end apart: 18, of which 9 were waited for; matrix products, arithmetic and copies ran while one was open for 1% of the time, Pallas kernels for 7%

profile of v5, /device:TPU:0, one launch (start us, length us, event | category | flops | bytes accessed | tf_op | source)
XLA Modules:
  0.0 51.8 jit_solution(837697563397714905)
XLA Ops:
  0.6 1.7 %shard_map.41 = (bf16[128,1408]{1,0:T(8,128)(2,1)}, f32[1,1536]{1,0:T(1,128)}) custom-call(bf16[128,1024]{1,0:T(8,128)(2,1)} %t_hbm.1, bf16[128,384]{1,0:T(8,128)(2,1)} %s_hbm.1), custom_call_target="tpu_custom_call" | custom-call | flops 524288 | bytes 360448 | tf_op jit(solution)/shard_map/pallas_call | solution.py:227
  2.4 3.1 %collective-permute-start.1 = (bf16[128,1408]{1,0:T(8,128)(2,1)}, bf16[128,1408]{1,0:T(8,128)(2,1)S(1)}, u32[]{:S(2)}, u32[]{:S(2)}) collective-permute-start(bf16[128,1408]{1,0:T(8,128)(2,1)} %get-tuple-element.37.refs_0_.packed_ref), channel_id=1, source_target_pairs={{0,1},{1,2},{2,3},{3,0},{4,5},{5,6},{6,7},{7,4},{8,9},{9,10},{10,1... | collective-permute-start | bytes 1081352 | tf_op jit(solution)/shard_map/ppermute | solution.py:24
  5.5 1.5 %collective-permute-start = (bf16[128,1408]{1,0:T(8,128)(2,1)}, bf16[128,1408]{1,0:T(8,128)(2,1)S(1)}, u32[]{:S(2)}, u32[]{:S(2)}) collective-permute-start(bf16[128,1408]{1,0:T(8,128)(2,1)} %get-tuple-element.37.refs_0_.packed_ref), channel_id=1, source_target_pairs={{0,8},{4,12},{8,0},{12,4},{1,9},{5,13},{9,1},{13,5},{2,10},{6,14},... | collective-permute-start | bytes 1081352 | tf_op jit(solution)/shard_map/ppermute | solution.py:19
  7.0 1.6 %collective-permute-start.2 = (f32[1,1536]{1,0:T(1,128)}, f32[1,1536]{1,0:T(1,128)S(1)}, u32[]{:S(2)}, u32[]{:S(2)}) collective-permute-start(f32[1,1536]{1,0:T(1,128)} %get-tuple-element.35), channel_id=1, source_target_pairs={{0,1},{1,0},{2,3},{3,2},{4,5},{5,4},{6,7},{7,6},{8,9},{9,8},{10,11... | collective-permute-start | bytes 18440 | tf_op jit(solution)/shard_map/ppermute | solution.py:19
  8.6 1.2 %collective-permute-start.3 = (f32[1,1536]{1,0:T(1,128)}, f32[1,1536]{1,0:T(1,128)S(1)}, u32[]{:S(2)}, u32[]{:S(2)}) collective-permute-start(f32[1,1536]{1,0:T(1,128)} %get-tuple-element.35), channel_id=1, source_target_pairs={{0,2},{1,3},{2,0},{3,1},{4,6},{5,7},{6,4},{7,5},{8,10},{9,11},{10,... | collective-permute-start | bytes 18440 | tf_op jit(solution)/shard_map/ppermute | solution.py:19
  9.8 1.6 %collective-permute-start.4 = (f32[1,1536]{1,0:T(1,128)}, f32[1,1536]{1,0:T(1,128)S(1)}, u32[]{:S(2)}, u32[]{:S(2)}) collective-permute-start(f32[1,1536]{1,0:T(1,128)} %get-tuple-element.35), channel_id=1, source_target_pairs={{0,3},{1,2},{2,1},{3,0},{4,7},{5,6},{6,5},{7,4},{8,11},{9,10},{10,... | collective-permute-start | bytes 18440 | tf_op jit(solution)/shard_map/ppermute | solution.py:19
  11.4 4.2 %collective-permute-done.2 = f32[1,1536]{1,0:T(1,128)S(1)} collective-permute-done((f32[1,1536]{1,0:T(1,128)}, f32[1,1536]{1,0:T(1,128)S(1)}, u32[]{:S(2)}, u32[]{:S(2)}) %collective-permute-start.2) | collective-permute-done | bytes 6176 | tf_op jit(solution)/shard_map/ppermute | solution.py:19
  15.5 1.1 %collective-permute-done.3 = f32[1,1536]{1,0:T(1,128)S(1)} collective-permute-done((f32[1,1536]{1,0:T(1,128)}, f32[1,1536]{1,0:T(1,128)S(1)}, u32[]{:S(2)}, u32[]{:S(2)}) %collective-permute-start.3) | collective-permute-done | bytes 6176 | tf_op jit(solution)/shard_map/ppermute | solution.py:19
  16.6 0.0 collective-permute-done.4
  16.6 0.0 collective-permute-done.1.refs_4_
  16.6 0.6 %collective-permute-start.9 = (bf16[128,1408]{1,0:T(8,128)(2,1)S(1)}, bf16[128,1408]{1,0:T(8,128)(2,1)S(1)}, u32[]{:S(2)}, u32[]{:S(2)}) collective-permute-start(bf16[128,1408]{1,0:T(8,128)(2,1)S(1)} %collective-permute-done.1.refs_4_), channel_id=1, source_target_pairs={{0,1},{1,2},{2,3},{3,0},{4,5},{5,6},{6,7},{7,4},{8,9},{9,10},{10,1... | collective-permute-start | bytes 1081352 | tf_op jit(solution)/shard_map/ppermute | solution.py:24
  17.2 0.0 collective-permute-done.refs_1_
  17.3 0.5 collective-permute-start.6
  17.8 0.7 %add_add_fusion = f32[1,1536]{1,0:T(1,128)S(1)} fusion(f32[1,1536]{1,0:T(1,128)S(1)} %collective-permute-done.4, f32[1,1536]{1,0:T(1,128)S(1)} %collective-permute-done.3, f32[1,1536]{1,0:T(1,128)} %get-tuple-element.35, f32[1,1536]{1,0:T(1,128)S(1)} %collective-permute-done.2), kind=kLoop, calls=%fused_computation | loop fusion | flops 4608 | bytes 30720 | tf_op jit(solution)/shard_map/add | solution.py:274
  18.5 1.6 %collective-permute-start.7 = (f32[1,1536]{1,0:T(1,128)S(1)}, f32[1,1536]{1,0:T(1,128)S(1)}, u32[]{:S(2)}, u32[]{:S(2)}) collective-permute-start(f32[1,1536]{1,0:T(1,128)S(1)} %add_add_fusion), channel_id=1, source_target_pairs={{0,8},{4,12},{8,0},{12,4},{1,9},{5,13},{9,1},{13,5},{2,10},{6,14},... | collective-permute-start | bytes 18440 | tf_op jit(solution)/shard_map/ppermute | solution.py:19
  20.0 2.1 %collective-permute-done.7 = f32[1,1536]{1,0:T(1,128)S(1)} collective-permute-done((f32[1,1536]{1,0:T(1,128)S(1)}, f32[1,1536]{1,0:T(1,128)S(1)}, u32[]{:S(2)}, u32[]{:S(2)}) %collective-permute-start.7) | collective-permute-done | bytes 6176 | tf_op jit(solution)/shard_map/ppermute | solution.py:19
  22.2 0.1 collective-permute-start.8
  22.3 1.2 %collective-permute-done.8.refs_6_ = f32[1,1536]{1,0:T(1,128)S(1)} collective-permute-done((f32[1,1536]{1,0:T(1,128)S(1)}, f32[1,1536]{1,0:T(1,128)S(1)}, u32[]{:S(2)}, u32[]{:S(2)}) %collective-permute-start.8) | collective-permute-done | bytes 6176 | tf_op jit(solution)/shard_map/ppermute | solution.py:19
  23.4 1.0 %copy-done = bf16[128,1408]{1,0:T(8,128)(2,1)S(1)} copy-done((bf16[128,1408]{1,0:T(8,128)(2,1)S(1)}, bf16[128,1408]{1,0:T(8,128)(2,1)}, u32[]{:S(2)}) %copy-start) | copy-done | bytes 360472
  24.4 2.2 %shard_map.42 = (f32[128,384]{1,0:T(8,128)S(1)}, f32[128,384]{1,0:T(8,128)S(1)}, f32[2,256,512]{2,1,0:T(8,128)S(1)}, f32[2,2,256,128]{3,2,1,0:T(8,128)S(1)}, f32...) custom-call(bf16[128,1408]{1,0:T(8,128)(2,1)S(1)} %copy-done, ...), custom_call_target="tpu_custom_call" | custom-call | flops 570425344 | bytes 1814528 | tf_op jit(solution)/shard_map/pallas_call | solution.py:227
  26.6 3.3 %collective-permute-start.10 = (f32[128,384]{1,0:T(8,128)S(1)}, f32[128,384]{1,0:T(8,128)S(1)}, u32[]{:S(2)}, u32[]{:S(2)}) collective-permute-start(f32[128,384]{1,0:T(8,128)S(1)} %get-tuple-element.50), channel_id=1, source_target_pairs={{0,3},{1,0},{2,1},{3,2},{4,7},{5,4},{6,5},{7,6},{8,11},{9,8},{10,9... | collective-permute-start | bytes 589832 | tf_op jit(solution)/shard_map/ppermute | solution.py:24
  29.9 0.0 collective-permute-done.9.refs_1_
  29.9 1.2 %shard_map.43 = (f32[256,384]{1,0:T(8,128)S(1)}, f32[256,384]{1,0:T(8,128)S(1)}, f32[2,128]{1,0:T(2,128)S(1)}) custom-call(bf16[2,256,1408]{2,1,0:T(8,128)(2,1)S(1)} %get-tuple-element.44.refs_0_, bf16[128,1408]{1,0:T(8,128)(2,1)S(1)} %collective-permute-done.9.refs_1_, f32[1,1536]{1,0:T(1,128)S(1)} %get-tuple-element.43.refs_2_.stats_ref, ...), custom_call_target="tpu_custom_call" | custom-call | flops 285212672 | bytes 3382272 | tf_op jit(solution)/shard_map/pallas_call | solution.py:227
  31.1 3.3 %collective-permute-done.10.refs_3_ = f32[128,384]{1,0:T(8,128)S(1)} collective-permute-done((f32[128,384]{1,0:T(8,128)S(1)}, f32[128,384]{1,0:T(8,128)S(1)}, u32[]{:S(2)}, u32[]{:S(2)}) %collective-permute-start.10) | collective-permute-done | bytes 196640 | tf_op jit(solution)/shard_map/ppermute | solution.py:24
  34.4 1.5 %collective-permute-start.12 = (f32[2,128]{1,0:T(2,128)S(1)}, f32[2,128]{1,0:T(2,128)S(1)}, u32[]{:S(2)}, u32[]{:S(2)}) collective-permute-start(f32[2,128]{1,0:T(2,128)S(1)} %get-tuple-element.53), channel_id=1, source_target_pairs={{0,8},{4,12},{8,0},{12,4},{1,9},{5,13},{9,1},{13,5},{2,10},{6,14},... | collective-permute-start | bytes 3080 | tf_op jit(solution)/shard_map/ppermute | solution.py:19
  35.9 2.1 %collective-permute-done.12 = f32[2,128]{1,0:T(2,128)S(1)} collective-permute-done((f32[2,128]{1,0:T(2,128)S(1)}, f32[2,128]{1,0:T(2,128)S(1)}, u32[]{:S(2)}, u32[]{:S(2)}) %collective-permute-start.12) | collective-permute-done | bytes 1056 | tf_op jit(solution)/shard_map/ppermute | solution.py:19
  38.0 1.6 %collective-permute-start.16 = (f32[128,384]{1,0:T(8,128)S(1)}, f32[128,384]{1,0:T(8,128)S(1)}, u32[]{:S(2)}, u32[]{:S(2)}) collective-permute-start(f32[128,384]{1,0:T(8,128)S(1)} %get-tuple-element.57), channel_id=1, source_target_pairs={{0,8},{4,12},{8,0},{12,4},{1,9},{5,13},{9,1},{13,5},{2,10},{6,14},... | collective-permute-start | bytes 589832 | tf_op jit(solution)/shard_map/ppermute | solution.py:19
  39.6 4.8 %collective-permute-start.14 = (f32[2,128]{1,0:T(2,128)S(1)}, f32[2,128]{1,0:T(2,128)S(1)}, u32[]{:S(2)}, u32[]{:S(2)}) collective-permute-start(f32[2,128]{1,0:T(2,128)S(1)} %add.28), channel_id=1, source_target_pairs={{0,2},{1,3},{2,0},{3,1},{4,6},{5,7},{6,4},{7,5},{8,10},{9,11},{10,... | collective-permute-start | bytes 3080 | tf_op jit(solution)/shard_map/ppermute | solution.py:19
  44.5 1.5 %collective-permute-done.14 = f32[2,128]{1,0:T(2,128)S(1)} collective-permute-done((f32[2,128]{1,0:T(2,128)S(1)}, f32[2,128]{1,0:T(2,128)S(1)}, u32[]{:S(2)}, u32[]{:S(2)}) %collective-permute-start.14) | collective-permute-done | bytes 1056 | tf_op jit(solution)/shard_map/ppermute | solution.py:19
  46.0 3.8 %collective-permute-done.15 = f32[2,128]{1,0:T(2,128)S(1)} collective-permute-done((f32[2,128]{1,0:T(2,128)S(1)}, f32[2,128]{1,0:T(2,128)S(1)}, u32[]{:S(2)}, u32[]{:S(2)}) %collective-permute-start.15) | collective-permute-done | bytes 1056 | tf_op jit(solution)/shard_map/ppermute | solution.py:19
  49.8 1.1 %collective-permute-done.17.refs_1_ = f32[2,128]{1,0:T(2,128)S(1)} collective-permute-done((f32[2,128]{1,0:T(2,128)S(1)}, f32[2,128]{1,0:T(2,128)S(1)}, u32[]{:S(2)}, u32[]{:S(2)}) %collective-permute-start.17) | collective-permute-done | bytes 1056 | tf_op jit(solution)/shard_map/ppermute | solution.py:19
  50.9 0.8 %shard_map.46 = (f32[128,384]{1,0:T(8,128)}, f32[1,128]{1,0:T(1,128)}) custom-call(bf16[128,1408]{1,0:T(8,128)(2,1)S(1)} %copy-done.1, f32[1,1536]{1,0:T(1,128)S(1)} %get-tuple-element.43.refs_2_.stats_ref, f32[128,384]{1,0:T(8,128)S(1)} %shard_map.45.direct_ref, f32[2,128]{1,0:T(2,128)S(1)} %add_add_fusion.1.refs_0_, ...), custom_call_target="tpu_custom_call" | custom-call | flops 393216 | bytes 565248 | tf_op jit(solution)/shard_map/pallas_call | solution.py:227
  (18 shorter events, 0.1 us)
Async XLA Ops:
  2.4 14.2 %collective-permute-start.1 = (bf16[128,1408]{1,0:T(8,128)(2,1)}, bf16[128,1408]{1,0:T(8,128)(2,1)S(1)}, u32[]{:S(2)}, u32[]{:S(2)}) collective-permute-start(bf16[128,1408]{1,0:T(8,128)(2,1)} %get-tuple-element.37.refs_0_.packed_ref), channel_id=1, source_target_pairs={{0,1},{1,2},{2,3},{3,0},{4,5},{5,6},{6,7},{7,4},{8,9},{9,10},{10,1... | collective-permute-start | bytes 1081352 | tf_op jit(solution)/shard_map/ppermute | solution.py:24
  5.5 11.8 %collective-permute-start = (bf16[128,1408]{1,0:T(8,128)(2,1)}, bf16[128,1408]{1,0:T(8,128)(2,1)S(1)}, u32[]{:S(2)}, u32[]{:S(2)}) collective-permute-start(bf16[128,1408]{1,0:T(8,128)(2,1)} %get-tuple-element.37.refs_0_.packed_ref), channel_id=1, source_target_pairs={{0,8},{4,12},{8,0},{12,4},{1,9},{5,13},{9,1},{13,5},{2,10},{6,14},... | collective-permute-start | bytes 1081352 | tf_op jit(solution)/shard_map/ppermute | solution.py:19
  7.0 8.6 %collective-permute-start.2 = (f32[1,1536]{1,0:T(1,128)}, f32[1,1536]{1,0:T(1,128)S(1)}, u32[]{:S(2)}, u32[]{:S(2)}) collective-permute-start(f32[1,1536]{1,0:T(1,128)} %get-tuple-element.35), channel_id=1, source_target_pairs={{0,1},{1,0},{2,3},{3,2},{4,5},{5,4},{6,7},{7,6},{8,9},{9,8},{10,11... | collective-permute-start | bytes 18440 | tf_op jit(solution)/shard_map/ppermute | solution.py:19
  8.6 8.1 %collective-permute-start.3 = (f32[1,1536]{1,0:T(1,128)}, f32[1,1536]{1,0:T(1,128)S(1)}, u32[]{:S(2)}, u32[]{:S(2)}) collective-permute-start(f32[1,1536]{1,0:T(1,128)} %get-tuple-element.35), channel_id=1, source_target_pairs={{0,2},{1,3},{2,0},{3,1},{4,6},{5,7},{6,4},{7,5},{8,10},{9,11},{10,... | collective-permute-start | bytes 18440 | tf_op jit(solution)/shard_map/ppermute | solution.py:19
  9.8 6.8 %collective-permute-start.4 = (f32[1,1536]{1,0:T(1,128)}, f32[1,1536]{1,0:T(1,128)S(1)}, u32[]{:S(2)}, u32[]{:S(2)}) collective-permute-start(f32[1,1536]{1,0:T(1,128)} %get-tuple-element.35), channel_id=1, source_target_pairs={{0,3},{1,2},{2,1},{3,0},{4,7},{5,6},{6,5},{7,4},{8,11},{9,10},{10,... | collective-permute-start | bytes 18440 | tf_op jit(solution)/shard_map/ppermute | solution.py:19
  16.6 13.3 %collective-permute-start.9 = (bf16[128,1408]{1,0:T(8,128)(2,1)S(1)}, bf16[128,1408]{1,0:T(8,128)(2,1)S(1)}, u32[]{:S(2)}, u32[]{:S(2)}) collective-permute-start(bf16[128,1408]{1,0:T(8,128)(2,1)S(1)} %collective-permute-done.1.refs_4_), channel_id=1, source_target_pairs={{0,1},{1,2},{2,3},{3,0},{4,5},{5,6},{6,7},{7,4},{8,9},{9,10},{10,1... | collective-permute-start | bytes 1081352 | tf_op jit(solution)/shard_map/ppermute | solution.py:24
  17.3 6.2 %collective-permute-start.5 = (bf16[128,1408]{1,0:T(8,128)(2,1)}, bf16[128,1408]{1,0:T(8,128)(2,1)S(1)}, u32[]{:S(2)}, u32[]{:S(2)}) collective-permute-start(bf16[128,1408]{1,0:T(8,128)(2,1)} %get-tuple-element.37.refs_0_.packed_ref), channel_id=1, source_target_pairs={{0,4},{4,0},{8,12},{12,8},{1,5},{5,1},{9,13},{13,9},{2,6},{6,2},{1... | collective-permute-start | bytes 1081352 | tf_op jit(solution)/shard_map/ppermute | solution.py:19
  17.3 6.2 %collective-permute-start.6 = (bf16[128,1408]{1,0:T(8,128)(2,1)S(1)}, bf16[128,1408]{1,0:T(8,128)(2,1)S(1)}, u32[]{:S(2)}, u32[]{:S(2)}) collective-permute-start(bf16[128,1408]{1,0:T(8,128)(2,1)S(1)} %collective-permute-done.refs_1_), channel_id=1, source_target_pairs={{0,4},{4,0},{8,12},{12,8},{1,5},{5,1},{9,13},{13,9},{2,6},{6,2},{1... | collective-permute-start | bytes 1081352 | tf_op jit(solution)/shard_map/ppermute | solution.py:19
  18.5 3.7 %collective-permute-start.7 = (f32[1,1536]{1,0:T(1,128)S(1)}, f32[1,1536]{1,0:T(1,128)S(1)}, u32[]{:S(2)}, u32[]{:S(2)}) collective-permute-start(f32[1,1536]{1,0:T(1,128)S(1)} %add_add_fusion), channel_id=1, source_target_pairs={{0,8},{4,12},{8,0},{12,4},{1,9},{5,13},{9,1},{13,5},{2,10},{6,14},... | collective-permute-start | bytes 18440 | tf_op jit(solution)/shard_map/ppermute | solution.py:19
  22.2 1.2 %collective-permute-start.8 = (f32[1,1536]{1,0:T(1,128)S(1)}, f32[1,1536]{1,0:T(1,128)S(1)}, u32[]{:S(2)}, u32[]{:S(2)}) collective-permute-start(f32[1,1536]{1,0:T(1,128)S(1)} %add.27.refs_5_), channel_id=1, source_target_pairs={{0,4},{4,0},{8,12},{12,8},{1,5},{5,1},{9,13},{13,9},{2,6},{6,2},{1... | collective-permute-start | bytes 18440 | tf_op jit(solution)/shard_map/ppermute | solution.py:19
  23.4 1.0 %copy-start = (bf16[128,1408]{1,0:T(8,128)(2,1)S(1)}, bf16[128,1408]{1,0:T(8,128)(2,1)}, u32[]{:S(2)}) copy-start(bf16[128,1408]{1,0:T(8,128)(2,1)} %get-tuple-element.37.refs_0_.packed_ref) | copy-start | bytes 1081348
  26.6 7.7 %collective-permute-start.10 = (f32[128,384]{1,0:T(8,128)S(1)}, f32[128,384]{1,0:T(8,128)S(1)}, u32[]{:S(2)}, u32[]{:S(2)}) collective-permute-start(f32[128,384]{1,0:T(8,128)S(1)} %get-tuple-element.50), channel_id=1, source_target_pairs={{0,3},{1,0},{2,1},{3,2},{4,7},{5,4},{6,5},{7,6},{8,11},{9,8},{10,9... | collective-permute-start | bytes 589832 | tf_op jit(solution)/shard_map/ppermute | solution.py:24
  31.1 19.8 %copy-start.1 = (bf16[128,1408]{1,0:T(8,128)(2,1)S(1)}, bf16[128,1408]{1,0:T(8,128)(2,1)}, u32[]{:S(2)}) copy-start(bf16[128,1408]{1,0:T(8,128)(2,1)} %get-tuple-element.37.refs_0_.packed_ref) | copy-start | bytes 1081348
  34.4 3.6 %collective-permute-start.11 = (f32[256,384]{1,0:T(8,128)S(1)}, f32[256,384]{1,0:T(8,128)S(1)}, u32[]{:S(2)}, u32[]{:S(2)}) collective-permute-start(f32[256,384]{1,0:T(8,128)S(1)} %get-tuple-element.51), channel_id=1, source_target_pairs={{0,4},{4,0},{8,12},{12,8},{1,5},{5,1},{9,13},{13,9},{2,6},{6,2},{1... | collective-permute-start | bytes 1179656 | tf_op jit(solution)/shard_map/ppermute | solution.py:19
  34.4 3.6 %collective-permute-start.12 = (f32[2,128]{1,0:T(2,128)S(1)}, f32[2,128]{1,0:T(2,128)S(1)}, u32[]{:S(2)}, u32[]{:S(2)}) collective-permute-start(f32[2,128]{1,0:T(2,128)S(1)} %get-tuple-element.53), channel_id=1, source_target_pairs={{0,8},{4,12},{8,0},{12,4},{1,9},{5,13},{9,1},{13,5},{2,10},{6,14},... | collective-permute-start | bytes 3080 | tf_op jit(solution)/shard_map/ppermute | solution.py:19
  38.0 6.4 %collective-permute-start.16 = (f32[128,384]{1,0:T(8,128)S(1)}, f32[128,384]{1,0:T(8,128)S(1)}, u32[]{:S(2)}, u32[]{:S(2)}) collective-permute-start(f32[128,384]{1,0:T(8,128)S(1)} %get-tuple-element.57), channel_id=1, source_target_pairs={{0,8},{4,12},{8,0},{12,4},{1,9},{5,13},{9,1},{13,5},{2,10},{6,14},... | collective-permute-start | bytes 589832 | tf_op jit(solution)/shard_map/ppermute | solution.py:19
  39.6 4.9 %collective-permute-start.13 = (f32[2,128]{1,0:T(2,128)S(1)}, f32[2,128]{1,0:T(2,128)S(1)}, u32[]{:S(2)}, u32[]{:S(2)}) collective-permute-start(f32[2,128]{1,0:T(2,128)S(1)} %add.28), channel_id=1, source_target_pairs={{0,1},{1,0},{2,3},{3,2},{4,5},{5,4},{6,7},{7,6},{8,9},{9,8},{10,11... | collective-permute-start | bytes 3080 | tf_op jit(solution)/shard_map/ppermute | solution.py:19
  39.6 6.4 %collective-permute-start.14 = (f32[2,128]{1,0:T(2,128)S(1)}, f32[2,128]{1,0:T(2,128)S(1)}, u32[]{:S(2)}, u32[]{:S(2)}) collective-permute-start(f32[2,128]{1,0:T(2,128)S(1)} %add.28), channel_id=1, source_target_pairs={{0,2},{1,3},{2,0},{3,1},{4,6},{5,7},{6,4},{7,5},{8,10},{9,11},{10,... | collective-permute-start | bytes 3080 | tf_op jit(solution)/shard_map/ppermute | solution.py:19
  44.4 5.4 %collective-permute-start.15 = (f32[2,128]{1,0:T(2,128)S(1)}, f32[2,128]{1,0:T(2,128)S(1)}, u32[]{:S(2)}, u32[]{:S(2)}) collective-permute-start(f32[2,128]{1,0:T(2,128)S(1)} %add.28), channel_id=1, source_target_pairs={{0,3},{1,2},{2,1},{3,0},{4,7},{5,6},{6,5},{7,4},{8,11},{9,10},{10,... | collective-permute-start | bytes 3080 | tf_op jit(solution)/shard_map/ppermute | solution.py:19
  49.8 1.1 %collective-permute-start.17 = (f32[2,128]{1,0:T(2,128)S(1)}, f32[2,128]{1,0:T(2,128)S(1)}, u32[]{:S(2)}, u32[]{:S(2)}) collective-permute-start(f32[2,128]{1,0:T(2,128)S(1)} %add_add_fusion.1.refs_0_), channel_id=1, source_target_pairs={{0,4},{4,0},{8,12},{12,8},{1,5},{5,1},{9,13},{13,9},{2,6},{6,2},{1... | collective-permute-start | bytes 3080 | tf_op jit(solution)/shard_map/ppermute | solution.py:19

commit v6 on v5

--- a/solution.py
+++ b/solution.py
@@ -24,16 +24,7 @@
     return lax.ppermute(value, axis, [(i, (i + distance) % size) for i in range(size)])
 
 
-def pack_kernel(t_hbm, s_hbm, packed_ref, stats_ref, sems):
-    t_width = t_hbm.shape[1]
-    copies = [
-        pltpu.make_async_copy(t_hbm, packed_ref.at[:, :t_width], sems.at[0]),
-        pltpu.make_async_copy(s_hbm, packed_ref.at[:, t_width:], sems.at[1]),
-    ]
-    for copy in copies:
-        copy.start()
-    for copy in copies:
-        copy.wait()
+def stats_kernel(t_width, packed_ref, stats_ref):
     value = packed_ref[...].astype(jnp.float32)
     squares = jnp.sum(value * value, axis=0, keepdims=True)
     square_t = jnp.sum(squares[:, :t_width], axis=1, keepdims=True)
@@ -187,8 +178,9 @@
         back = jnp.dot(weights, with_ones(v[1]), preferred_element_type=jnp.float32)
         to_ref = (keep_ref, give_ref)[h]
         to_ref[at, :] = direct_of(cs, acc_ref[h, at, :] + back)
-    sums_ref[0:1, :] = loss
-    sums_ref[1:2, :] = spread
+    for i in range(sums_ref.shape[0]):
+        sums_ref[i, 0:1, :] = loss
+        sums_ref[i, 1:2, :] = spread
 
 
 def halve_kernel(rows, keep_ref, got_ref, *out_refs):
@@ -196,27 +188,19 @@
     out_refs[1][...] = keep_ref[rows : 2 * rows, :] + got_ref[rows : 2 * rows, :]
 
 
-def add_kernel(*refs):
-    *parts, out_ref = refs
-    total = parts[0][...]
+def final_kernel(t_width, total_rows, packed_ref, stats_ref, sums_ref, *refs):
+    *parts, grad_ref, loss_ref = refs
+    direct = parts[0][...]
     for part in parts[1:]:
-        total = total + part[...]
-    out_ref[...] = total
-
-
-def final_kernel(t_width, total_rows, packed_ref, stats_ref, direct_ref, *refs):
-    *sums, grad_ref, loss_ref = refs
-    rows, s_width = direct_ref.shape
-    both = sums[0][...]
-    for one in sums[1:]:
-        both = both + one[...]
-    both = jnp.sum(both, axis=1, keepdims=True)
+        direct = direct + part[...]
+    s_width = direct.shape[1]
+    both = jnp.sum(jnp.sum(sums_ref[...], axis=0), axis=1, keepdims=True)
     loss_total, spread_total = both[0:1, :], -both[1:2, :]
     _, spread_s, centre = spreads_of(stats_ref[...], t_width, s_width, total_rows)
     pairs = total_rows * (total_rows - 1.0)
     correction = 2.0 * spread_total / (pairs * spread_s * spread_s)
     student = packed_ref[:, t_width:].astype(jnp.float32)
-    grad_ref[...] = (2.0 / (total_rows - 1.0)) * direct_ref[...] + correction * (student - centre)
+    grad_ref[...] = (2.0 / (total_rows - 1.0)) * direct + correction * (student - centre)
     loss_ref[...] = jnp.broadcast_to(loss_total / pairs, loss_ref.shape)
 
 
@@ -244,6 +228,10 @@
     return [size >> i for i in range(1, size.bit_length())]
 
 
+def to_all(value):
+    return lax.all_to_all(value, ("blk", "sub"), 0, 0, tiled=True)
+
+
 def per_device(teacher, student):
     rows, t_width = teacher.shape
     s_width = student.shape[1]
@@ -254,17 +242,12 @@
     side = rows * n_blk // 2
     f32 = functools.partial(jax.ShapeDtypeStruct, dtype=jnp.float32)
 
-    packed, stats = call(
-        pack_kernel,
-        [
-            jax.ShapeDtypeStruct((rows, t_width + s_width), teacher.dtype),
-            f32((1, t_width + s_width + LANES)),
-        ],
-        (teacher, student),
-        4 * teacher.size,
-        vmem=62,
-        in_specs=[pl.BlockSpec(memory_space=pl.ANY)] * 2,
-        scratch_shapes=[pltpu.SemaphoreType.DMA((2,))],
+    packed = jnp.concatenate([teacher, student], axis=1)
+    stats = call(
+        functools.partial(stats_kernel, t_width),
+        f32((1, t_width + s_width + LANES)),
+        (packed,),
+        4 * packed.size,
     )
     line = [packed, shifted(packed, "sub", 1)]
     tz = [exchange(stats, "sub", d) for d in range(1, n_sub)]
@@ -298,14 +281,11 @@
     returned = [shifted(x, "sub", -k) for k, x in enumerate(backs, 1)]
     keep, give, sums = call(
         functools.partial(late_kernel, t_width, total_rows),
-        [f32((side, s_width))] * 2 + [f32((2, LANES))],
+        [f32((side, s_width))] * 2 + [f32((n_blk * n_sub, 2, LANES))],
         [plane, line[half], totals, acc, norms, early_sums],
         pair_flops,
     )
-    give, returned = lax.optimization_barrier((give, returned))
     got = exchange(give, "blk", 1)
-    for distance in halvings("blk")[:-1]:
-        sums = sums + exchange(sums, "blk", distance)
     tiles, distance = n_blk // 2, 2
     while tiles > 1:
         tiles //= 2
@@ -313,19 +293,14 @@
         keep, give = call(
             functools.partial(halve_kernel, rows * tiles), out_shape, (keep, got), 2 * keep.size
         )
-        if tiles == n_blk // 4:
-            give, sums = lax.optimization_barrier((give, sums))
         got = exchange(give, "blk", distance)
         distance *= 2
-    sums = gathered(sums, "sub")
-    direct = call(add_kernel, f32((rows, s_width)), [own, keep, got] + returned, 4 * own.size)
-    *sums, direct = lax.optimization_barrier((*sums, direct))
-    sums = functools.reduce(jnp.add, sums)
-    all_sums = [sums, exchange(sums, "blk", 1)]
+    all_sums = to_all(sums)
+    parts = [own, keep, got] + returned
     grad, loss = call(
         functools.partial(final_kernel, t_width, total_rows),
         [f32((rows, s_width)), f32((1, LANES))],
-        [packed, totals, direct] + all_sums,
+        [packed, totals, all_sums] + parts,
         8 * student.size,
     )
     return grad, loss[0, :1]

time: 52 us -> 42.3 us (0.81)
  starting transfers between devices: 22.9 us -> 13.5 us
  blocking collectives: 0 us -> 8.97 us
  waiting for transfers between devices: 20.3 us -> 12.5 us
  Pallas kernels: 6.1 us -> 4.57 us
  local copies, waits for them, and re-layouts: 0.99 us -> 1.88 us
  other arithmetic: 0.72 us -> 0.02 us
    all_to_all x0 -> x1, blocking collectives: none -> 8.97 us  [to_all(): return lax.all_to_all(value, ('blk', 'sub'), 0, 0, tiled=True)]
    ppermute x15 -> x10, waiting for transfers between devices: 17.1 us -> 9.51 us  [exchange(): return lax.ppermute(value, axis, [(i, i ^ distance) for i in range(size)])]
    ppermute x15 -> x10, starting transfers between devices: 15.9 us -> 9.42 us  [exchange(): return lax.ppermute(value, axis, [(i, i ^ distance) for i in range(size)])]
    ppermute x3, starting transfers between devices: 6.95 us -> 4.08 us  [shifted(): lax.ppermute(value, axis, [(i, (i + distance) % size) for i in range(size)])]
    pallas_call x6 -> x5, Pallas kernels: 6.1 us -> 4.57 us  [call(): pl.pallas_call(kernel, out_shape=out_shape, in_specs=in_specs, out_specs=...]
    concatenate x0 -> x1, local copies, waits for them, and re-layouts: none -> 0.91 us  [per_device(): packed = jnp.concatenate([teacher, student], axis=1)]
    add x1, other arithmetic: 0.7 us -> 0.01 us  [per_device(): stats = functools.reduce(jnp.add, [stats] + tz)]
  transfers between devices with their start and end apart: 18 -> 13, of which waited for: 9 -> 6; matrix products, arithmetic and copies ran while one was open for 1% -> 0% of each run, Pallas kernels for 7% -> 6%
where the time goes in v6:
time: 42.3 us; the launch traced here: 42.1 us
  starting transfers between devices  13.5 us (32%)
  waiting for transfers between devices  12.5 us (30%)
  blocking collectives  8.97 us (21%)
  Pallas kernels  4.57 us (11%)
  local copies, waits for them, and re-layouts  1.88 us (4%)
  between operations  0.68 us (2%)
    ppermute x10, waiting for transfers between devices, exchange(): return lax.ppermute(value, axis, [(i, i ^ distance) for i in range(size)])  9.51 us
    ppermute x10, starting transfers between devices, exchange(): return lax.ppermute(value, axis, [(i, i ^ distance) for i in range(size)])  9.42 us
    all_to_all x1, blocking collectives, to_all(): return lax.all_to_all(value, ('blk', 'sub'), 0, 0, tiled=True)  8.97 us
    pallas_call x5, Pallas kernels, call(): pl.pallas_call(kernel, out_shape=out_shape, in_specs=in_specs, out_specs=...  4.57 us
    ppermute x3, starting transfers between devices, shifted(): lax.ppermute(value, axis, [(i, (i + distance) % size) for i in range(size)])  4.08 us
    ppermute x3, waiting for transfers between devices, shifted(): lax.ppermute(value, axis, [(i, (i + distance) % size) for i in range(size)])  2.98 us
    unnamed x1, local copies, waits for them, and re-layouts  0.97 us
    concatenate x1, local copies, waits for them, and re-layouts, per_device(): packed = jnp.concatenate([teacher, student], axis=1)  0.91 us
  transfers between devices with their start and end apart: 13, of which 6 were waited for; matrix products, arithmetic and copies ran while one was open for 0% of the time, Pallas kernels for 6%

profile of v6, /device:TPU:0, one launch (start us, length us, event | category | flops | bytes accessed | tf_op | source)
XLA Modules:
  0.0 42.1 jit_solution(8090689422930776522)
XLA Ops:
  0.6 1.0 %constant_dynamic-update-slice_fusion.1 = bf16[128,1408]{1,0:T(8,128)(2,1)S(1)} fusion(bf16[128,1024]{1,0:T(8,128)(2,1)} %param.2), kind=kLoop, calls=%fused_computation.1 | loop fusion | bytes 524288
  1.6 0.9 %constant_dynamic-update-slice_fusion.packed_ref.refs_0_ = bf16[128,1408]{1,0:T(8,128)(2,1)S(1)} fusion(bf16[128,1408]{1,0:T(8,128)(2,1)S(1)} %constant_dynamic-update-slice_fusion.1, bf16[128,384]{1,0:T(8,128)(2,1)} %param.3), kind=kLoop, calls=%fused_computation | loop fusion | bytes 196608 | tf_op jit(solution)/shard_map/concatenate | solution.py:245
  2.5 3.1 %collective-permute-start.1 = (bf16[128,1408]{1,0:T(8,128)(2,1)S(1)}, bf16[128,1408]{1,0:T(8,128)(2,1)S(1)}, u32[]{:S(2)}, u32[]{:S(2)}) collective-permute-start(bf16[128,1408]{1,0:T(8,128)(2,1)S(1)} %constant_dynamic-update-slice_fusion.packed_ref.refs_0_), channel_id=1, source_target_pairs={{0,1},{1,2},{2,3},{3,0},{4,5},{5,6},{6,7},{7,4},{8,9},{9,10},{10,1... | collective-permute-start | bytes 1081352 | tf_op jit(solution)/shard_map/ppermute | solution.py:24
  5.6 1.5 %collective-permute-start = (bf16[128,1408]{1,0:T(8,128)(2,1)S(1)}, bf16[128,1408]{1,0:T(8,128)(2,1)S(1)}, u32[]{:S(2)}, u32[]{:S(2)}) collective-permute-start(bf16[128,1408]{1,0:T(8,128)(2,1)S(1)} %constant_dynamic-update-slice_fusion.packed_ref.refs_0_), channel_id=1, source_target_pairs={{0,8},{4,12},{8,0},{12,4},{1,9},{5,13},{9,1},{13,5},{2,10},{6,14},... | collective-permute-start | bytes 1081352 | tf_op jit(solution)/shard_map/ppermute | solution.py:19
  7.1 0.2 shard_map.41
  7.3 1.6 %collective-permute-start.2 = (f32[1,1536]{1,0:T(1,128)S(1)}, f32[1,1536]{1,0:T(1,128)S(1)}, u32[]{:S(2)}, u32[]{:S(2)}) collective-permute-start(f32[1,1536]{1,0:T(1,128)S(1)} %shard_map.41), channel_id=1, source_target_pairs={{0,1},{1,0},{2,3},{3,2},{4,5},{5,4},{6,7},{7,6},{8,9},{9,8},{10,11... | collective-permute-start | bytes 18440 | tf_op jit(solution)/shard_map/ppermute | solution.py:19
  8.9 1.2 %collective-permute-start.3 = (f32[1,1536]{1,0:T(1,128)S(1)}, f32[1,1536]{1,0:T(1,128)S(1)}, u32[]{:S(2)}, u32[]{:S(2)}) collective-permute-start(f32[1,1536]{1,0:T(1,128)S(1)} %shard_map.41), channel_id=1, source_target_pairs={{0,2},{1,3},{2,0},{3,1},{4,6},{5,7},{6,4},{7,5},{8,10},{9,11},{10,... | collective-permute-start | bytes 18440 | tf_op jit(solution)/shard_map/ppermute | solution.py:19
  10.1 1.6 %collective-permute-start.4 = (f32[1,1536]{1,0:T(1,128)S(1)}, f32[1,1536]{1,0:T(1,128)S(1)}, u32[]{:S(2)}, u32[]{:S(2)}) collective-permute-start(f32[1,1536]{1,0:T(1,128)S(1)} %shard_map.41), channel_id=1, source_target_pairs={{0,3},{1,2},{2,1},{3,0},{4,7},{5,6},{6,5},{7,4},{8,11},{9,10},{10,... | collective-permute-start | bytes 18440 | tf_op jit(solution)/shard_map/ppermute | solution.py:19
  11.7 3.8 %collective-permute-done.2 = f32[1,1536]{1,0:T(1,128)S(1)} collective-permute-done((f32[1,1536]{1,0:T(1,128)S(1)}, f32[1,1536]{1,0:T(1,128)S(1)}, u32[]{:S(2)}, u32[]{:S(2)}) %collective-permute-start.2) | collective-permute-done | bytes 6176 | tf_op jit(solution)/shard_map/ppermute | solution.py:19
  15.5 1.1 %collective-permute-done.3 = f32[1,1536]{1,0:T(1,128)S(1)} collective-permute-done((f32[1,1536]{1,0:T(1,128)S(1)}, f32[1,1536]{1,0:T(1,128)S(1)}, u32[]{:S(2)}, u32[]{:S(2)}) %collective-permute-start.3) | collective-permute-done | bytes 6176 | tf_op jit(solution)/shard_map/ppermute | solution.py:19
  16.5 0.0 collective-permute-done.4
  16.5 0.0 collective-permute-done.1.refs_4_
  16.5 0.6 %collective-permute-start.9 = (bf16[128,1408]{1,0:T(8,128)(2,1)S(1)}, bf16[128,1408]{1,0:T(8,128)(2,1)S(1)}, u32[]{:S(2)}, u32[]{:S(2)}) collective-permute-start(bf16[128,1408]{1,0:T(8,128)(2,1)S(1)} %collective-permute-done.1.refs_4_), channel_id=1, source_target_pairs={{0,1},{1,2},{2,3},{3,0},{4,5},{5,6},{6,7},{7,4},{8,9},{9,10},{10,1... | collective-permute-start | bytes 1081352 | tf_op jit(solution)/shard_map/ppermute | solution.py:24
  17.2 0.0 collective-permute-done.refs_1_
  17.2 0.0 collective-permute-start.5
  17.2 0.5 %collective-permute-start.6 = (bf16[128,1408]{1,0:T(8,128)(2,1)S(1)}, bf16[128,1408]{1,0:T(8,128)(2,1)S(1)}, u32[]{:S(2)}, u32[]{:S(2)}) collective-permute-start(bf16[128,1408]{1,0:T(8,128)(2,1)S(1)} %collective-permute-done.refs_1_), channel_id=1, source_target_pairs={{0,4},{4,0},{8,12},{12,8},{1,5},{5,1},{9,13},{13,9},{2,6},{6,2},{1... | collective-permute-start | bytes 1081352 | tf_op jit(solution)/shard_map/ppermute | solution.py:19
  17.7 1.6 %collective-permute-start.7 = (f32[1,1536]{1,0:T(1,128)S(1)}, f32[1,1536]{1,0:T(1,128)S(1)}, u32[]{:S(2)}, u32[]{:S(2)}) collective-permute-start(f32[1,1536]{1,0:T(1,128)S(1)} %add_add_fusion), channel_id=1, source_target_pairs={{0,8},{4,12},{8,0},{12,4},{1,9},{5,13},{9,1},{13,5},{2,10},{6,14},... | collective-permute-start | bytes 18440 | tf_op jit(solution)/shard_map/ppermute | solution.py:19
  19.3 2.1 %collective-permute-done.7 = f32[1,1536]{1,0:T(1,128)S(1)} collective-permute-done((f32[1,1536]{1,0:T(1,128)S(1)}, f32[1,1536]{1,0:T(1,128)S(1)}, u32[]{:S(2)}, u32[]{:S(2)}) %collective-permute-start.7) | collective-permute-done | bytes 6176 | tf_op jit(solution)/shard_map/ppermute | solution.py:19
  21.4 0.1 collective-permute-start.8
  21.5 1.2 %collective-permute-done.8.refs_6_ = f32[1,1536]{1,0:T(1,128)S(1)} collective-permute-done((f32[1,1536]{1,0:T(1,128)S(1)}, f32[1,1536]{1,0:T(1,128)S(1)}, u32[]{:S(2)}, u32[]{:S(2)}) %collective-permute-start.8) | collective-permute-done | bytes 6176 | tf_op jit(solution)/shard_map/ppermute | solution.py:19
  22.6 0.0 collective-permute-done.5.refs_2_
  22.6 0.0 collective-permute-done.6.refs_3_
  22.6 2.3 %shard_map.42 = (f32[128,384]{1,0:T(8,128)S(1)}, f32[128,384]{1,0:T(8,128)S(1)}, f32[2,256,512]{2,1,0:T(8,128)S(1)}, f32[2,2,256,128]{3,2,1,0:T(8,128)S(1)}, f32...) custom-call(bf16[128,1408]{1,0:T(8,128)(2,1)S(1)} %constant_dynamic-update-slice_fusion.packed_ref.refs_0, ...), custom_call_target="tpu_custom_call" | custom-call | flops 570425344 | bytes 1814528 | tf_op jit(solution)/shard_map/pallas_call | solution.py:211
  24.9 3.0 %collective-permute-done.9.refs_1_ = bf16[128,1408]{1,0:T(8,128)(2,1)S(1)} collective-permute-done((bf16[128,1408]{1,0:T(8,128)(2,1)S(1)}, bf16[128,1408]{1,0:T(8,128)(2,1)S(1)}, u32[]{:S(2)}, u32[]{:S(2)}) %collective-permute-start.9) | collective-permute-done | bytes 360480 | tf_op jit(solution)/shard_map/ppermute | solution.py:24
  27.9 1.2 %shard_map.43 = (f32[256,384]{1,0:T(8,128)S(1)}, f32[256,384]{1,0:T(8,128)S(1)}, f32[16,2,128]{2,1,0:T(2,128)S(1)}) custom-call(bf16[2,256,1408]{2,1,0:T(8,128)(2,1)S(1)} %get-tuple-element.31.refs_0_, bf16[128,1408]{1,0:T(8,128)(2,1)S(1)} %collective-permute-done.9.refs_1_, f32[1,1536]{1,0:T(1,128)S(1)} %get-tuple-element.30.refs_2_.stats_ref, ...), custom_call_target="tpu_custom_call" | custom-call | flops 285212672 | bytes 3382272 | tf_op jit(solution)/shard_map/pallas_call | solution.py:211
  29.1 0.1 collective-permute-start.10
  29.2 0.4 collective-permute-start.12
  29.6 1.3 %collective-permute-done.10.got_ref = f32[256,384]{1,0:T(8,128)S(1)} collective-permute-done((f32[256,384]{1,0:T(8,128)S(1)}, f32[256,384]{1,0:T(8,128)S(1)}, u32[]{:S(2)}, u32[]{:S(2)}) %collective-permute-start.10) | collective-permute-done | bytes 393248 | tf_op jit(solution)/shard_map/ppermute | solution.py:19
  31.0 1.3 %collective-permute-start.11 = (f32[128,384]{1,0:T(8,128)S(1)}, f32[128,384]{1,0:T(8,128)S(1)}, u32[]{:S(2)}, u32[]{:S(2)}) collective-permute-start(f32[128,384]{1,0:T(8,128)S(1)} %get-tuple-element.40), channel_id=1, source_target_pairs={{0,8},{4,12},{8,0},{12,4},{1,9},{5,13},{9,1},{13,5},{2,10},{6,14},... | collective-permute-start | bytes 589832 | tf_op jit(solution)/shard_map/ppermute | solution.py:19
  32.3 9.0 %all_to_all.5.sums_ref = f32[16,2,128]{2,1,0:T(2,128)S(1)} all-to-all(f32[16,2,128]{2,1,0:T(2,128)S(1)} %get-tuple-element.35), channel_id=1, replica_groups=mesh['groups'=2,'blk'=4,'sub'=4] {'blk','sub'}, dimensions={0} | all-to-all | bytes 32768 | tf_op jit(solution)/shard_map/all_to_all | solution.py:232
  41.2 0.0 collective-permute-done.12.refs_3_
  41.3 0.9 %shard_map.45 = (f32[128,384]{1,0:T(8,128)}, f32[1,128]{1,0:T(1,128)}) custom-call(bf16[128,1408]{1,0:T(8,128)(2,1)S(1)} %constant_dynamic-update-slice_fusion.packed_ref.refs_0_, f32[1,1536]{1,0:T(1,128)S(1)} %get-tuple-element.30.refs_2_.stats_ref, f32[16,2,128]{2,1,0:T(2,128)S(1)} %all_to_all.5.sums_ref, f32[128,384]{1,0:T(8,128)S(1)} %get-tuple-element.36.refs_0_, ...), custom_call_target="tpu_custom_call" | custom-call | flops 393216 | bytes 1169408 | tf_op jit(solution)/shard_map/pallas_call | solution.py:211
  (4 shorter events, 0.1 us)
Async XLA Ops:
  2.5 14.0 %collective-permute-start.1 = (bf16[128,1408]{1,0:T(8,128)(2,1)S(1)}, bf16[128,1408]{1,0:T(8,128)(2,1)S(1)}, u32[]{:S(2)}, u32[]{:S(2)}) collective-permute-start(bf16[128,1408]{1,0:T(8,128)(2,1)S(1)} %constant_dynamic-update-slice_fusion.packed_ref.refs_0_), channel_id=1, source_target_pairs={{0,1},{1,2},{2,3},{3,0},{4,5},{5,6},{6,7},{7,4},{8,9},{9,10},{10,1... | collective-permute-start | bytes 1081352 | tf_op jit(solution)/shard_map/ppermute | solution.py:24
  5.6 11.6 %collective-permute-start = (bf16[128,1408]{1,0:T(8,128)(2,1)S(1)}, bf16[128,1408]{1,0:T(8,128)(2,1)S(1)}, u32[]{:S(2)}, u32[]{:S(2)}) collective-permute-start(bf16[128,1408]{1,0:T(8,128)(2,1)S(1)} %constant_dynamic-update-slice_fusion.packed_ref.refs_0_), channel_id=1, source_target_pairs={{0,8},{4,12},{8,0},{12,4},{1,9},{5,13},{9,1},{13,5},{2,10},{6,14},... | collective-permute-start | bytes 1081352 | tf_op jit(solution)/shard_map/ppermute | solution.py:19
  7.3 8.2 %collective-permute-start.2 = (f32[1,1536]{1,0:T(1,128)S(1)}, f32[1,1536]{1,0:T(1,128)S(1)}, u32[]{:S(2)}, u32[]{:S(2)}) collective-permute-start(f32[1,1536]{1,0:T(1,128)S(1)} %shard_map.41), channel_id=1, source_target_pairs={{0,1},{1,0},{2,3},{3,2},{4,5},{5,4},{6,7},{7,6},{8,9},{9,8},{10,11... | collective-permute-start | bytes 18440 | tf_op jit(solution)/shard_map/ppermute | solution.py:19
  8.9 7.7 %collective-permute-start.3 = (f32[1,1536]{1,0:T(1,128)S(1)}, f32[1,1536]{1,0:T(1,128)S(1)}, u32[]{:S(2)}, u32[]{:S(2)}) collective-permute-start(f32[1,1536]{1,0:T(1,128)S(1)} %shard_map.41), channel_id=1, source_target_pairs={{0,2},{1,3},{2,0},{3,1},{4,6},{5,7},{6,4},{7,5},{8,10},{9,11},{10,... | collective-permute-start | bytes 18440 | tf_op jit(solution)/shard_map/ppermute | solution.py:19
  10.1 6.4 %collective-permute-start.4 = (f32[1,1536]{1,0:T(1,128)S(1)}, f32[1,1536]{1,0:T(1,128)S(1)}, u32[]{:S(2)}, u32[]{:S(2)}) collective-permute-start(f32[1,1536]{1,0:T(1,128)S(1)} %shard_map.41), channel_id=1, source_target_pairs={{0,3},{1,2},{2,1},{3,0},{4,7},{5,6},{6,5},{7,4},{8,11},{9,10},{10,... | collective-permute-start | bytes 18440 | tf_op jit(solution)/shard_map/ppermute | solution.py:19
  16.5 11.4 %collective-permute-start.9 = (bf16[128,1408]{1,0:T(8,128)(2,1)S(1)}, bf16[128,1408]{1,0:T(8,128)(2,1)S(1)}, u32[]{:S(2)}, u32[]{:S(2)}) collective-permute-start(bf16[128,1408]{1,0:T(8,128)(2,1)S(1)} %collective-permute-done.1.refs_4_), channel_id=1, source_target_pairs={{0,1},{1,2},{2,3},{3,0},{4,5},{5,6},{6,7},{7,4},{8,9},{9,10},{10,1... | collective-permute-start | bytes 1081352 | tf_op jit(solution)/shard_map/ppermute | solution.py:24
  17.2 5.5 %collective-permute-start.5 = (bf16[128,1408]{1,0:T(8,128)(2,1)S(1)}, bf16[128,1408]{1,0:T(8,128)(2,1)S(1)}, u32[]{:S(2)}, u32[]{:S(2)}) collective-permute-start(bf16[128,1408]{1,0:T(8,128)(2,1)S(1)} %constant_dynamic-update-slice_fusion.packed_ref.refs_0_), channel_id=1, source_target_pairs={{0,4},{4,0},{8,12},{12,8},{1,5},{5,1},{9,13},{13,9},{2,6},{6,2},{1... | collective-permute-start | bytes 1081352 | tf_op jit(solution)/shard_map/ppermute | solution.py:19
  17.2 5.5 %collective-permute-start.6 = (bf16[128,1408]{1,0:T(8,128)(2,1)S(1)}, bf16[128,1408]{1,0:T(8,128)(2,1)S(1)}, u32[]{:S(2)}, u32[]{:S(2)}) collective-permute-start(bf16[128,1408]{1,0:T(8,128)(2,1)S(1)} %collective-permute-done.refs_1_), channel_id=1, source_target_pairs={{0,4},{4,0},{8,12},{12,8},{1,5},{5,1},{9,13},{13,9},{2,6},{6,2},{1... | collective-permute-start | bytes 1081352 | tf_op jit(solution)/shard_map/ppermute | solution.py:19
  17.7 3.7 %collective-permute-start.7 = (f32[1,1536]{1,0:T(1,128)S(1)}, f32[1,1536]{1,0:T(1,128)S(1)}, u32[]{:S(2)}, u32[]{:S(2)}) collective-permute-start(f32[1,1536]{1,0:T(1,128)S(1)} %add_add_fusion), channel_id=1, source_target_pairs={{0,8},{4,12},{8,0},{12,4},{1,9},{5,13},{9,1},{13,5},{2,10},{6,14},... | collective-permute-start | bytes 18440 | tf_op jit(solution)/shard_map/ppermute | solution.py:19
  21.4 1.2 %collective-permute-start.8 = (f32[1,1536]{1,0:T(1,128)S(1)}, f32[1,1536]{1,0:T(1,128)S(1)}, u32[]{:S(2)}, u32[]{:S(2)}) collective-permute-start(f32[1,1536]{1,0:T(1,128)S(1)} %add.15.refs_5_), channel_id=1, source_target_pairs={{0,4},{4,0},{8,12},{12,8},{1,5},{5,1},{9,13},{13,9},{2,6},{6,2},{1... | collective-permute-start | bytes 18440 | tf_op jit(solution)/shard_map/ppermute | solution.py:19
  29.1 1.8 %collective-permute-start.10 = (f32[256,384]{1,0:T(8,128)S(1)}, f32[256,384]{1,0:T(8,128)S(1)}, u32[]{:S(2)}, u32[]{:S(2)}) collective-permute-start(f32[256,384]{1,0:T(8,128)S(1)} %get-tuple-element.38), channel_id=1, source_target_pairs={{0,4},{4,0},{8,12},{12,8},{1,5},{5,1},{9,13},{13,9},{2,6},{6,2},{1... | collective-permute-start | bytes 1179656 | tf_op jit(solution)/shard_map/ppermute | solution.py:19
  29.2 12.0 %collective-permute-start.12 = (f32[128,384]{1,0:T(8,128)S(1)}, f32[128,384]{1,0:T(8,128)S(1)}, u32[]{:S(2)}, u32[]{:S(2)}) collective-permute-start(f32[128,384]{1,0:T(8,128)S(1)} %get-tuple-element.41), channel_id=1, source_target_pairs={{0,3},{1,0},{2,1},{3,2},{4,7},{5,4},{6,5},{7,6},{8,11},{9,8},{10,9... | collective-permute-start | bytes 589832 | tf_op jit(solution)/shard_map/ppermute | solution.py:24
  31.0 10.3 %collective-permute-start.11 = (f32[128,384]{1,0:T(8,128)S(1)}, f32[128,384]{1,0:T(8,128)S(1)}, u32[]{:S(2)}, u32[]{:S(2)}) collective-permute-start(f32[128,384]{1,0:T(8,128)S(1)} %get-tuple-element.40), channel_id=1, source_target_pairs={{0,8},{4,12},{8,0},{12,4},{1,9},{5,13},{9,1},{13,5},{2,10},{6,14},... | collective-permute-start | bytes 589832 | tf_op jit(solution)/shard_map/ppermute | solution.py:19

commit v7 on v6

--- a/solution.py
+++ b/solution.py
@@ -21,7 +21,21 @@
 
 def shifted(value, axis, distance):
     size = lax.axis_size(axis)
-    return lax.ppermute(value, axis, [(i, (i + distance) % size) for i in range(size)])
+    places = [*range(0, size, 2), *reversed(range(1, size, 2))]
+    route = [(places[i], places[(i + distance) % size]) for i in range(size)]
+    return lax.ppermute(value, axis, route)
+
+
+def pack_kernel(t_hbm, s_hbm, packed_ref, sems):
+    t_width = t_hbm.shape[1]
+    copies = [
+        pltpu.make_async_copy(t_hbm, packed_ref.at[:, :t_width], sems.at[0]),
+        pltpu.make_async_copy(s_hbm, packed_ref.at[:, t_width:], sems.at[1]),
+    ]
+    for copy in copies:
+        copy.start()
+    for copy in copies:
+        copy.wait()
 
 
 def stats_kernel(t_width, packed_ref, stats_ref):
@@ -242,7 +256,16 @@
     side = rows * n_blk // 2
     f32 = functools.partial(jax.ShapeDtypeStruct, dtype=jnp.float32)
 
-    packed = jnp.concatenate([teacher, student], axis=1)
+    teacher, student = (pltpu.with_memory_space_constraint(x, pltpu.HBM) for x in (teacher, student))
+    packed = call(
+        pack_kernel,
+        jax.ShapeDtypeStruct((rows, t_width + s_width), teacher.dtype),
+        (teacher, student),
+        0,
+        vmem=48,
+        in_specs=[pl.BlockSpec(memory_space=pl.ANY)] * 2,
+        scratch_shapes=[pltpu.SemaphoreType.DMA((2,))],
+    )
     stats = call(
         functools.partial(stats_kernel, t_width),
         f32((1, t_width + s_width + LANES)),

time: 42.3 us -> 41.7 us (0.986)
  waiting for transfers between devices: 12.5 us -> 7.15 us
  starting transfers between devices: 13.5 us -> 17.8 us
  local copies, waits for them, and re-layouts: 1.88 us -> 0 us
  blocking collectives: 8.97 us -> 10.3 us
  Pallas kernels: 4.57 us -> 5.55 us
    ppermute x3, starting transfers between devices: 4.08 us -> 7.96 us  [shifted(): return lax.ppermute(value, axis, route)]
    ppermute x3, waiting for transfers between devices: 2.98 us -> 0.01 us  [shifted(): return lax.ppermute(value, axis, route)]
    ppermute x10, waiting for transfers between devices: 9.51 us -> 7.14 us  [exchange(): return lax.ppermute(value, axis, [(i, i ^ distance) for i in range(size)])]
    all_to_all x1, blocking collectives: 8.97 us -> 10.3 us  [to_all(): return lax.all_to_all(value, ('blk', 'sub'), 0, 0, tiled=True)]
    pallas_call x5 -> x6, Pallas kernels: 4.57 us -> 5.55 us  [call(): pl.pallas_call(kernel, out_shape=out_shape, in_specs=in_specs, out_specs=...]
    unnamed x1 -> x0, local copies, waits for them, and re-layouts: 0.97 us -> none
    concatenate x1 -> x0, local copies, waits for them, and re-layouts: 0.91 us -> none  [per_device(): packed = jnp.concatenate([teacher, student], axis=1)]
    ppermute x10, starting transfers between devices: 9.42 us -> 9.88 us  [exchange(): return lax.ppermute(value, axis, [(i, i ^ distance) for i in range(size)])]
  transfers between devices with their start and end apart: 13 -> 13, of which waited for: 6 -> 4; matrix products, arithmetic and copies ran while one was open for 0% -> 0% of each run, Pallas kernels for 6% -> 6%
where the time goes in v7:
time: 41.7 us; the launch traced here: 41.5 us
  starting transfers between devices  17.8 us (43%)
  blocking collectives  10.3 us (25%)
  waiting for transfers between devices  7.15 us (17%)
  Pallas kernels  5.55 us (13%)
  between operations  0.69 us (2%)
    all_to_all x1, blocking collectives, to_all(): return lax.all_to_all(value, ('blk', 'sub'), 0, 0, tiled=True)  10.3 us
    ppermute x10, starting transfers between devices, exchange(): return lax.ppermute(value, axis, [(i, i ^ distance) for i in range(size)])  9.88 us
    ppermute x3, starting transfers between devices, shifted(): return lax.ppermute(value, axis, route)  7.96 us
    ppermute x10, waiting for transfers between devices, exchange(): return lax.ppermute(value, axis, [(i, i ^ distance) for i in range(size)])  7.14 us
    pallas_call x6, Pallas kernels, call(): pl.pallas_call(kernel, out_shape=out_shape, in_specs=in_specs, out_specs=...  5.55 us
  transfers between devices with their start and end apart: 13, of which 4 were waited for; matrix products, arithmetic and copies ran while one was open for 0% of the time, Pallas kernels for 6%

profile of v7, /device:TPU:0, one launch (start us, length us, event | category | flops | bytes accessed | tf_op | source)
XLA Modules:
  0.0 41.5 jit_solution(2011369367045769581)
XLA Ops:
  0.6 1.0 %shard_map.41.packed_ref.refs_0_ = bf16[128,1408]{1,0:T(8,128)(2,1)S(1)} custom-call(bf16[128,1024]{1,0:T(8,128)(2,1)} %t_hbm.1, bf16[128,384]{1,0:T(8,128)(2,1)} %s_hbm.1), custom_call_target="tpu_custom_call" | custom-call | bytes 360448 | tf_op jit(solution)/shard_map/pallas_call | solution.py:225
  1.6 4.1 %collective-permute-start.1 = (bf16[128,1408]{1,0:T(8,128)(2,1)S(1)}, bf16[128,1408]{1,0:T(8,128)(2,1)S(1)}, u32[]{:S(2)}, u32[]{:S(2)}) collective-permute-start(bf16[128,1408]{1,0:T(8,128)(2,1)S(1)} %shard_map.41.packed_ref.refs_0_), channel_id=1, source_target_pairs={{0,2},{2,3},{3,1},{1,0},{4,6},{6,7},{7,5},{5,4},{8,10},{10,11},{11... | collective-permute-start | bytes 1081352 | tf_op jit(solution)/shard_map/ppermute | solution.py:26
  5.7 1.5 %collective-permute-start = (bf16[128,1408]{1,0:T(8,128)(2,1)S(1)}, bf16[128,1408]{1,0:T(8,128)(2,1)S(1)}, u32[]{:S(2)}, u32[]{:S(2)}) collective-permute-start(bf16[128,1408]{1,0:T(8,128)(2,1)S(1)} %shard_map.41.packed_ref.refs_0_), channel_id=1, source_target_pairs={{0,8},{4,12},{8,0},{12,4},{1,9},{5,13},{9,1},{13,5},{2,10},{6,14},... | collective-permute-start | bytes 1081352 | tf_op jit(solution)/shard_map/ppermute | solution.py:19
  7.2 0.2 shard_map.42
  7.4 0.0 collective-permute-start.2
  7.4 1.9 %collective-permute-start.3 = (f32[1,1536]{1,0:T(1,128)S(1)}, f32[1,1536]{1,0:T(1,128)S(1)}, u32[]{:S(2)}, u32[]{:S(2)}) collective-permute-start(f32[1,1536]{1,0:T(1,128)S(1)} %shard_map.42), channel_id=1, source_target_pairs={{0,2},{1,3},{2,0},{3,1},{4,6},{5,7},{6,4},{7,5},{8,10},{9,11},{10,... | collective-permute-start | bytes 18440 | tf_op jit(solution)/shard_map/ppermute | solution.py:19
  9.3 2.5 %collective-permute-start.4 = (f32[1,1536]{1,0:T(1,128)S(1)}, f32[1,1536]{1,0:T(1,128)S(1)}, u32[]{:S(2)}, u32[]{:S(2)}) collective-permute-start(f32[1,1536]{1,0:T(1,128)S(1)} %shard_map.42), channel_id=1, source_target_pairs={{0,3},{1,2},{2,1},{3,0},{4,7},{5,6},{6,5},{7,4},{8,11},{9,10},{10,... | collective-permute-start | bytes 18440 | tf_op jit(solution)/shard_map/ppermute | solution.py:19
  11.8 1.9 %collective-permute-done.2 = f32[1,1536]{1,0:T(1,128)S(1)} collective-permute-done((f32[1,1536]{1,0:T(1,128)S(1)}, f32[1,1536]{1,0:T(1,128)S(1)}, u32[]{:S(2)}, u32[]{:S(2)}) %collective-permute-start.2) | collective-permute-done | bytes 6176 | tf_op jit(solution)/shard_map/ppermute | solution.py:19
  13.7 2.0 %collective-permute-done.3 = f32[1,1536]{1,0:T(1,128)S(1)} collective-permute-done((f32[1,1536]{1,0:T(1,128)S(1)}, f32[1,1536]{1,0:T(1,128)S(1)}, u32[]{:S(2)}, u32[]{:S(2)}) %collective-permute-start.3) | collective-permute-done | bytes 6176 | tf_op jit(solution)/shard_map/ppermute | solution.py:19
  15.7 0.0 collective-permute-done.4
  15.7 0.0 collective-permute-done.1.refs_4_
  15.7 1.6 %collective-permute-start.9 = (bf16[128,1408]{1,0:T(8,128)(2,1)S(1)}, bf16[128,1408]{1,0:T(8,128)(2,1)S(1)}, u32[]{:S(2)}, u32[]{:S(2)}) collective-permute-start(bf16[128,1408]{1,0:T(8,128)(2,1)S(1)} %collective-permute-done.1.refs_4_), channel_id=1, source_target_pairs={{0,2},{2,3},{3,1},{1,0},{4,6},{6,7},{7,5},{5,4},{8,10},{10,11},{11... | collective-permute-start | bytes 1081352 | tf_op jit(solution)/shard_map/ppermute | solution.py:26
  17.3 0.0 collective-permute-done.refs_1_
  17.3 0.0 collective-permute-start.5
  17.3 0.5 %collective-permute-start.6 = (bf16[128,1408]{1,0:T(8,128)(2,1)S(1)}, bf16[128,1408]{1,0:T(8,128)(2,1)S(1)}, u32[]{:S(2)}, u32[]{:S(2)}) collective-permute-start(bf16[128,1408]{1,0:T(8,128)(2,1)S(1)} %collective-permute-done.refs_1_), channel_id=1, source_target_pairs={{0,4},{4,0},{8,12},{12,8},{1,5},{5,1},{9,13},{13,9},{2,6},{6,2},{1... | collective-permute-start | bytes 1081352 | tf_op jit(solution)/shard_map/ppermute | solution.py:19
  17.8 1.6 %collective-permute-start.7 = (f32[1,1536]{1,0:T(1,128)S(1)}, f32[1,1536]{1,0:T(1,128)S(1)}, u32[]{:S(2)}, u32[]{:S(2)}) collective-permute-start(f32[1,1536]{1,0:T(1,128)S(1)} %add_add_fusion), channel_id=1, source_target_pairs={{0,8},{4,12},{8,0},{12,4},{1,9},{5,13},{9,1},{13,5},{2,10},{6,14},... | collective-permute-start | bytes 18440 | tf_op jit(solution)/shard_map/ppermute | solution.py:19
  19.4 2.1 %collective-permute-done.7 = f32[1,1536]{1,0:T(1,128)S(1)} collective-permute-done((f32[1,1536]{1,0:T(1,128)S(1)}, f32[1,1536]{1,0:T(1,128)S(1)}, u32[]{:S(2)}, u32[]{:S(2)}) %collective-permute-start.7) | collective-permute-done | bytes 6176 | tf_op jit(solution)/shard_map/ppermute | solution.py:19
  21.5 0.1 collective-permute-start.8
  21.6 1.2 %collective-permute-done.8.refs_6_ = f32[1,1536]{1,0:T(1,128)S(1)} collective-permute-done((f32[1,1536]{1,0:T(1,128)S(1)}, f32[1,1536]{1,0:T(1,128)S(1)}, u32[]{:S(2)}, u32[]{:S(2)}) %collective-permute-start.8) | collective-permute-done | bytes 6176 | tf_op jit(solution)/shard_map/ppermute | solution.py:19
  22.8 0.0 collective-permute-done.5.refs_2_
  22.8 0.0 collective-permute-done.6.refs_3_
  22.8 2.3 %shard_map.43 = (f32[128,384]{1,0:T(8,128)S(1)}, f32[128,384]{1,0:T(8,128)S(1)}, f32[2,256,512]{2,1,0:T(8,128)S(1)}, f32[2,2,256,128]{3,2,1,0:T(8,128)S(1)}, f32...) custom-call(bf16[128,1408]{1,0:T(8,128)(2,1)S(1)} %shard_map.41.packed_ref.refs_0_, ...), custom_call_target="tpu_custom_call" | custom-call | flops 570425344 | bytes 1814528 | tf_op jit(solution)/shard_map/pallas_call | solution.py:225
  25.1 0.0 collective-permute-done.9.refs_1_
  25.1 1.2 %shard_map.44 = (f32[256,384]{1,0:T(8,128)S(1)}, f32[256,384]{1,0:T(8,128)S(1)}, f32[16,2,128]{2,1,0:T(2,128)S(1)}) custom-call(bf16[2,256,1408]{2,1,0:T(8,128)(2,1)S(1)} %get-tuple-element.31.refs_0_, bf16[128,1408]{1,0:T(8,128)(2,1)S(1)} %collective-permute-done.9.refs_1_, f32[1,1536]{1,0:T(1,128)S(1)} %get-tuple-element.30.refs_2_.stats_ref, ...), custom_call_target="tpu_custom_call" | custom-call | flops 285212672 | bytes 3382272 | tf_op jit(solution)/shard_map/pallas_call | solution.py:225
  26.3 0.2 collective-permute-start.10
  26.5 2.2 %collective-permute-start.12 = (f32[128,384]{1,0:T(8,128)S(1)}, f32[128,384]{1,0:T(8,128)S(1)}, u32[]{:S(2)}, u32[]{:S(2)}) collective-permute-start(f32[128,384]{1,0:T(8,128)S(1)} %get-tuple-element.41), channel_id=1, source_target_pairs={{0,1},{2,0},{3,2},{1,3},{4,5},{6,4},{7,6},{5,7},{8,9},{10,8},{11,1... | collective-permute-start | bytes 589832 | tf_op jit(solution)/shard_map/ppermute | solution.py:26
  28.8 0.0 collective-permute-done.10.got_ref
  28.8 1.6 %collective-permute-start.11 = (f32[128,384]{1,0:T(8,128)S(1)}, f32[128,384]{1,0:T(8,128)S(1)}, u32[]{:S(2)}, u32[]{:S(2)}) collective-permute-start(f32[128,384]{1,0:T(8,128)S(1)} %get-tuple-element.40), channel_id=1, source_target_pairs={{0,8},{4,12},{8,0},{12,4},{1,9},{5,13},{9,1},{13,5},{2,10},{6,14},... | collective-permute-start | bytes 589832 | tf_op jit(solution)/shard_map/ppermute | solution.py:19
  30.4 10.3 %all_to_all.5.sums_ref = f32[16,2,128]{2,1,0:T(2,128)S(1)} all-to-all(f32[16,2,128]{2,1,0:T(2,128)S(1)} %get-tuple-element.35), channel_id=1, replica_groups=mesh['groups'=2,'blk'=4,'sub'=4] {'blk','sub'}, dimensions={0} | all-to-all | bytes 32768 | tf_op jit(solution)/shard_map/all_to_all | solution.py:246
  40.6 0.0 collective-permute-done.12.refs_3_
  40.6 0.0 collective-permute-done.11.refs_2_
  40.6 0.9 %shard_map.46 = (f32[128,384]{1,0:T(8,128)}, f32[1,128]{1,0:T(1,128)}) custom-call(bf16[128,1408]{1,0:T(8,128)(2,1)S(1)} %shard_map.41.packed_ref.refs_0_, f32[1,1536]{1,0:T(1,128)S(1)} %get-tuple-element.30.refs_2_.stats_ref, f32[16,2,128]{2,1,0:T(2,128)S(1)} %all_to_all.5.sums_ref, f32[128,384]{1,0:T(8,128)S(1)} %get-tuple-element.36.refs_0_, ...), custom_call_target="tpu_custom_call" | custom-call | flops 393216 | bytes 1169408 | tf_op jit(solution)/shard_map/pallas_call | solution.py:225
  (3 shorter events, 0.1 us)
Async XLA Ops:
  1.6 14.0 %collective-permute-start.1 = (bf16[128,1408]{1,0:T(8,128)(2,1)S(1)}, bf16[128,1408]{1,0:T(8,128)(2,1)S(1)}, u32[]{:S(2)}, u32[]{:S(2)}) collective-permute-start(bf16[128,1408]{1,0:T(8,128)(2,1)S(1)} %shard_map.41.packed_ref.refs_0_), channel_id=1, source_target_pairs={{0,2},{2,3},{3,1},{1,0},{4,6},{6,7},{7,5},{5,4},{8,10},{10,11},{11... | collective-permute-start | bytes 1081352 | tf_op jit(solution)/shard_map/ppermute | solution.py:26
  5.7 11.6 %collective-permute-start = (bf16[128,1408]{1,0:T(8,128)(2,1)S(1)}, bf16[128,1408]{1,0:T(8,128)(2,1)S(1)}, u32[]{:S(2)}, u32[]{:S(2)}) collective-permute-start(bf16[128,1408]{1,0:T(8,128)(2,1)S(1)} %shard_map.41.packed_ref.refs_0_), channel_id=1, source_target_pairs={{0,8},{4,12},{8,0},{12,4},{1,9},{5,13},{9,1},{13,5},{2,10},{6,14},... | collective-permute-start | bytes 1081352 | tf_op jit(solution)/shard_map/ppermute | solution.py:19
  7.4 6.3 %collective-permute-start.2 = (f32[1,1536]{1,0:T(1,128)S(1)}, f32[1,1536]{1,0:T(1,128)S(1)}, u32[]{:S(2)}, u32[]{:S(2)}) collective-permute-start(f32[1,1536]{1,0:T(1,128)S(1)} %shard_map.42), channel_id=1, source_target_pairs={{0,1},{1,0},{2,3},{3,2},{4,5},{5,4},{6,7},{7,6},{8,9},{9,8},{10,11... | collective-permute-start | bytes 18440 | tf_op jit(solution)/shard_map/ppermute | solution.py:19
  7.4 8.2 %collective-permute-start.3 = (f32[1,1536]{1,0:T(1,128)S(1)}, f32[1,1536]{1,0:T(1,128)S(1)}, u32[]{:S(2)}, u32[]{:S(2)}) collective-permute-start(f32[1,1536]{1,0:T(1,128)S(1)} %shard_map.42), channel_id=1, source_target_pairs={{0,2},{1,3},{2,0},{3,1},{4,6},{5,7},{6,4},{7,5},{8,10},{9,11},{10,... | collective-permute-start | bytes 18440 | tf_op jit(solution)/shard_map/ppermute | solution.py:19
  9.3 6.3 %collective-permute-start.4 = (f32[1,1536]{1,0:T(1,128)S(1)}, f32[1,1536]{1,0:T(1,128)S(1)}, u32[]{:S(2)}, u32[]{:S(2)}) collective-permute-start(f32[1,1536]{1,0:T(1,128)S(1)} %shard_map.42), channel_id=1, source_target_pairs={{0,3},{1,2},{2,1},{3,0},{4,7},{5,6},{6,5},{7,4},{8,11},{9,10},{10,... | collective-permute-start | bytes 18440 | tf_op jit(solution)/shard_map/ppermute | solution.py:19
  15.7 9.4 %collective-permute-start.9 = (bf16[128,1408]{1,0:T(8,128)(2,1)S(1)}, bf16[128,1408]{1,0:T(8,128)(2,1)S(1)}, u32[]{:S(2)}, u32[]{:S(2)}) collective-permute-start(bf16[128,1408]{1,0:T(8,128)(2,1)S(1)} %collective-permute-done.1.refs_4_), channel_id=1, source_target_pairs={{0,2},{2,3},{3,1},{1,0},{4,6},{6,7},{7,5},{5,4},{8,10},{10,11},{11... | collective-permute-start | bytes 1081352 | tf_op jit(solution)/shard_map/ppermute | solution.py:26
  17.3 5.5 %collective-permute-start.5 = (bf16[128,1408]{1,0:T(8,128)(2,1)S(1)}, bf16[128,1408]{1,0:T(8,128)(2,1)S(1)}, u32[]{:S(2)}, u32[]{:S(2)}) collective-permute-start(bf16[128,1408]{1,0:T(8,128)(2,1)S(1)} %shard_map.41.packed_ref.refs_0_), channel_id=1, source_target_pairs={{0,4},{4,0},{8,12},{12,8},{1,5},{5,1},{9,13},{13,9},{2,6},{6,2},{1... | collective-permute-start | bytes 1081352 | tf_op jit(solution)/shard_map/ppermute | solution.py:19
  17.3 5.5 %collective-permute-start.6 = (bf16[128,1408]{1,0:T(8,128)(2,1)S(1)}, bf16[128,1408]{1,0:T(8,128)(2,1)S(1)}, u32[]{:S(2)}, u32[]{:S(2)}) collective-permute-start(bf16[128,1408]{1,0:T(8,128)(2,1)S(1)} %collective-permute-done.refs_1_), channel_id=1, source_target_pairs={{0,4},{4,0},{8,12},{12,8},{1,5},{5,1},{9,13},{13,9},{2,6},{6,2},{1... | collective-permute-start | bytes 1081352 | tf_op jit(solution)/shard_map/ppermute | solution.py:19
  17.8 3.7 %collective-permute-start.7 = (f32[1,1536]{1,0:T(1,128)S(1)}, f32[1,1536]{1,0:T(1,128)S(1)}, u32[]{:S(2)}, u32[]{:S(2)}) collective-permute-start(f32[1,1536]{1,0:T(1,128)S(1)} %add_add_fusion), channel_id=1, source_target_pairs={{0,8},{4,12},{8,0},{12,4},{1,9},{5,13},{9,1},{13,5},{2,10},{6,14},... | collective-permute-start | bytes 18440 | tf_op jit(solution)/shard_map/ppermute | solution.py:19
  21.5 1.2 %collective-permute-start.8 = (f32[1,1536]{1,0:T(1,128)S(1)}, f32[1,1536]{1,0:T(1,128)S(1)}, u32[]{:S(2)}, u32[]{:S(2)}) collective-permute-start(f32[1,1536]{1,0:T(1,128)S(1)} %add.15.refs_5_), channel_id=1, source_target_pairs={{0,4},{4,0},{8,12},{12,8},{1,5},{5,1},{9,13},{13,9},{2,6},{6,2},{1... | collective-permute-start | bytes 18440 | tf_op jit(solution)/shard_map/ppermute | solution.py:19
  26.3 2.5 %collective-permute-start.10 = (f32[256,384]{1,0:T(8,128)S(1)}, f32[256,384]{1,0:T(8,128)S(1)}, u32[]{:S(2)}, u32[]{:S(2)}) collective-permute-start(f32[256,384]{1,0:T(8,128)S(1)} %get-tuple-element.38), channel_id=1, source_target_pairs={{0,4},{4,0},{8,12},{12,8},{1,5},{5,1},{9,13},{13,9},{2,6},{6,2},{1... | collective-permute-start | bytes 1179656 | tf_op jit(solution)/shard_map/ppermute | solution.py:19
  26.5 14.1 %collective-permute-start.12 = (f32[128,384]{1,0:T(8,128)S(1)}, f32[128,384]{1,0:T(8,128)S(1)}, u32[]{:S(2)}, u32[]{:S(2)}) collective-permute-start(f32[128,384]{1,0:T(8,128)S(1)} %get-tuple-element.41), channel_id=1, source_target_pairs={{0,1},{2,0},{3,2},{1,3},{4,5},{6,4},{7,6},{5,7},{8,9},{10,8},{11,1... | collective-permute-start | bytes 589832 | tf_op jit(solution)/shard_map/ppermute | solution.py:26
  28.8 11.8 %collective-permute-start.11 = (f32[128,384]{1,0:T(8,128)S(1)}, f32[128,384]{1,0:T(8,128)S(1)}, u32[]{:S(2)}, u32[]{:S(2)}) collective-permute-start(f32[128,384]{1,0:T(8,128)S(1)} %get-tuple-element.40), channel_id=1, source_target_pairs={{0,8},{4,12},{8,0},{12,4},{1,9},{5,13},{9,1},{13,5},{2,10},{6,14},... | collective-permute-start | bytes 589832 | tf_op jit(solution)/shard_map/ppermute | solution.py:19

commit v8 on v7

--- a/solution.py
+++ b/solution.py
@@ -301,7 +301,6 @@
         half * pair_flops,
     )
     own, backs = tiles[0], tiles[1:]
-    returned = [shifted(x, "sub", -k) for k, x in enumerate(backs, 1)]
     keep, give, sums = call(
         functools.partial(late_kernel, t_width, total_rows),
         [f32((side, s_width))] * 2 + [f32((n_blk * n_sub, 2, LANES))],
@@ -309,6 +308,9 @@
         pair_flops,
     )
     got = exchange(give, "blk", 1)
+    all_sums = to_all(sums)
+    got, all_sums, backs = lax.optimization_barrier((got, all_sums, backs))
+    returned = [shifted(x, "sub", -k) for k, x in enumerate(backs, 1)]
     tiles, distance = n_blk // 2, 2
     while tiles > 1:
         tiles //= 2
@@ -318,7 +320,6 @@
         )
         got = exchange(give, "blk", distance)
         distance *= 2
-    all_sums = to_all(sums)
     parts = [own, keep, got] + returned
     grad, loss = call(
         functools.partial(final_kernel, t_width, total_rows),

time: 41.7 us -> 47.6 us (1.14)
  waiting for transfers between devices: 7.15 us -> 14.1 us
  starting transfers between devices: 17.8 us -> 15.2 us
  blocking collectives: 10.3 us -> 11.8 us
    ppermute x10, waiting for transfers between devices: 7.14 us -> 13 us  [exchange(): return lax.ppermute(value, axis, [(i, i ^ distance) for i in range(size)])]
    ppermute x3, starting transfers between devices: 7.96 us -> 6.22 us  [shifted(): return lax.ppermute(value, axis, route)]
    all_to_all x1, blocking collectives: 10.3 us -> 11.8 us  [to_all(): return lax.all_to_all(value, ('blk', 'sub'), 0, 0, tiled=True)]
    ppermute x3, waiting for transfers between devices: 0.01 us -> 1.18 us  [shifted(): return lax.ppermute(value, axis, route)]
    ppermute x10, starting transfers between devices: 9.88 us -> 8.97 us  [exchange(): return lax.ppermute(value, axis, [(i, i ^ distance) for i in range(size)])]
  transfers between devices with their start and end apart: 13 -> 13, of which waited for: 4 -> 6; matrix products, arithmetic and copies ran while one was open for 0% -> 0% of each run, Pallas kernels for 6% -> 5%
where the time goes in v8:
time: 47.6 us; the launch traced here: 47.4 us
  starting transfers between devices  15.2 us (32%)
  waiting for transfers between devices  14.1 us (30%)
  blocking collectives  11.8 us (25%)
  Pallas kernels  5.55 us (12%)
  between operations  0.69 us (1%)
    ppermute x10, waiting for transfers between devices, exchange(): return lax.ppermute(value, axis, [(i, i ^ distance) for i in range(size)])  13 us
    all_to_all x1, blocking collectives, to_all(): return lax.all_to_all(value, ('blk', 'sub'), 0, 0, tiled=True)  11.8 us
    ppermute x10, starting transfers between devices, exchange(): return lax.ppermute(value, axis, [(i, i ^ distance) for i in range(size)])  8.97 us
    ppermute x3, starting transfers between devices, shifted(): return lax.ppermute(value, axis, route)  6.22 us
    pallas_call x6, Pallas kernels, call(): pl.pallas_call(kernel, out_shape=out_shape, in_specs=in_specs, out_specs=...  5.55 us
    ppermute x3, waiting for transfers between devices, shifted(): return lax.ppermute(value, axis, route)  1.18 us
  transfers between devices with their start and end apart: 13, of which 6 were waited for; matrix products, arithmetic and copies ran while one was open for 0% of the time, Pallas kernels for 5%

profile of v8, /device:TPU:0, one launch (start us, length us, event | category | flops | bytes accessed | tf_op | source)
XLA Modules:
  0.0 47.4 jit_solution(142491755078851475)
XLA Ops:
  0.6 1.0 %shard_map.41.packed_ref.refs_0_ = bf16[128,1408]{1,0:T(8,128)(2,1)S(1)} custom-call(bf16[128,1024]{1,0:T(8,128)(2,1)} %t_hbm.1, bf16[128,384]{1,0:T(8,128)(2,1)} %s_hbm.1), custom_call_target="tpu_custom_call" | custom-call | bytes 360448 | tf_op jit(solution)/shard_map/pallas_call | solution.py:225
  1.6 4.1 %collective-permute-start.1 = (bf16[128,1408]{1,0:T(8,128)(2,1)S(1)}, bf16[128,1408]{1,0:T(8,128)(2,1)S(1)}, u32[]{:S(2)}, u32[]{:S(2)}) collective-permute-start(bf16[128,1408]{1,0:T(8,128)(2,1)S(1)} %shard_map.41.packed_ref.refs_0_), channel_id=1, source_target_pairs={{0,2},{2,3},{3,1},{1,0},{4,6},{6,7},{7,5},{5,4},{8,10},{10,11},{11... | collective-permute-start | bytes 1081352 | tf_op jit(solution)/shard_map/ppermute | solution.py:26
  5.7 1.5 %collective-permute-start = (bf16[128,1408]{1,0:T(8,128)(2,1)S(1)}, bf16[128,1408]{1,0:T(8,128)(2,1)S(1)}, u32[]{:S(2)}, u32[]{:S(2)}) collective-permute-start(bf16[128,1408]{1,0:T(8,128)(2,1)S(1)} %shard_map.41.packed_ref.refs_0_), channel_id=1, source_target_pairs={{0,8},{4,12},{8,0},{12,4},{1,9},{5,13},{9,1},{13,5},{2,10},{6,14},... | collective-permute-start | bytes 1081352 | tf_op jit(solution)/shard_map/ppermute | solution.py:19
  7.2 0.2 shard_map.42
  7.4 0.0 collective-permute-start.2
  7.4 1.9 %collective-permute-start.3 = (f32[1,1536]{1,0:T(1,128)S(1)}, f32[1,1536]{1,0:T(1,128)S(1)}, u32[]{:S(2)}, u32[]{:S(2)}) collective-permute-start(f32[1,1536]{1,0:T(1,128)S(1)} %shard_map.42), channel_id=1, source_target_pairs={{0,2},{1,3},{2,0},{3,1},{4,6},{5,7},{6,4},{7,5},{8,10},{9,11},{10,... | collective-permute-start | bytes 18440 | tf_op jit(solution)/shard_map/ppermute | solution.py:19
  9.3 2.5 %collective-permute-start.4 = (f32[1,1536]{1,0:T(1,128)S(1)}, f32[1,1536]{1,0:T(1,128)S(1)}, u32[]{:S(2)}, u32[]{:S(2)}) collective-permute-start(f32[1,1536]{1,0:T(1,128)S(1)} %shard_map.42), channel_id=1, source_target_pairs={{0,3},{1,2},{2,1},{3,0},{4,7},{5,6},{6,5},{7,4},{8,11},{9,10},{10,... | collective-permute-start | bytes 18440 | tf_op jit(solution)/shard_map/ppermute | solution.py:19
  11.8 1.9 %collective-permute-done.2 = f32[1,1536]{1,0:T(1,128)S(1)} collective-permute-done((f32[1,1536]{1,0:T(1,128)S(1)}, f32[1,1536]{1,0:T(1,128)S(1)}, u32[]{:S(2)}, u32[]{:S(2)}) %collective-permute-start.2) | collective-permute-done | bytes 6176 | tf_op jit(solution)/shard_map/ppermute | solution.py:19
  13.7 2.0 %collective-permute-done.3 = f32[1,1536]{1,0:T(1,128)S(1)} collective-permute-done((f32[1,1536]{1,0:T(1,128)S(1)}, f32[1,1536]{1,0:T(1,128)S(1)}, u32[]{:S(2)}, u32[]{:S(2)}) %collective-permute-start.3) | collective-permute-done | bytes 6176 | tf_op jit(solution)/shard_map/ppermute | solution.py:19
  15.7 0.0 collective-permute-done.4
  15.7 0.0 collective-permute-done.1.refs_4_
  15.7 1.6 %collective-permute-start.9 = (bf16[128,1408]{1,0:T(8,128)(2,1)S(1)}, bf16[128,1408]{1,0:T(8,128)(2,1)S(1)}, u32[]{:S(2)}, u32[]{:S(2)}) collective-permute-start(bf16[128,1408]{1,0:T(8,128)(2,1)S(1)} %collective-permute-done.1.refs_4_), channel_id=1, source_target_pairs={{0,2},{2,3},{3,1},{1,0},{4,6},{6,7},{7,5},{5,4},{8,10},{10,11},{11... | collective-permute-start | bytes 1081352 | tf_op jit(solution)/shard_map/ppermute | solution.py:26
  17.3 0.0 collective-permute-done.refs_1_
  17.3 0.0 collective-permute-start.5
  17.3 0.5 %collective-permute-start.6 = (bf16[128,1408]{1,0:T(8,128)(2,1)S(1)}, bf16[128,1408]{1,0:T(8,128)(2,1)S(1)}, u32[]{:S(2)}, u32[]{:S(2)}) collective-permute-start(bf16[128,1408]{1,0:T(8,128)(2,1)S(1)} %collective-permute-done.refs_1_), channel_id=1, source_target_pairs={{0,4},{4,0},{8,12},{12,8},{1,5},{5,1},{9,13},{13,9},{2,6},{6,2},{1... | collective-permute-start | bytes 1081352 | tf_op jit(solution)/shard_map/ppermute | solution.py:19
  17.8 1.6 %collective-permute-start.7 = (f32[1,1536]{1,0:T(1,128)S(1)}, f32[1,1536]{1,0:T(1,128)S(1)}, u32[]{:S(2)}, u32[]{:S(2)}) collective-permute-start(f32[1,1536]{1,0:T(1,128)S(1)} %add_add_fusion), channel_id=1, source_target_pairs={{0,8},{4,12},{8,0},{12,4},{1,9},{5,13},{9,1},{13,5},{2,10},{6,14},... | collective-permute-start | bytes 18440 | tf_op jit(solution)/shard_map/ppermute | solution.py:19
  19.4 2.1 %collective-permute-done.7 = f32[1,1536]{1,0:T(1,128)S(1)} collective-permute-done((f32[1,1536]{1,0:T(1,128)S(1)}, f32[1,1536]{1,0:T(1,128)S(1)}, u32[]{:S(2)}, u32[]{:S(2)}) %collective-permute-start.7) | collective-permute-done | bytes 6176 | tf_op jit(solution)/shard_map/ppermute | solution.py:19
  21.5 0.1 collective-permute-start.8
  21.6 1.2 %collective-permute-done.8.refs_6_ = f32[1,1536]{1,0:T(1,128)S(1)} collective-permute-done((f32[1,1536]{1,0:T(1,128)S(1)}, f32[1,1536]{1,0:T(1,128)S(1)}, u32[]{:S(2)}, u32[]{:S(2)}) %collective-permute-start.8) | collective-permute-done | bytes 6176 | tf_op jit(solution)/shard_map/ppermute | solution.py:19
  22.8 0.0 collective-permute-done.5.refs_2_
  22.8 0.0 collective-permute-done.6.refs_3_
  22.8 2.3 %shard_map.43 = (f32[128,384]{1,0:T(8,128)S(1)}, f32[128,384]{1,0:T(8,128)S(1)}, f32[2,256,512]{2,1,0:T(8,128)S(1)}, f32[2,2,256,128]{3,2,1,0:T(8,128)S(1)}, f32...) custom-call(bf16[128,1408]{1,0:T(8,128)(2,1)S(1)} %shard_map.41.packed_ref.refs_0_, ...), custom_call_target="tpu_custom_call" | custom-call | flops 570425344 | bytes 1814528 | tf_op jit(solution)/shard_map/pallas_call | solution.py:225
  25.1 0.0 collective-permute-done.9.refs_1_
  25.1 1.2 %shard_map.44 = (f32[256,384]{1,0:T(8,128)S(1)}, f32[256,384]{1,0:T(8,128)S(1)}, f32[16,2,128]{2,1,0:T(2,128)S(1)}) custom-call(bf16[2,256,1408]{2,1,0:T(8,128)(2,1)S(1)} %get-tuple-element.34.refs_0_, bf16[128,1408]{1,0:T(8,128)(2,1)S(1)} %collective-permute-done.9.refs_1_, f32[1,1536]{1,0:T(1,128)S(1)} %get-tuple-element.33.refs_2_.stats_ref, ...), custom_call_target="tpu_custom_call" | custom-call | flops 285212672 | bytes 3382272 | tf_op jit(solution)/shard_map/pallas_call | solution.py:225
  26.3 0.2 collective-permute-start.10
  26.5 11.8 %all_to_all.5.sums_ref = f32[16,2,128]{2,1,0:T(2,128)S(1)} all-to-all(f32[16,2,128]{2,1,0:T(2,128)S(1)} %get-tuple-element.39), channel_id=1, replica_groups=mesh['groups'=2,'blk'=4,'sub'=4] {'blk','sub'}, dimensions={0} | all-to-all | bytes 32768 | tf_op jit(solution)/shard_map/all_to_all | solution.py:246
  38.4 0.0 collective-permute-done.10.got_ref
  38.4 0.7 %collective-permute-start.11 = (f32[128,384]{1,0:T(8,128)S(1)}, f32[128,384]{1,0:T(8,128)S(1)}, u32[]{:S(2)}, u32[]{:S(2)}) collective-permute-start(f32[128,384]{1,0:T(8,128)S(1)} %get-tuple-element.46), channel_id=1, source_target_pairs={{0,8},{4,12},{8,0},{12,4},{1,9},{5,13},{9,1},{13,5},{2,10},{6,14},... | collective-permute-start | bytes 589832 | tf_op jit(solution)/shard_map/ppermute | solution.py:19
  39.1 0.5 %collective-permute-start.12 = (f32[128,384]{1,0:T(8,128)S(1)}, f32[128,384]{1,0:T(8,128)S(1)}, u32[]{:S(2)}, u32[]{:S(2)}) collective-permute-start(f32[128,384]{1,0:T(8,128)S(1)} %get-tuple-element.47), channel_id=1, source_target_pairs={{0,1},{2,0},{3,2},{1,3},{4,5},{6,4},{7,6},{5,7},{8,9},{10,8},{11,1... | collective-permute-start | bytes 589832 | tf_op jit(solution)/shard_map/ppermute | solution.py:26
  39.6 5.8 %collective-permute-done.11.refs_2_ = f32[128,384]{1,0:T(8,128)S(1)} collective-permute-done((f32[128,384]{1,0:T(8,128)S(1)}, f32[128,384]{1,0:T(8,128)S(1)}, u32[]{:S(2)}, u32[]{:S(2)}) %collective-permute-start.11) | collective-permute-done | bytes 196640 | tf_op jit(solution)/shard_map/ppermute | solution.py:19
  45.4 1.2 %collective-permute-done.12.refs_3_ = f32[128,384]{1,0:T(8,128)S(1)} collective-permute-done((f32[128,384]{1,0:T(8,128)S(1)}, f32[128,384]{1,0:T(8,128)S(1)}, u32[]{:S(2)}, u32[]{:S(2)}) %collective-permute-start.12) | collective-permute-done | bytes 196640 | tf_op jit(solution)/shard_map/ppermute | solution.py:26
  46.6 0.9 %shard_map.46 = (f32[128,384]{1,0:T(8,128)}, f32[1,128]{1,0:T(1,128)}) custom-call(bf16[128,1408]{1,0:T(8,128)(2,1)S(1)} %shard_map.41.packed_ref.refs_0_, f32[1,1536]{1,0:T(1,128)S(1)} %get-tuple-element.33.refs_2_.stats_ref, f32[16,2,128]{2,1,0:T(2,128)S(1)} %all_to_all.5.sums_ref, f32[128,384]{1,0:T(8,128)S(1)} %get-tuple-element.42.refs_0_, ...), custom_call_target="tpu_custom_call" | custom-call | flops 393216 | bytes 1169408 | tf_op jit(solution)/shard_map/pallas_call | solution.py:225
  (3 shorter events, 0.1 us)
Async XLA Ops:
  1.6 14.0 %collective-permute-start.1 = (bf16[128,1408]{1,0:T(8,128)(2,1)S(1)}, bf16[128,1408]{1,0:T(8,128)(2,1)S(1)}, u32[]{:S(2)}, u32[]{:S(2)}) collective-permute-start(bf16[128,1408]{1,0:T(8,128)(2,1)S(1)} %shard_map.41.packed_ref.refs_0_), channel_id=1, source_target_pairs={{0,2},{2,3},{3,1},{1,0},{4,6},{6,7},{7,5},{5,4},{8,10},{10,11},{11... | collective-permute-start | bytes 1081352 | tf_op jit(solution)/shard_map/ppermute | solution.py:26
  5.7 11.6 %collective-permute-start = (bf16[128,1408]{1,0:T(8,128)(2,1)S(1)}, bf16[128,1408]{1,0:T(8,128)(2,1)S(1)}, u32[]{:S(2)}, u32[]{:S(2)}) collective-permute-start(bf16[128,1408]{1,0:T(8,128)(2,1)S(1)} %shard_map.41.packed_ref.refs_0_), channel_id=1, source_target_pairs={{0,8},{4,12},{8,0},{12,4},{1,9},{5,13},{9,1},{13,5},{2,10},{6,14},... | collective-permute-start | bytes 1081352 | tf_op jit(solution)/shard_map/ppermute | solution.py:19
  7.4 6.3 %collective-permute-start.2 = (f32[1,1536]{1,0:T(1,128)S(1)}, f32[1,1536]{1,0:T(1,128)S(1)}, u32[]{:S(2)}, u32[]{:S(2)}) collective-permute-start(f32[1,1536]{1,0:T(1,128)S(1)} %shard_map.42), channel_id=1, source_target_pairs={{0,1},{1,0},{2,3},{3,2},{4,5},{5,4},{6,7},{7,6},{8,9},{9,8},{10,11... | collective-permute-start | bytes 18440 | tf_op jit(solution)/shard_map/ppermute | solution.py:19
  7.4 8.2 %collective-permute-start.3 = (f32[1,1536]{1,0:T(1,128)S(1)}, f32[1,1536]{1,0:T(1,128)S(1)}, u32[]{:S(2)}, u32[]{:S(2)}) collective-permute-start(f32[1,1536]{1,0:T(1,128)S(1)} %shard_map.42), channel_id=1, source_target_pairs={{0,2},{1,3},{2,0},{3,1},{4,6},{5,7},{6,4},{7,5},{8,10},{9,11},{10,... | collective-permute-start | bytes 18440 | tf_op jit(solution)/shard_map/ppermute | solution.py:19
  9.3 6.3 %collective-permute-start.4 = (f32[1,1536]{1,0:T(1,128)S(1)}, f32[1,1536]{1,0:T(1,128)S(1)}, u32[]{:S(2)}, u32[]{:S(2)}) collective-permute-start(f32[1,1536]{1,0:T(1,128)S(1)} %shard_map.42), channel_id=1, source_target_pairs={{0,3},{1,2},{2,1},{3,0},{4,7},{5,6},{6,5},{7,4},{8,11},{9,10},{10,... | collective-permute-start | bytes 18440 | tf_op jit(solution)/shard_map/ppermute | solution.py:19
  15.7 9.4 %collective-permute-start.9 = (bf16[128,1408]{1,0:T(8,128)(2,1)S(1)}, bf16[128,1408]{1,0:T(8,128)(2,1)S(1)}, u32[]{:S(2)}, u32[]{:S(2)}) collective-permute-start(bf16[128,1408]{1,0:T(8,128)(2,1)S(1)} %collective-permute-done.1.refs_4_), channel_id=1, source_target_pairs={{0,2},{2,3},{3,1},{1,0},{4,6},{6,7},{7,5},{5,4},{8,10},{10,11},{11... | collective-permute-start | bytes 1081352 | tf_op jit(solution)/shard_map/ppermute | solution.py:26
  17.3 5.5 %collective-permute-start.5 = (bf16[128,1408]{1,0:T(8,128)(2,1)S(1)}, bf16[128,1408]{1,0:T(8,128)(2,1)S(1)}, u32[]{:S(2)}, u32[]{:S(2)}) collective-permute-start(bf16[128,1408]{1,0:T(8,128)(2,1)S(1)} %shard_map.41.packed_ref.refs_0_), channel_id=1, source_target_pairs={{0,4},{4,0},{8,12},{12,8},{1,5},{5,1},{9,13},{13,9},{2,6},{6,2},{1... | collective-permute-start | bytes 1081352 | tf_op jit(solution)/shard_map/ppermute | solution.py:19
  17.3 5.5 %collective-permute-start.6 = (bf16[128,1408]{1,0:T(8,128)(2,1)S(1)}, bf16[128,1408]{1,0:T(8,128)(2,1)S(1)}, u32[]{:S(2)}, u32[]{:S(2)}) collective-permute-start(bf16[128,1408]{1,0:T(8,128)(2,1)S(1)} %collective-permute-done.refs_1_), channel_id=1, source_target_pairs={{0,4},{4,0},{8,12},{12,8},{1,5},{5,1},{9,13},{13,9},{2,6},{6,2},{1... | collective-permute-start | bytes 1081352 | tf_op jit(solution)/shard_map/ppermute | solution.py:19
  17.8 3.7 %collective-permute-start.7 = (f32[1,1536]{1,0:T(1,128)S(1)}, f32[1,1536]{1,0:T(1,128)S(1)}, u32[]{:S(2)}, u32[]{:S(2)}) collective-permute-start(f32[1,1536]{1,0:T(1,128)S(1)} %add_add_fusion), channel_id=1, source_target_pairs={{0,8},{4,12},{8,0},{12,4},{1,9},{5,13},{9,1},{13,5},{2,10},{6,14},... | collective-permute-start | bytes 18440 | tf_op jit(solution)/shard_map/ppermute | solution.py:19
  21.5 1.2 %collective-permute-start.8 = (f32[1,1536]{1,0:T(1,128)S(1)}, f32[1,1536]{1,0:T(1,128)S(1)}, u32[]{:S(2)}, u32[]{:S(2)}) collective-permute-start(f32[1,1536]{1,0:T(1,128)S(1)} %add.15.refs_5_), channel_id=1, source_target_pairs={{0,4},{4,0},{8,12},{12,8},{1,5},{5,1},{9,13},{13,9},{2,6},{6,2},{1... | collective-permute-start | bytes 18440 | tf_op jit(solution)/shard_map/ppermute | solution.py:19
  26.3 12.1 %collective-permute-start.10 = (f32[256,384]{1,0:T(8,128)S(1)}, f32[256,384]{1,0:T(8,128)S(1)}, u32[]{:S(2)}, u32[]{:S(2)}) collective-permute-start(f32[256,384]{1,0:T(8,128)S(1)} %get-tuple-element.38), channel_id=1, source_target_pairs={{0,4},{4,0},{8,12},{12,8},{1,5},{5,1},{9,13},{13,9},{2,6},{6,2},{1... | collective-permute-start | bytes 1179656 | tf_op jit(solution)/shard_map/ppermute | solution.py:19
  38.4 7.0 %collective-permute-start.11 = (f32[128,384]{1,0:T(8,128)S(1)}, f32[128,384]{1,0:T(8,128)S(1)}, u32[]{:S(2)}, u32[]{:S(2)}) collective-permute-start(f32[128,384]{1,0:T(8,128)S(1)} %get-tuple-element.46), channel_id=1, source_target_pairs={{0,8},{4,12},{8,0},{12,4},{1,9},{5,13},{9,1},{13,5},{2,10},{6,14},... | collective-permute-start | bytes 589832 | tf_op jit(solution)/shard_map/ppermute | solution.py:19
  39.1 7.5 %collective-permute-start.12 = (f32[128,384]{1,0:T(8,128)S(1)}, f32[128,384]{1,0:T(8,128)S(1)}, u32[]{:S(2)}, u32[]{:S(2)}) collective-permute-start(f32[128,384]{1,0:T(8,128)S(1)} %get-tuple-element.47), channel_id=1, source_target_pairs={{0,1},{2,0},{3,2},{1,3},{4,5},{6,4},{7,6},{5,7},{8,9},{10,8},{11,1... | collective-permute-start | bytes 589832 | tf_op jit(solution)/shard_map/ppermute | solution.py:26

commit v9 on v7

--- a/solution.py
+++ b/solution.py
@@ -192,9 +192,8 @@
         back = jnp.dot(weights, with_ones(v[1]), preferred_element_type=jnp.float32)
         to_ref = (keep_ref, give_ref)[h]
         to_ref[at, :] = direct_of(cs, acc_ref[h, at, :] + back)
-    for i in range(sums_ref.shape[0]):
-        sums_ref[i, 0:1, :] = loss
-        sums_ref[i, 1:2, :] = spread
+    sums_ref[0:1, :] = loss
+    sums_ref[1:2, :] = spread
 
 
 def halve_kernel(rows, keep_ref, got_ref, *out_refs):
@@ -202,13 +201,16 @@
     out_refs[1][...] = keep_ref[rows : 2 * rows, :] + got_ref[rows : 2 * rows, :]
 
 
-def final_kernel(t_width, total_rows, packed_ref, stats_ref, sums_ref, *refs):
-    *parts, grad_ref, loss_ref = refs
-    direct = parts[0][...]
-    for part in parts[1:]:
+def final_kernel(n_parts, t_width, total_rows, packed_ref, stats_ref, *refs):
+    *inputs, grad_ref, loss_ref = refs
+    direct = inputs[0][...]
+    for part in inputs[1:n_parts]:
         direct = direct + part[...]
+    both = inputs[n_parts][...]
+    for sums in inputs[n_parts + 1 :]:
+        both = both + sums[...]
     s_width = direct.shape[1]
-    both = jnp.sum(jnp.sum(sums_ref[...], axis=0), axis=1, keepdims=True)
+    both = jnp.sum(both, axis=1, keepdims=True)
     loss_total, spread_total = both[0:1, :], -both[1:2, :]
     _, spread_s, centre = spreads_of(stats_ref[...], t_width, s_width, total_rows)
     pairs = total_rows * (total_rows - 1.0)
@@ -240,10 +242,6 @@
 def halvings(axis):
     size = lax.axis_size(axis)
     return [size >> i for i in range(1, size.bit_length())]
-
-
-def to_all(value):
-    return lax.all_to_all(value, ("blk", "sub"), 0, 0, tiled=True)
 
 
 def per_device(teacher, student):
@@ -304,11 +302,16 @@
     returned = [shifted(x, "sub", -k) for k, x in enumerate(backs, 1)]
     keep, give, sums = call(
         functools.partial(late_kernel, t_width, total_rows),
-        [f32((side, s_width))] * 2 + [f32((n_blk * n_sub, 2, LANES))],
+        [f32((side, s_width))] * 2 + [f32((2, LANES))],
         [plane, line[half], totals, acc, norms, early_sums],
         pair_flops,
     )
     got = exchange(give, "blk", 1)
+    for distance in halvings("blk")[:-1]:
+        sums = sums + exchange(sums, "blk", distance)
+    got, sums = lax.optimization_barrier((got, sums))
+    sums = sums + exchange(sums, "blk", 1)
+    all_sums = gathered(sums, "sub")
     tiles, distance = n_blk // 2, 2
     while tiles > 1:
         tiles //= 2
@@ -318,12 +321,11 @@
         )
         got = exchange(give, "blk", distance)
         distance *= 2
-    all_sums = to_all(sums)
     parts = [own, keep, got] + returned
     grad, loss = call(
-        functools.partial(final_kernel, t_width, total_rows),
+        functools.partial(final_kernel, len(parts), t_width, total_rows),
         [f32((rows, s_width)), f32((1, LANES))],
-        [packed, totals, all_sums] + parts,
+        [packed, totals] + parts + all_sums,
         8 * student.size,
     )
     return grad, loss[0, :1]

time: 41.7 us -> 42.5 us (1.019)
  blocking collectives: 10.3 us -> 0 us
  starting transfers between devices: 17.8 us -> 23.9 us
  waiting for transfers between devices: 7.15 us -> 12.2 us
    all_to_all x1 -> x0, blocking collectives: 10.3 us -> none  [to_all(): return lax.all_to_all(value, ('blk', 'sub'), 0, 0, tiled=True)]
    ppermute x10 -> x15, starting transfers between devices: 9.88 us -> 15.9 us  [exchange(): return lax.ppermute(value, axis, [(i, i ^ distance) for i in range(size)])]
    ppermute x10 -> x15, waiting for transfers between devices: 7.14 us -> 12.2 us  [exchange(): return lax.ppermute(value, axis, [(i, i ^ distance) for i in range(size)])]
  transfers between devices with their start and end apart: 13 -> 18, of which waited for: 4 -> 7; matrix products, arithmetic and copies ran while one was open for 0% -> 0% of each run, Pallas kernels for 6% -> 6%
where the time goes in v9:
time: 42.5 us; the launch traced here: 42.4 us
  starting transfers between devices  23.9 us (56%)
  waiting for transfers between devices  12.2 us (29%)
  Pallas kernels  5.57 us (13%)
  between operations  0.7 us (2%)
    ppermute x15, starting transfers between devices, exchange(): return lax.ppermute(value, axis, [(i, i ^ distance) for i in range(size)])  15.9 us
    ppermute x15, waiting for transfers between devices, exchange(): return lax.ppermute(value, axis, [(i, i ^ distance) for i in range(size)])  12.2 us
    ppermute x3, starting transfers between devices, shifted(): return lax.ppermute(value, axis, route)  7.97 us
    pallas_call x6, Pallas kernels, call(): pl.pallas_call(kernel, out_shape=out_shape, in_specs=in_specs, out_specs=...  5.57 us
  transfers between devices with their start and end apart: 18, of which 7 were waited for; matrix products, arithmetic and copies ran while one was open for 0% of the time, Pallas kernels for 6%

profile of v9, /device:TPU:0, one launch (start us, length us, event | category | flops | bytes accessed | tf_op | source)
XLA Modules:
  0.0 42.4 jit_solution(6564364365605169959)
XLA Ops:
  0.6 1.0 %shard_map.41.packed_ref.refs_0_ = bf16[128,1408]{1,0:T(8,128)(2,1)S(1)} custom-call(bf16[128,1024]{1,0:T(8,128)(2,1)} %t_hbm.1, bf16[128,384]{1,0:T(8,128)(2,1)} %s_hbm.1), custom_call_target="tpu_custom_call" | custom-call | bytes 360448 | tf_op jit(solution)/shard_map/pallas_call | solution.py:227
  1.6 4.1 %collective-permute-start.1 = (bf16[128,1408]{1,0:T(8,128)(2,1)S(1)}, bf16[128,1408]{1,0:T(8,128)(2,1)S(1)}, u32[]{:S(2)}, u32[]{:S(2)}) collective-permute-start(bf16[128,1408]{1,0:T(8,128)(2,1)S(1)} %shard_map.41.packed_ref.refs_0_), channel_id=1, source_target_pairs={{0,2},{2,3},{3,1},{1,0},{4,6},{6,7},{7,5},{5,4},{8,10},{10,11},{11... | collective-permute-start | bytes 1081352 | tf_op jit(solution)/shard_map/ppermute | solution.py:26
  5.7 1.5 %collective-permute-start = (bf16[128,1408]{1,0:T(8,128)(2,1)S(1)}, bf16[128,1408]{1,0:T(8,128)(2,1)S(1)}, u32[]{:S(2)}, u32[]{:S(2)}) collective-permute-start(bf16[128,1408]{1,0:T(8,128)(2,1)S(1)} %shard_map.41.packed_ref.refs_0_), channel_id=1, source_target_pairs={{0,8},{4,12},{8,0},{12,4},{1,9},{5,13},{9,1},{13,5},{2,10},{6,14},... | collective-permute-start | bytes 1081352 | tf_op jit(solution)/shard_map/ppermute | solution.py:19
  7.2 0.2 shard_map.42
  7.4 0.0 collective-permute-start.2
  7.4 1.9 %collective-permute-start.3 = (f32[1,1536]{1,0:T(1,128)S(1)}, f32[1,1536]{1,0:T(1,128)S(1)}, u32[]{:S(2)}, u32[]{:S(2)}) collective-permute-start(f32[1,1536]{1,0:T(1,128)S(1)} %shard_map.42), channel_id=1, source_target_pairs={{0,2},{1,3},{2,0},{3,1},{4,6},{5,7},{6,4},{7,5},{8,10},{9,11},{10,... | collective-permute-start | bytes 18440 | tf_op jit(solution)/shard_map/ppermute | solution.py:19
  9.3 2.5 %collective-permute-start.4 = (f32[1,1536]{1,0:T(1,128)S(1)}, f32[1,1536]{1,0:T(1,128)S(1)}, u32[]{:S(2)}, u32[]{:S(2)}) collective-permute-start(f32[1,1536]{1,0:T(1,128)S(1)} %shard_map.42), channel_id=1, source_target_pairs={{0,3},{1,2},{2,1},{3,0},{4,7},{5,6},{6,5},{7,4},{8,11},{9,10},{10,... | collective-permute-start | bytes 18440 | tf_op jit(solution)/shard_map/ppermute | solution.py:19
  11.8 1.9 %collective-permute-done.2 = f32[1,1536]{1,0:T(1,128)S(1)} collective-permute-done((f32[1,1536]{1,0:T(1,128)S(1)}, f32[1,1536]{1,0:T(1,128)S(1)}, u32[]{:S(2)}, u32[]{:S(2)}) %collective-permute-start.2) | collective-permute-done | bytes 6176 | tf_op jit(solution)/shard_map/ppermute | solution.py:19
  13.7 2.0 %collective-permute-done.3 = f32[1,1536]{1,0:T(1,128)S(1)} collective-permute-done((f32[1,1536]{1,0:T(1,128)S(1)}, f32[1,1536]{1,0:T(1,128)S(1)}, u32[]{:S(2)}, u32[]{:S(2)}) %collective-permute-start.3) | collective-permute-done | bytes 6176 | tf_op jit(solution)/shard_map/ppermute | solution.py:19
  15.7 0.0 collective-permute-done.4
  15.7 0.0 collective-permute-done.1.refs_4_
  15.7 1.6 %collective-permute-start.9 = (bf16[128,1408]{1,0:T(8,128)(2,1)S(1)}, bf16[128,1408]{1,0:T(8,128)(2,1)S(1)}, u32[]{:S(2)}, u32[]{:S(2)}) collective-permute-start(bf16[128,1408]{1,0:T(8,128)(2,1)S(1)} %collective-permute-done.1.refs_4_), channel_id=1, source_target_pairs={{0,2},{2,3},{3,1},{1,0},{4,6},{6,7},{7,5},{5,4},{8,10},{10,11},{11... | collective-permute-start | bytes 1081352 | tf_op jit(solution)/shard_map/ppermute | solution.py:26
  17.3 0.0 collective-permute-done.refs_1_
  17.3 0.0 collective-permute-start.5
  17.3 0.5 %collective-permute-start.6 = (bf16[128,1408]{1,0:T(8,128)(2,1)S(1)}, bf16[128,1408]{1,0:T(8,128)(2,1)S(1)}, u32[]{:S(2)}, u32[]{:S(2)}) collective-permute-start(bf16[128,1408]{1,0:T(8,128)(2,1)S(1)} %collective-permute-done.refs_1_), channel_id=1, source_target_pairs={{0,4},{4,0},{8,12},{12,8},{1,5},{5,1},{9,13},{13,9},{2,6},{6,2},{1... | collective-permute-start | bytes 1081352 | tf_op jit(solution)/shard_map/ppermute | solution.py:19
  17.8 1.6 %collective-permute-start.7 = (f32[1,1536]{1,0:T(1,128)S(1)}, f32[1,1536]{1,0:T(1,128)S(1)}, u32[]{:S(2)}, u32[]{:S(2)}) collective-permute-start(f32[1,1536]{1,0:T(1,128)S(1)} %add_add_fusion), channel_id=1, source_target_pairs={{0,8},{4,12},{8,0},{12,4},{1,9},{5,13},{9,1},{13,5},{2,10},{6,14},... | collective-permute-start | bytes 18440 | tf_op jit(solution)/shard_map/ppermute | solution.py:19
  19.4 2.1 %collective-permute-done.7 = f32[1,1536]{1,0:T(1,128)S(1)} collective-permute-done((f32[1,1536]{1,0:T(1,128)S(1)}, f32[1,1536]{1,0:T(1,128)S(1)}, u32[]{:S(2)}, u32[]{:S(2)}) %collective-permute-start.7) | collective-permute-done | bytes 6176 | tf_op jit(solution)/shard_map/ppermute | solution.py:19
  21.5 0.1 collective-permute-start.8
  21.6 1.2 %collective-permute-done.8.refs_6_ = f32[1,1536]{1,0:T(1,128)S(1)} collective-permute-done((f32[1,1536]{1,0:T(1,128)S(1)}, f32[1,1536]{1,0:T(1,128)S(1)}, u32[]{:S(2)}, u32[]{:S(2)}) %collective-permute-start.8) | collective-permute-done | bytes 6176 | tf_op jit(solution)/shard_map/ppermute | solution.py:19
  22.8 2.3 %shard_map.43 = (f32[128,384]{1,0:T(8,128)S(1)}, f32[128,384]{1,0:T(8,128)S(1)}, f32[2,256,512]{2,1,0:T(8,128)S(1)}, f32[2,2,256,128]{3,2,1,0:T(8,128)S(1)}, f32...) custom-call(bf16[128,1408]{1,0:T(8,128)(2,1)S(1)} %shard_map.41.packed_ref.refs_0_, ...), custom_call_target="tpu_custom_call" | custom-call | flops 570425344 | bytes 1814528 | tf_op jit(solution)/shard_map/pallas_call | solution.py:227
  25.1 1.2 %shard_map.44 = (f32[256,384]{1,0:T(8,128)S(1)}, f32[256,384]{1,0:T(8,128)S(1)}, f32[2,128]{1,0:T(2,128)S(1)}) custom-call(bf16[2,256,1408]{2,1,0:T(8,128)(2,1)S(1)} %get-tuple-element.34.refs_0_, bf16[128,1408]{1,0:T(8,128)(2,1)S(1)} %collective-permute-done.9.refs_1_, f32[1,1536]{1,0:T(1,128)S(1)} %get-tuple-element.32.refs_2_.stats_ref, ...), custom_call_target="tpu_custom_call" | custom-call | flops 285212672 | bytes 3382272 | tf_op jit(solution)/shard_map/pallas_call | solution.py:227
  26.3 0.2 collective-permute-start.10
  26.5 1.5 %collective-permute-start.11 = (f32[2,128]{1,0:T(2,128)S(1)}, f32[2,128]{1,0:T(2,128)S(1)}, u32[]{:S(2)}, u32[]{:S(2)}) collective-permute-start(f32[2,128]{1,0:T(2,128)S(1)} %get-tuple-element.40), channel_id=1, source_target_pairs={{0,8},{4,12},{8,0},{12,4},{1,9},{5,13},{9,1},{13,5},{2,10},{6,14},... | collective-permute-start | bytes 3080 | tf_op jit(solution)/shard_map/ppermute | solution.py:19
  28.1 2.2 %collective-permute-start.13 = (f32[128,384]{1,0:T(8,128)S(1)}, f32[128,384]{1,0:T(8,128)S(1)}, u32[]{:S(2)}, u32[]{:S(2)}) collective-permute-start(f32[128,384]{1,0:T(8,128)S(1)} %get-tuple-element.44), channel_id=1, source_target_pairs={{0,1},{2,0},{3,2},{1,3},{4,5},{6,4},{7,6},{5,7},{8,9},{10,8},{11,1... | collective-permute-start | bytes 589832 | tf_op jit(solution)/shard_map/ppermute | solution.py:26
  30.4 1.4 %collective-permute-start.12 = (f32[128,384]{1,0:T(8,128)S(1)}, f32[128,384]{1,0:T(8,128)S(1)}, u32[]{:S(2)}, u32[]{:S(2)}) collective-permute-start(f32[128,384]{1,0:T(8,128)S(1)} %get-tuple-element.43), channel_id=1, source_target_pairs={{0,8},{4,12},{8,0},{12,4},{1,9},{5,13},{9,1},{13,5},{2,10},{6,14},... | collective-permute-start | bytes 589832 | tf_op jit(solution)/shard_map/ppermute | solution.py:19
  31.8 1.1 %collective-permute-done.14 = f32[2,128]{1,0:T(2,128)S(1)} collective-permute-done((f32[2,128]{1,0:T(2,128)S(1)}, f32[2,128]{1,0:T(2,128)S(1)}, u32[]{:S(2)}, u32[]{:S(2)}) %collective-permute-start.14) | collective-permute-done | bytes 1056 | tf_op jit(solution)/shard_map/ppermute | solution.py:19
  32.9 2.2 %collective-permute-start.15 = (f32[2,128]{1,0:T(2,128)S(1)}, f32[2,128]{1,0:T(2,128)S(1)}, u32[]{:S(2)}, u32[]{:S(2)}) collective-permute-start(f32[2,128]{1,0:T(2,128)S(1)} %add.23.refs_4_), channel_id=1, source_target_pairs={{0,1},{1,0},{2,3},{3,2},{4,5},{5,4},{6,7},{7,6},{8,9},{9,8},{10,11... | collective-permute-start | bytes 3080 | tf_op jit(solution)/shard_map/ppermute | solution.py:19
  35.1 1.0 %collective-permute-start.16 = (f32[2,128]{1,0:T(2,128)S(1)}, f32[2,128]{1,0:T(2,128)S(1)}, u32[]{:S(2)}, u32[]{:S(2)}) collective-permute-start(f32[2,128]{1,0:T(2,128)S(1)} %add.23.refs_4_), channel_id=1, source_target_pairs={{0,2},{1,3},{2,0},{3,1},{4,6},{5,7},{6,4},{7,5},{8,10},{9,11},{10,... | collective-permute-start | bytes 3080 | tf_op jit(solution)/shard_map/ppermute | solution.py:19
  36.1 1.5 %collective-permute-start.17 = (f32[2,128]{1,0:T(2,128)S(1)}, f32[2,128]{1,0:T(2,128)S(1)}, u32[]{:S(2)}, u32[]{:S(2)}) collective-permute-start(f32[2,128]{1,0:T(2,128)S(1)} %add.23.refs_4_), channel_id=1, source_target_pairs={{0,3},{1,2},{2,1},{3,0},{4,7},{5,6},{6,5},{7,4},{8,11},{9,10},{10,... | collective-permute-start | bytes 3080 | tf_op jit(solution)/shard_map/ppermute | solution.py:19
  37.6 2.0 %collective-permute-done.16.refs_6_ = f32[2,128]{1,0:T(2,128)S(1)} collective-permute-done((f32[2,128]{1,0:T(2,128)S(1)}, f32[2,128]{1,0:T(2,128)S(1)}, u32[]{:S(2)}, u32[]{:S(2)}) %collective-permute-start.16) | collective-permute-done | bytes 1056 | tf_op jit(solution)/shard_map/ppermute | solution.py:19
  39.6 1.9 %collective-permute-done.17.refs_7_ = f32[2,128]{1,0:T(2,128)S(1)} collective-permute-done((f32[2,128]{1,0:T(2,128)S(1)}, f32[2,128]{1,0:T(2,128)S(1)}, u32[]{:S(2)}, u32[]{:S(2)}) %collective-permute-start.17) | collective-permute-done | bytes 1056 | tf_op jit(solution)/shard_map/ppermute | solution.py:19
  41.5 0.9 %shard_map.46 = (f32[128,384]{1,0:T(8,128)}, f32[1,128]{1,0:T(1,128)}) custom-call(bf16[128,1408]{1,0:T(8,128)(2,1)S(1)} %shard_map.41.packed_ref.refs_0_, f32[1,1536]{1,0:T(1,128)S(1)} %get-tuple-element.32.refs_2_.stats_ref, f32[128,384]{1,0:T(8,128)S(1)} %get-tuple-element.33.refs_0_, f32[128,384]{1,0:T(8,128)S(1)} %get-tuple-element.42.refs_1_, ...), custom_call_target="tpu_custom_call" | custom-call | flops 393216 | bytes 1157120 | tf_op jit(solution)/shard_map/pallas_call | solution.py:227
  (14 shorter events, 0.1 us)
Async XLA Ops:
  1.6 14.0 %collective-permute-start.1 = (bf16[128,1408]{1,0:T(8,128)(2,1)S(1)}, bf16[128,1408]{1,0:T(8,128)(2,1)S(1)}, u32[]{:S(2)}, u32[]{:S(2)}) collective-permute-start(bf16[128,1408]{1,0:T(8,128)(2,1)S(1)} %shard_map.41.packed_ref.refs_0_), channel_id=1, source_target_pairs={{0,2},{2,3},{3,1},{1,0},{4,6},{6,7},{7,5},{5,4},{8,10},{10,11},{11... | collective-permute-start | bytes 1081352 | tf_op jit(solution)/shard_map/ppermute | solution.py:26
  5.7 11.6 %collective-permute-start = (bf16[128,1408]{1,0:T(8,128)(2,1)S(1)}, bf16[128,1408]{1,0:T(8,128)(2,1)S(1)}, u32[]{:S(2)}, u32[]{:S(2)}) collective-permute-start(bf16[128,1408]{1,0:T(8,128)(2,1)S(1)} %shard_map.41.packed_ref.refs_0_), channel_id=1, source_target_pairs={{0,8},{4,12},{8,0},{12,4},{1,9},{5,13},{9,1},{13,5},{2,10},{6,14},... | collective-permute-start | bytes 1081352 | tf_op jit(solution)/shard_map/ppermute | solution.py:19
  7.4 6.3 %collective-permute-start.2 = (f32[1,1536]{1,0:T(1,128)S(1)}, f32[1,1536]{1,0:T(1,128)S(1)}, u32[]{:S(2)}, u32[]{:S(2)}) collective-permute-start(f32[1,1536]{1,0:T(1,128)S(1)} %shard_map.42), channel_id=1, source_target_pairs={{0,1},{1,0},{2,3},{3,2},{4,5},{5,4},{6,7},{7,6},{8,9},{9,8},{10,11... | collective-permute-start | bytes 18440 | tf_op jit(solution)/shard_map/ppermute | solution.py:19
  7.4 8.2 %collective-permute-start.3 = (f32[1,1536]{1,0:T(1,128)S(1)}, f32[1,1536]{1,0:T(1,128)S(1)}, u32[]{:S(2)}, u32[]{:S(2)}) collective-permute-start(f32[1,1536]{1,0:T(1,128)S(1)} %shard_map.42), channel_id=1, source_target_pairs={{0,2},{1,3},{2,0},{3,1},{4,6},{5,7},{6,4},{7,5},{8,10},{9,11},{10,... | collective-permute-start | bytes 18440 | tf_op jit(solution)/shard_map/ppermute | solution.py:19
  9.3 6.3 %collective-permute-start.4 = (f32[1,1536]{1,0:T(1,128)S(1)}, f32[1,1536]{1,0:T(1,128)S(1)}, u32[]{:S(2)}, u32[]{:S(2)}) collective-permute-start(f32[1,1536]{1,0:T(1,128)S(1)} %shard_map.42), channel_id=1, source_target_pairs={{0,3},{1,2},{2,1},{3,0},{4,7},{5,6},{6,5},{7,4},{8,11},{9,10},{10,... | collective-permute-start | bytes 18440 | tf_op jit(solution)/shard_map/ppermute | solution.py:19
  15.7 9.4 %collective-permute-start.9 = (bf16[128,1408]{1,0:T(8,128)(2,1)S(1)}, bf16[128,1408]{1,0:T(8,128)(2,1)S(1)}, u32[]{:S(2)}, u32[]{:S(2)}) collective-permute-start(bf16[128,1408]{1,0:T(8,128)(2,1)S(1)} %collective-permute-done.1.refs_4_), channel_id=1, source_target_pairs={{0,2},{2,3},{3,1},{1,0},{4,6},{6,7},{7,5},{5,4},{8,10},{10,11},{11... | collective-permute-start | bytes 1081352 | tf_op jit(solution)/shard_map/ppermute | solution.py:26
  17.3 5.5 %collective-permute-start.5 = (bf16[128,1408]{1,0:T(8,128)(2,1)S(1)}, bf16[128,1408]{1,0:T(8,128)(2,1)S(1)}, u32[]{:S(2)}, u32[]{:S(2)}) collective-permute-start(bf16[128,1408]{1,0:T(8,128)(2,1)S(1)} %shard_map.41.packed_ref.refs_0_), channel_id=1, source_target_pairs={{0,4},{4,0},{8,12},{12,8},{1,5},{5,1},{9,13},{13,9},{2,6},{6,2},{1... | collective-permute-start | bytes 1081352 | tf_op jit(solution)/shard_map/ppermute | solution.py:19
  17.3 5.5 %collective-permute-start.6 = (bf16[128,1408]{1,0:T(8,128)(2,1)S(1)}, bf16[128,1408]{1,0:T(8,128)(2,1)S(1)}, u32[]{:S(2)}, u32[]{:S(2)}) collective-permute-start(bf16[128,1408]{1,0:T(8,128)(2,1)S(1)} %collective-permute-done.refs_1_), channel_id=1, source_target_pairs={{0,4},{4,0},{8,12},{12,8},{1,5},{5,1},{9,13},{13,9},{2,6},{6,2},{1... | collective-permute-start | bytes 1081352 | tf_op jit(solution)/shard_map/ppermute | solution.py:19
  17.8 3.7 %collective-permute-start.7 = (f32[1,1536]{1,0:T(1,128)S(1)}, f32[1,1536]{1,0:T(1,128)S(1)}, u32[]{:S(2)}, u32[]{:S(2)}) collective-permute-start(f32[1,1536]{1,0:T(1,128)S(1)} %add_add_fusion), channel_id=1, source_target_pairs={{0,8},{4,12},{8,0},{12,4},{1,9},{5,13},{9,1},{13,5},{2,10},{6,14},... | collective-permute-start | bytes 18440 | tf_op jit(solution)/shard_map/ppermute | solution.py:19
  21.5 1.2 %collective-permute-start.8 = (f32[1,1536]{1,0:T(1,128)S(1)}, f32[1,1536]{1,0:T(1,128)S(1)}, u32[]{:S(2)}, u32[]{:S(2)}) collective-permute-start(f32[1,1536]{1,0:T(1,128)S(1)} %add.21.refs_5_), channel_id=1, source_target_pairs={{0,4},{4,0},{8,12},{12,8},{1,5},{5,1},{9,13},{13,9},{2,6},{6,2},{1... | collective-permute-start | bytes 18440 | tf_op jit(solution)/shard_map/ppermute | solution.py:19
  26.3 4.0 %collective-permute-start.10 = (f32[256,384]{1,0:T(8,128)S(1)}, f32[256,384]{1,0:T(8,128)S(1)}, u32[]{:S(2)}, u32[]{:S(2)}) collective-permute-start(f32[256,384]{1,0:T(8,128)S(1)} %get-tuple-element.39), channel_id=1, source_target_pairs={{0,4},{4,0},{8,12},{12,8},{1,5},{5,1},{9,13},{13,9},{2,6},{6,2},{1... | collective-permute-start | bytes 1179656 | tf_op jit(solution)/shard_map/ppermute | solution.py:19
  26.5 3.8 %collective-permute-start.11 = (f32[2,128]{1,0:T(2,128)S(1)}, f32[2,128]{1,0:T(2,128)S(1)}, u32[]{:S(2)}, u32[]{:S(2)}) collective-permute-start(f32[2,128]{1,0:T(2,128)S(1)} %get-tuple-element.40), channel_id=1, source_target_pairs={{0,8},{4,12},{8,0},{12,4},{1,9},{5,13},{9,1},{13,5},{2,10},{6,14},... | collective-permute-start | bytes 3080 | tf_op jit(solution)/shard_map/ppermute | solution.py:19
  28.1 9.5 %collective-permute-start.13 = (f32[128,384]{1,0:T(8,128)S(1)}, f32[128,384]{1,0:T(8,128)S(1)}, u32[]{:S(2)}, u32[]{:S(2)}) collective-permute-start(f32[128,384]{1,0:T(8,128)S(1)} %get-tuple-element.44), channel_id=1, source_target_pairs={{0,1},{2,0},{3,2},{1,3},{4,5},{6,4},{7,6},{5,7},{8,9},{10,8},{11,1... | collective-permute-start | bytes 589832 | tf_op jit(solution)/shard_map/ppermute | solution.py:26
  30.4 11.1 %collective-permute-start.12 = (f32[128,384]{1,0:T(8,128)S(1)}, f32[128,384]{1,0:T(8,128)S(1)}, u32[]{:S(2)}, u32[]{:S(2)}) collective-permute-start(f32[128,384]{1,0:T(8,128)S(1)} %get-tuple-element.43), channel_id=1, source_target_pairs={{0,8},{4,12},{8,0},{12,4},{1,9},{5,13},{9,1},{13,5},{2,10},{6,14},... | collective-permute-start | bytes 589832 | tf_op jit(solution)/shard_map/ppermute | solution.py:19
  31.7 1.1 %collective-permute-start.14 = (f32[2,128]{1,0:T(2,128)S(1)}, f32[2,128]{1,0:T(2,128)S(1)}, u32[]{:S(2)}, u32[]{:S(2)}) collective-permute-start(f32[2,128]{1,0:T(2,128)S(1)} %add.22), channel_id=1, source_target_pairs={{0,4},{4,0},{8,12},{12,8},{1,5},{5,1},{9,13},{13,9},{2,6},{6,2},{1... | collective-permute-start | bytes 3080 | tf_op jit(solution)/shard_map/ppermute | solution.py:19
  32.9 4.7 %collective-permute-start.15 = (f32[2,128]{1,0:T(2,128)S(1)}, f32[2,128]{1,0:T(2,128)S(1)}, u32[]{:S(2)}, u32[]{:S(2)}) collective-permute-start(f32[2,128]{1,0:T(2,128)S(1)} %add.23.refs_4_), channel_id=1, source_target_pairs={{0,1},{1,0},{2,3},{3,2},{4,5},{5,4},{6,7},{7,6},{8,9},{9,8},{10,11... | collective-permute-start | bytes 3080 | tf_op jit(solution)/shard_map/ppermute | solution.py:19
  35.1 4.5 %collective-permute-start.16 = (f32[2,128]{1,0:T(2,128)S(1)}, f32[2,128]{1,0:T(2,128)S(1)}, u32[]{:S(2)}, u32[]{:S(2)}) collective-permute-start(f32[2,128]{1,0:T(2,128)S(1)} %add.23.refs_4_), channel_id=1, source_target_pairs={{0,2},{1,3},{2,0},{3,1},{4,6},{5,7},{6,4},{7,5},{8,10},{9,11},{10,... | collective-permute-start | bytes 3080 | tf_op jit(solution)/shard_map/ppermute | solution.py:19
  36.1 5.4 %collective-permute-start.17 = (f32[2,128]{1,0:T(2,128)S(1)}, f32[2,128]{1,0:T(2,128)S(1)}, u32[]{:S(2)}, u32[]{:S(2)}) collective-permute-start(f32[2,128]{1,0:T(2,128)S(1)} %add.23.refs_4_), channel_id=1, source_target_pairs={{0,3},{1,2},{2,1},{3,0},{4,7},{5,6},{6,5},{7,4},{8,11},{9,10},{10,... | collective-permute-start | bytes 3080 | tf_op jit(solution)/shard_map/ppermute | solution.py:19

commit v10 on v7

--- a/solution.py
+++ b/solution.py
@@ -242,8 +242,8 @@
     return [size >> i for i in range(1, size.bit_length())]
 
 
-def to_all(value):
-    return lax.all_to_all(value, ("blk", "sub"), 0, 0, tiled=True)
+def to_all(value, axis):
+    return lax.all_to_all(value, axis, 0, 0, tiled=True)
 
 
 def per_device(teacher, student):
@@ -304,11 +304,14 @@
     returned = [shifted(x, "sub", -k) for k, x in enumerate(backs, 1)]
     keep, give, sums = call(
         functools.partial(late_kernel, t_width, total_rows),
-        [f32((side, s_width))] * 2 + [f32((n_blk * n_sub, 2, LANES))],
+        [f32((side, s_width))] * 2 + [f32((n_blk, 2, LANES))],
         [plane, line[half], totals, acc, norms, early_sums],
         pair_flops,
     )
     got = exchange(give, "blk", 1)
+    sums = jnp.sum(to_all(sums, "blk"), axis=0)
+    got, sums = lax.optimization_barrier((got, sums))
+    all_sums = to_all(jnp.broadcast_to(sums[None], (n_sub, *sums.shape)), "sub")
     tiles, distance = n_blk // 2, 2
     while tiles > 1:
         tiles //= 2
@@ -318,7 +321,6 @@
         )
         got = exchange(give, "blk", distance)
         distance *= 2
-    all_sums = to_all(sums)
     parts = [own, keep, got] + returned
     grad, loss = call(
         functools.partial(final_kernel, t_width, total_rows),

time: 41.7 us -> 45.7 us (1.096)
  blocking collectives: 10.3 us -> 0 us
  waiting for transfers between devices: 7.15 us -> 14.2 us
  starting transfers between devices: 17.8 us -> 24.1 us
  local copies, waits for them, and re-layouts: 0 us -> 0.59 us
    all_to_all x1 -> x0, blocking collectives: 10.3 us -> none  [to_all(): return lax.all_to_all(value, ('blk', 'sub'), 0, 0, tiled=True)]
    all_to_all x0 -> x2, starting transfers between devices: none -> 7.29 us  [to_all(): return lax.all_to_all(value, axis, 0, 0, tiled=True)]
    all_to_all x0 -> x2, waiting for transfers between devices: none -> 7.05 us  [to_all(): return lax.all_to_all(value, axis, 0, 0, tiled=True)]
    ppermute x10, starting transfers between devices: 9.88 us -> 8.76 us  [exchange(): return lax.ppermute(value, axis, [(i, i ^ distance) for i in range(size)])]
    broadcast_in_dim x0 -> x1, local copies, waits for them, and re-layouts: none -> 0.59 us  [per_device(): all_sums = to_all(jnp.broadcast_to(sums[None], (n_sub, *sums.shape)), 'sub')]
  transfers between devices with their start and end apart: 13 -> 15, of which waited for: 4 -> 6; matrix products, arithmetic and copies ran while one was open for 0% -> 1% of each run, Pallas kernels for 6% -> 5%
where the time goes in v10:
time: 45.7 us; the launch traced here: 45.4 us
  starting transfers between devices  24.1 us (53%)
  waiting for transfers between devices  14.2 us (31%)
  Pallas kernels  5.86 us (13%)
  between operations  0.69 us (2%)
  local copies, waits for them, and re-layouts  0.59 us (1%)
    ppermute x10, starting transfers between devices, exchange(): return lax.ppermute(value, axis, [(i, i ^ distance) for i in range(size)])  8.76 us
    ppermute x3, starting transfers between devices, shifted(): return lax.ppermute(value, axis, route)  8 us
    all_to_all x2, starting transfers between devices, to_all(): return lax.all_to_all(value, axis, 0, 0, tiled=True)  7.29 us
    ppermute x10, waiting for transfers between devices, exchange(): return lax.ppermute(value, axis, [(i, i ^ distance) for i in range(size)])  7.14 us
    all_to_all x2, waiting for transfers between devices, to_all(): return lax.all_to_all(value, axis, 0, 0, tiled=True)  7.05 us
    pallas_call x6, Pallas kernels, call(): pl.pallas_call(kernel, out_shape=out_shape, in_specs=in_specs, out_specs=...  5.86 us
  transfers between devices with their start and end apart: 15, of which 6 were waited for; matrix products, arithmetic and copies ran while one was open for 1% of the time, Pallas kernels for 5%

profile of v10, /device:TPU:0, one launch (start us, length us, event | category | flops | bytes accessed | tf_op | source)
XLA Modules:
  0.0 45.4 jit_solution(6458674012163533307)
XLA Ops:
  0.6 1.0 %shard_map.41.packed_ref.refs_0_ = bf16[128,1408]{1,0:T(8,128)(2,1)S(1)} custom-call(bf16[128,1024]{1,0:T(8,128)(2,1)} %t_hbm.1, bf16[128,384]{1,0:T(8,128)(2,1)} %s_hbm.1), custom_call_target="tpu_custom_call" | custom-call | bytes 360448 | tf_op jit(solution)/shard_map/pallas_call | solution.py:225
  1.6 4.1 %collective-permute-start.1 = (bf16[128,1408]{1,0:T(8,128)(2,1)S(1)}, bf16[128,1408]{1,0:T(8,128)(2,1)S(1)}, u32[]{:S(2)}, u32[]{:S(2)}) collective-permute-start(bf16[128,1408]{1,0:T(8,128)(2,1)S(1)} %shard_map.41.packed_ref.refs_0_), channel_id=1, source_target_pairs={{0,2},{2,3},{3,1},{1,0},{4,6},{6,7},{7,5},{5,4},{8,10},{10,11},{11... | collective-permute-start | bytes 1081352 | tf_op jit(solution)/shard_map/ppermute | solution.py:26
  5.7 1.5 %collective-permute-start = (bf16[128,1408]{1,0:T(8,128)(2,1)S(1)}, bf16[128,1408]{1,0:T(8,128)(2,1)S(1)}, u32[]{:S(2)}, u32[]{:S(2)}) collective-permute-start(bf16[128,1408]{1,0:T(8,128)(2,1)S(1)} %shard_map.41.packed_ref.refs_0_), channel_id=1, source_target_pairs={{0,8},{4,12},{8,0},{12,4},{1,9},{5,13},{9,1},{13,5},{2,10},{6,14},... | collective-permute-start | bytes 1081352 | tf_op jit(solution)/shard_map/ppermute | solution.py:19
  7.2 0.2 shard_map.42
  7.4 0.0 collective-permute-start.2
  7.4 1.9 %collective-permute-start.3 = (f32[1,1536]{1,0:T(1,128)S(1)}, f32[1,1536]{1,0:T(1,128)S(1)}, u32[]{:S(2)}, u32[]{:S(2)}) collective-permute-start(f32[1,1536]{1,0:T(1,128)S(1)} %shard_map.42), channel_id=1, source_target_pairs={{0,2},{1,3},{2,0},{3,1},{4,6},{5,7},{6,4},{7,5},{8,10},{9,11},{10,... | collective-permute-start | bytes 18440 | tf_op jit(solution)/shard_map/ppermute | solution.py:19
  9.3 2.5 %collective-permute-start.4 = (f32[1,1536]{1,0:T(1,128)S(1)}, f32[1,1536]{1,0:T(1,128)S(1)}, u32[]{:S(2)}, u32[]{:S(2)}) collective-permute-start(f32[1,1536]{1,0:T(1,128)S(1)} %shard_map.42), channel_id=1, source_target_pairs={{0,3},{1,2},{2,1},{3,0},{4,7},{5,6},{6,5},{7,4},{8,11},{9,10},{10,... | collective-permute-start | bytes 18440 | tf_op jit(solution)/shard_map/ppermute | solution.py:19
  11.8 1.9 %collective-permute-done.2 = f32[1,1536]{1,0:T(1,128)S(1)} collective-permute-done((f32[1,1536]{1,0:T(1,128)S(1)}, f32[1,1536]{1,0:T(1,128)S(1)}, u32[]{:S(2)}, u32[]{:S(2)}) %collective-permute-start.2) | collective-permute-done | bytes 6176 | tf_op jit(solution)/shard_map/ppermute | solution.py:19
  13.7 2.0 %collective-permute-done.3 = f32[1,1536]{1,0:T(1,128)S(1)} collective-permute-done((f32[1,1536]{1,0:T(1,128)S(1)}, f32[1,1536]{1,0:T(1,128)S(1)}, u32[]{:S(2)}, u32[]{:S(2)}) %collective-permute-start.3) | collective-permute-done | bytes 6176 | tf_op jit(solution)/shard_map/ppermute | solution.py:19
  15.7 1.6 %collective-permute-start.9 = (bf16[128,1408]{1,0:T(8,128)(2,1)S(1)}, bf16[128,1408]{1,0:T(8,128)(2,1)S(1)}, u32[]{:S(2)}, u32[]{:S(2)}) collective-permute-start(bf16[128,1408]{1,0:T(8,128)(2,1)S(1)} %collective-permute-done.1.refs_4_), channel_id=1, source_target_pairs={{0,2},{2,3},{3,1},{1,0},{4,6},{6,7},{7,5},{5,4},{8,10},{10,11},{11... | collective-permute-start | bytes 1081352 | tf_op jit(solution)/shard_map/ppermute | solution.py:26
  17.3 0.0 collective-permute-done.refs_1_
  17.3 0.5 %collective-permute-start.6 = (bf16[128,1408]{1,0:T(8,128)(2,1)S(1)}, bf16[128,1408]{1,0:T(8,128)(2,1)S(1)}, u32[]{:S(2)}, u32[]{:S(2)}) collective-permute-start(bf16[128,1408]{1,0:T(8,128)(2,1)S(1)} %collective-permute-done.refs_1_), channel_id=1, source_target_pairs={{0,4},{4,0},{8,12},{12,8},{1,5},{5,1},{9,13},{13,9},{2,6},{6,2},{1... | collective-permute-start | bytes 1081352 | tf_op jit(solution)/shard_map/ppermute | solution.py:19
  17.8 1.6 %collective-permute-start.7 = (f32[1,1536]{1,0:T(1,128)S(1)}, f32[1,1536]{1,0:T(1,128)S(1)}, u32[]{:S(2)}, u32[]{:S(2)}) collective-permute-start(f32[1,1536]{1,0:T(1,128)S(1)} %add_add_fusion), channel_id=1, source_target_pairs={{0,8},{4,12},{8,0},{12,4},{1,9},{5,13},{9,1},{13,5},{2,10},{6,14},... | collective-permute-start | bytes 18440 | tf_op jit(solution)/shard_map/ppermute | solution.py:19
  19.4 2.1 %collective-permute-done.7 = f32[1,1536]{1,0:T(1,128)S(1)} collective-permute-done((f32[1,1536]{1,0:T(1,128)S(1)}, f32[1,1536]{1,0:T(1,128)S(1)}, u32[]{:S(2)}, u32[]{:S(2)}) %collective-permute-start.7) | collective-permute-done | bytes 6176 | tf_op jit(solution)/shard_map/ppermute | solution.py:19
  21.5 0.1 collective-permute-start.8
  21.6 1.2 %collective-permute-done.8.refs_6_ = f32[1,1536]{1,0:T(1,128)S(1)} collective-permute-done((f32[1,1536]{1,0:T(1,128)S(1)}, f32[1,1536]{1,0:T(1,128)S(1)}, u32[]{:S(2)}, u32[]{:S(2)}) %collective-permute-start.8) | collective-permute-done | bytes 6176 | tf_op jit(solution)/shard_map/ppermute | solution.py:19
  22.8 0.0 collective-permute-done.6.refs_3_
  22.8 2.2 %shard_map.43 = (f32[128,384]{1,0:T(8,128)S(1)}, f32[128,384]{1,0:T(8,128)S(1)}, f32[2,256,512]{2,1,0:T(8,128)S(1)}, f32[2,2,256,128]{3,2,1,0:T(8,128)S(1)}, f32...) custom-call(bf16[128,1408]{1,0:T(8,128)(2,1)S(1)} %shard_map.41.packed_ref.refs_0_, ...), custom_call_target="tpu_custom_call" | custom-call | flops 570425344 | bytes 1814528 | tf_op jit(solution)/shard_map/pallas_call | solution.py:225
  25.0 0.0 collective-permute-done.9.refs_1_
  25.0 1.6 %shard_map.44 = (f32[256,384]{1,0:T(8,128)S(1)}, f32[256,384]{1,0:T(8,128)S(1)}, f32[4,2,128]{2,1,0:T(2,128)}) custom-call(bf16[2,256,1408]{2,1,0:T(8,128)(2,1)S(1)} %get-tuple-element.33.refs_0_, bf16[128,1408]{1,0:T(8,128)(2,1)S(1)} %collective-permute-done.9.refs_1_, f32[1,1536]{1,0:T(1,128)S(1)} %get-tuple-element.32.refs_2_.stats_ref, ...), custom_call_target="tpu_custom_call" | custom-call | flops 285212672 | bytes 3382272 | tf_op jit(solution)/shard_map/pallas_call | solution.py:225
  26.6 0.2 collective-permute-start.10
  26.8 3.2 %all-to-all-start = ((f32[4,2,128]{2,1,0:T(2,128)}), f32[4,2,128]{2,1,0:T(2,128)S(1)}, u32[]{:S(2)}, u32[]{:S(2)}) async-start(f32[4,2,128]{2,1,0:T(2,128)} %get-tuple-element.38), calls=%async_computation | async-start | bytes 8192 | tf_op jit(solution)/shard_map/all_to_all | solution.py:246
  30.0 2.3 %collective-permute-start.12 = (f32[128,384]{1,0:T(8,128)S(1)}, f32[128,384]{1,0:T(8,128)S(1)}, u32[]{:S(2)}, u32[]{:S(2)}) collective-permute-start(f32[128,384]{1,0:T(8,128)S(1)} %get-tuple-element.45), channel_id=1, source_target_pairs={{0,1},{2,0},{3,2},{1,3},{4,5},{6,4},{7,6},{5,7},{8,9},{10,8},{11,1... | collective-permute-start | bytes 589832 | tf_op jit(solution)/shard_map/ppermute | solution.py:26
  32.3 1.5 %all-to-all-done = f32[4,2,128]{2,1,0:T(2,128)S(1)} async-done(((f32[4,2,128]{2,1,0:T(2,128)}), f32[4,2,128]{2,1,0:T(2,128)S(1)}, u32[]{:S(2)}, u32[]{:S(2)}) %all-to-all-start) | async-done | bytes 4128 | tf_op jit(solution)/shard_map/all_to_all | solution.py:246
  33.8 0.0 collective-permute-done.10.got_ref
  33.9 0.5 %collective-permute-start.11 = (f32[128,384]{1,0:T(8,128)S(1)}, f32[128,384]{1,0:T(8,128)S(1)}, u32[]{:S(2)}, u32[]{:S(2)}) collective-permute-start(f32[128,384]{1,0:T(8,128)S(1)} %get-tuple-element.44), channel_id=1, source_target_pairs={{0,8},{4,12},{8,0},{12,4},{1,9},{5,13},{9,1},{13,5},{2,10},{6,14},... | collective-permute-start | bytes 589832 | tf_op jit(solution)/shard_map/ppermute | solution.py:19
  34.4 0.6 %broadcast_in_dim.2 = f32[4,2,128]{2,1,0:T(2,128)} broadcast(f32[2,128]{1,0:T(2,128)S(1)} %reduce_sum.9), dimensions={1,2} | broadcast | bytes 5120 | tf_op jit(solution)/shard_map/broadcast_in_dim | solution.py:314
  35.0 4.0 %all-to-all-start.1 = ((f32[4,2,128]{2,1,0:T(2,128)}), f32[4,2,128]{2,1,0:T(2,128)S(1)}, u32[]{:S(2)}, u32[]{:S(2)}) async-start(f32[4,2,128]{2,1,0:T(2,128)} %broadcast_in_dim.2), calls=%async_computation.1 | async-start | bytes 8192 | tf_op jit(solution)/shard_map/all_to_all | solution.py:246
  39.0 0.0 collective-permute-done.12.refs_3_
  39.0 5.6 %all-to-all-done.1.sums_ref = f32[4,2,128]{2,1,0:T(2,128)S(1)} async-done(((f32[4,2,128]{2,1,0:T(2,128)}), f32[4,2,128]{2,1,0:T(2,128)S(1)}, u32[]{:S(2)}, u32[]{:S(2)}) %all-to-all-start.1) | async-done | bytes 4128 | tf_op jit(solution)/shard_map/all_to_all | solution.py:246
  44.6 0.0 collective-permute-done.11.refs_2_
  44.6 0.8 %shard_map.46 = (f32[128,384]{1,0:T(8,128)}, f32[1,128]{1,0:T(1,128)}) custom-call(bf16[128,1408]{1,0:T(8,128)(2,1)S(1)} %shard_map.41.packed_ref.refs_0_, f32[1,1536]{1,0:T(1,128)S(1)} %get-tuple-element.32.refs_2_.stats_ref, f32[4,2,128]{2,1,0:T(2,128)S(1)} %all-to-all-done.1.sums_ref, f32[128,384]{1,0:T(8,128)S(1)} %get-tuple-element.40.refs_0_, ...), custom_call_target="tpu_custom_call" | custom-call | flops 393216 | bytes 1157120 | tf_op jit(solution)/shard_map/pallas_call | solution.py:225
  (8 shorter events, 0.1 us)
Async XLA Ops:
  1.6 14.0 %collective-permute-start.1 = (bf16[128,1408]{1,0:T(8,128)(2,1)S(1)}, bf16[128,1408]{1,0:T(8,128)(2,1)S(1)}, u32[]{:S(2)}, u32[]{:S(2)}) collective-permute-start(bf16[128,1408]{1,0:T(8,128)(2,1)S(1)} %shard_map.41.packed_ref.refs_0_), channel_id=1, source_target_pairs={{0,2},{2,3},{3,1},{1,0},{4,6},{6,7},{7,5},{5,4},{8,10},{10,11},{11... | collective-permute-start | bytes 1081352 | tf_op jit(solution)/shard_map/ppermute | solution.py:26
  5.7 11.6 %collective-permute-start = (bf16[128,1408]{1,0:T(8,128)(2,1)S(1)}, bf16[128,1408]{1,0:T(8,128)(2,1)S(1)}, u32[]{:S(2)}, u32[]{:S(2)}) collective-permute-start(bf16[128,1408]{1,0:T(8,128)(2,1)S(1)} %shard_map.41.packed_ref.refs_0_), channel_id=1, source_target_pairs={{0,8},{4,12},{8,0},{12,4},{1,9},{5,13},{9,1},{13,5},{2,10},{6,14},... | collective-permute-start | bytes 1081352 | tf_op jit(solution)/shard_map/ppermute | solution.py:19
  7.4 6.3 %collective-permute-start.2 = (f32[1,1536]{1,0:T(1,128)S(1)}, f32[1,1536]{1,0:T(1,128)S(1)}, u32[]{:S(2)}, u32[]{:S(2)}) collective-permute-start(f32[1,1536]{1,0:T(1,128)S(1)} %shard_map.42), channel_id=1, source_target_pairs={{0,1},{1,0},{2,3},{3,2},{4,5},{5,4},{6,7},{7,6},{8,9},{9,8},{10,11... | collective-permute-start | bytes 18440 | tf_op jit(solution)/shard_map/ppermute | solution.py:19
  7.4 8.2 %collective-permute-start.3 = (f32[1,1536]{1,0:T(1,128)S(1)}, f32[1,1536]{1,0:T(1,128)S(1)}, u32[]{:S(2)}, u32[]{:S(2)}) collective-permute-start(f32[1,1536]{1,0:T(1,128)S(1)} %shard_map.42), channel_id=1, source_target_pairs={{0,2},{1,3},{2,0},{3,1},{4,6},{5,7},{6,4},{7,5},{8,10},{9,11},{10,... | collective-permute-start | bytes 18440 | tf_op jit(solution)/shard_map/ppermute | solution.py:19
  9.3 6.3 %collective-permute-start.4 = (f32[1,1536]{1,0:T(1,128)S(1)}, f32[1,1536]{1,0:T(1,128)S(1)}, u32[]{:S(2)}, u32[]{:S(2)}) collective-permute-start(f32[1,1536]{1,0:T(1,128)S(1)} %shard_map.42), channel_id=1, source_target_pairs={{0,3},{1,2},{2,1},{3,0},{4,7},{5,6},{6,5},{7,4},{8,11},{9,10},{10,... | collective-permute-start | bytes 18440 | tf_op jit(solution)/shard_map/ppermute | solution.py:19
  15.7 9.4 %collective-permute-start.9 = (bf16[128,1408]{1,0:T(8,128)(2,1)S(1)}, bf16[128,1408]{1,0:T(8,128)(2,1)S(1)}, u32[]{:S(2)}, u32[]{:S(2)}) collective-permute-start(bf16[128,1408]{1,0:T(8,128)(2,1)S(1)} %collective-permute-done.1.refs_4_), channel_id=1, source_target_pairs={{0,2},{2,3},{3,1},{1,0},{4,6},{6,7},{7,5},{5,4},{8,10},{10,11},{11... | collective-permute-start | bytes 1081352 | tf_op jit(solution)/shard_map/ppermute | solution.py:26
  17.3 5.5 %collective-permute-start.5 = (bf16[128,1408]{1,0:T(8,128)(2,1)S(1)}, bf16[128,1408]{1,0:T(8,128)(2,1)S(1)}, u32[]{:S(2)}, u32[]{:S(2)}) collective-permute-start(bf16[128,1408]{1,0:T(8,128)(2,1)S(1)} %shard_map.41.packed_ref.refs_0_), channel_id=1, source_target_pairs={{0,4},{4,0},{8,12},{12,8},{1,5},{5,1},{9,13},{13,9},{2,6},{6,2},{1... | collective-permute-start | bytes 1081352 | tf_op jit(solution)/shard_map/ppermute | solution.py:19
  17.3 5.5 %collective-permute-start.6 = (bf16[128,1408]{1,0:T(8,128)(2,1)S(1)}, bf16[128,1408]{1,0:T(8,128)(2,1)S(1)}, u32[]{:S(2)}, u32[]{:S(2)}) collective-permute-start(bf16[128,1408]{1,0:T(8,128)(2,1)S(1)} %collective-permute-done.refs_1_), channel_id=1, source_target_pairs={{0,4},{4,0},{8,12},{12,8},{1,5},{5,1},{9,13},{13,9},{2,6},{6,2},{1... | collective-permute-start | bytes 1081352 | tf_op jit(solution)/shard_map/ppermute | solution.py:19
  17.8 3.7 %collective-permute-start.7 = (f32[1,1536]{1,0:T(1,128)S(1)}, f32[1,1536]{1,0:T(1,128)S(1)}, u32[]{:S(2)}, u32[]{:S(2)}) collective-permute-start(f32[1,1536]{1,0:T(1,128)S(1)} %add_add_fusion), channel_id=1, source_target_pairs={{0,8},{4,12},{8,0},{12,4},{1,9},{5,13},{9,1},{13,5},{2,10},{6,14},... | collective-permute-start | bytes 18440 | tf_op jit(solution)/shard_map/ppermute | solution.py:19
  21.5 1.2 %collective-permute-start.8 = (f32[1,1536]{1,0:T(1,128)S(1)}, f32[1,1536]{1,0:T(1,128)S(1)}, u32[]{:S(2)}, u32[]{:S(2)}) collective-permute-start(f32[1,1536]{1,0:T(1,128)S(1)} %add.15.refs_5_), channel_id=1, source_target_pairs={{0,4},{4,0},{8,12},{12,8},{1,5},{5,1},{9,13},{13,9},{2,6},{6,2},{1... | collective-permute-start | bytes 18440 | tf_op jit(solution)/shard_map/ppermute | solution.py:19
  26.6 7.2 %collective-permute-start.10 = (f32[256,384]{1,0:T(8,128)S(1)}, f32[256,384]{1,0:T(8,128)S(1)}, u32[]{:S(2)}, u32[]{:S(2)}) collective-permute-start(f32[256,384]{1,0:T(8,128)S(1)} %get-tuple-element.37), channel_id=1, source_target_pairs={{0,4},{4,0},{8,12},{12,8},{1,5},{5,1},{9,13},{13,9},{2,6},{6,2},{1... | collective-permute-start | bytes 1179656 | tf_op jit(solution)/shard_map/ppermute | solution.py:19
  26.8 7.0 %all-to-all-start = ((f32[4,2,128]{2,1,0:T(2,128)}), f32[4,2,128]{2,1,0:T(2,128)S(1)}, u32[]{:S(2)}, u32[]{:S(2)}) async-start(f32[4,2,128]{2,1,0:T(2,128)} %get-tuple-element.38), calls=%async_computation | async-start | bytes 8192 | tf_op jit(solution)/shard_map/all_to_all | solution.py:246
  30.0 9.0 %collective-permute-start.12 = (f32[128,384]{1,0:T(8,128)S(1)}, f32[128,384]{1,0:T(8,128)S(1)}, u32[]{:S(2)}, u32[]{:S(2)}) collective-permute-start(f32[128,384]{1,0:T(8,128)S(1)} %get-tuple-element.45), channel_id=1, source_target_pairs={{0,1},{2,0},{3,2},{1,3},{4,5},{6,4},{7,6},{5,7},{8,9},{10,8},{11,1... | collective-permute-start | bytes 589832 | tf_op jit(solution)/shard_map/ppermute | solution.py:26
  33.9 10.8 %collective-permute-start.11 = (f32[128,384]{1,0:T(8,128)S(1)}, f32[128,384]{1,0:T(8,128)S(1)}, u32[]{:S(2)}, u32[]{:S(2)}) collective-permute-start(f32[128,384]{1,0:T(8,128)S(1)} %get-tuple-element.44), channel_id=1, source_target_pairs={{0,8},{4,12},{8,0},{12,4},{1,9},{5,13},{9,1},{13,5},{2,10},{6,14},... | collective-permute-start | bytes 589832 | tf_op jit(solution)/shard_map/ppermute | solution.py:19
  35.0 9.6 %all-to-all-start.1 = ((f32[4,2,128]{2,1,0:T(2,128)}), f32[4,2,128]{2,1,0:T(2,128)S(1)}, u32[]{:S(2)}, u32[]{:S(2)}) async-start(f32[4,2,128]{2,1,0:T(2,128)} %broadcast_in_dim.2), calls=%async_computation.1 | async-start | bytes 8192 | tf_op jit(solution)/shard_map/all_to_all | solution.py:246

commit v11 on v7

--- a/solution.py
+++ b/solution.py
@@ -10,11 +10,16 @@
 FLOOR = 0.01
 EPSILON = 1e-06
 LANES = 128
+SUBLANES = 8
 CHUNK = 256
 WHOLE = pl.BlockSpec(memory_space=pltpu.VMEM)
 
 
-def exchange(value, axis, distance):
+BLK = ("y", "core")
+PART = ("y", "core", "sub")
+
+
+def exchange(value, distance, axis=BLK):
     size = lax.axis_size(axis)
     return lax.ppermute(value, axis, [(i, i ^ distance) for i in range(size)])
 
@@ -176,7 +181,7 @@
 
 
 def late_kernel(t_width, total_rows, *refs):
-    plane_ref, ref, stats_ref, acc_ref, norm_ref, early_sums, keep_ref, give_ref, sums_ref = refs
+    plane_ref, ref, stats_ref, acc_ref, norm_ref, early_sums, keep_ref, give_ref = refs
     s_width = keep_ref.shape[1]
     spread_t, spread_s, _ = spreads_of(stats_ref[...], t_width, s_width, total_rows)
     inv_t, inv_s = 1.0 / spread_t, 1.0 / spread_s
@@ -192,12 +197,17 @@
         back = jnp.dot(weights, with_ones(v[1]), preferred_element_type=jnp.float32)
         to_ref = (keep_ref, give_ref)[h]
         to_ref[at, :] = direct_of(cs, acc_ref[h, at, :] + back)
-    for i in range(sums_ref.shape[0]):
-        sums_ref[i, 0:1, :] = loss
-        sums_ref[i, 1:2, :] = spread
+    for ref in (keep_ref, give_ref):
+        ref[-SUBLANES:, :] = jnp.zeros((SUBLANES, s_width), jnp.float32)
+        ref[-SUBLANES : 1 - SUBLANES, :LANES] = loss
+        ref[1 - SUBLANES : 2 - SUBLANES, :LANES] = spread
 
 
 def halve_kernel(rows, keep_ref, got_ref, *out_refs):
+    for ref in out_refs[2:]:
+        sums = keep_ref[-SUBLANES:, :LANES] + got_ref[-SUBLANES:, :LANES]
+        for i in range(ref.shape[0]):
+            ref[i] = sums[: ref.shape[1]]
     out_refs[0][...] = keep_ref[:rows, :] + got_ref[:rows, :]
     out_refs[1][...] = keep_ref[rows : 2 * rows, :] + got_ref[rows : 2 * rows, :]
 
@@ -234,7 +244,7 @@
 
 
 def gathered(value, axis):
-    return [value] + [exchange(value, axis, d) for d in range(1, lax.axis_size(axis))]
+    return [value] + [exchange(value, d, axis) for d in range(1, lax.axis_size(axis))]
 
 
 def halvings(axis):
@@ -243,13 +253,13 @@
 
 
 def to_all(value):
-    return lax.all_to_all(value, ("blk", "sub"), 0, 0, tiled=True)
+    return lax.all_to_all(value, ("y", "sub"), 0, 0, tiled=True)
 
 
 def per_device(teacher, student):
     rows, t_width = teacher.shape
     s_width = student.shape[1]
-    n_blk = lax.axis_size("blk")
+    n_blk = lax.axis_size(BLK)
     n_sub = lax.axis_size("sub")
     total_rows = float(rows * n_blk * n_sub)
     half = n_sub // 2
@@ -273,19 +283,19 @@
         4 * packed.size,
     )
     line = [packed, shifted(packed, "sub", 1)]
-    tz = [exchange(stats, "sub", d) for d in range(1, n_sub)]
+    tz = [exchange(stats, d, "sub") for d in range(1, n_sub)]
     line[1], *tz = lax.optimization_barrier((line[1], *tz))
     for _ in range(half - 1):
         line.append(shifted(line[-1], "sub", 1))
     stats = functools.reduce(jnp.add, [stats] + tz)
     tiles = [packed]
-    for distance in halvings("blk"):
+    for distance in halvings(BLK):
         if distance == 1:
             *tiles, line[1] = lax.optimization_barrier((*tiles, line[1]))
         else:
-            stats = stats + exchange(stats, "blk", distance)
-        tiles = tiles + [exchange(x, "blk", distance) for x in tiles]
-    stats = [stats, exchange(stats, "blk", 1)]
+            stats = stats + exchange(stats, distance)
+        tiles = tiles + [exchange(x, distance) for x in tiles]
+    stats = [stats, exchange(stats, 1)]
 
     pair_flops = 2 * rows * rows * n_blk * (t_width + 3 * s_width)
     out_shape = (
@@ -302,23 +312,26 @@
     )
     own, backs = tiles[0], tiles[1:]
     returned = [shifted(x, "sub", -k) for k, x in enumerate(backs, 1)]
-    keep, give, sums = call(
+    keep, give = call(
         functools.partial(late_kernel, t_width, total_rows),
-        [f32((side, s_width))] * 2 + [f32((n_blk * n_sub, 2, LANES))],
+        [f32((side + SUBLANES, s_width))] * 2,
         [plane, line[half], totals, acc, norms, early_sums],
         pair_flops,
     )
-    got = exchange(give, "blk", 1)
-    tiles, distance = n_blk // 2, 2
+    got = exchange(give, 1)
+    tiles, distance, all_sums = n_blk // 2, 2, None
     while tiles > 1:
         tiles //= 2
         out_shape = [f32((rows * tiles, s_width))] * 2
-        keep, give = call(
+        if all_sums is None:
+            out_shape = out_shape + [f32((n_blk // 2 * n_sub, 2, LANES))]
+        keep, give, *sums = call(
             functools.partial(halve_kernel, rows * tiles), out_shape, (keep, got), 2 * keep.size
         )
-        got = exchange(give, "blk", distance)
+        got = exchange(give, distance)
+        if all_sums is None:
+            all_sums = to_all(sums[0])
         distance *= 2
-    all_sums = to_all(sums)
     parts = [own, keep, got] + returned
     grad, loss = call(
         functools.partial(final_kernel, t_width, total_rows),
@@ -330,10 +343,13 @@
 
 
 def solution(mesh):
-    placed = P(("groups", "blk", "sub"), None)
+    groups, blk, sub = (mesh.shape[name] for name in ("groups", "blk", "sub"))
+    devices = mesh.devices.reshape(groups, blk // 2, 2, sub)
+    split = jax.sharding.Mesh(devices, ("groups", *PART))
+    placed = P(("groups", *PART), None)
     return jax.shard_map(
         per_device,
-        mesh=mesh,
+        mesh=split,
         in_specs=(placed, placed),
         out_specs=(placed, P("groups")),
         check_vma=False,

time: 41.7 us -> 42.4 us (1.017)
  blocking collectives: 10.3 us -> 0 us
  waiting for transfers between devices: 7.15 us -> 13.7 us
  starting transfers between devices: 17.8 us -> 21.7 us
  Pallas kernels: 5.55 us -> 6.15 us
    all_to_all x1 -> x0, blocking collectives: 10.3 us -> none  [to_all(): return lax.all_to_all(value, ('blk', 'sub'), 0, 0, tiled=True)]
    all_to_all x0 -> x1, waiting for transfers between devices: none -> 6.13 us  [to_all(): return lax.all_to_all(value, ('y', 'sub'), 0, 0, tiled=True)]
    all_to_all x0 -> x1, starting transfers between devices: none -> 3.95 us  [to_all(): return lax.all_to_all(value, ('y', 'sub'), 0, 0, tiled=True)]
    pallas_call x6, Pallas kernels: 5.55 us -> 6.15 us  [call(): pl.pallas_call(kernel, out_shape=out_shape, in_specs=in_specs, out_specs=...]
  transfers between devices with their start and end apart: 13 -> 14, of which waited for: 4 -> 6; matrix products, arithmetic and copies ran while one was open for 0% -> 0% of each run, Pallas kernels for 6% -> 7%
where the time goes in v11:
time: 42.4 us; the launch traced here: 42.2 us
  starting transfers between devices  21.7 us (51%)
  waiting for transfers between devices  13.7 us (32%)
  Pallas kernels  6.15 us (15%)
  between operations  0.69 us (2%)
    ppermute x10, starting transfers between devices, exchange(): return lax.ppermute(value, axis, [(i, i ^ distance) for i in range(size)])  9.82 us
    ppermute x3, starting transfers between devices, shifted(): return lax.ppermute(value, axis, route)  7.95 us
    ppermute x10, waiting for transfers between devices, exchange(): return lax.ppermute(value, axis, [(i, i ^ distance) for i in range(size)])  7.14 us
    pallas_call x6, Pallas kernels, call(): pl.pallas_call(kernel, out_shape=out_shape, in_specs=in_specs, out_specs=...  6.15 us
    all_to_all x1, waiting for transfers between devices, to_all(): return lax.all_to_all(value, ('y', 'sub'), 0, 0, tiled=True)  6.13 us
    all_to_all x1, starting transfers between devices, to_all(): return lax.all_to_all(value, ('y', 'sub'), 0, 0, tiled=True)  3.95 us
  transfers between devices with their start and end apart: 14, of which 6 were waited for; matrix products, arithmetic and copies ran while one was open for 0% of the time, Pallas kernels for 7%

profile of v11, /device:TPU:0, one launch (start us, length us, event | category | flops | bytes accessed | tf_op | source)
XLA Modules:
  0.0 42.2 jit_solution(17983291669411858258)
XLA Ops:
  0.6 1.0 %shard_map.41.packed_ref.refs_0_ = bf16[128,1408]{1,0:T(8,128)(2,1)S(1)} custom-call(bf16[128,1024]{1,0:T(8,128)(2,1)} %t_hbm.1, bf16[128,384]{1,0:T(8,128)(2,1)} %s_hbm.1), custom_call_target="tpu_custom_call" | custom-call | bytes 360448 | tf_op jit(solution)/shard_map/pallas_call | solution.py:235
  1.6 4.1 %collective-permute-start.1 = (bf16[128,1408]{1,0:T(8,128)(2,1)S(1)}, bf16[128,1408]{1,0:T(8,128)(2,1)S(1)}, u32[]{:S(2)}, u32[]{:S(2)}) collective-permute-start(bf16[128,1408]{1,0:T(8,128)(2,1)S(1)} %shard_map.41.packed_ref.refs_0_), channel_id=1, source_target_pairs={{0,2},{2,3},{3,1},{1,0},{4,6},{6,7},{7,5},{5,4},{8,10},{10,11},{11... | collective-permute-start | bytes 1081352 | tf_op jit(solution)/shard_map/ppermute | solution.py:31
  5.7 1.5 %collective-permute-start = (bf16[128,1408]{1,0:T(8,128)(2,1)S(1)}, bf16[128,1408]{1,0:T(8,128)(2,1)S(1)}, u32[]{:S(2)}, u32[]{:S(2)}) collective-permute-start(bf16[128,1408]{1,0:T(8,128)(2,1)S(1)} %shard_map.41.packed_ref.refs_0_), channel_id=1, source_target_pairs={{0,8},{4,12},{8,0},{12,4},{1,9},{5,13},{9,1},{13,5},{2,10},{6,14},... | collective-permute-start | bytes 1081352 | tf_op jit(solution)/shard_map/ppermute | solution.py:24
  7.2 0.2 shard_map.42
  7.4 0.0 collective-permute-start.2
  7.4 1.9 %collective-permute-start.3 = (f32[1,1536]{1,0:T(1,128)S(1)}, f32[1,1536]{1,0:T(1,128)S(1)}, u32[]{:S(2)}, u32[]{:S(2)}) collective-permute-start(f32[1,1536]{1,0:T(1,128)S(1)} %shard_map.42), channel_id=1, source_target_pairs={{0,2},{1,3},{2,0},{3,1},{4,6},{5,7},{6,4},{7,5},{8,10},{9,11},{10,... | collective-permute-start | bytes 18440 | tf_op jit(solution)/shard_map/ppermute | solution.py:24
  9.3 2.5 %collective-permute-start.4 = (f32[1,1536]{1,0:T(1,128)S(1)}, f32[1,1536]{1,0:T(1,128)S(1)}, u32[]{:S(2)}, u32[]{:S(2)}) collective-permute-start(f32[1,1536]{1,0:T(1,128)S(1)} %shard_map.42), channel_id=1, source_target_pairs={{0,3},{1,2},{2,1},{3,0},{4,7},{5,6},{6,5},{7,4},{8,11},{9,10},{10,... | collective-permute-start | bytes 18440 | tf_op jit(solution)/shard_map/ppermute | solution.py:24
  11.8 1.9 %collective-permute-done.2 = f32[1,1536]{1,0:T(1,128)S(1)} collective-permute-done((f32[1,1536]{1,0:T(1,128)S(1)}, f32[1,1536]{1,0:T(1,128)S(1)}, u32[]{:S(2)}, u32[]{:S(2)}) %collective-permute-start.2) | collective-permute-done | bytes 6176 | tf_op jit(solution)/shard_map/ppermute | solution.py:24
  13.7 2.0 %collective-permute-done.3 = f32[1,1536]{1,0:T(1,128)S(1)} collective-permute-done((f32[1,1536]{1,0:T(1,128)S(1)}, f32[1,1536]{1,0:T(1,128)S(1)}, u32[]{:S(2)}, u32[]{:S(2)}) %collective-permute-start.3) | collective-permute-done | bytes 6176 | tf_op jit(solution)/shard_map/ppermute | solution.py:24
  15.7 0.0 collective-permute-done.4
  15.7 0.0 collective-permute-done.1.refs_4_
  15.7 1.6 %collective-permute-start.9 = (bf16[128,1408]{1,0:T(8,128)(2,1)S(1)}, bf16[128,1408]{1,0:T(8,128)(2,1)S(1)}, u32[]{:S(2)}, u32[]{:S(2)}) collective-permute-start(bf16[128,1408]{1,0:T(8,128)(2,1)S(1)} %collective-permute-done.1.refs_4_), channel_id=1, source_target_pairs={{0,2},{2,3},{3,1},{1,0},{4,6},{6,7},{7,5},{5,4},{8,10},{10,11},{11... | collective-permute-start | bytes 1081352 | tf_op jit(solution)/shard_map/ppermute | solution.py:31
  17.3 0.0 collective-permute-done.refs_1_
  17.3 0.0 collective-permute-start.5
  17.3 0.5 %collective-permute-start.6 = (bf16[128,1408]{1,0:T(8,128)(2,1)S(1)}, bf16[128,1408]{1,0:T(8,128)(2,1)S(1)}, u32[]{:S(2)}, u32[]{:S(2)}) collective-permute-start(bf16[128,1408]{1,0:T(8,128)(2,1)S(1)} %collective-permute-done.refs_1_), channel_id=1, source_target_pairs={{0,4},{4,0},{8,12},{12,8},{1,5},{5,1},{9,13},{13,9},{2,6},{6,2},{1... | collective-permute-start | bytes 1081352 | tf_op jit(solution)/shard_map/ppermute | solution.py:24
  17.8 1.6 %collective-permute-start.7 = (f32[1,1536]{1,0:T(1,128)S(1)}, f32[1,1536]{1,0:T(1,128)S(1)}, u32[]{:S(2)}, u32[]{:S(2)}) collective-permute-start(f32[1,1536]{1,0:T(1,128)S(1)} %add_add_fusion), channel_id=1, source_target_pairs={{0,8},{4,12},{8,0},{12,4},{1,9},{5,13},{9,1},{13,5},{2,10},{6,14},... | collective-permute-start | bytes 18440 | tf_op jit(solution)/shard_map/ppermute | solution.py:24
  19.4 2.1 %collective-permute-done.7 = f32[1,1536]{1,0:T(1,128)S(1)} collective-permute-done((f32[1,1536]{1,0:T(1,128)S(1)}, f32[1,1536]{1,0:T(1,128)S(1)}, u32[]{:S(2)}, u32[]{:S(2)}) %collective-permute-start.7) | collective-permute-done | bytes 6176 | tf_op jit(solution)/shard_map/ppermute | solution.py:24
  21.5 0.1 collective-permute-start.8
  21.6 1.2 %collective-permute-done.8.refs_6_ = f32[1,1536]{1,0:T(1,128)S(1)} collective-permute-done((f32[1,1536]{1,0:T(1,128)S(1)}, f32[1,1536]{1,0:T(1,128)S(1)}, u32[]{:S(2)}, u32[]{:S(2)}) %collective-permute-start.8) | collective-permute-done | bytes 6176 | tf_op jit(solution)/shard_map/ppermute | solution.py:24
  22.8 0.0 collective-permute-done.5.refs_2_
  22.8 0.0 collective-permute-done.6.refs_3_
  22.8 2.3 %shard_map.43 = (f32[128,384]{1,0:T(8,128)S(1)}, f32[128,384]{1,0:T(8,128)S(1)}, f32[2,256,512]{2,1,0:T(8,128)S(1)}, f32[2,2,256,128]{3,2,1,0:T(8,128)S(1)}, f32...) custom-call(bf16[128,1408]{1,0:T(8,128)(2,1)S(1)} %shard_map.41.packed_ref.refs_0_, ...), custom_call_target="tpu_custom_call" | custom-call | flops 570425344 | bytes 1814528 | tf_op jit(solution)/shard_map/pallas_call | solution.py:235
  25.1 1.2 %shard_map.44 = (f32[264,384]{1,0:T(8,128)S(1)}, f32[264,384]{1,0:T(8,128)S(1)}) custom-call(bf16[2,256,1408]{2,1,0:T(8,128)(2,1)S(1)} %get-tuple-element.31.refs_0_, bf16[128,1408]{1,0:T(8,128)(2,1)S(1)} %collective-permute-done.9.refs_1_, f32[1,1536]{1,0:T(1,128)S(1)} %get-tuple-element.30.refs_2_.stats_ref, f32[2,256,512]{2,1,0:T(8,128)S(1)} %get-tuple-element.32.refs_3_, ...), custom_call_target="tpu_custom_call" | custom-call | flops 285212672 | bytes 3382272 | tf_op jit(solution)/shard_map/pallas_call | solution.py:235
  26.3 0.2 collective-permute-start.10
  26.5 2.2 %collective-permute-start.12 = (f32[128,384]{1,0:T(8,128)S(1)}, f32[128,384]{1,0:T(8,128)S(1)}, u32[]{:S(2)}, u32[]{:S(2)}) collective-permute-start(f32[128,384]{1,0:T(8,128)S(1)} %get-tuple-element.41), channel_id=1, source_target_pairs={{0,1},{2,0},{3,2},{1,3},{4,5},{6,4},{7,6},{5,7},{8,9},{10,8},{11,1... | collective-permute-start | bytes 589832 | tf_op jit(solution)/shard_map/ppermute | solution.py:31
  28.8 0.0 collective-permute-done.10.got_ref
  28.8 0.6 %shard_map.45 = (f32[128,384]{1,0:T(8,128)S(1)}, f32[128,384]{1,0:T(8,128)S(1)}, f32[8,2,128]{2,1,0:T(2,128)}) custom-call(f32[264,384]{1,0:T(8,128)S(1)} %get-tuple-element.35.keep_ref, f32[264,384]{1,0:T(8,128)S(1)} %collective-permute-done.10.got_ref), custom_call_target="tpu_custom_call" | custom-call | flops 202752 | bytes 811008 | tf_op jit(solution)/shard_map/pallas_call | solution.py:235
  29.4 1.5 %collective-permute-start.11 = (f32[128,384]{1,0:T(8,128)S(1)}, f32[128,384]{1,0:T(8,128)S(1)}, u32[]{:S(2)}, u32[]{:S(2)}) collective-permute-start(f32[128,384]{1,0:T(8,128)S(1)} %get-tuple-element.40), channel_id=1, source_target_pairs={{0,8},{4,12},{8,0},{12,4},{1,9},{5,13},{9,1},{13,5},{2,10},{6,14},... | collective-permute-start | bytes 589832 | tf_op jit(solution)/shard_map/ppermute | solution.py:24
  30.9 3.9 %all-to-all-start = ((f32[8,2,128]{2,1,0:T(2,128)}), f32[8,2,128]{2,1,0:T(2,128)S(1)}, u32[]{:S(2)}, u32[]{:S(2)}) async-start(f32[8,2,128]{2,1,0:T(2,128)} %get-tuple-element.37), calls=%async_computation | async-start | bytes 16384 | tf_op jit(solution)/shard_map/all_to_all | solution.py:256
  34.9 0.4 collective-permute-done.12.refs_3_
  35.3 6.1 %all-to-all-done.sums_ref = f32[8,2,128]{2,1,0:T(2,128)S(1)} async-done(((f32[8,2,128]{2,1,0:T(2,128)}), f32[8,2,128]{2,1,0:T(2,128)S(1)}, u32[]{:S(2)}, u32[]{:S(2)}) %all-to-all-start) | async-done | bytes 8224 | tf_op jit(solution)/shard_map/all_to_all | solution.py:256
  41.4 0.8 %shard_map.46 = (f32[128,384]{1,0:T(8,128)}, f32[1,128]{1,0:T(1,128)}) custom-call(bf16[128,1408]{1,0:T(8,128)(2,1)S(1)} %shard_map.41.packed_ref.refs_0_, f32[1,1536]{1,0:T(1,128)S(1)} %get-tuple-element.30.refs_2_.stats_ref, f32[8,2,128]{2,1,0:T(2,128)S(1)} %all-to-all-done.sums_ref, f32[128,384]{1,0:T(8,128)S(1)} %get-tuple-element.38.refs_0_, ...), custom_call_target="tpu_custom_call" | custom-call | flops 393216 | bytes 1161216 | tf_op jit(solution)/shard_map/pallas_call | solution.py:235
  (4 shorter events, 0.0 us)
Async XLA Ops:
  1.6 14.0 %collective-permute-start.1 = (bf16[128,1408]{1,0:T(8,128)(2,1)S(1)}, bf16[128,1408]{1,0:T(8,128)(2,1)S(1)}, u32[]{:S(2)}, u32[]{:S(2)}) collective-permute-start(bf16[128,1408]{1,0:T(8,128)(2,1)S(1)} %shard_map.41.packed_ref.refs_0_), channel_id=1, source_target_pairs={{0,2},{2,3},{3,1},{1,0},{4,6},{6,7},{7,5},{5,4},{8,10},{10,11},{11... | collective-permute-start | bytes 1081352 | tf_op jit(solution)/shard_map/ppermute | solution.py:31
  5.7 11.6 %collective-permute-start = (bf16[128,1408]{1,0:T(8,128)(2,1)S(1)}, bf16[128,1408]{1,0:T(8,128)(2,1)S(1)}, u32[]{:S(2)}, u32[]{:S(2)}) collective-permute-start(bf16[128,1408]{1,0:T(8,128)(2,1)S(1)} %shard_map.41.packed_ref.refs_0_), channel_id=1, source_target_pairs={{0,8},{4,12},{8,0},{12,4},{1,9},{5,13},{9,1},{13,5},{2,10},{6,14},... | collective-permute-start | bytes 1081352 | tf_op jit(solution)/shard_map/ppermute | solution.py:24
  7.4 6.3 %collective-permute-start.2 = (f32[1,1536]{1,0:T(1,128)S(1)}, f32[1,1536]{1,0:T(1,128)S(1)}, u32[]{:S(2)}, u32[]{:S(2)}) collective-permute-start(f32[1,1536]{1,0:T(1,128)S(1)} %shard_map.42), channel_id=1, source_target_pairs={{0,1},{1,0},{2,3},{3,2},{4,5},{5,4},{6,7},{7,6},{8,9},{9,8},{10,11... | collective-permute-start | bytes 18440 | tf_op jit(solution)/shard_map/ppermute | solution.py:24
  7.4 8.2 %collective-permute-start.3 = (f32[1,1536]{1,0:T(1,128)S(1)}, f32[1,1536]{1,0:T(1,128)S(1)}, u32[]{:S(2)}, u32[]{:S(2)}) collective-permute-start(f32[1,1536]{1,0:T(1,128)S(1)} %shard_map.42), channel_id=1, source_target_pairs={{0,2},{1,3},{2,0},{3,1},{4,6},{5,7},{6,4},{7,5},{8,10},{9,11},{10,... | collective-permute-start | bytes 18440 | tf_op jit(solution)/shard_map/ppermute | solution.py:24
  9.3 6.3 %collective-permute-start.4 = (f32[1,1536]{1,0:T(1,128)S(1)}, f32[1,1536]{1,0:T(1,128)S(1)}, u32[]{:S(2)}, u32[]{:S(2)}) collective-permute-start(f32[1,1536]{1,0:T(1,128)S(1)} %shard_map.42), channel_id=1, source_target_pairs={{0,3},{1,2},{2,1},{3,0},{4,7},{5,6},{6,5},{7,4},{8,11},{9,10},{10,... | collective-permute-start | bytes 18440 | tf_op jit(solution)/shard_map/ppermute | solution.py:24
  15.7 9.4 %collective-permute-start.9 = (bf16[128,1408]{1,0:T(8,128)(2,1)S(1)}, bf16[128,1408]{1,0:T(8,128)(2,1)S(1)}, u32[]{:S(2)}, u32[]{:S(2)}) collective-permute-start(bf16[128,1408]{1,0:T(8,128)(2,1)S(1)} %collective-permute-done.1.refs_4_), channel_id=1, source_target_pairs={{0,2},{2,3},{3,1},{1,0},{4,6},{6,7},{7,5},{5,4},{8,10},{10,11},{11... | collective-permute-start | bytes 1081352 | tf_op jit(solution)/shard_map/ppermute | solution.py:31
  17.3 5.5 %collective-permute-start.5 = (bf16[128,1408]{1,0:T(8,128)(2,1)S(1)}, bf16[128,1408]{1,0:T(8,128)(2,1)S(1)}, u32[]{:S(2)}, u32[]{:S(2)}) collective-permute-start(bf16[128,1408]{1,0:T(8,128)(2,1)S(1)} %shard_map.41.packed_ref.refs_0_), channel_id=1, source_target_pairs={{0,4},{4,0},{8,12},{12,8},{1,5},{5,1},{9,13},{13,9},{2,6},{6,2},{1... | collective-permute-start | bytes 1081352 | tf_op jit(solution)/shard_map/ppermute | solution.py:24
  17.3 5.5 %collective-permute-start.6 = (bf16[128,1408]{1,0:T(8,128)(2,1)S(1)}, bf16[128,1408]{1,0:T(8,128)(2,1)S(1)}, u32[]{:S(2)}, u32[]{:S(2)}) collective-permute-start(bf16[128,1408]{1,0:T(8,128)(2,1)S(1)} %collective-permute-done.refs_1_), channel_id=1, source_target_pairs={{0,4},{4,0},{8,12},{12,8},{1,5},{5,1},{9,13},{13,9},{2,6},{6,2},{1... | collective-permute-start | bytes 1081352 | tf_op jit(solution)/shard_map/ppermute | solution.py:24
  17.8 3.7 %collective-permute-start.7 = (f32[1,1536]{1,0:T(1,128)S(1)}, f32[1,1536]{1,0:T(1,128)S(1)}, u32[]{:S(2)}, u32[]{:S(2)}) collective-permute-start(f32[1,1536]{1,0:T(1,128)S(1)} %add_add_fusion), channel_id=1, source_target_pairs={{0,8},{4,12},{8,0},{12,4},{1,9},{5,13},{9,1},{13,5},{2,10},{6,14},... | collective-permute-start | bytes 18440 | tf_op jit(solution)/shard_map/ppermute | solution.py:24
  21.5 1.2 %collective-permute-start.8 = (f32[1,1536]{1,0:T(1,128)S(1)}, f32[1,1536]{1,0:T(1,128)S(1)}, u32[]{:S(2)}, u32[]{:S(2)}) collective-permute-start(f32[1,1536]{1,0:T(1,128)S(1)} %add.15.refs_5_), channel_id=1, source_target_pairs={{0,4},{4,0},{8,12},{12,8},{1,5},{5,1},{9,13},{13,9},{2,6},{6,2},{1... | collective-permute-start | bytes 18440 | tf_op jit(solution)/shard_map/ppermute | solution.py:24
  26.3 2.5 %collective-permute-start.10 = (f32[264,384]{1,0:T(8,128)S(1)}, f32[264,384]{1,0:T(8,128)S(1)}, u32[]{:S(2)}, u32[]{:S(2)}) collective-permute-start(f32[264,384]{1,0:T(8,128)S(1)} %get-tuple-element.36), channel_id=1, source_target_pairs={{0,4},{4,0},{8,12},{12,8},{1,5},{5,1},{9,13},{13,9},{2,6},{6,2},{1... | collective-permute-start | bytes 1216520 | tf_op jit(solution)/shard_map/ppermute | solution.py:24
  26.5 8.7 %collective-permute-start.12 = (f32[128,384]{1,0:T(8,128)S(1)}, f32[128,384]{1,0:T(8,128)S(1)}, u32[]{:S(2)}, u32[]{:S(2)}) collective-permute-start(f32[128,384]{1,0:T(8,128)S(1)} %get-tuple-element.41), channel_id=1, source_target_pairs={{0,1},{2,0},{3,2},{1,3},{4,5},{6,4},{7,6},{5,7},{8,9},{10,8},{11,1... | collective-permute-start | bytes 589832 | tf_op jit(solution)/shard_map/ppermute | solution.py:31
  29.4 12.0 %collective-permute-start.11 = (f32[128,384]{1,0:T(8,128)S(1)}, f32[128,384]{1,0:T(8,128)S(1)}, u32[]{:S(2)}, u32[]{:S(2)}) collective-permute-start(f32[128,384]{1,0:T(8,128)S(1)} %get-tuple-element.40), channel_id=1, source_target_pairs={{0,8},{4,12},{8,0},{12,4},{1,9},{5,13},{9,1},{13,5},{2,10},{6,14},... | collective-permute-start | bytes 589832 | tf_op jit(solution)/shard_map/ppermute | solution.py:24
  30.9 10.5 %all-to-all-start = ((f32[8,2,128]{2,1,0:T(2,128)}), f32[8,2,128]{2,1,0:T(2,128)S(1)}, u32[]{:S(2)}, u32[]{:S(2)}) async-start(f32[8,2,128]{2,1,0:T(2,128)} %get-tuple-element.37), calls=%async_computation | async-start | bytes 16384 | tf_op jit(solution)/shard_map/all_to_all | solution.py:256

commit v12 on v11

--- a/solution.py
+++ b/solution.py
@@ -10,7 +10,6 @@
 FLOOR = 0.01
 EPSILON = 1e-06
 LANES = 128
-SUBLANES = 8
 CHUNK = 256
 WHOLE = pl.BlockSpec(memory_space=pltpu.VMEM)
 
@@ -181,7 +180,7 @@
 
 
 def late_kernel(t_width, total_rows, *refs):
-    plane_ref, ref, stats_ref, acc_ref, norm_ref, early_sums, keep_ref, give_ref = refs
+    plane_ref, ref, stats_ref, acc_ref, norm_ref, early_sums, keep_ref, give_ref, sums_ref = refs
     s_width = keep_ref.shape[1]
     spread_t, spread_s, _ = spreads_of(stats_ref[...], t_width, s_width, total_rows)
     inv_t, inv_s = 1.0 / spread_t, 1.0 / spread_s
@@ -197,28 +196,23 @@
         back = jnp.dot(weights, with_ones(v[1]), preferred_element_type=jnp.float32)
         to_ref = (keep_ref, give_ref)[h]
         to_ref[at, :] = direct_of(cs, acc_ref[h, at, :] + back)
-    for ref in (keep_ref, give_ref):
-        ref[-SUBLANES:, :] = jnp.zeros((SUBLANES, s_width), jnp.float32)
-        ref[-SUBLANES : 1 - SUBLANES, :LANES] = loss
-        ref[1 - SUBLANES : 2 - SUBLANES, :LANES] = spread
+    for i in range(sums_ref.shape[0]):
+        sums_ref[i, 0:1, :] = loss
+        sums_ref[i, 1:2, :] = spread
 
 
 def halve_kernel(rows, keep_ref, got_ref, *out_refs):
-    for ref in out_refs[2:]:
-        sums = keep_ref[-SUBLANES:, :LANES] + got_ref[-SUBLANES:, :LANES]
-        for i in range(ref.shape[0]):
-            ref[i] = sums[: ref.shape[1]]
     out_refs[0][...] = keep_ref[:rows, :] + got_ref[:rows, :]
     out_refs[1][...] = keep_ref[rows : 2 * rows, :] + got_ref[rows : 2 * rows, :]
 
 
-def final_kernel(t_width, total_rows, packed_ref, stats_ref, sums_ref, *refs):
+def final_kernel(t_width, total_rows, packed_ref, stats_ref, sums_ref, other_ref, *refs):
     *parts, grad_ref, loss_ref = refs
     direct = parts[0][...]
     for part in parts[1:]:
         direct = direct + part[...]
     s_width = direct.shape[1]
-    both = jnp.sum(jnp.sum(sums_ref[...], axis=0), axis=1, keepdims=True)
+    both = jnp.sum(sums_ref[...] + other_ref[...], axis=1, keepdims=True)
     loss_total, spread_total = both[0:1, :], -both[1:2, :]
     _, spread_s, centre = spreads_of(stats_ref[...], t_width, s_width, total_rows)
     pairs = total_rows * (total_rows - 1.0)
@@ -312,31 +306,30 @@
     )
     own, backs = tiles[0], tiles[1:]
     returned = [shifted(x, "sub", -k) for k, x in enumerate(backs, 1)]
-    keep, give = call(
+    keep, give, sums = call(
         functools.partial(late_kernel, t_width, total_rows),
-        [f32((side + SUBLANES, s_width))] * 2,
+        [f32((side, s_width))] * 2 + [f32((n_blk // 2 * n_sub, 2, LANES))],
         [plane, line[half], totals, acc, norms, early_sums],
         pair_flops,
     )
     got = exchange(give, 1)
-    tiles, distance, all_sums = n_blk // 2, 2, None
+    sums = jnp.sum(to_all(sums), axis=0)
+    got, sums = lax.optimization_barrier((got, sums))
+    tiles, distance = n_blk // 2, 2
     while tiles > 1:
         tiles //= 2
         out_shape = [f32((rows * tiles, s_width))] * 2
-        if all_sums is None:
-            out_shape = out_shape + [f32((n_blk // 2 * n_sub, 2, LANES))]
-        keep, give, *sums = call(
+        keep, give = call(
             functools.partial(halve_kernel, rows * tiles), out_shape, (keep, got), 2 * keep.size
         )
         got = exchange(give, distance)
-        if all_sums is None:
-            all_sums = to_all(sums[0])
         distance *= 2
+    all_sums = [sums, exchange(sums, 1)]
     parts = [own, keep, got] + returned
     grad, loss = call(
         functools.partial(final_kernel, t_width, total_rows),
         [f32((rows, s_width)), f32((1, LANES))],
-        [packed, totals, all_sums] + parts,
+        [packed, totals, *all_sums] + parts,
         8 * student.size,
     )
     return grad, loss[0, :1]

time: 42.4 us -> 46 us (1.085)
  waiting for transfers between devices: 13.7 us -> 17.1 us
    ppermute x10 -> x11, waiting for transfers between devices: 7.14 us -> 11.5 us  [exchange(): return lax.ppermute(value, axis, [(i, i ^ distance) for i in range(size)])]
    all_to_all x1, waiting for transfers between devices: 6.13 us -> 4.61 us  [to_all(): return lax.all_to_all(value, ('y', 'sub'), 0, 0, tiled=True)]
    all_to_all x1, starting transfers between devices: 3.95 us -> 5.38 us  [to_all(): return lax.all_to_all(value, ('y', 'sub'), 0, 0, tiled=True)]
    ppermute x10 -> x11, starting transfers between devices: 9.82 us -> 8.87 us  [exchange(): return lax.ppermute(value, axis, [(i, i ^ distance) for i in range(size)])]
    ppermute x3, waiting for transfers between devices: 0.4 us -> 0.98 us  [shifted(): return lax.ppermute(value, axis, route)]
  transfers between devices with their start and end apart: 14 -> 15, of which waited for: 6 -> 8; matrix products, arithmetic and copies ran while one was open for 0% -> 0% of each run, Pallas kernels for 7% -> 5%
where the time goes in v12:
time: 46 us; the launch traced here: 45.8 us
  starting transfers between devices  22 us (48%)
  waiting for transfers between devices  17.1 us (37%)
  Pallas kernels  5.97 us (13%)
  between operations  0.69 us (2%)
    ppermute x11, waiting for transfers between devices, exchange(): return lax.ppermute(value, axis, [(i, i ^ distance) for i in range(size)])  11.5 us
    ppermute x11, starting transfers between devices, exchange(): return lax.ppermute(value, axis, [(i, i ^ distance) for i in range(size)])  8.87 us
    ppermute x3, starting transfers between devices, shifted(): return lax.ppermute(value, axis, route)  7.75 us
    pallas_call x6, Pallas kernels, call(): pl.pallas_call(kernel, out_shape=out_shape, in_specs=in_specs, out_specs=...  5.97 us
    all_to_all x1, starting transfers between devices, to_all(): return lax.all_to_all(value, ('y', 'sub'), 0, 0, tiled=True)  5.38 us
    all_to_all x1, waiting for transfers between devices, to_all(): return lax.all_to_all(value, ('y', 'sub'), 0, 0, tiled=True)  4.61 us
    ppermute x3, waiting for transfers between devices, shifted(): return lax.ppermute(value, axis, route)  0.98 us
  transfers between devices with their start and end apart: 15, of which 8 were waited for; matrix products, arithmetic and copies ran while one was open for 0% of the time, Pallas kernels for 5%

profile of v12, /device:TPU:0, one launch (start us, length us, event | category | flops | bytes accessed | tf_op | source)
XLA Modules:
  0.0 45.8 jit_solution(14703272126504842028)
XLA Ops:
  0.6 1.0 %shard_map.41.packed_ref.refs_0_ = bf16[128,1408]{1,0:T(8,128)(2,1)S(1)} custom-call(bf16[128,1024]{1,0:T(8,128)(2,1)} %t_hbm.1, bf16[128,384]{1,0:T(8,128)(2,1)} %s_hbm.1), custom_call_target="tpu_custom_call" | custom-call | bytes 360448 | tf_op jit(solution)/shard_map/pallas_call | solution.py:229
  1.6 4.1 %collective-permute-start.1 = (bf16[128,1408]{1,0:T(8,128)(2,1)S(1)}, bf16[128,1408]{1,0:T(8,128)(2,1)S(1)}, u32[]{:S(2)}, u32[]{:S(2)}) collective-permute-start(bf16[128,1408]{1,0:T(8,128)(2,1)S(1)} %shard_map.41.packed_ref.refs_0_), channel_id=1, source_target_pairs={{0,2},{2,3},{3,1},{1,0},{4,6},{6,7},{7,5},{5,4},{8,10},{10,11},{11... | collective-permute-start | bytes 1081352 | tf_op jit(solution)/shard_map/ppermute | solution.py:30
  5.7 1.5 %collective-permute-start = (bf16[128,1408]{1,0:T(8,128)(2,1)S(1)}, bf16[128,1408]{1,0:T(8,128)(2,1)S(1)}, u32[]{:S(2)}, u32[]{:S(2)}) collective-permute-start(bf16[128,1408]{1,0:T(8,128)(2,1)S(1)} %shard_map.41.packed_ref.refs_0_), channel_id=1, source_target_pairs={{0,8},{4,12},{8,0},{12,4},{1,9},{5,13},{9,1},{13,5},{2,10},{6,14},... | collective-permute-start | bytes 1081352 | tf_op jit(solution)/shard_map/ppermute | solution.py:23
  7.2 0.2 shard_map.42
  7.4 0.0 collective-permute-start.2
  7.4 1.9 %collective-permute-start.3 = (f32[1,1536]{1,0:T(1,128)S(1)}, f32[1,1536]{1,0:T(1,128)S(1)}, u32[]{:S(2)}, u32[]{:S(2)}) collective-permute-start(f32[1,1536]{1,0:T(1,128)S(1)} %shard_map.42), channel_id=1, source_target_pairs={{0,2},{1,3},{2,0},{3,1},{4,6},{5,7},{6,4},{7,5},{8,10},{9,11},{10,... | collective-permute-start | bytes 18440 | tf_op jit(solution)/shard_map/ppermute | solution.py:23
  9.3 2.5 %collective-permute-start.4 = (f32[1,1536]{1,0:T(1,128)S(1)}, f32[1,1536]{1,0:T(1,128)S(1)}, u32[]{:S(2)}, u32[]{:S(2)}) collective-permute-start(f32[1,1536]{1,0:T(1,128)S(1)} %shard_map.42), channel_id=1, source_target_pairs={{0,3},{1,2},{2,1},{3,0},{4,7},{5,6},{6,5},{7,4},{8,11},{9,10},{10,... | collective-permute-start | bytes 18440 | tf_op jit(solution)/shard_map/ppermute | solution.py:23
  11.8 1.9 %collective-permute-done.2 = f32[1,1536]{1,0:T(1,128)S(1)} collective-permute-done((f32[1,1536]{1,0:T(1,128)S(1)}, f32[1,1536]{1,0:T(1,128)S(1)}, u32[]{:S(2)}, u32[]{:S(2)}) %collective-permute-start.2) | collective-permute-done | bytes 6176 | tf_op jit(solution)/shard_map/ppermute | solution.py:23
  13.7 2.0 %collective-permute-done.3 = f32[1,1536]{1,0:T(1,128)S(1)} collective-permute-done((f32[1,1536]{1,0:T(1,128)S(1)}, f32[1,1536]{1,0:T(1,128)S(1)}, u32[]{:S(2)}, u32[]{:S(2)}) %collective-permute-start.3) | collective-permute-done | bytes 6176 | tf_op jit(solution)/shard_map/ppermute | solution.py:23
  15.7 0.0 collective-permute-done.4
  15.7 0.0 collective-permute-done.1.refs_4_
  15.7 1.6 %collective-permute-start.9 = (bf16[128,1408]{1,0:T(8,128)(2,1)S(1)}, bf16[128,1408]{1,0:T(8,128)(2,1)S(1)}, u32[]{:S(2)}, u32[]{:S(2)}) collective-permute-start(bf16[128,1408]{1,0:T(8,128)(2,1)S(1)} %collective-permute-done.1.refs_4_), channel_id=1, source_target_pairs={{0,2},{2,3},{3,1},{1,0},{4,6},{6,7},{7,5},{5,4},{8,10},{10,11},{11... | collective-permute-start | bytes 1081352 | tf_op jit(solution)/shard_map/ppermute | solution.py:30
  17.3 0.0 collective-permute-done.refs_1_
  17.3 0.5 %collective-permute-start.6 = (bf16[128,1408]{1,0:T(8,128)(2,1)S(1)}, bf16[128,1408]{1,0:T(8,128)(2,1)S(1)}, u32[]{:S(2)}, u32[]{:S(2)}) collective-permute-start(bf16[128,1408]{1,0:T(8,128)(2,1)S(1)} %collective-permute-done.refs_1_), channel_id=1, source_target_pairs={{0,4},{4,0},{8,12},{12,8},{1,5},{5,1},{9,13},{13,9},{2,6},{6,2},{1... | collective-permute-start | bytes 1081352 | tf_op jit(solution)/shard_map/ppermute | solution.py:23
  17.8 1.6 %collective-permute-start.7 = (f32[1,1536]{1,0:T(1,128)S(1)}, f32[1,1536]{1,0:T(1,128)S(1)}, u32[]{:S(2)}, u32[]{:S(2)}) collective-permute-start(f32[1,1536]{1,0:T(1,128)S(1)} %add_add_fusion), channel_id=1, source_target_pairs={{0,8},{4,12},{8,0},{12,4},{1,9},{5,13},{9,1},{13,5},{2,10},{6,14},... | collective-permute-start | bytes 18440 | tf_op jit(solution)/shard_map/ppermute | solution.py:23
  19.4 2.1 %collective-permute-done.7 = f32[1,1536]{1,0:T(1,128)S(1)} collective-permute-done((f32[1,1536]{1,0:T(1,128)S(1)}, f32[1,1536]{1,0:T(1,128)S(1)}, u32[]{:S(2)}, u32[]{:S(2)}) %collective-permute-start.7) | collective-permute-done | bytes 6176 | tf_op jit(solution)/shard_map/ppermute | solution.py:23
  21.5 0.1 collective-permute-start.8
  21.6 1.2 %collective-permute-done.8.refs_6_ = f32[1,1536]{1,0:T(1,128)S(1)} collective-permute-done((f32[1,1536]{1,0:T(1,128)S(1)}, f32[1,1536]{1,0:T(1,128)S(1)}, u32[]{:S(2)}, u32[]{:S(2)}) %collective-permute-start.8) | collective-permute-done | bytes 6176 | tf_op jit(solution)/shard_map/ppermute | solution.py:23
  22.8 0.0 collective-permute-done.5.refs_2_
  22.8 0.0 collective-permute-done.6.refs_3_
  22.8 2.3 %shard_map.43 = (f32[128,384]{1,0:T(8,128)S(1)}, f32[128,384]{1,0:T(8,128)S(1)}, f32[2,256,512]{2,1,0:T(8,128)S(1)}, f32[2,2,256,128]{3,2,1,0:T(8,128)S(1)}, f32...) custom-call(bf16[128,1408]{1,0:T(8,128)(2,1)S(1)} %shard_map.41.packed_ref.refs_0_, ...), custom_call_target="tpu_custom_call" | custom-call | flops 570425344 | bytes 1814528 | tf_op jit(solution)/shard_map/pallas_call | solution.py:229
  25.1 1.6 %shard_map.44 = (f32[256,384]{1,0:T(8,128)S(1)}, f32[256,384]{1,0:T(8,128)S(1)}, f32[8,2,128]{2,1,0:T(2,128)}) custom-call(bf16[2,256,1408]{2,1,0:T(8,128)(2,1)S(1)} %get-tuple-element.33.refs_0_, bf16[128,1408]{1,0:T(8,128)(2,1)S(1)} %collective-permute-done.9.refs_1_, f32[1,1536]{1,0:T(1,128)S(1)} %get-tuple-element.32.refs_2_.stats_ref, ...), custom_call_target="tpu_custom_call" | custom-call | flops 285212672 | bytes 3382272 | tf_op jit(solution)/shard_map/pallas_call | solution.py:229
  26.7 0.2 collective-permute-start.10
  26.9 5.4 %all-to-all-start = ((f32[8,2,128]{2,1,0:T(2,128)}), f32[8,2,128]{2,1,0:T(2,128)S(1)}, u32[]{:S(2)}, u32[]{:S(2)}) async-start(f32[8,2,128]{2,1,0:T(2,128)} %get-tuple-element.38), calls=%async_computation | async-start | bytes 16384 | tf_op jit(solution)/shard_map/all_to_all | solution.py:250
  32.3 2.0 %collective-permute-start.13 = (f32[128,384]{1,0:T(8,128)S(1)}, f32[128,384]{1,0:T(8,128)S(1)}, u32[]{:S(2)}, u32[]{:S(2)}) collective-permute-start(f32[128,384]{1,0:T(8,128)S(1)} %get-tuple-element.45), channel_id=1, source_target_pairs={{0,1},{2,0},{3,2},{1,3},{4,5},{6,4},{7,6},{5,7},{8,9},{10,8},{11,1... | collective-permute-start | bytes 589832 | tf_op jit(solution)/shard_map/ppermute | solution.py:30
  34.3 4.6 %all-to-all-done = f32[8,2,128]{2,1,0:T(2,128)S(1)} async-done(((f32[8,2,128]{2,1,0:T(2,128)}), f32[8,2,128]{2,1,0:T(2,128)S(1)}, u32[]{:S(2)}, u32[]{:S(2)}) %all-to-all-start) | async-done | bytes 8224 | tf_op jit(solution)/shard_map/all_to_all | solution.py:250
  39.0 0.6 %collective-permute-start.12 = (f32[128,384]{1,0:T(8,128)S(1)}, f32[128,384]{1,0:T(8,128)S(1)}, u32[]{:S(2)}, u32[]{:S(2)}) collective-permute-start(f32[128,384]{1,0:T(8,128)S(1)} %get-tuple-element.44), channel_id=1, source_target_pairs={{0,8},{4,12},{8,0},{12,4},{1,9},{5,13},{9,1},{13,5},{2,10},{6,14},... | collective-permute-start | bytes 589832 | tf_op jit(solution)/shard_map/ppermute | solution.py:23
  39.6 0.0 collective-permute-start.11
  39.6 1.0 %collective-permute-done.13.refs_3_ = f32[128,384]{1,0:T(8,128)S(1)} collective-permute-done((f32[128,384]{1,0:T(8,128)S(1)}, f32[128,384]{1,0:T(8,128)S(1)}, u32[]{:S(2)}, u32[]{:S(2)}) %collective-permute-start.13) | collective-permute-done | bytes 196640 | tf_op jit(solution)/shard_map/ppermute | solution.py:30
  40.6 0.2 collective-permute-done.11.other_ref
  40.7 4.2 %collective-permute-done.12.refs_2_ = f32[128,384]{1,0:T(8,128)S(1)} collective-permute-done((f32[128,384]{1,0:T(8,128)S(1)}, f32[128,384]{1,0:T(8,128)S(1)}, u32[]{:S(2)}, u32[]{:S(2)}) %collective-permute-start.12) | collective-permute-done | bytes 196640 | tf_op jit(solution)/shard_map/ppermute | solution.py:23
  44.9 0.9 %shard_map.46 = (f32[128,384]{1,0:T(8,128)}, f32[1,128]{1,0:T(1,128)}) custom-call(bf16[128,1408]{1,0:T(8,128)(2,1)S(1)} %shard_map.41.packed_ref.refs_0_, f32[1,1536]{1,0:T(1,128)S(1)} %get-tuple-element.32.refs_2_.stats_ref, f32[2,128]{1,0:T(2,128)S(1)} %reduce_sum.9.sums_ref, f32[2,128]{1,0:T(2,128)S(1)} %collective-permute-done.11.other_ref, ...), custom_call_target="tpu_custom_call" | custom-call | flops 393216 | bytes 1155072 | tf_op jit(solution)/shard_map/pallas_call | solution.py:229
  (7 shorter events, 0.1 us)
Async XLA Ops:
  1.6 14.0 %collective-permute-start.1 = (bf16[128,1408]{1,0:T(8,128)(2,1)S(1)}, bf16[128,1408]{1,0:T(8,128)(2,1)S(1)}, u32[]{:S(2)}, u32[]{:S(2)}) collective-permute-start(bf16[128,1408]{1,0:T(8,128)(2,1)S(1)} %shard_map.41.packed_ref.refs_0_), channel_id=1, source_target_pairs={{0,2},{2,3},{3,1},{1,0},{4,6},{6,7},{7,5},{5,4},{8,10},{10,11},{11... | collective-permute-start | bytes 1081352 | tf_op jit(solution)/shard_map/ppermute | solution.py:30
  5.7 11.6 %collective-permute-start = (bf16[128,1408]{1,0:T(8,128)(2,1)S(1)}, bf16[128,1408]{1,0:T(8,128)(2,1)S(1)}, u32[]{:S(2)}, u32[]{:S(2)}) collective-permute-start(bf16[128,1408]{1,0:T(8,128)(2,1)S(1)} %shard_map.41.packed_ref.refs_0_), channel_id=1, source_target_pairs={{0,8},{4,12},{8,0},{12,4},{1,9},{5,13},{9,1},{13,5},{2,10},{6,14},... | collective-permute-start | bytes 1081352 | tf_op jit(solution)/shard_map/ppermute | solution.py:23
  7.4 6.3 %collective-permute-start.2 = (f32[1,1536]{1,0:T(1,128)S(1)}, f32[1,1536]{1,0:T(1,128)S(1)}, u32[]{:S(2)}, u32[]{:S(2)}) collective-permute-start(f32[1,1536]{1,0:T(1,128)S(1)} %shard_map.42), channel_id=1, source_target_pairs={{0,1},{1,0},{2,3},{3,2},{4,5},{5,4},{6,7},{7,6},{8,9},{9,8},{10,11... | collective-permute-start | bytes 18440 | tf_op jit(solution)/shard_map/ppermute | solution.py:23
  7.4 8.2 %collective-permute-start.3 = (f32[1,1536]{1,0:T(1,128)S(1)}, f32[1,1536]{1,0:T(1,128)S(1)}, u32[]{:S(2)}, u32[]{:S(2)}) collective-permute-start(f32[1,1536]{1,0:T(1,128)S(1)} %shard_map.42), channel_id=1, source_target_pairs={{0,2},{1,3},{2,0},{3,1},{4,6},{5,7},{6,4},{7,5},{8,10},{9,11},{10,... | collective-permute-start | bytes 18440 | tf_op jit(solution)/shard_map/ppermute | solution.py:23
  9.3 6.3 %collective-permute-start.4 = (f32[1,1536]{1,0:T(1,128)S(1)}, f32[1,1536]{1,0:T(1,128)S(1)}, u32[]{:S(2)}, u32[]{:S(2)}) collective-permute-start(f32[1,1536]{1,0:T(1,128)S(1)} %shard_map.42), channel_id=1, source_target_pairs={{0,3},{1,2},{2,1},{3,0},{4,7},{5,6},{6,5},{7,4},{8,11},{9,10},{10,... | collective-permute-start | bytes 18440 | tf_op jit(solution)/shard_map/ppermute | solution.py:23
  15.7 9.4 %collective-permute-start.9 = (bf16[128,1408]{1,0:T(8,128)(2,1)S(1)}, bf16[128,1408]{1,0:T(8,128)(2,1)S(1)}, u32[]{:S(2)}, u32[]{:S(2)}) collective-permute-start(bf16[128,1408]{1,0:T(8,128)(2,1)S(1)} %collective-permute-done.1.refs_4_), channel_id=1, source_target_pairs={{0,2},{2,3},{3,1},{1,0},{4,6},{6,7},{7,5},{5,4},{8,10},{10,11},{11... | collective-permute-start | bytes 1081352 | tf_op jit(solution)/shard_map/ppermute | solution.py:30
  17.3 5.5 %collective-permute-start.5 = (bf16[128,1408]{1,0:T(8,128)(2,1)S(1)}, bf16[128,1408]{1,0:T(8,128)(2,1)S(1)}, u32[]{:S(2)}, u32[]{:S(2)}) collective-permute-start(bf16[128,1408]{1,0:T(8,128)(2,1)S(1)} %shard_map.41.packed_ref.refs_0_), channel_id=1, source_target_pairs={{0,4},{4,0},{8,12},{12,8},{1,5},{5,1},{9,13},{13,9},{2,6},{6,2},{1... | collective-permute-start | bytes 1081352 | tf_op jit(solution)/shard_map/ppermute | solution.py:23
  17.3 5.5 %collective-permute-start.6 = (bf16[128,1408]{1,0:T(8,128)(2,1)S(1)}, bf16[128,1408]{1,0:T(8,128)(2,1)S(1)}, u32[]{:S(2)}, u32[]{:S(2)}) collective-permute-start(bf16[128,1408]{1,0:T(8,128)(2,1)S(1)} %collective-permute-done.refs_1_), channel_id=1, source_target_pairs={{0,4},{4,0},{8,12},{12,8},{1,5},{5,1},{9,13},{13,9},{2,6},{6,2},{1... | collective-permute-start | bytes 1081352 | tf_op jit(solution)/shard_map/ppermute | solution.py:23
  17.8 3.7 %collective-permute-start.7 = (f32[1,1536]{1,0:T(1,128)S(1)}, f32[1,1536]{1,0:T(1,128)S(1)}, u32[]{:S(2)}, u32[]{:S(2)}) collective-permute-start(f32[1,1536]{1,0:T(1,128)S(1)} %add_add_fusion), channel_id=1, source_target_pairs={{0,8},{4,12},{8,0},{12,4},{1,9},{5,13},{9,1},{13,5},{2,10},{6,14},... | collective-permute-start | bytes 18440 | tf_op jit(solution)/shard_map/ppermute | solution.py:23
  21.5 1.2 %collective-permute-start.8 = (f32[1,1536]{1,0:T(1,128)S(1)}, f32[1,1536]{1,0:T(1,128)S(1)}, u32[]{:S(2)}, u32[]{:S(2)}) collective-permute-start(f32[1,1536]{1,0:T(1,128)S(1)} %add.15.refs_5_), channel_id=1, source_target_pairs={{0,4},{4,0},{8,12},{12,8},{1,5},{5,1},{9,13},{13,9},{2,6},{6,2},{1... | collective-permute-start | bytes 18440 | tf_op jit(solution)/shard_map/ppermute | solution.py:23
  26.7 12.2 %collective-permute-start.10 = (f32[256,384]{1,0:T(8,128)S(1)}, f32[256,384]{1,0:T(8,128)S(1)}, u32[]{:S(2)}, u32[]{:S(2)}) collective-permute-start(f32[256,384]{1,0:T(8,128)S(1)} %get-tuple-element.37), channel_id=1, source_target_pairs={{0,4},{4,0},{8,12},{12,8},{1,5},{5,1},{9,13},{13,9},{2,6},{6,2},{1... | collective-permute-start | bytes 1179656 | tf_op jit(solution)/shard_map/ppermute | solution.py:23
  26.9 12.0 %all-to-all-start = ((f32[8,2,128]{2,1,0:T(2,128)}), f32[8,2,128]{2,1,0:T(2,128)S(1)}, u32[]{:S(2)}, u32[]{:S(2)}) async-start(f32[8,2,128]{2,1,0:T(2,128)} %get-tuple-element.38), calls=%async_computation | async-start | bytes 16384 | tf_op jit(solution)/shard_map/all_to_all | solution.py:250
  32.3 8.3 %collective-permute-start.13 = (f32[128,384]{1,0:T(8,128)S(1)}, f32[128,384]{1,0:T(8,128)S(1)}, u32[]{:S(2)}, u32[]{:S(2)}) collective-permute-start(f32[128,384]{1,0:T(8,128)S(1)} %get-tuple-element.45), channel_id=1, source_target_pairs={{0,1},{2,0},{3,2},{1,3},{4,5},{6,4},{7,6},{5,7},{8,9},{10,8},{11,1... | collective-permute-start | bytes 589832 | tf_op jit(solution)/shard_map/ppermute | solution.py:30
  39.0 5.9 %collective-permute-start.12 = (f32[128,384]{1,0:T(8,128)S(1)}, f32[128,384]{1,0:T(8,128)S(1)}, u32[]{:S(2)}, u32[]{:S(2)}) collective-permute-start(f32[128,384]{1,0:T(8,128)S(1)} %get-tuple-element.44), channel_id=1, source_target_pairs={{0,8},{4,12},{8,0},{12,4},{1,9},{5,13},{9,1},{13,5},{2,10},{6,14},... | collective-permute-start | bytes 589832 | tf_op jit(solution)/shard_map/ppermute | solution.py:23
  39.6 1.1 %collective-permute-start.11 = (f32[2,128]{1,0:T(2,128)S(1)}, f32[2,128]{1,0:T(2,128)S(1)}, u32[]{:S(2)}, u32[]{:S(2)}) collective-permute-start(f32[2,128]{1,0:T(2,128)S(1)} %reduce_sum.9.sums_ref), channel_id=1, source_target_pairs={{0,4},{4,0},{8,12},{12,8},{1,5},{5,1},{9,13},{13,9},{2,6},{6,2},{1... | collective-permute-start | bytes 3080 | tf_op jit(solution)/shard_map/ppermute | solution.py:23

commit v13 on v9

--- a/solution.py
+++ b/solution.py
@@ -311,7 +311,9 @@
         sums = sums + exchange(sums, "blk", distance)
     got, sums = lax.optimization_barrier((got, sums))
     sums = sums + exchange(sums, "blk", 1)
-    all_sums = gathered(sums, "sub")
+    for distance in reversed(halvings("sub")):
+        all_sums = [sums, exchange(sums, "sub", distance)]
+        sums = sum(all_sums[1:], all_sums[0])
     tiles, distance = n_blk // 2, 2
     while tiles > 1:
         tiles //= 2

time: 42.5 us -> 42.3 us (level)
  waiting for transfers between devices: 12.2 us -> 11.4 us
  starting transfers between devices: 23.9 us -> 24.4 us
    ppermute x15 -> x14, waiting for transfers between devices: 12.2 us -> 11.4 us  [exchange(): return lax.ppermute(value, axis, [(i, i ^ distance) for i in range(size)])]
    ppermute x15 -> x14, starting transfers between devices: 15.9 us -> 16.5 us  [exchange(): return lax.ppermute(value, axis, [(i, i ^ distance) for i in range(size)])]
  transfers between devices with their start and end apart: 18 -> 17, of which waited for: 7 -> 7; matrix products, arithmetic and copies ran while one was open for 0% -> 0% of each run, Pallas kernels for 6% -> 6%
where the time goes in v13:
time: 42.3 us; the launch traced here: 42.1 us
  starting transfers between devices  24.4 us (58%)
  waiting for transfers between devices  11.4 us (27%)
  Pallas kernels  5.57 us (13%)
  between operations  0.7 us (2%)
    ppermute x14, starting transfers between devices, exchange(): return lax.ppermute(value, axis, [(i, i ^ distance) for i in range(size)])  16.5 us
    ppermute x14, waiting for transfers between devices, exchange(): return lax.ppermute(value, axis, [(i, i ^ distance) for i in range(size)])  11.4 us
    ppermute x3, starting transfers between devices, shifted(): return lax.ppermute(value, axis, route)  7.97 us
    pallas_call x6, Pallas kernels, call(): pl.pallas_call(kernel, out_shape=out_shape, in_specs=in_specs, out_specs=...  5.57 us
  transfers between devices with their start and end apart: 17, of which 7 were waited for; matrix products, arithmetic and copies ran while one was open for 0% of the time, Pallas kernels for 6%

profile of v13, /device:TPU:0, one launch (start us, length us, event | category | flops | bytes accessed | tf_op | source)
XLA Modules:
  0.0 42.1 jit_solution(16838979883404693554)
XLA Ops:
  0.6 1.0 %shard_map.41.packed_ref.refs_0_ = bf16[128,1408]{1,0:T(8,128)(2,1)S(1)} custom-call(bf16[128,1024]{1,0:T(8,128)(2,1)} %t_hbm.1, bf16[128,384]{1,0:T(8,128)(2,1)} %s_hbm.1), custom_call_target="tpu_custom_call" | custom-call | bytes 360448 | tf_op jit(solution)/shard_map/pallas_call | solution.py:227
  1.6 4.1 %collective-permute-start.1 = (bf16[128,1408]{1,0:T(8,128)(2,1)S(1)}, bf16[128,1408]{1,0:T(8,128)(2,1)S(1)}, u32[]{:S(2)}, u32[]{:S(2)}) collective-permute-start(bf16[128,1408]{1,0:T(8,128)(2,1)S(1)} %shard_map.41.packed_ref.refs_0_), channel_id=1, source_target_pairs={{0,2},{2,3},{3,1},{1,0},{4,6},{6,7},{7,5},{5,4},{8,10},{10,11},{11... | collective-permute-start | bytes 1081352 | tf_op jit(solution)/shard_map/ppermute | solution.py:26
  5.7 1.5 %collective-permute-start = (bf16[128,1408]{1,0:T(8,128)(2,1)S(1)}, bf16[128,1408]{1,0:T(8,128)(2,1)S(1)}, u32[]{:S(2)}, u32[]{:S(2)}) collective-permute-start(bf16[128,1408]{1,0:T(8,128)(2,1)S(1)} %shard_map.41.packed_ref.refs_0_), channel_id=1, source_target_pairs={{0,8},{4,12},{8,0},{12,4},{1,9},{5,13},{9,1},{13,5},{2,10},{6,14},... | collective-permute-start | bytes 1081352 | tf_op jit(solution)/shard_map/ppermute | solution.py:19
  7.2 0.2 shard_map.42
  7.4 1.9 %collective-permute-start.3 = (f32[1,1536]{1,0:T(1,128)S(1)}, f32[1,1536]{1,0:T(1,128)S(1)}, u32[]{:S(2)}, u32[]{:S(2)}) collective-permute-start(f32[1,1536]{1,0:T(1,128)S(1)} %shard_map.42), channel_id=1, source_target_pairs={{0,2},{1,3},{2,0},{3,1},{4,6},{5,7},{6,4},{7,5},{8,10},{9,11},{10,... | collective-permute-start | bytes 18440 | tf_op jit(solution)/shard_map/ppermute | solution.py:19
  9.3 2.5 %collective-permute-start.4 = (f32[1,1536]{1,0:T(1,128)S(1)}, f32[1,1536]{1,0:T(1,128)S(1)}, u32[]{:S(2)}, u32[]{:S(2)}) collective-permute-start(f32[1,1536]{1,0:T(1,128)S(1)} %shard_map.42), channel_id=1, source_target_pairs={{0,3},{1,2},{2,1},{3,0},{4,7},{5,6},{6,5},{7,4},{8,11},{9,10},{10,... | collective-permute-start | bytes 18440 | tf_op jit(solution)/shard_map/ppermute | solution.py:19
  11.8 1.9 %collective-permute-done.2 = f32[1,1536]{1,0:T(1,128)S(1)} collective-permute-done((f32[1,1536]{1,0:T(1,128)S(1)}, f32[1,1536]{1,0:T(1,128)S(1)}, u32[]{:S(2)}, u32[]{:S(2)}) %collective-permute-start.2) | collective-permute-done | bytes 6176 | tf_op jit(solution)/shard_map/ppermute | solution.py:19
  13.7 2.0 %collective-permute-done.3 = f32[1,1536]{1,0:T(1,128)S(1)} collective-permute-done((f32[1,1536]{1,0:T(1,128)S(1)}, f32[1,1536]{1,0:T(1,128)S(1)}, u32[]{:S(2)}, u32[]{:S(2)}) %collective-permute-start.3) | collective-permute-done | bytes 6176 | tf_op jit(solution)/shard_map/ppermute | solution.py:19
  15.7 0.0 collective-permute-done.4
  15.7 0.0 collective-permute-done.1.refs_4_
  15.7 1.6 %collective-permute-start.9 = (bf16[128,1408]{1,0:T(8,128)(2,1)S(1)}, bf16[128,1408]{1,0:T(8,128)(2,1)S(1)}, u32[]{:S(2)}, u32[]{:S(2)}) collective-permute-start(bf16[128,1408]{1,0:T(8,128)(2,1)S(1)} %collective-permute-done.1.refs_4_), channel_id=1, source_target_pairs={{0,2},{2,3},{3,1},{1,0},{4,6},{6,7},{7,5},{5,4},{8,10},{10,11},{11... | collective-permute-start | bytes 1081352 | tf_op jit(solution)/shard_map/ppermute | solution.py:26
  17.3 0.0 collective-permute-start.5
  17.3 0.5 %collective-permute-start.6 = (bf16[128,1408]{1,0:T(8,128)(2,1)S(1)}, bf16[128,1408]{1,0:T(8,128)(2,1)S(1)}, u32[]{:S(2)}, u32[]{:S(2)}) collective-permute-start(bf16[128,1408]{1,0:T(8,128)(2,1)S(1)} %collective-permute-done.refs_1_), channel_id=1, source_target_pairs={{0,4},{4,0},{8,12},{12,8},{1,5},{5,1},{9,13},{13,9},{2,6},{6,2},{1... | collective-permute-start | bytes 1081352 | tf_op jit(solution)/shard_map/ppermute | solution.py:19
  17.8 1.6 %collective-permute-start.7 = (f32[1,1536]{1,0:T(1,128)S(1)}, f32[1,1536]{1,0:T(1,128)S(1)}, u32[]{:S(2)}, u32[]{:S(2)}) collective-permute-start(f32[1,1536]{1,0:T(1,128)S(1)} %add_add_fusion), channel_id=1, source_target_pairs={{0,8},{4,12},{8,0},{12,4},{1,9},{5,13},{9,1},{13,5},{2,10},{6,14},... | collective-permute-start | bytes 18440 | tf_op jit(solution)/shard_map/ppermute | solution.py:19
  19.4 2.1 %collective-permute-done.7 = f32[1,1536]{1,0:T(1,128)S(1)} collective-permute-done((f32[1,1536]{1,0:T(1,128)S(1)}, f32[1,1536]{1,0:T(1,128)S(1)}, u32[]{:S(2)}, u32[]{:S(2)}) %collective-permute-start.7) | collective-permute-done | bytes 6176 | tf_op jit(solution)/shard_map/ppermute | solution.py:19
  21.5 0.1 collective-permute-start.8
  21.6 1.2 %collective-permute-done.8.refs_6_ = f32[1,1536]{1,0:T(1,128)S(1)} collective-permute-done((f32[1,1536]{1,0:T(1,128)S(1)}, f32[1,1536]{1,0:T(1,128)S(1)}, u32[]{:S(2)}, u32[]{:S(2)}) %collective-permute-start.8) | collective-permute-done | bytes 6176 | tf_op jit(solution)/shard_map/ppermute | solution.py:19
  22.8 0.0 collective-permute-done.5.refs_2_
  22.8 0.0 collective-permute-done.6.refs_3_
  22.8 2.3 %shard_map.43 = (f32[128,384]{1,0:T(8,128)S(1)}, f32[128,384]{1,0:T(8,128)S(1)}, f32[2,256,512]{2,1,0:T(8,128)S(1)}, f32[2,2,256,128]{3,2,1,0:T(8,128)S(1)}, f32...) custom-call(bf16[128,1408]{1,0:T(8,128)(2,1)S(1)} %shard_map.41.packed_ref.refs_0_, ...), custom_call_target="tpu_custom_call" | custom-call | flops 570425344 | bytes 1814528 | tf_op jit(solution)/shard_map/pallas_call | solution.py:227
  25.1 0.0 collective-permute-done.9.refs_1_
  25.1 1.2 %shard_map.44 = (f32[256,384]{1,0:T(8,128)S(1)}, f32[256,384]{1,0:T(8,128)S(1)}, f32[2,128]{1,0:T(2,128)S(1)}) custom-call(bf16[2,256,1408]{2,1,0:T(8,128)(2,1)S(1)} %get-tuple-element.34.refs_0_, bf16[128,1408]{1,0:T(8,128)(2,1)S(1)} %collective-permute-done.9.refs_1_, f32[1,1536]{1,0:T(1,128)S(1)} %get-tuple-element.32.refs_2_.stats_ref, ...), custom_call_target="tpu_custom_call" | custom-call | flops 285212672 | bytes 3382272 | tf_op jit(solution)/shard_map/pallas_call | solution.py:227
  26.3 0.2 collective-permute-start.10
  26.5 1.5 %collective-permute-start.11 = (f32[2,128]{1,0:T(2,128)S(1)}, f32[2,128]{1,0:T(2,128)S(1)}, u32[]{:S(2)}, u32[]{:S(2)}) collective-permute-start(f32[2,128]{1,0:T(2,128)S(1)} %get-tuple-element.40), channel_id=1, source_target_pairs={{0,8},{4,12},{8,0},{12,4},{1,9},{5,13},{9,1},{13,5},{2,10},{6,14},... | collective-permute-start | bytes 3080 | tf_op jit(solution)/shard_map/ppermute | solution.py:19
  28.1 2.2 %collective-permute-start.13 = (f32[128,384]{1,0:T(8,128)S(1)}, f32[128,384]{1,0:T(8,128)S(1)}, u32[]{:S(2)}, u32[]{:S(2)}) collective-permute-start(f32[128,384]{1,0:T(8,128)S(1)} %get-tuple-element.44), channel_id=1, source_target_pairs={{0,1},{2,0},{3,2},{1,3},{4,5},{6,4},{7,6},{5,7},{8,9},{10,8},{11,1... | collective-permute-start | bytes 589832 | tf_op jit(solution)/shard_map/ppermute | solution.py:26
  30.4 1.4 %collective-permute-start.12 = (f32[128,384]{1,0:T(8,128)S(1)}, f32[128,384]{1,0:T(8,128)S(1)}, u32[]{:S(2)}, u32[]{:S(2)}) collective-permute-start(f32[128,384]{1,0:T(8,128)S(1)} %get-tuple-element.43), channel_id=1, source_target_pairs={{0,8},{4,12},{8,0},{12,4},{1,9},{5,13},{9,1},{13,5},{2,10},{6,14},... | collective-permute-start | bytes 589832 | tf_op jit(solution)/shard_map/ppermute | solution.py:19
  31.8 1.1 %collective-permute-done.14 = f32[2,128]{1,0:T(2,128)S(1)} collective-permute-done((f32[2,128]{1,0:T(2,128)S(1)}, f32[2,128]{1,0:T(2,128)S(1)}, u32[]{:S(2)}, u32[]{:S(2)}) %collective-permute-start.14) | collective-permute-done | bytes 1056 | tf_op jit(solution)/shard_map/ppermute | solution.py:19
  32.9 2.2 %collective-permute-start.15 = (f32[2,128]{1,0:T(2,128)S(1)}, f32[2,128]{1,0:T(2,128)S(1)}, u32[]{:S(2)}, u32[]{:S(2)}) collective-permute-start(f32[2,128]{1,0:T(2,128)S(1)} %add.26), channel_id=1, source_target_pairs={{0,1},{1,0},{2,3},{3,2},{4,5},{5,4},{6,7},{7,6},{8,9},{9,8},{10,11... | collective-permute-start | bytes 3080 | tf_op jit(solution)/shard_map/ppermute | solution.py:19
  35.1 1.5 %collective-permute-done.15 = f32[2,128]{1,0:T(2,128)S(1)} collective-permute-done((f32[2,128]{1,0:T(2,128)S(1)}, f32[2,128]{1,0:T(2,128)S(1)}, u32[]{:S(2)}, u32[]{:S(2)}) %collective-permute-start.15) | collective-permute-done | bytes 1056 | tf_op jit(solution)/shard_map/ppermute | solution.py:19
  36.7 3.0 %collective-permute-start.16 = (f32[2,128]{1,0:T(2,128)S(1)}, f32[2,128]{1,0:T(2,128)S(1)}, u32[]{:S(2)}, u32[]{:S(2)}) collective-permute-start(f32[2,128]{1,0:T(2,128)S(1)} %add.27.refs_4_), channel_id=1, source_target_pairs={{0,2},{1,3},{2,0},{3,1},{4,6},{5,7},{6,4},{7,5},{8,10},{9,11},{10,... | collective-permute-start | bytes 3080 | tf_op jit(solution)/shard_map/ppermute | solution.py:19
  39.7 1.5 %collective-permute-done.16.refs_5_ = f32[2,128]{1,0:T(2,128)S(1)} collective-permute-done((f32[2,128]{1,0:T(2,128)S(1)}, f32[2,128]{1,0:T(2,128)S(1)}, u32[]{:S(2)}, u32[]{:S(2)}) %collective-permute-start.16) | collective-permute-done | bytes 1056 | tf_op jit(solution)/shard_map/ppermute | solution.py:19
  41.3 0.9 %shard_map.46 = (f32[128,384]{1,0:T(8,128)}, f32[1,128]{1,0:T(1,128)}) custom-call(bf16[128,1408]{1,0:T(8,128)(2,1)S(1)} %shard_map.41.packed_ref.refs_0_, f32[1,1536]{1,0:T(1,128)S(1)} %get-tuple-element.32.refs_2_.stats_ref, f32[128,384]{1,0:T(8,128)S(1)} %get-tuple-element.33.refs_0_, f32[128,384]{1,0:T(8,128)S(1)} %get-tuple-element.42.refs_1_, ...), custom_call_target="tpu_custom_call" | custom-call | flops 393216 | bytes 1155072 | tf_op jit(solution)/shard_map/pallas_call | solution.py:227
  (13 shorter events, 0.1 us)
Async XLA Ops:
  1.6 14.0 %collective-permute-start.1 = (bf16[128,1408]{1,0:T(8,128)(2,1)S(1)}, bf16[128,1408]{1,0:T(8,128)(2,1)S(1)}, u32[]{:S(2)}, u32[]{:S(2)}) collective-permute-start(bf16[128,1408]{1,0:T(8,128)(2,1)S(1)} %shard_map.41.packed_ref.refs_0_), channel_id=1, source_target_pairs={{0,2},{2,3},{3,1},{1,0},{4,6},{6,7},{7,5},{5,4},{8,10},{10,11},{11... | collective-permute-start | bytes 1081352 | tf_op jit(solution)/shard_map/ppermute | solution.py:26
  5.7 11.6 %collective-permute-start = (bf16[128,1408]{1,0:T(8,128)(2,1)S(1)}, bf16[128,1408]{1,0:T(8,128)(2,1)S(1)}, u32[]{:S(2)}, u32[]{:S(2)}) collective-permute-start(bf16[128,1408]{1,0:T(8,128)(2,1)S(1)} %shard_map.41.packed_ref.refs_0_), channel_id=1, source_target_pairs={{0,8},{4,12},{8,0},{12,4},{1,9},{5,13},{9,1},{13,5},{2,10},{6,14},... | collective-permute-start | bytes 1081352 | tf_op jit(solution)/shard_map/ppermute | solution.py:19
  7.4 6.3 %collective-permute-start.2 = (f32[1,1536]{1,0:T(1,128)S(1)}, f32[1,1536]{1,0:T(1,128)S(1)}, u32[]{:S(2)}, u32[]{:S(2)}) collective-permute-start(f32[1,1536]{1,0:T(1,128)S(1)} %shard_map.42), channel_id=1, source_target_pairs={{0,1},{1,0},{2,3},{3,2},{4,5},{5,4},{6,7},{7,6},{8,9},{9,8},{10,11... | collective-permute-start | bytes 18440 | tf_op jit(solution)/shard_map/ppermute | solution.py:19
  7.4 8.2 %collective-permute-start.3 = (f32[1,1536]{1,0:T(1,128)S(1)}, f32[1,1536]{1,0:T(1,128)S(1)}, u32[]{:S(2)}, u32[]{:S(2)}) collective-permute-start(f32[1,1536]{1,0:T(1,128)S(1)} %shard_map.42), channel_id=1, source_target_pairs={{0,2},{1,3},{2,0},{3,1},{4,6},{5,7},{6,4},{7,5},{8,10},{9,11},{10,... | collective-permute-start | bytes 18440 | tf_op jit(solution)/shard_map/ppermute | solution.py:19
  9.3 6.3 %collective-permute-start.4 = (f32[1,1536]{1,0:T(1,128)S(1)}, f32[1,1536]{1,0:T(1,128)S(1)}, u32[]{:S(2)}, u32[]{:S(2)}) collective-permute-start(f32[1,1536]{1,0:T(1,128)S(1)} %shard_map.42), channel_id=1, source_target_pairs={{0,3},{1,2},{2,1},{3,0},{4,7},{5,6},{6,5},{7,4},{8,11},{9,10},{10,... | collective-permute-start | bytes 18440 | tf_op jit(solution)/shard_map/ppermute | solution.py:19
  15.7 9.4 %collective-permute-start.9 = (bf16[128,1408]{1,0:T(8,128)(2,1)S(1)}, bf16[128,1408]{1,0:T(8,128)(2,1)S(1)}, u32[]{:S(2)}, u32[]{:S(2)}) collective-permute-start(bf16[128,1408]{1,0:T(8,128)(2,1)S(1)} %collective-permute-done.1.refs_4_), channel_id=1, source_target_pairs={{0,2},{2,3},{3,1},{1,0},{4,6},{6,7},{7,5},{5,4},{8,10},{10,11},{11... | collective-permute-start | bytes 1081352 | tf_op jit(solution)/shard_map/ppermute | solution.py:26
  17.3 5.5 %collective-permute-start.5 = (bf16[128,1408]{1,0:T(8,128)(2,1)S(1)}, bf16[128,1408]{1,0:T(8,128)(2,1)S(1)}, u32[]{:S(2)}, u32[]{:S(2)}) collective-permute-start(bf16[128,1408]{1,0:T(8,128)(2,1)S(1)} %shard_map.41.packed_ref.refs_0_), channel_id=1, source_target_pairs={{0,4},{4,0},{8,12},{12,8},{1,5},{5,1},{9,13},{13,9},{2,6},{6,2},{1... | collective-permute-start | bytes 1081352 | tf_op jit(solution)/shard_map/ppermute | solution.py:19
  17.3 5.5 %collective-permute-start.6 = (bf16[128,1408]{1,0:T(8,128)(2,1)S(1)}, bf16[128,1408]{1,0:T(8,128)(2,1)S(1)}, u32[]{:S(2)}, u32[]{:S(2)}) collective-permute-start(bf16[128,1408]{1,0:T(8,128)(2,1)S(1)} %collective-permute-done.refs_1_), channel_id=1, source_target_pairs={{0,4},{4,0},{8,12},{12,8},{1,5},{5,1},{9,13},{13,9},{2,6},{6,2},{1... | collective-permute-start | bytes 1081352 | tf_op jit(solution)/shard_map/ppermute | solution.py:19
  17.8 3.7 %collective-permute-start.7 = (f32[1,1536]{1,0:T(1,128)S(1)}, f32[1,1536]{1,0:T(1,128)S(1)}, u32[]{:S(2)}, u32[]{:S(2)}) collective-permute-start(f32[1,1536]{1,0:T(1,128)S(1)} %add_add_fusion), channel_id=1, source_target_pairs={{0,8},{4,12},{8,0},{12,4},{1,9},{5,13},{9,1},{13,5},{2,10},{6,14},... | collective-permute-start | bytes 18440 | tf_op jit(solution)/shard_map/ppermute | solution.py:19
  21.5 1.2 %collective-permute-start.8 = (f32[1,1536]{1,0:T(1,128)S(1)}, f32[1,1536]{1,0:T(1,128)S(1)}, u32[]{:S(2)}, u32[]{:S(2)}) collective-permute-start(f32[1,1536]{1,0:T(1,128)S(1)} %add.24.refs_5_), channel_id=1, source_target_pairs={{0,4},{4,0},{8,12},{12,8},{1,5},{5,1},{9,13},{13,9},{2,6},{6,2},{1... | collective-permute-start | bytes 18440 | tf_op jit(solution)/shard_map/ppermute | solution.py:19
  26.3 4.0 %collective-permute-start.10 = (f32[256,384]{1,0:T(8,128)S(1)}, f32[256,384]{1,0:T(8,128)S(1)}, u32[]{:S(2)}, u32[]{:S(2)}) collective-permute-start(f32[256,384]{1,0:T(8,128)S(1)} %get-tuple-element.39), channel_id=1, source_target_pairs={{0,4},{4,0},{8,12},{12,8},{1,5},{5,1},{9,13},{13,9},{2,6},{6,2},{1... | collective-permute-start | bytes 1179656 | tf_op jit(solution)/shard_map/ppermute | solution.py:19
  26.5 3.8 %collective-permute-start.11 = (f32[2,128]{1,0:T(2,128)S(1)}, f32[2,128]{1,0:T(2,128)S(1)}, u32[]{:S(2)}, u32[]{:S(2)}) collective-permute-start(f32[2,128]{1,0:T(2,128)S(1)} %get-tuple-element.40), channel_id=1, source_target_pairs={{0,8},{4,12},{8,0},{12,4},{1,9},{5,13},{9,1},{13,5},{2,10},{6,14},... | collective-permute-start | bytes 3080 | tf_op jit(solution)/shard_map/ppermute | solution.py:19
  28.1 11.6 %collective-permute-start.13 = (f32[128,384]{1,0:T(8,128)S(1)}, f32[128,384]{1,0:T(8,128)S(1)}, u32[]{:S(2)}, u32[]{:S(2)}) collective-permute-start(f32[128,384]{1,0:T(8,128)S(1)} %get-tuple-element.44), channel_id=1, source_target_pairs={{0,1},{2,0},{3,2},{1,3},{4,5},{6,4},{7,6},{5,7},{8,9},{10,8},{11,1... | collective-permute-start | bytes 589832 | tf_op jit(solution)/shard_map/ppermute | solution.py:26
  30.4 10.9 %collective-permute-start.12 = (f32[128,384]{1,0:T(8,128)S(1)}, f32[128,384]{1,0:T(8,128)S(1)}, u32[]{:S(2)}, u32[]{:S(2)}) collective-permute-start(f32[128,384]{1,0:T(8,128)S(1)} %get-tuple-element.43), channel_id=1, source_target_pairs={{0,8},{4,12},{8,0},{12,4},{1,9},{5,13},{9,1},{13,5},{2,10},{6,14},... | collective-permute-start | bytes 589832 | tf_op jit(solution)/shard_map/ppermute | solution.py:19
  31.7 1.1 %collective-permute-start.14 = (f32[2,128]{1,0:T(2,128)S(1)}, f32[2,128]{1,0:T(2,128)S(1)}, u32[]{:S(2)}, u32[]{:S(2)}) collective-permute-start(f32[2,128]{1,0:T(2,128)S(1)} %add.25), channel_id=1, source_target_pairs={{0,4},{4,0},{8,12},{12,8},{1,5},{5,1},{9,13},{13,9},{2,6},{6,2},{1... | collective-permute-start | bytes 3080 | tf_op jit(solution)/shard_map/ppermute | solution.py:19
  32.9 3.8 %collective-permute-start.15 = (f32[2,128]{1,0:T(2,128)S(1)}, f32[2,128]{1,0:T(2,128)S(1)}, u32[]{:S(2)}, u32[]{:S(2)}) collective-permute-start(f32[2,128]{1,0:T(2,128)S(1)} %add.26), channel_id=1, source_target_pairs={{0,1},{1,0},{2,3},{3,2},{4,5},{5,4},{6,7},{7,6},{8,9},{9,8},{10,11... | collective-permute-start | bytes 3080 | tf_op jit(solution)/shard_map/ppermute | solution.py:19
  36.7 4.6 %collective-permute-start.16 = (f32[2,128]{1,0:T(2,128)S(1)}, f32[2,128]{1,0:T(2,128)S(1)}, u32[]{:S(2)}, u32[]{:S(2)}) collective-permute-start(f32[2,128]{1,0:T(2,128)S(1)} %add.27.refs_4_), channel_id=1, source_target_pairs={{0,2},{1,3},{2,0},{3,1},{4,6},{5,7},{6,4},{7,5},{8,10},{9,11},{10,... | collective-permute-start | bytes 3080 | tf_op jit(solution)/shard_map/ppermute | solution.py:19

commit v14 on v7

--- a/solution.py
+++ b/solution.py
@@ -192,9 +192,8 @@
         back = jnp.dot(weights, with_ones(v[1]), preferred_element_type=jnp.float32)
         to_ref = (keep_ref, give_ref)[h]
         to_ref[at, :] = direct_of(cs, acc_ref[h, at, :] + back)
-    for i in range(sums_ref.shape[0]):
-        sums_ref[i, 0:1, :] = loss
-        sums_ref[i, 1:2, :] = spread
+    sums_ref[0:1, :] = loss
+    sums_ref[1:2, :] = spread
 
 
 def halve_kernel(rows, keep_ref, got_ref, *out_refs):
@@ -208,7 +207,7 @@
     for part in parts[1:]:
         direct = direct + part[...]
     s_width = direct.shape[1]
-    both = jnp.sum(jnp.sum(sums_ref[...], axis=0), axis=1, keepdims=True)
+    both = jnp.sum(sums_ref[...], axis=1, keepdims=True)
     loss_total, spread_total = both[0:1, :], -both[1:2, :]
     _, spread_s, centre = spreads_of(stats_ref[...], t_width, s_width, total_rows)
     pairs = total_rows * (total_rows - 1.0)
@@ -240,10 +239,6 @@
 def halvings(axis):
     size = lax.axis_size(axis)
     return [size >> i for i in range(1, size.bit_length())]
-
-
-def to_all(value):
-    return lax.all_to_all(value, ("blk", "sub"), 0, 0, tiled=True)
 
 
 def per_device(teacher, student):
@@ -304,7 +299,7 @@
     returned = [shifted(x, "sub", -k) for k, x in enumerate(backs, 1)]
     keep, give, sums = call(
         functools.partial(late_kernel, t_width, total_rows),
-        [f32((side, s_width))] * 2 + [f32((n_blk * n_sub, 2, LANES))],
+        [f32((side, s_width))] * 2 + [f32((2, LANES))],
         [plane, line[half], totals, acc, norms, early_sums],
         pair_flops,
     )
@@ -318,7 +313,7 @@
         )
         got = exchange(give, "blk", distance)
         distance *= 2
-    all_sums = to_all(sums)
+    all_sums = lax.psum(sums, ("blk", "sub"))
     parts = [own, keep, got] + returned
     grad, loss = call(
         functools.partial(final_kernel, t_width, total_rows),

time: 41.7 us -> 63 us (1.51)
  blocking collectives: 10.3 us -> 31.6 us
    psum x0 -> x1, blocking collectives: none -> 31.6 us  [per_device(): all_sums = lax.psum(sums, ('blk', 'sub'))]
    all_to_all x1 -> x0, blocking collectives: 10.3 us -> none  [to_all(): return lax.all_to_all(value, ('blk', 'sub'), 0, 0, tiled=True)]
  transfers between devices with their start and end apart: 13 -> 13, of which waited for: 4 -> 4; matrix products, arithmetic and copies ran while one was open for 0% -> 0% of each run, Pallas kernels for 6% -> 4%
where the time goes in v14:
time: 63 us; the launch traced here: 62.8 us
  blocking collectives  31.6 us (50%)
  starting transfers between devices  17.9 us (28%)
  waiting for transfers between devices  7.16 us (11%)
  Pallas kernels  5.47 us (9%)
  between operations  0.68 us (1%)
    psum x1, blocking collectives, per_device(): all_sums = lax.psum(sums, ('blk', 'sub'))  31.6 us
    ppermute x10, starting transfers between devices, exchange(): return lax.ppermute(value, axis, [(i, i ^ distance) for i in range(size)])  9.88 us
    ppermute x3, starting transfers between devices, shifted(): return lax.ppermute(value, axis, route)  8.01 us
    ppermute x10, waiting for transfers between devices, exchange(): return lax.ppermute(value, axis, [(i, i ^ distance) for i in range(size)])  7.14 us
    pallas_call x6, Pallas kernels, call(): pl.pallas_call(kernel, out_shape=out_shape, in_specs=in_specs, out_specs=...  5.47 us
  transfers between devices with their start and end apart: 13, of which 4 were waited for; matrix products, arithmetic and copies ran while one was open for 0% of the time, Pallas kernels for 4%

profile of v14, /device:TPU:0, one launch (start us, length us, event | category | flops | bytes accessed | tf_op | source)
XLA Modules:
  0.0 62.8 jit_solution(18107973522706858259)
XLA Ops:
  0.6 1.0 %shard_map.41.packed_ref.refs_0_ = bf16[128,1408]{1,0:T(8,128)(2,1)S(1)} custom-call(bf16[128,1024]{1,0:T(8,128)(2,1)} %t_hbm.1, bf16[128,384]{1,0:T(8,128)(2,1)} %s_hbm.1), custom_call_target="tpu_custom_call" | custom-call | bytes 360448 | tf_op jit(solution)/shard_map/pallas_call | solution.py:224
  1.6 4.1 %collective-permute-start.1 = (bf16[128,1408]{1,0:T(8,128)(2,1)S(1)}, bf16[128,1408]{1,0:T(8,128)(2,1)S(1)}, u32[]{:S(2)}, u32[]{:S(2)}) collective-permute-start(bf16[128,1408]{1,0:T(8,128)(2,1)S(1)} %shard_map.41.packed_ref.refs_0_), channel_id=1, source_target_pairs={{0,2},{2,3},{3,1},{1,0},{4,6},{6,7},{7,5},{5,4},{8,10},{10,11},{11... | collective-permute-start | bytes 1081352 | tf_op jit(solution)/shard_map/ppermute | solution.py:26
  5.7 1.5 %collective-permute-start = (bf16[128,1408]{1,0:T(8,128)(2,1)S(1)}, bf16[128,1408]{1,0:T(8,128)(2,1)S(1)}, u32[]{:S(2)}, u32[]{:S(2)}) collective-permute-start(bf16[128,1408]{1,0:T(8,128)(2,1)S(1)} %shard_map.41.packed_ref.refs_0_), channel_id=1, source_target_pairs={{0,8},{4,12},{8,0},{12,4},{1,9},{5,13},{9,1},{13,5},{2,10},{6,14},... | collective-permute-start | bytes 1081352 | tf_op jit(solution)/shard_map/ppermute | solution.py:19
  7.2 0.2 shard_map.42
  7.4 0.0 collective-permute-start.2
  7.4 1.9 %collective-permute-start.3 = (f32[1,1536]{1,0:T(1,128)S(1)}, f32[1,1536]{1,0:T(1,128)S(1)}, u32[]{:S(2)}, u32[]{:S(2)}) collective-permute-start(f32[1,1536]{1,0:T(1,128)S(1)} %shard_map.42), channel_id=1, source_target_pairs={{0,2},{1,3},{2,0},{3,1},{4,6},{5,7},{6,4},{7,5},{8,10},{9,11},{10,... | collective-permute-start | bytes 18440 | tf_op jit(solution)/shard_map/ppermute | solution.py:19
  9.3 2.5 %collective-permute-start.4 = (f32[1,1536]{1,0:T(1,128)S(1)}, f32[1,1536]{1,0:T(1,128)S(1)}, u32[]{:S(2)}, u32[]{:S(2)}) collective-permute-start(f32[1,1536]{1,0:T(1,128)S(1)} %shard_map.42), channel_id=1, source_target_pairs={{0,3},{1,2},{2,1},{3,0},{4,7},{5,6},{6,5},{7,4},{8,11},{9,10},{10,... | collective-permute-start | bytes 18440 | tf_op jit(solution)/shard_map/ppermute | solution.py:19
  11.8 1.9 %collective-permute-done.2 = f32[1,1536]{1,0:T(1,128)S(1)} collective-permute-done((f32[1,1536]{1,0:T(1,128)S(1)}, f32[1,1536]{1,0:T(1,128)S(1)}, u32[]{:S(2)}, u32[]{:S(2)}) %collective-permute-start.2) | collective-permute-done | bytes 6176 | tf_op jit(solution)/shard_map/ppermute | solution.py:19
  13.7 2.0 %collective-permute-done.3 = f32[1,1536]{1,0:T(1,128)S(1)} collective-permute-done((f32[1,1536]{1,0:T(1,128)S(1)}, f32[1,1536]{1,0:T(1,128)S(1)}, u32[]{:S(2)}, u32[]{:S(2)}) %collective-permute-start.3) | collective-permute-done | bytes 6176 | tf_op jit(solution)/shard_map/ppermute | solution.py:19
  15.7 0.0 collective-permute-done.4
  15.7 0.0 collective-permute-done.1.refs_4_
  15.7 1.6 %collective-permute-start.9 = (bf16[128,1408]{1,0:T(8,128)(2,1)S(1)}, bf16[128,1408]{1,0:T(8,128)(2,1)S(1)}, u32[]{:S(2)}, u32[]{:S(2)}) collective-permute-start(bf16[128,1408]{1,0:T(8,128)(2,1)S(1)} %collective-permute-done.1.refs_4_), channel_id=1, source_target_pairs={{0,2},{2,3},{3,1},{1,0},{4,6},{6,7},{7,5},{5,4},{8,10},{10,11},{11... | collective-permute-start | bytes 1081352 | tf_op jit(solution)/shard_map/ppermute | solution.py:26
  17.3 0.0 collective-permute-done.refs_1_
  17.3 0.0 collective-permute-start.5
  17.3 0.5 collective-permute-start.6
  17.8 1.6 %collective-permute-start.7 = (f32[1,1536]{1,0:T(1,128)S(1)}, f32[1,1536]{1,0:T(1,128)S(1)}, u32[]{:S(2)}, u32[]{:S(2)}) collective-permute-start(f32[1,1536]{1,0:T(1,128)S(1)} %add_add_fusion), channel_id=1, source_target_pairs={{0,8},{4,12},{8,0},{12,4},{1,9},{5,13},{9,1},{13,5},{2,10},{6,14},... | collective-permute-start | bytes 18440 | tf_op jit(solution)/shard_map/ppermute | solution.py:19
  19.4 2.1 %collective-permute-done.7 = f32[1,1536]{1,0:T(1,128)S(1)} collective-permute-done((f32[1,1536]{1,0:T(1,128)S(1)}, f32[1,1536]{1,0:T(1,128)S(1)}, u32[]{:S(2)}, u32[]{:S(2)}) %collective-permute-start.7) | collective-permute-done | bytes 6176 | tf_op jit(solution)/shard_map/ppermute | solution.py:19
  21.5 0.1 collective-permute-start.8
  21.6 1.2 %collective-permute-done.8.refs_6_ = f32[1,1536]{1,0:T(1,128)S(1)} collective-permute-done((f32[1,1536]{1,0:T(1,128)S(1)}, f32[1,1536]{1,0:T(1,128)S(1)}, u32[]{:S(2)}, u32[]{:S(2)}) %collective-permute-start.8) | collective-permute-done | bytes 6176 | tf_op jit(solution)/shard_map/ppermute | solution.py:19
  22.8 0.0 collective-permute-done.5.refs_2_
  22.8 0.0 collective-permute-done.6.refs_3_
  22.8 2.2 %shard_map.43 = (f32[128,384]{1,0:T(8,128)S(1)}, f32[128,384]{1,0:T(8,128)S(1)}, f32[2,256,512]{2,1,0:T(8,128)S(1)}, f32[2,2,256,128]{3,2,1,0:T(8,128)S(1)}, f32...) custom-call(bf16[128,1408]{1,0:T(8,128)(2,1)S(1)} %shard_map.41.packed_ref.refs_0_, ...), custom_call_target="tpu_custom_call" | custom-call | flops 570425344 | bytes 1814528 | tf_op jit(solution)/shard_map/pallas_call | solution.py:224
  25.0 0.0 collective-permute-done.9.refs_1_
  25.0 1.2 %shard_map.44 = (f32[256,384]{1,0:T(8,128)S(1)}, f32[256,384]{1,0:T(8,128)S(1)}, f32[2,128]{1,0:T(2,128)S(1)}) custom-call(bf16[2,256,1408]{2,1,0:T(8,128)(2,1)S(1)} %get-tuple-element.31.refs_0_, bf16[128,1408]{1,0:T(8,128)(2,1)S(1)} %collective-permute-done.9.refs_1_, f32[1,1536]{1,0:T(1,128)S(1)} %get-tuple-element.30.refs_2_.stats_ref, ...), custom_call_target="tpu_custom_call" | custom-call | flops 285212672 | bytes 3382272 | tf_op jit(solution)/shard_map/pallas_call | solution.py:224
  26.2 0.2 collective-permute-start.10
  26.5 2.3 %collective-permute-start.12 = (f32[128,384]{1,0:T(8,128)S(1)}, f32[128,384]{1,0:T(8,128)S(1)}, u32[]{:S(2)}, u32[]{:S(2)}) collective-permute-start(f32[128,384]{1,0:T(8,128)S(1)} %get-tuple-element.41), channel_id=1, source_target_pairs={{0,1},{2,0},{3,2},{1,3},{4,5},{6,4},{7,6},{5,7},{8,9},{10,8},{11,1... | collective-permute-start | bytes 589832 | tf_op jit(solution)/shard_map/ppermute | solution.py:26
  28.7 0.0 collective-permute-done.10.got_ref
  28.8 1.6 %collective-permute-start.11 = (f32[128,384]{1,0:T(8,128)S(1)}, f32[128,384]{1,0:T(8,128)S(1)}, u32[]{:S(2)}, u32[]{:S(2)}) collective-permute-start(f32[128,384]{1,0:T(8,128)S(1)} %get-tuple-element.40), channel_id=1, source_target_pairs={{0,8},{4,12},{8,0},{12,4},{1,9},{5,13},{9,1},{13,5},{2,10},{6,14},... | collective-permute-start | bytes 589832 | tf_op jit(solution)/shard_map/ppermute | solution.py:19
  30.4 31.6 %psum.7.sums_ref = f32[2,128]{1,0:T(2,128)S(1)} all-reduce(f32[2,128]{1,0:T(2,128)S(1)} %get-tuple-element.35), channel_id=1, replica_groups=mesh['groups'=2,'blk'=4,'sub'=4] {'blk','sub'}, use_global_device_ids=true, to_apply=%region_0.0 | all-reduce | flops 256 | bytes 2048 | tf_op jit(solution)/shard_map/psum | solution.py:316
  62.0 0.0 collective-permute-done.12.refs_3_
  62.0 0.0 collective-permute-done.11.refs_2_
  62.0 0.8 %shard_map.46 = (f32[128,384]{1,0:T(8,128)}, f32[1,128]{1,0:T(1,128)}) custom-call(bf16[128,1408]{1,0:T(8,128)(2,1)S(1)} %shard_map.41.packed_ref.refs_0_, f32[1,1536]{1,0:T(1,128)S(1)} %get-tuple-element.30.refs_2_.stats_ref, f32[2,128]{1,0:T(2,128)S(1)} %psum.7.sums_ref, f32[128,384]{1,0:T(8,128)S(1)} %get-tuple-element.36.refs_0_, ...), custom_call_target="tpu_custom_call" | custom-call | flops 393216 | bytes 1154048 | tf_op jit(solution)/shard_map/pallas_call | solution.py:224
  (3 shorter events, 0.1 us)
Async XLA Ops:
  1.6 14.0 %collective-permute-start.1 = (bf16[128,1408]{1,0:T(8,128)(2,1)S(1)}, bf16[128,1408]{1,0:T(8,128)(2,1)S(1)}, u32[]{:S(2)}, u32[]{:S(2)}) collective-permute-start(bf16[128,1408]{1,0:T(8,128)(2,1)S(1)} %shard_map.41.packed_ref.refs_0_), channel_id=1, source_target_pairs={{0,2},{2,3},{3,1},{1,0},{4,6},{6,7},{7,5},{5,4},{8,10},{10,11},{11... | collective-permute-start | bytes 1081352 | tf_op jit(solution)/shard_map/ppermute | solution.py:26
  5.7 11.6 %collective-permute-start = (bf16[128,1408]{1,0:T(8,128)(2,1)S(1)}, bf16[128,1408]{1,0:T(8,128)(2,1)S(1)}, u32[]{:S(2)}, u32[]{:S(2)}) collective-permute-start(bf16[128,1408]{1,0:T(8,128)(2,1)S(1)} %shard_map.41.packed_ref.refs_0_), channel_id=1, source_target_pairs={{0,8},{4,12},{8,0},{12,4},{1,9},{5,13},{9,1},{13,5},{2,10},{6,14},... | collective-permute-start | bytes 1081352 | tf_op jit(solution)/shard_map/ppermute | solution.py:19
  7.4 6.3 %collective-permute-start.2 = (f32[1,1536]{1,0:T(1,128)S(1)}, f32[1,1536]{1,0:T(1,128)S(1)}, u32[]{:S(2)}, u32[]{:S(2)}) collective-permute-start(f32[1,1536]{1,0:T(1,128)S(1)} %shard_map.42), channel_id=1, source_target_pairs={{0,1},{1,0},{2,3},{3,2},{4,5},{5,4},{6,7},{7,6},{8,9},{9,8},{10,11... | collective-permute-start | bytes 18440 | tf_op jit(solution)/shard_map/ppermute | solution.py:19
  7.4 8.2 %collective-permute-start.3 = (f32[1,1536]{1,0:T(1,128)S(1)}, f32[1,1536]{1,0:T(1,128)S(1)}, u32[]{:S(2)}, u32[]{:S(2)}) collective-permute-start(f32[1,1536]{1,0:T(1,128)S(1)} %shard_map.42), channel_id=1, source_target_pairs={{0,2},{1,3},{2,0},{3,1},{4,6},{5,7},{6,4},{7,5},{8,10},{9,11},{10,... | collective-permute-start | bytes 18440 | tf_op jit(solution)/shard_map/ppermute | solution.py:19
  9.3 6.3 %collective-permute-start.4 = (f32[1,1536]{1,0:T(1,128)S(1)}, f32[1,1536]{1,0:T(1,128)S(1)}, u32[]{:S(2)}, u32[]{:S(2)}) collective-permute-start(f32[1,1536]{1,0:T(1,128)S(1)} %shard_map.42), channel_id=1, source_target_pairs={{0,3},{1,2},{2,1},{3,0},{4,7},{5,6},{6,5},{7,4},{8,11},{9,10},{10,... | collective-permute-start | bytes 18440 | tf_op jit(solution)/shard_map/ppermute | solution.py:19
  15.7 9.4 %collective-permute-start.9 = (bf16[128,1408]{1,0:T(8,128)(2,1)S(1)}, bf16[128,1408]{1,0:T(8,128)(2,1)S(1)}, u32[]{:S(2)}, u32[]{:S(2)}) collective-permute-start(bf16[128,1408]{1,0:T(8,128)(2,1)S(1)} %collective-permute-done.1.refs_4_), channel_id=1, source_target_pairs={{0,2},{2,3},{3,1},{1,0},{4,6},{6,7},{7,5},{5,4},{8,10},{10,11},{11... | collective-permute-start | bytes 1081352 | tf_op jit(solution)/shard_map/ppermute | solution.py:26
  17.3 5.5 %collective-permute-start.5 = (bf16[128,1408]{1,0:T(8,128)(2,1)S(1)}, bf16[128,1408]{1,0:T(8,128)(2,1)S(1)}, u32[]{:S(2)}, u32[]{:S(2)}) collective-permute-start(bf16[128,1408]{1,0:T(8,128)(2,1)S(1)} %shard_map.41.packed_ref.refs_0_), channel_id=1, source_target_pairs={{0,4},{4,0},{8,12},{12,8},{1,5},{5,1},{9,13},{13,9},{2,6},{6,2},{1... | collective-permute-start | bytes 1081352 | tf_op jit(solution)/shard_map/ppermute | solution.py:19
  17.3 5.5 %collective-permute-start.6 = (bf16[128,1408]{1,0:T(8,128)(2,1)S(1)}, bf16[128,1408]{1,0:T(8,128)(2,1)S(1)}, u32[]{:S(2)}, u32[]{:S(2)}) collective-permute-start(bf16[128,1408]{1,0:T(8,128)(2,1)S(1)} %collective-permute-done.refs_1_), channel_id=1, source_target_pairs={{0,4},{4,0},{8,12},{12,8},{1,5},{5,1},{9,13},{13,9},{2,6},{6,2},{1... | collective-permute-start | bytes 1081352 | tf_op jit(solution)/shard_map/ppermute | solution.py:19
  17.8 3.7 %collective-permute-start.7 = (f32[1,1536]{1,0:T(1,128)S(1)}, f32[1,1536]{1,0:T(1,128)S(1)}, u32[]{:S(2)}, u32[]{:S(2)}) collective-permute-start(f32[1,1536]{1,0:T(1,128)S(1)} %add_add_fusion), channel_id=1, source_target_pairs={{0,8},{4,12},{8,0},{12,4},{1,9},{5,13},{9,1},{13,5},{2,10},{6,14},... | collective-permute-start | bytes 18440 | tf_op jit(solution)/shard_map/ppermute | solution.py:19
  21.5 1.2 %collective-permute-start.8 = (f32[1,1536]{1,0:T(1,128)S(1)}, f32[1,1536]{1,0:T(1,128)S(1)}, u32[]{:S(2)}, u32[]{:S(2)}) collective-permute-start(f32[1,1536]{1,0:T(1,128)S(1)} %add.17.refs_5_), channel_id=1, source_target_pairs={{0,4},{4,0},{8,12},{12,8},{1,5},{5,1},{9,13},{13,9},{2,6},{6,2},{1... | collective-permute-start | bytes 18440 | tf_op jit(solution)/shard_map/ppermute | solution.py:19
  26.2 2.5 %collective-permute-start.10 = (f32[256,384]{1,0:T(8,128)S(1)}, f32[256,384]{1,0:T(8,128)S(1)}, u32[]{:S(2)}, u32[]{:S(2)}) collective-permute-start(f32[256,384]{1,0:T(8,128)S(1)} %get-tuple-element.38), channel_id=1, source_target_pairs={{0,4},{4,0},{8,12},{12,8},{1,5},{5,1},{9,13},{13,9},{2,6},{6,2},{1... | collective-permute-start | bytes 1179656 | tf_op jit(solution)/shard_map/ppermute | solution.py:19
  26.5 35.5 %collective-permute-start.12 = (f32[128,384]{1,0:T(8,128)S(1)}, f32[128,384]{1,0:T(8,128)S(1)}, u32[]{:S(2)}, u32[]{:S(2)}) collective-permute-start(f32[128,384]{1,0:T(8,128)S(1)} %get-tuple-element.41), channel_id=1, source_target_pairs={{0,1},{2,0},{3,2},{1,3},{4,5},{6,4},{7,6},{5,7},{8,9},{10,8},{11,1... | collective-permute-start | bytes 589832 | tf_op jit(solution)/shard_map/ppermute | solution.py:26
  28.8 33.2 %collective-permute-start.11 = (f32[128,384]{1,0:T(8,128)S(1)}, f32[128,384]{1,0:T(8,128)S(1)}, u32[]{:S(2)}, u32[]{:S(2)}) collective-permute-start(f32[128,384]{1,0:T(8,128)S(1)} %get-tuple-element.40), channel_id=1, source_target_pairs={{0,8},{4,12},{8,0},{12,4},{1,9},{5,13},{9,1},{13,5},{2,10},{6,14},... | collective-permute-start | bytes 589832 | tf_op jit(solution)/shard_map/ppermute | solution.py:19

commit v15 on v7

--- a/solution.py
+++ b/solution.py
@@ -175,26 +175,33 @@
     sums_ref[1:2, :] = spread
 
 
-def late_kernel(t_width, total_rows, *refs):
-    plane_ref, ref, stats_ref, acc_ref, norm_ref, early_sums, keep_ref, give_ref, sums_ref = refs
-    s_width = keep_ref.shape[1]
+def late_kernel(side, t_width, total_rows, *refs):
+    if side:
+        plane_ref, ref, stats_ref, acc_ref, norm_ref, sums_in, out_ref, sums_ref, visit_ref = refs
+        v = visiting(ref, t_width)
+        visit_ref[0:1, :], visit_ref[1:2, :] = v[2:]
+    else:
+        plane_ref, ref, stats_ref, acc_ref, norm_ref, sums_in, visit_ref, out_ref, sums_ref = refs
+        v = (ref[:, :t_width], ref[:, t_width:], visit_ref[0:1, :], visit_ref[1:2, :])
+    s_width = out_ref.shape[1]
     spread_t, spread_s, _ = spreads_of(stats_ref[...], t_width, s_width, total_rows)
     inv_t, inv_s = 1.0 / spread_t, 1.0 / spread_s
-    loss = early_sums[0:1, :]
-    spread = early_sums[1:2, :]
-    v = visiting(ref, t_width)
+    loss = sums_in[0:1, :]
+    spread = sums_in[1:2, :]
     for h, at in chunks_of(plane_ref):
+        if h != side:
+            continue
         cs = plane_ref[h, at, t_width:]
         c = (plane_ref[h, at, :t_width], cs, norm_ref[h, 0, at, :], norm_ref[h, 1, at, :])
         weights, loss_part, spread_part = pair_tile(c, v, inv_t, inv_s, False)
         loss = loss + loss_part
         spread = spread + spread_part
         back = jnp.dot(weights, with_ones(v[1]), preferred_element_type=jnp.float32)
-        to_ref = (keep_ref, give_ref)[h]
-        to_ref[at, :] = direct_of(cs, acc_ref[h, at, :] + back)
-    for i in range(sums_ref.shape[0]):
-        sums_ref[i, 0:1, :] = loss
-        sums_ref[i, 1:2, :] = spread
+        out_ref[at, :] = direct_of(cs, acc_ref[h, at, :] + back)
+    for i in range(1 if side else sums_ref.shape[0]):
+        at = sums_ref if side else sums_ref.at[i]
+        at[0:1, :] = loss
+        at[1:2, :] = spread
 
 
 def halve_kernel(rows, keep_ref, got_ref, *out_refs):
@@ -302,11 +309,18 @@
     )
     own, backs = tiles[0], tiles[1:]
     returned = [shifted(x, "sub", -k) for k, x in enumerate(backs, 1)]
-    keep, give, sums = call(
-        functools.partial(late_kernel, t_width, total_rows),
-        [f32((side, s_width))] * 2 + [f32((n_blk * n_sub, 2, LANES))],
-        [plane, line[half], totals, acc, norms, early_sums],
-        pair_flops,
+    given = [plane, line[half], totals, acc, norms]
+    give, late_sums, visit_norms = call(
+        functools.partial(late_kernel, 1, t_width, total_rows),
+        [f32((side, s_width)), f32((2, LANES)), f32((2, rows))],
+        [*given, early_sums],
+        pair_flops // 2,
+    )
+    keep, sums = call(
+        functools.partial(late_kernel, 0, t_width, total_rows),
+        [f32((side, s_width)), f32((n_blk * n_sub, 2, LANES))],
+        [*given, late_sums, visit_norms],
+        pair_flops // 2,
     )
     got = exchange(give, "blk", 1)
     tiles, distance = n_blk // 2, 2

time: 41.7 us -> 41.6 us (level)
    pallas_call x6 -> x7, Pallas kernels: 5.55 us -> 5.61 us  [call(): pl.pallas_call(kernel, out_shape=out_shape, in_specs=in_specs, out_specs=...]
  transfers between devices with their start and end apart: 13 -> 13, of which waited for: 4 -> 4; matrix products, arithmetic and copies ran while one was open for 0% -> 0% of each run, Pallas kernels for 6% -> 7%
where the time goes in v15:
time: 41.6 us; the launch traced here: 41.5 us
  starting transfers between devices  17.9 us (43%)
  blocking collectives  10.1 us (24%)
  waiting for transfers between devices  7.16 us (17%)
  Pallas kernels  5.61 us (13%)
  between operations  0.7 us (2%)
    all_to_all x1, blocking collectives, to_all(): return lax.all_to_all(value, ('blk', 'sub'), 0, 0, tiled=True)  10.1 us
    ppermute x10, starting transfers between devices, exchange(): return lax.ppermute(value, axis, [(i, i ^ distance) for i in range(size)])  9.88 us
    ppermute x3, starting transfers between devices, shifted(): return lax.ppermute(value, axis, route)  8.02 us
    ppermute x10, waiting for transfers between devices, exchange(): return lax.ppermute(value, axis, [(i, i ^ distance) for i in range(size)])  7.14 us
    pallas_call x7, Pallas kernels, call(): pl.pallas_call(kernel, out_shape=out_shape, in_specs=in_specs, out_specs=...  5.61 us
  transfers between devices with their start and end apart: 13, of which 4 were waited for; matrix products, arithmetic and copies ran while one was open for 0% of the time, Pallas kernels for 7%

profile of v15, /device:TPU:0, one launch (start us, length us, event | category | flops | bytes accessed | tf_op | source)
XLA Modules:
  0.0 41.5 jit_solution(1784326689033635588)
XLA Ops:
  0.6 1.0 %shard_map.41.packed_ref.refs_0_ = bf16[128,1408]{1,0:T(8,128)(2,1)S(1)} custom-call(bf16[128,1024]{1,0:T(8,128)(2,1)} %t_hbm.1, bf16[128,384]{1,0:T(8,128)(2,1)} %s_hbm.1), custom_call_target="tpu_custom_call" | custom-call | bytes 360448 | tf_op jit(solution)/shard_map/pallas_call | solution.py:232
  1.6 4.1 %collective-permute-start.1 = (bf16[128,1408]{1,0:T(8,128)(2,1)S(1)}, bf16[128,1408]{1,0:T(8,128)(2,1)S(1)}, u32[]{:S(2)}, u32[]{:S(2)}) collective-permute-start(bf16[128,1408]{1,0:T(8,128)(2,1)S(1)} %shard_map.41.packed_ref.refs_0_), channel_id=1, source_target_pairs={{0,2},{2,3},{3,1},{1,0},{4,6},{6,7},{7,5},{5,4},{8,10},{10,11},{11... | collective-permute-start | bytes 1081352 | tf_op jit(solution)/shard_map/ppermute | solution.py:26
  5.7 1.5 %collective-permute-start = (bf16[128,1408]{1,0:T(8,128)(2,1)S(1)}, bf16[128,1408]{1,0:T(8,128)(2,1)S(1)}, u32[]{:S(2)}, u32[]{:S(2)}) collective-permute-start(bf16[128,1408]{1,0:T(8,128)(2,1)S(1)} %shard_map.41.packed_ref.refs_0_), channel_id=1, source_target_pairs={{0,8},{4,12},{8,0},{12,4},{1,9},{5,13},{9,1},{13,5},{2,10},{6,14},... | collective-permute-start | bytes 1081352 | tf_op jit(solution)/shard_map/ppermute | solution.py:19
  7.2 0.2 shard_map.42
  7.4 0.0 collective-permute-start.2
  7.4 1.9 %collective-permute-start.3 = (f32[1,1536]{1,0:T(1,128)S(1)}, f32[1,1536]{1,0:T(1,128)S(1)}, u32[]{:S(2)}, u32[]{:S(2)}) collective-permute-start(f32[1,1536]{1,0:T(1,128)S(1)} %shard_map.42), channel_id=1, source_target_pairs={{0,2},{1,3},{2,0},{3,1},{4,6},{5,7},{6,4},{7,5},{8,10},{9,11},{10,... | collective-permute-start | bytes 18440 | tf_op jit(solution)/shard_map/ppermute | solution.py:19
  9.3 2.5 %collective-permute-start.4 = (f32[1,1536]{1,0:T(1,128)S(1)}, f32[1,1536]{1,0:T(1,128)S(1)}, u32[]{:S(2)}, u32[]{:S(2)}) collective-permute-start(f32[1,1536]{1,0:T(1,128)S(1)} %shard_map.42), channel_id=1, source_target_pairs={{0,3},{1,2},{2,1},{3,0},{4,7},{5,6},{6,5},{7,4},{8,11},{9,10},{10,... | collective-permute-start | bytes 18440 | tf_op jit(solution)/shard_map/ppermute | solution.py:19
  11.8 1.9 %collective-permute-done.2 = f32[1,1536]{1,0:T(1,128)S(1)} collective-permute-done((f32[1,1536]{1,0:T(1,128)S(1)}, f32[1,1536]{1,0:T(1,128)S(1)}, u32[]{:S(2)}, u32[]{:S(2)}) %collective-permute-start.2) | collective-permute-done | bytes 6176 | tf_op jit(solution)/shard_map/ppermute | solution.py:19
  13.7 2.0 %collective-permute-done.3 = f32[1,1536]{1,0:T(1,128)S(1)} collective-permute-done((f32[1,1536]{1,0:T(1,128)S(1)}, f32[1,1536]{1,0:T(1,128)S(1)}, u32[]{:S(2)}, u32[]{:S(2)}) %collective-permute-start.3) | collective-permute-done | bytes 6176 | tf_op jit(solution)/shard_map/ppermute | solution.py:19
  15.7 0.0 collective-permute-done.4
  15.7 0.0 collective-permute-done.1.refs_4_
  15.7 1.6 %collective-permute-start.9 = (bf16[128,1408]{1,0:T(8,128)(2,1)S(1)}, bf16[128,1408]{1,0:T(8,128)(2,1)S(1)}, u32[]{:S(2)}, u32[]{:S(2)}) collective-permute-start(bf16[128,1408]{1,0:T(8,128)(2,1)S(1)} %collective-permute-done.1.refs_4_), channel_id=1, source_target_pairs={{0,2},{2,3},{3,1},{1,0},{4,6},{6,7},{7,5},{5,4},{8,10},{10,11},{11... | collective-permute-start | bytes 1081352 | tf_op jit(solution)/shard_map/ppermute | solution.py:26
  17.3 0.0 collective-permute-done.refs_1_
  17.3 0.5 %collective-permute-start.6 = (bf16[128,1408]{1,0:T(8,128)(2,1)S(1)}, bf16[128,1408]{1,0:T(8,128)(2,1)S(1)}, u32[]{:S(2)}, u32[]{:S(2)}) collective-permute-start(bf16[128,1408]{1,0:T(8,128)(2,1)S(1)} %collective-permute-done.refs_1_), channel_id=1, source_target_pairs={{0,4},{4,0},{8,12},{12,8},{1,5},{5,1},{9,13},{13,9},{2,6},{6,2},{1... | collective-permute-start | bytes 1081352 | tf_op jit(solution)/shard_map/ppermute | solution.py:19
  17.8 1.6 %collective-permute-start.7 = (f32[1,1536]{1,0:T(1,128)S(1)}, f32[1,1536]{1,0:T(1,128)S(1)}, u32[]{:S(2)}, u32[]{:S(2)}) collective-permute-start(f32[1,1536]{1,0:T(1,128)S(1)} %add_add_fusion), channel_id=1, source_target_pairs={{0,8},{4,12},{8,0},{12,4},{1,9},{5,13},{9,1},{13,5},{2,10},{6,14},... | collective-permute-start | bytes 18440 | tf_op jit(solution)/shard_map/ppermute | solution.py:19
  19.4 2.1 %collective-permute-done.7 = f32[1,1536]{1,0:T(1,128)S(1)} collective-permute-done((f32[1,1536]{1,0:T(1,128)S(1)}, f32[1,1536]{1,0:T(1,128)S(1)}, u32[]{:S(2)}, u32[]{:S(2)}) %collective-permute-start.7) | collective-permute-done | bytes 6176 | tf_op jit(solution)/shard_map/ppermute | solution.py:19
  21.5 0.1 collective-permute-start.8
  21.6 1.2 %collective-permute-done.8.refs_6_ = f32[1,1536]{1,0:T(1,128)S(1)} collective-permute-done((f32[1,1536]{1,0:T(1,128)S(1)}, f32[1,1536]{1,0:T(1,128)S(1)}, u32[]{:S(2)}, u32[]{:S(2)}) %collective-permute-start.8) | collective-permute-done | bytes 6176 | tf_op jit(solution)/shard_map/ppermute | solution.py:19
  22.8 0.0 collective-permute-done.5.refs_2_
  22.8 0.0 collective-permute-done.6.refs_3_
  22.8 2.2 %shard_map.43 = (f32[128,384]{1,0:T(8,128)S(1)}, f32[128,384]{1,0:T(8,128)S(1)}, f32[2,256,512]{2,1,0:T(8,128)S(1)}, f32[2,2,256,128]{3,2,1,0:T(8,128)S(1)}, f32...) custom-call(bf16[128,1408]{1,0:T(8,128)(2,1)S(1)} %shard_map.41.packed_ref.refs_0_, ...), custom_call_target="tpu_custom_call" | custom-call | flops 570425344 | bytes 1814528 | tf_op jit(solution)/shard_map/pallas_call | solution.py:232
  25.0 0.0 collective-permute-done.9.refs_1_
  25.0 0.7 %shard_map.44 = (f32[256,384]{1,0:T(8,128)S(1)}, f32[2,128]{1,0:T(2,128)S(1)}, f32[2,128]{1,0:T(2,128)S(1)}) custom-call(bf16[2,256,1408]{2,1,0:T(8,128)(2,1)S(1)} %get-tuple-element.33.refs_0_, bf16[128,1408]{1,0:T(8,128)(2,1)S(1)} %collective-permute-done.9.refs_1_, f32[1,1536]{1,0:T(1,128)S(1)} %get-tuple-element.32.refs_2_.stats_ref, ...), custom_call_target="tpu_custom_call" | custom-call | flops 142606336 | bytes 3382272 | tf_op jit(solution)/shard_map/pallas_call | solution.py:232
  25.7 0.2 collective-permute-start.10
  25.9 2.3 %collective-permute-start.12 = (f32[128,384]{1,0:T(8,128)S(1)}, f32[128,384]{1,0:T(8,128)S(1)}, u32[]{:S(2)}, u32[]{:S(2)}) collective-permute-start(f32[128,384]{1,0:T(8,128)S(1)} %get-tuple-element.45), channel_id=1, source_target_pairs={{0,1},{2,0},{3,2},{1,3},{4,5},{6,4},{7,6},{5,7},{8,9},{10,8},{11,1... | collective-permute-start | bytes 589832 | tf_op jit(solution)/shard_map/ppermute | solution.py:26
  28.2 0.7 %shard_map.45 = (f32[256,384]{1,0:T(8,128)S(1)}, f32[16,2,128]{2,1,0:T(2,128)S(1)}) custom-call(bf16[2,256,1408]{2,1,0:T(8,128)(2,1)S(1)} %get-tuple-element.33.refs_0_, bf16[128,1408]{1,0:T(8,128)(2,1)S(1)} %collective-permute-done.9.refs_1_, f32[1,1536]{1,0:T(1,128)S(1)} %get-tuple-element.32.refs_2_.stats_ref, ...), custom_call_target="tpu_custom_call" | custom-call | flops 142606336 | bytes 3383296 | tf_op jit(solution)/shard_map/pallas_call | solution.py:232
  28.9 0.0 collective-permute-done.10.got_ref
  28.9 1.6 %collective-permute-start.11 = (f32[128,384]{1,0:T(8,128)S(1)}, f32[128,384]{1,0:T(8,128)S(1)}, u32[]{:S(2)}, u32[]{:S(2)}) collective-permute-start(f32[128,384]{1,0:T(8,128)S(1)} %get-tuple-element.44), channel_id=1, source_target_pairs={{0,8},{4,12},{8,0},{12,4},{1,9},{5,13},{9,1},{13,5},{2,10},{6,14},... | collective-permute-start | bytes 589832 | tf_op jit(solution)/shard_map/ppermute | solution.py:19
  30.5 10.1 %all_to_all.5.sums_ref = f32[16,2,128]{2,1,0:T(2,128)S(1)} all-to-all(f32[16,2,128]{2,1,0:T(2,128)S(1)} %get-tuple-element.39), channel_id=1, replica_groups=mesh['groups'=2,'blk'=4,'sub'=4] {'blk','sub'}, dimensions={0} | all-to-all | bytes 32768 | tf_op jit(solution)/shard_map/all_to_all | solution.py:253
  40.6 0.0 collective-permute-done.12.refs_3_
  40.6 0.0 collective-permute-done.11.refs_2_
  40.6 0.9 %shard_map.47 = (f32[128,384]{1,0:T(8,128)}, f32[1,128]{1,0:T(1,128)}) custom-call(bf16[128,1408]{1,0:T(8,128)(2,1)S(1)} %shard_map.41.packed_ref.refs_0_, f32[1,1536]{1,0:T(1,128)S(1)} %get-tuple-element.32.refs_2_.stats_ref, f32[16,2,128]{2,1,0:T(2,128)S(1)} %all_to_all.5.sums_ref, f32[128,384]{1,0:T(8,128)S(1)} %get-tuple-element.40.refs_0_, ...), custom_call_target="tpu_custom_call" | custom-call | flops 393216 | bytes 1169408 | tf_op jit(solution)/shard_map/pallas_call | solution.py:232
  (4 shorter events, 0.1 us)
Async XLA Ops:
  1.6 14.0 %collective-permute-start.1 = (bf16[128,1408]{1,0:T(8,128)(2,1)S(1)}, bf16[128,1408]{1,0:T(8,128)(2,1)S(1)}, u32[]{:S(2)}, u32[]{:S(2)}) collective-permute-start(bf16[128,1408]{1,0:T(8,128)(2,1)S(1)} %shard_map.41.packed_ref.refs_0_), channel_id=1, source_target_pairs={{0,2},{2,3},{3,1},{1,0},{4,6},{6,7},{7,5},{5,4},{8,10},{10,11},{11... | collective-permute-start | bytes 1081352 | tf_op jit(solution)/shard_map/ppermute | solution.py:26
  5.7 11.6 %collective-permute-start = (bf16[128,1408]{1,0:T(8,128)(2,1)S(1)}, bf16[128,1408]{1,0:T(8,128)(2,1)S(1)}, u32[]{:S(2)}, u32[]{:S(2)}) collective-permute-start(bf16[128,1408]{1,0:T(8,128)(2,1)S(1)} %shard_map.41.packed_ref.refs_0_), channel_id=1, source_target_pairs={{0,8},{4,12},{8,0},{12,4},{1,9},{5,13},{9,1},{13,5},{2,10},{6,14},... | collective-permute-start | bytes 1081352 | tf_op jit(solution)/shard_map/ppermute | solution.py:19
  7.4 6.3 %collective-permute-start.2 = (f32[1,1536]{1,0:T(1,128)S(1)}, f32[1,1536]{1,0:T(1,128)S(1)}, u32[]{:S(2)}, u32[]{:S(2)}) collective-permute-start(f32[1,1536]{1,0:T(1,128)S(1)} %shard_map.42), channel_id=1, source_target_pairs={{0,1},{1,0},{2,3},{3,2},{4,5},{5,4},{6,7},{7,6},{8,9},{9,8},{10,11... | collective-permute-start | bytes 18440 | tf_op jit(solution)/shard_map/ppermute | solution.py:19
  7.4 8.2 %collective-permute-start.3 = (f32[1,1536]{1,0:T(1,128)S(1)}, f32[1,1536]{1,0:T(1,128)S(1)}, u32[]{:S(2)}, u32[]{:S(2)}) collective-permute-start(f32[1,1536]{1,0:T(1,128)S(1)} %shard_map.42), channel_id=1, source_target_pairs={{0,2},{1,3},{2,0},{3,1},{4,6},{5,7},{6,4},{7,5},{8,10},{9,11},{10,... | collective-permute-start | bytes 18440 | tf_op jit(solution)/shard_map/ppermute | solution.py:19
  9.3 6.3 %collective-permute-start.4 = (f32[1,1536]{1,0:T(1,128)S(1)}, f32[1,1536]{1,0:T(1,128)S(1)}, u32[]{:S(2)}, u32[]{:S(2)}) collective-permute-start(f32[1,1536]{1,0:T(1,128)S(1)} %shard_map.42), channel_id=1, source_target_pairs={{0,3},{1,2},{2,1},{3,0},{4,7},{5,6},{6,5},{7,4},{8,11},{9,10},{10,... | collective-permute-start | bytes 18440 | tf_op jit(solution)/shard_map/ppermute | solution.py:19
  15.7 9.4 %collective-permute-start.9 = (bf16[128,1408]{1,0:T(8,128)(2,1)S(1)}, bf16[128,1408]{1,0:T(8,128)(2,1)S(1)}, u32[]{:S(2)}, u32[]{:S(2)}) collective-permute-start(bf16[128,1408]{1,0:T(8,128)(2,1)S(1)} %collective-permute-done.1.refs_4_), channel_id=1, source_target_pairs={{0,2},{2,3},{3,1},{1,0},{4,6},{6,7},{7,5},{5,4},{8,10},{10,11},{11... | collective-permute-start | bytes 1081352 | tf_op jit(solution)/shard_map/ppermute | solution.py:26
  17.3 5.5 %collective-permute-start.5 = (bf16[128,1408]{1,0:T(8,128)(2,1)S(1)}, bf16[128,1408]{1,0:T(8,128)(2,1)S(1)}, u32[]{:S(2)}, u32[]{:S(2)}) collective-permute-start(bf16[128,1408]{1,0:T(8,128)(2,1)S(1)} %shard_map.41.packed_ref.refs_0_), channel_id=1, source_target_pairs={{0,4},{4,0},{8,12},{12,8},{1,5},{5,1},{9,13},{13,9},{2,6},{6,2},{1... | collective-permute-start | bytes 1081352 | tf_op jit(solution)/shard_map/ppermute | solution.py:19
  17.3 5.5 %collective-permute-start.6 = (bf16[128,1408]{1,0:T(8,128)(2,1)S(1)}, bf16[128,1408]{1,0:T(8,128)(2,1)S(1)}, u32[]{:S(2)}, u32[]{:S(2)}) collective-permute-start(bf16[128,1408]{1,0:T(8,128)(2,1)S(1)} %collective-permute-done.refs_1_), channel_id=1, source_target_pairs={{0,4},{4,0},{8,12},{12,8},{1,5},{5,1},{9,13},{13,9},{2,6},{6,2},{1... | collective-permute-start | bytes 1081352 | tf_op jit(solution)/shard_map/ppermute | solution.py:19
  17.8 3.7 %collective-permute-start.7 = (f32[1,1536]{1,0:T(1,128)S(1)}, f32[1,1536]{1,0:T(1,128)S(1)}, u32[]{:S(2)}, u32[]{:S(2)}) collective-permute-start(f32[1,1536]{1,0:T(1,128)S(1)} %add_add_fusion), channel_id=1, source_target_pairs={{0,8},{4,12},{8,0},{12,4},{1,9},{5,13},{9,1},{13,5},{2,10},{6,14},... | collective-permute-start | bytes 18440 | tf_op jit(solution)/shard_map/ppermute | solution.py:19
  21.5 1.2 %collective-permute-start.8 = (f32[1,1536]{1,0:T(1,128)S(1)}, f32[1,1536]{1,0:T(1,128)S(1)}, u32[]{:S(2)}, u32[]{:S(2)}) collective-permute-start(f32[1,1536]{1,0:T(1,128)S(1)} %add.15.refs_5_), channel_id=1, source_target_pairs={{0,4},{4,0},{8,12},{12,8},{1,5},{5,1},{9,13},{13,9},{2,6},{6,2},{1... | collective-permute-start | bytes 18440 | tf_op jit(solution)/shard_map/ppermute | solution.py:19
  25.7 3.2 %collective-permute-start.10 = (f32[256,384]{1,0:T(8,128)S(1)}, f32[256,384]{1,0:T(8,128)S(1)}, u32[]{:S(2)}, u32[]{:S(2)}) collective-permute-start(f32[256,384]{1,0:T(8,128)S(1)} %get-tuple-element.42), channel_id=1, source_target_pairs={{0,4},{4,0},{8,12},{12,8},{1,5},{5,1},{9,13},{13,9},{2,6},{6,2},{1... | collective-permute-start | bytes 1179656 | tf_op jit(solution)/shard_map/ppermute | solution.py:19
  25.9 14.7 %collective-permute-start.12 = (f32[128,384]{1,0:T(8,128)S(1)}, f32[128,384]{1,0:T(8,128)S(1)}, u32[]{:S(2)}, u32[]{:S(2)}) collective-permute-start(f32[128,384]{1,0:T(8,128)S(1)} %get-tuple-element.45), channel_id=1, source_target_pairs={{0,1},{2,0},{3,2},{1,3},{4,5},{6,4},{7,6},{5,7},{8,9},{10,8},{11,1... | collective-permute-start | bytes 589832 | tf_op jit(solution)/shard_map/ppermute | solution.py:26
  28.9 11.6 %collective-permute-start.11 = (f32[128,384]{1,0:T(8,128)S(1)}, f32[128,384]{1,0:T(8,128)S(1)}, u32[]{:S(2)}, u32[]{:S(2)}) collective-permute-start(f32[128,384]{1,0:T(8,128)S(1)} %get-tuple-element.44), channel_id=1, source_target_pairs={{0,8},{4,12},{8,0},{12,4},{1,9},{5,13},{9,1},{13,5},{2,10},{6,14},... | collective-permute-start | bytes 589832 | tf_op jit(solution)/shard_map/ppermute | solution.py:19

commit v16 on v15

--- a/solution.py
+++ b/solution.py
@@ -11,6 +11,7 @@
 EPSILON = 1e-06
 LANES = 128
 CHUNK = 256
+PIECES = 4
 WHOLE = pl.BlockSpec(memory_space=pltpu.VMEM)
 
 
@@ -28,10 +29,13 @@
 
 def pack_kernel(t_hbm, s_hbm, packed_ref, sems):
     t_width = t_hbm.shape[1]
-    copies = [
-        pltpu.make_async_copy(t_hbm, packed_ref.at[:, :t_width], sems.at[0]),
-        pltpu.make_async_copy(s_hbm, packed_ref.at[:, t_width:], sems.at[1]),
-    ]
+    rows = t_hbm.shape[0] // PIECES
+    copies = []
+    for i in range(PIECES):
+        at = pl.ds(i * rows, rows)
+        to_t, to_s = packed_ref.at[at, :t_width], packed_ref.at[at, t_width:]
+        copies.append(pltpu.make_async_copy(t_hbm.at[at, :], to_t, sems.at[0, i]))
+        copies.append(pltpu.make_async_copy(s_hbm.at[at, :], to_s, sems.at[1, i]))
     for copy in copies:
         copy.start()
     for copy in copies:
@@ -138,9 +142,11 @@
     stats = stats_refs[0][...]
     for ref in stats_refs[1:]:
         stats = stats + ref[...]
-    total_ref[...] = stats
-    spread_t, spread_s, _ = spreads_of(stats, t_width, s_width, total_rows)
+    spread_t, spread_s, centre_s = spreads_of(stats, t_width, s_width, total_rows)
     inv_t, inv_s = 1.0 / spread_t, 1.0 / spread_s
+    for row, value in enumerate((inv_t, inv_s, spread_s)):
+        total_ref[row : row + 1, :] = jnp.broadcast_to(value, (1, s_width))
+    total_ref[3:4, :] = centre_s
     loss = jnp.zeros((1, LANES), jnp.float32)
     spread = jnp.zeros((1, LANES), jnp.float32)
     if steps == 1:
@@ -175,7 +181,7 @@
     sums_ref[1:2, :] = spread
 
 
-def late_kernel(side, t_width, total_rows, *refs):
+def late_kernel(side, t_width, *refs):
     if side:
         plane_ref, ref, stats_ref, acc_ref, norm_ref, sums_in, out_ref, sums_ref, visit_ref = refs
         v = visiting(ref, t_width)
@@ -183,9 +189,7 @@
     else:
         plane_ref, ref, stats_ref, acc_ref, norm_ref, sums_in, visit_ref, out_ref, sums_ref = refs
         v = (ref[:, :t_width], ref[:, t_width:], visit_ref[0:1, :], visit_ref[1:2, :])
-    s_width = out_ref.shape[1]
-    spread_t, spread_s, _ = spreads_of(stats_ref[...], t_width, s_width, total_rows)
-    inv_t, inv_s = 1.0 / spread_t, 1.0 / spread_s
+    inv_t, inv_s = stats_ref[0:1, :LANES], stats_ref[1:2, :LANES]
     loss = sums_in[0:1, :]
     spread = sums_in[1:2, :]
     for h, at in chunks_of(plane_ref):
@@ -210,19 +214,26 @@
 
 
 def final_kernel(t_width, total_rows, packed_ref, stats_ref, sums_ref, *refs):
-    *parts, grad_ref, loss_ref = refs
-    direct = parts[0][...]
-    for part in parts[1:]:
-        direct = direct + part[...]
-    s_width = direct.shape[1]
+    *parts, grad_hbm, loss_ref, grad_ref, sems = refs
     both = jnp.sum(jnp.sum(sums_ref[...], axis=0), axis=1, keepdims=True)
     loss_total, spread_total = both[0:1, :], -both[1:2, :]
-    _, spread_s, centre = spreads_of(stats_ref[...], t_width, s_width, total_rows)
+    spread_s, centre = stats_ref[2:3, :], stats_ref[3:4, :]
     pairs = total_rows * (total_rows - 1.0)
     correction = 2.0 * spread_total / (pairs * spread_s * spread_s)
-    student = packed_ref[:, t_width:].astype(jnp.float32)
-    grad_ref[...] = (2.0 / (total_rows - 1.0)) * direct + correction * (student - centre)
+    copies = []
+    rows = grad_ref.shape[0] // PIECES
+    for i in range(PIECES):
+        at = pl.ds(i * rows, rows)
+        direct = parts[0][at, :]
+        for part in parts[1:]:
+            direct = direct + part[at, :]
+        student = packed_ref[at, t_width:].astype(jnp.float32)
+        grad_ref[at, :] = (2.0 / (total_rows - 1.0)) * direct + correction * (student - centre)
+        copies.append(pltpu.make_async_copy(grad_ref.at[at, :], grad_hbm.at[at, :], sems.at[i]))
+        copies[-1].start()
     loss_ref[...] = jnp.broadcast_to(loss_total / pairs, loss_ref.shape)
+    for copy in copies:
+        copy.wait()
 
 
 def call(kernel, out_shape, operands, flops, vmem=48, **more):
@@ -271,7 +282,7 @@
         0,
         vmem=48,
         in_specs=[pl.BlockSpec(memory_space=pl.ANY)] * 2,
-        scratch_shapes=[pltpu.SemaphoreType.DMA((2,))],
+        scratch_shapes=[pltpu.SemaphoreType.DMA((2, PIECES))],
     )
     stats = call(
         functools.partial(stats_kernel, t_width),
@@ -298,7 +309,7 @@
     out_shape = (
         [f32((rows, s_width))] * half
         + [f32((2, side, s_width + LANES)), f32((2, 2, side, LANES))]
-        + [f32(stats[0].shape), f32((2, LANES))]
+        + [f32((4, s_width)), f32((2, LANES))]
         + [jax.ShapeDtypeStruct((2, side, t_width + s_width), packed.dtype)]
     )
     *tiles, acc, norms, totals, early_sums, plane = call(
@@ -311,13 +322,13 @@
     returned = [shifted(x, "sub", -k) for k, x in enumerate(backs, 1)]
     given = [plane, line[half], totals, acc, norms]
     give, late_sums, visit_norms = call(
-        functools.partial(late_kernel, 1, t_width, total_rows),
+        functools.partial(late_kernel, 1, t_width),
         [f32((side, s_width)), f32((2, LANES)), f32((2, rows))],
         [*given, early_sums],
         pair_flops // 2,
     )
     keep, sums = call(
-        functools.partial(late_kernel, 0, t_width, total_rows),
+        functools.partial(late_kernel, 0, t_width),
         [f32((side, s_width)), f32((n_blk * n_sub, 2, LANES))],
         [*given, late_sums, visit_norms],
         pair_flops // 2,
@@ -339,6 +350,11 @@
         [f32((rows, s_width)), f32((1, LANES))],
         [packed, totals, all_sums] + parts,
         8 * student.size,
+        out_specs=[pl.BlockSpec(memory_space=pl.ANY), WHOLE],
+        scratch_shapes=[
+            pltpu.VMEM((rows, s_width), jnp.float32),
+            pltpu.SemaphoreType.DMA((PIECES,)),
+        ],
     )
     return grad, loss[0, :1]
 

time: 41.6 us -> 42.2 us (1.014)
  Pallas kernels: 5.61 us -> 6.12 us
    pallas_call x7, Pallas kernels: 5.61 us -> 6.12 us  [call(): pl.pallas_call(kernel, out_shape=out_shape, in_specs=in_specs, out_specs=...]
where the time goes in v16:
time: 42.2 us; the launch traced here: 42 us
  starting transfers between devices  17.9 us (42%)
  blocking collectives  10.1 us (24%)
  waiting for transfers between devices  7.16 us (17%)
  Pallas kernels  6.12 us (15%)
  between operations  0.7 us (2%)
    all_to_all x1, blocking collectives, to_all(): return lax.all_to_all(value, ('blk', 'sub'), 0, 0, tiled=True)  10.1 us
    ppermute x10, starting transfers between devices, exchange(): return lax.ppermute(value, axis, [(i, i ^ distance) for i in range(size)])  9.89 us
    ppermute x3, starting transfers between devices, shifted(): return lax.ppermute(value, axis, route)  8 us
    ppermute x10, waiting for transfers between devices, exchange(): return lax.ppermute(value, axis, [(i, i ^ distance) for i in range(size)])  7.14 us
    pallas_call x7, Pallas kernels, call(): pl.pallas_call(kernel, out_shape=out_shape, in_specs=in_specs, out_specs=...  6.12 us
  transfers between devices with their start and end apart: 13, of which 4 were waited for; matrix products, arithmetic and copies ran while one was open for 0% of the time, Pallas kernels for 7%

profile of v16, /device:TPU:0, one launch (start us, length us, event | category | flops | bytes accessed | tf_op | source)
XLA Modules:
  0.0 42.0 jit_solution(12897473081968132136)
XLA Ops:
  0.6 1.1 %shard_map.41.packed_ref.refs_0_ = bf16[128,1408]{1,0:T(8,128)(2,1)S(1)} custom-call(bf16[128,1024]{1,0:T(8,128)(2,1)} %t_hbm.1, bf16[128,384]{1,0:T(8,128)(2,1)} %s_hbm.1), custom_call_target="tpu_custom_call" | custom-call | bytes 360448 | tf_op jit(solution)/shard_map/pallas_call | solution.py:243
  1.7 4.1 %collective-permute-start.1 = (bf16[128,1408]{1,0:T(8,128)(2,1)S(1)}, bf16[128,1408]{1,0:T(8,128)(2,1)S(1)}, u32[]{:S(2)}, u32[]{:S(2)}) collective-permute-start(bf16[128,1408]{1,0:T(8,128)(2,1)S(1)} %shard_map.41.packed_ref.refs_0_), channel_id=1, source_target_pairs={{0,2},{2,3},{3,1},{1,0},{4,6},{6,7},{7,5},{5,4},{8,10},{10,11},{11... | collective-permute-start | bytes 1081352 | tf_op jit(solution)/shard_map/ppermute | solution.py:27
  5.8 1.5 %collective-permute-start = (bf16[128,1408]{1,0:T(8,128)(2,1)S(1)}, bf16[128,1408]{1,0:T(8,128)(2,1)S(1)}, u32[]{:S(2)}, u32[]{:S(2)}) collective-permute-start(bf16[128,1408]{1,0:T(8,128)(2,1)S(1)} %shard_map.41.packed_ref.refs_0_), channel_id=1, source_target_pairs={{0,8},{4,12},{8,0},{12,4},{1,9},{5,13},{9,1},{13,5},{2,10},{6,14},... | collective-permute-start | bytes 1081352 | tf_op jit(solution)/shard_map/ppermute | solution.py:20
  7.3 0.2 shard_map.42
  7.5 0.0 collective-permute-start.2
  7.5 1.9 %collective-permute-start.3 = (f32[1,1536]{1,0:T(1,128)S(1)}, f32[1,1536]{1,0:T(1,128)S(1)}, u32[]{:S(2)}, u32[]{:S(2)}) collective-permute-start(f32[1,1536]{1,0:T(1,128)S(1)} %shard_map.42), channel_id=1, source_target_pairs={{0,2},{1,3},{2,0},{3,1},{4,6},{5,7},{6,4},{7,5},{8,10},{9,11},{10,... | collective-permute-start | bytes 18440 | tf_op jit(solution)/shard_map/ppermute | solution.py:20
  9.4 2.5 %collective-permute-start.4 = (f32[1,1536]{1,0:T(1,128)S(1)}, f32[1,1536]{1,0:T(1,128)S(1)}, u32[]{:S(2)}, u32[]{:S(2)}) collective-permute-start(f32[1,1536]{1,0:T(1,128)S(1)} %shard_map.42), channel_id=1, source_target_pairs={{0,3},{1,2},{2,1},{3,0},{4,7},{5,6},{6,5},{7,4},{8,11},{9,10},{10,... | collective-permute-start | bytes 18440 | tf_op jit(solution)/shard_map/ppermute | solution.py:20
  11.9 1.9 %collective-permute-done.2 = f32[1,1536]{1,0:T(1,128)S(1)} collective-permute-done((f32[1,1536]{1,0:T(1,128)S(1)}, f32[1,1536]{1,0:T(1,128)S(1)}, u32[]{:S(2)}, u32[]{:S(2)}) %collective-permute-start.2) | collective-permute-done | bytes 6176 | tf_op jit(solution)/shard_map/ppermute | solution.py:20
  13.8 2.0 %collective-permute-done.3 = f32[1,1536]{1,0:T(1,128)S(1)} collective-permute-done((f32[1,1536]{1,0:T(1,128)S(1)}, f32[1,1536]{1,0:T(1,128)S(1)}, u32[]{:S(2)}, u32[]{:S(2)}) %collective-permute-start.3) | collective-permute-done | bytes 6176 | tf_op jit(solution)/shard_map/ppermute | solution.py:20
  15.7 0.0 collective-permute-done.4
  15.7 0.0 collective-permute-done.1.refs_4_
  15.7 1.6 %collective-permute-start.9 = (bf16[128,1408]{1,0:T(8,128)(2,1)S(1)}, bf16[128,1408]{1,0:T(8,128)(2,1)S(1)}, u32[]{:S(2)}, u32[]{:S(2)}) collective-permute-start(bf16[128,1408]{1,0:T(8,128)(2,1)S(1)} %collective-permute-done.1.refs_4_), channel_id=1, source_target_pairs={{0,2},{2,3},{3,1},{1,0},{4,6},{6,7},{7,5},{5,4},{8,10},{10,11},{11... | collective-permute-start | bytes 1081352 | tf_op jit(solution)/shard_map/ppermute | solution.py:27
  17.4 0.0 collective-permute-done.refs_1_
  17.4 0.0 collective-permute-start.5
  17.4 0.5 %collective-permute-start.6 = (bf16[128,1408]{1,0:T(8,128)(2,1)S(1)}, bf16[128,1408]{1,0:T(8,128)(2,1)S(1)}, u32[]{:S(2)}, u32[]{:S(2)}) collective-permute-start(bf16[128,1408]{1,0:T(8,128)(2,1)S(1)} %collective-permute-done.refs_1_), channel_id=1, source_target_pairs={{0,4},{4,0},{8,12},{12,8},{1,5},{5,1},{9,13},{13,9},{2,6},{6,2},{1... | collective-permute-start | bytes 1081352 | tf_op jit(solution)/shard_map/ppermute | solution.py:20
  17.9 1.6 %collective-permute-start.7 = (f32[1,1536]{1,0:T(1,128)S(1)}, f32[1,1536]{1,0:T(1,128)S(1)}, u32[]{:S(2)}, u32[]{:S(2)}) collective-permute-start(f32[1,1536]{1,0:T(1,128)S(1)} %add_add_fusion), channel_id=1, source_target_pairs={{0,8},{4,12},{8,0},{12,4},{1,9},{5,13},{9,1},{13,5},{2,10},{6,14},... | collective-permute-start | bytes 18440 | tf_op jit(solution)/shard_map/ppermute | solution.py:20
  19.5 2.1 %collective-permute-done.7 = f32[1,1536]{1,0:T(1,128)S(1)} collective-permute-done((f32[1,1536]{1,0:T(1,128)S(1)}, f32[1,1536]{1,0:T(1,128)S(1)}, u32[]{:S(2)}, u32[]{:S(2)}) %collective-permute-start.7) | collective-permute-done | bytes 6176 | tf_op jit(solution)/shard_map/ppermute | solution.py:20
  21.6 0.1 collective-permute-start.8
  21.7 1.2 %collective-permute-done.8.refs_6_ = f32[1,1536]{1,0:T(1,128)S(1)} collective-permute-done((f32[1,1536]{1,0:T(1,128)S(1)}, f32[1,1536]{1,0:T(1,128)S(1)}, u32[]{:S(2)}, u32[]{:S(2)}) %collective-permute-start.8) | collective-permute-done | bytes 6176 | tf_op jit(solution)/shard_map/ppermute | solution.py:20
  22.8 0.0 collective-permute-done.5.refs_2_
  22.8 0.0 collective-permute-done.6.refs_3_
  22.8 2.2 %shard_map.43 = (f32[128,384]{1,0:T(8,128)S(1)}, f32[128,384]{1,0:T(8,128)S(1)}, f32[2,256,512]{2,1,0:T(8,128)S(1)}, f32[2,2,256,128]{3,2,1,0:T(8,128)S(1)}, f32...) custom-call(bf16[128,1408]{1,0:T(8,128)(2,1)S(1)} %shard_map.41.packed_ref.refs_0_, ...), custom_call_target="tpu_custom_call" | custom-call | flops 570425344 | bytes 1814528 | tf_op jit(solution)/shard_map/pallas_call | solution.py:243
  25.1 0.0 collective-permute-done.9.refs_1_
  25.1 0.7 %shard_map.44 = (f32[256,384]{1,0:T(8,128)S(1)}, f32[2,128]{1,0:T(2,128)S(1)}, f32[2,128]{1,0:T(2,128)S(1)}) custom-call(bf16[2,256,1408]{2,1,0:T(8,128)(2,1)S(1)} %get-tuple-element.33.refs_0_, bf16[128,1408]{1,0:T(8,128)(2,1)S(1)} %collective-permute-done.9.refs_1_, f32[4,384]{1,0:T(4,128)S(1)} %get-tuple-element.32.refs_2_.stats_ref, ...), custom_call_target="tpu_custom_call" | custom-call | flops 142606336 | bytes 3382272 | tf_op jit(solution)/shard_map/pallas_call | solution.py:243
  25.8 0.2 collective-permute-start.10
  26.0 2.3 %collective-permute-start.12 = (f32[128,384]{1,0:T(8,128)S(1)}, f32[128,384]{1,0:T(8,128)S(1)}, u32[]{:S(2)}, u32[]{:S(2)}) collective-permute-start(f32[128,384]{1,0:T(8,128)S(1)} %get-tuple-element.45), channel_id=1, source_target_pairs={{0,1},{2,0},{3,2},{1,3},{4,5},{6,4},{7,6},{5,7},{8,9},{10,8},{11,1... | collective-permute-start | bytes 589832 | tf_op jit(solution)/shard_map/ppermute | solution.py:27
  28.3 0.6 %shard_map.45 = (f32[256,384]{1,0:T(8,128)S(1)}, f32[16,2,128]{2,1,0:T(2,128)S(1)}) custom-call(bf16[2,256,1408]{2,1,0:T(8,128)(2,1)S(1)} %get-tuple-element.33.refs_0_, bf16[128,1408]{1,0:T(8,128)(2,1)S(1)} %collective-permute-done.9.refs_1_, f32[4,384]{1,0:T(4,128)S(1)} %get-tuple-element.32.refs_2_.stats_ref, ...), custom_call_target="tpu_custom_call" | custom-call | flops 142606336 | bytes 3383296 | tf_op jit(solution)/shard_map/pallas_call | solution.py:243
  29.0 1.6 %collective-permute-start.11 = (f32[128,384]{1,0:T(8,128)S(1)}, f32[128,384]{1,0:T(8,128)S(1)}, u32[]{:S(2)}, u32[]{:S(2)}) collective-permute-start(f32[128,384]{1,0:T(8,128)S(1)} %get-tuple-element.44), channel_id=1, source_target_pairs={{0,8},{4,12},{8,0},{12,4},{1,9},{5,13},{9,1},{13,5},{2,10},{6,14},... | collective-permute-start | bytes 589832 | tf_op jit(solution)/shard_map/ppermute | solution.py:20
  30.6 10.1 %all_to_all.5.sums_ref = f32[16,2,128]{2,1,0:T(2,128)S(1)} all-to-all(f32[16,2,128]{2,1,0:T(2,128)S(1)} %get-tuple-element.39), channel_id=1, replica_groups=mesh['groups'=2,'blk'=4,'sub'=4] {'blk','sub'}, dimensions={0} | all-to-all | bytes 32768 | tf_op jit(solution)/shard_map/all_to_all | solution.py:264
  40.6 0.0 collective-permute-done.12.refs_3_
  40.6 0.0 collective-permute-done.11.refs_2_
  40.6 1.3 %shard_map.47 = (f32[128,384]{1,0:T(8,128)}, f32[1,128]{1,0:T(1,128)}) custom-call(bf16[128,1408]{1,0:T(8,128)(2,1)S(1)} %shard_map.41.packed_ref.refs_0_, f32[4,384]{1,0:T(4,128)S(1)} %get-tuple-element.32.refs_2_.stats_ref, f32[16,2,128]{2,1,0:T(2,128)S(1)} %all_to_all.5.sums_ref, f32[128,384]{1,0:T(8,128)S(1)} %get-tuple-element.40.refs_0_, ...), custom_call_target="tpu_custom_call" | custom-call | flops 393216 | bytes 1169408 | tf_op jit(solution)/shard_map/pallas_call | solution.py:243
  (4 shorter events, 0.1 us)
Async XLA Ops:
  1.7 14.0 %collective-permute-start.1 = (bf16[128,1408]{1,0:T(8,128)(2,1)S(1)}, bf16[128,1408]{1,0:T(8,128)(2,1)S(1)}, u32[]{:S(2)}, u32[]{:S(2)}) collective-permute-start(bf16[128,1408]{1,0:T(8,128)(2,1)S(1)} %shard_map.41.packed_ref.refs_0_), channel_id=1, source_target_pairs={{0,2},{2,3},{3,1},{1,0},{4,6},{6,7},{7,5},{5,4},{8,10},{10,11},{11... | collective-permute-start | bytes 1081352 | tf_op jit(solution)/shard_map/ppermute | solution.py:27
  5.8 11.6 %collective-permute-start = (bf16[128,1408]{1,0:T(8,128)(2,1)S(1)}, bf16[128,1408]{1,0:T(8,128)(2,1)S(1)}, u32[]{:S(2)}, u32[]{:S(2)}) collective-permute-start(bf16[128,1408]{1,0:T(8,128)(2,1)S(1)} %shard_map.41.packed_ref.refs_0_), channel_id=1, source_target_pairs={{0,8},{4,12},{8,0},{12,4},{1,9},{5,13},{9,1},{13,5},{2,10},{6,14},... | collective-permute-start | bytes 1081352 | tf_op jit(solution)/shard_map/ppermute | solution.py:20
  7.5 6.3 %collective-permute-start.2 = (f32[1,1536]{1,0:T(1,128)S(1)}, f32[1,1536]{1,0:T(1,128)S(1)}, u32[]{:S(2)}, u32[]{:S(2)}) collective-permute-start(f32[1,1536]{1,0:T(1,128)S(1)} %shard_map.42), channel_id=1, source_target_pairs={{0,1},{1,0},{2,3},{3,2},{4,5},{5,4},{6,7},{7,6},{8,9},{9,8},{10,11... | collective-permute-start | bytes 18440 | tf_op jit(solution)/shard_map/ppermute | solution.py:20
  7.5 8.2 %collective-permute-start.3 = (f32[1,1536]{1,0:T(1,128)S(1)}, f32[1,1536]{1,0:T(1,128)S(1)}, u32[]{:S(2)}, u32[]{:S(2)}) collective-permute-start(f32[1,1536]{1,0:T(1,128)S(1)} %shard_map.42), channel_id=1, source_target_pairs={{0,2},{1,3},{2,0},{3,1},{4,6},{5,7},{6,4},{7,5},{8,10},{9,11},{10,... | collective-permute-start | bytes 18440 | tf_op jit(solution)/shard_map/ppermute | solution.py:20
  9.4 6.3 %collective-permute-start.4 = (f32[1,1536]{1,0:T(1,128)S(1)}, f32[1,1536]{1,0:T(1,128)S(1)}, u32[]{:S(2)}, u32[]{:S(2)}) collective-permute-start(f32[1,1536]{1,0:T(1,128)S(1)} %shard_map.42), channel_id=1, source_target_pairs={{0,3},{1,2},{2,1},{3,0},{4,7},{5,6},{6,5},{7,4},{8,11},{9,10},{10,... | collective-permute-start | bytes 18440 | tf_op jit(solution)/shard_map/ppermute | solution.py:20
  15.7 9.4 %collective-permute-start.9 = (bf16[128,1408]{1,0:T(8,128)(2,1)S(1)}, bf16[128,1408]{1,0:T(8,128)(2,1)S(1)}, u32[]{:S(2)}, u32[]{:S(2)}) collective-permute-start(bf16[128,1408]{1,0:T(8,128)(2,1)S(1)} %collective-permute-done.1.refs_4_), channel_id=1, source_target_pairs={{0,2},{2,3},{3,1},{1,0},{4,6},{6,7},{7,5},{5,4},{8,10},{10,11},{11... | collective-permute-start | bytes 1081352 | tf_op jit(solution)/shard_map/ppermute | solution.py:27
  17.4 5.5 %collective-permute-start.5 = (bf16[128,1408]{1,0:T(8,128)(2,1)S(1)}, bf16[128,1408]{1,0:T(8,128)(2,1)S(1)}, u32[]{:S(2)}, u32[]{:S(2)}) collective-permute-start(bf16[128,1408]{1,0:T(8,128)(2,1)S(1)} %shard_map.41.packed_ref.refs_0_), channel_id=1, source_target_pairs={{0,4},{4,0},{8,12},{12,8},{1,5},{5,1},{9,13},{13,9},{2,6},{6,2},{1... | collective-permute-start | bytes 1081352 | tf_op jit(solution)/shard_map/ppermute | solution.py:20
  17.4 5.5 %collective-permute-start.6 = (bf16[128,1408]{1,0:T(8,128)(2,1)S(1)}, bf16[128,1408]{1,0:T(8,128)(2,1)S(1)}, u32[]{:S(2)}, u32[]{:S(2)}) collective-permute-start(bf16[128,1408]{1,0:T(8,128)(2,1)S(1)} %collective-permute-done.refs_1_), channel_id=1, source_target_pairs={{0,4},{4,0},{8,12},{12,8},{1,5},{5,1},{9,13},{13,9},{2,6},{6,2},{1... | collective-permute-start | bytes 1081352 | tf_op jit(solution)/shard_map/ppermute | solution.py:20
  17.9 3.7 %collective-permute-start.7 = (f32[1,1536]{1,0:T(1,128)S(1)}, f32[1,1536]{1,0:T(1,128)S(1)}, u32[]{:S(2)}, u32[]{:S(2)}) collective-permute-start(f32[1,1536]{1,0:T(1,128)S(1)} %add_add_fusion), channel_id=1, source_target_pairs={{0,8},{4,12},{8,0},{12,4},{1,9},{5,13},{9,1},{13,5},{2,10},{6,14},... | collective-permute-start | bytes 18440 | tf_op jit(solution)/shard_map/ppermute | solution.py:20
  21.6 1.2 %collective-permute-start.8 = (f32[1,1536]{1,0:T(1,128)S(1)}, f32[1,1536]{1,0:T(1,128)S(1)}, u32[]{:S(2)}, u32[]{:S(2)}) collective-permute-start(f32[1,1536]{1,0:T(1,128)S(1)} %add.15.refs_5_), channel_id=1, source_target_pairs={{0,4},{4,0},{8,12},{12,8},{1,5},{5,1},{9,13},{13,9},{2,6},{6,2},{1... | collective-permute-start | bytes 18440 | tf_op jit(solution)/shard_map/ppermute | solution.py:20
  25.8 3.2 %collective-permute-start.10 = (f32[256,384]{1,0:T(8,128)S(1)}, f32[256,384]{1,0:T(8,128)S(1)}, u32[]{:S(2)}, u32[]{:S(2)}) collective-permute-start(f32[256,384]{1,0:T(8,128)S(1)} %get-tuple-element.42), channel_id=1, source_target_pairs={{0,4},{4,0},{8,12},{12,8},{1,5},{5,1},{9,13},{13,9},{2,6},{6,2},{1... | collective-permute-start | bytes 1179656 | tf_op jit(solution)/shard_map/ppermute | solution.py:20
  26.0 14.6 %collective-permute-start.12 = (f32[128,384]{1,0:T(8,128)S(1)}, f32[128,384]{1,0:T(8,128)S(1)}, u32[]{:S(2)}, u32[]{:S(2)}) collective-permute-start(f32[128,384]{1,0:T(8,128)S(1)} %get-tuple-element.45), channel_id=1, source_target_pairs={{0,1},{2,0},{3,2},{1,3},{4,5},{6,4},{7,6},{5,7},{8,9},{10,8},{11,1... | collective-permute-start | bytes 589832 | tf_op jit(solution)/shard_map/ppermute | solution.py:27
  29.0 11.7 %collective-permute-start.11 = (f32[128,384]{1,0:T(8,128)S(1)}, f32[128,384]{1,0:T(8,128)S(1)}, u32[]{:S(2)}, u32[]{:S(2)}) collective-permute-start(f32[128,384]{1,0:T(8,128)S(1)} %get-tuple-element.44), channel_id=1, source_target_pairs={{0,8},{4,12},{8,0},{12,4},{1,9},{5,13},{9,1},{13,5},{2,10},{6,14},... | collective-permute-start | bytes 589832 | tf_op jit(solution)/shard_map/ppermute | solution.py:20

commit v17 on v15

--- a/solution.py
+++ b/solution.py
@@ -21,9 +21,7 @@
 
 def shifted(value, axis, distance):
     size = lax.axis_size(axis)
-    places = [*range(0, size, 2), *reversed(range(1, size, 2))]
-    route = [(places[i], places[(i + distance) % size]) for i in range(size)]
-    return lax.ppermute(value, axis, route)
+    return lax.ppermute(value, axis, [(i, (i + distance) % size) for i in range(size)])
 
 
 def pack_kernel(t_hbm, s_hbm, packed_ref, sems):
@@ -138,9 +136,11 @@
     stats = stats_refs[0][...]
     for ref in stats_refs[1:]:
         stats = stats + ref[...]
-    total_ref[...] = stats
-    spread_t, spread_s, _ = spreads_of(stats, t_width, s_width, total_rows)
+    spread_t, spread_s, centre_s = spreads_of(stats, t_width, s_width, total_rows)
     inv_t, inv_s = 1.0 / spread_t, 1.0 / spread_s
+    for row, value in enumerate((inv_t, inv_s, spread_s)):
+        total_ref[row : row + 1, :] = jnp.broadcast_to(value, (1, s_width))
+    total_ref[3:4, :] = centre_s
     loss = jnp.zeros((1, LANES), jnp.float32)
     spread = jnp.zeros((1, LANES), jnp.float32)
     if steps == 1:
@@ -175,7 +175,7 @@
     sums_ref[1:2, :] = spread
 
 
-def late_kernel(side, t_width, total_rows, *refs):
+def late_kernel(side, t_width, *refs):
     if side:
         plane_ref, ref, stats_ref, acc_ref, norm_ref, sums_in, out_ref, sums_ref, visit_ref = refs
         v = visiting(ref, t_width)
@@ -183,9 +183,7 @@
     else:
         plane_ref, ref, stats_ref, acc_ref, norm_ref, sums_in, visit_ref, out_ref, sums_ref = refs
         v = (ref[:, :t_width], ref[:, t_width:], visit_ref[0:1, :], visit_ref[1:2, :])
-    s_width = out_ref.shape[1]
-    spread_t, spread_s, _ = spreads_of(stats_ref[...], t_width, s_width, total_rows)
-    inv_t, inv_s = 1.0 / spread_t, 1.0 / spread_s
+    inv_t, inv_s = stats_ref[0:1, :LANES], stats_ref[1:2, :LANES]
     loss = sums_in[0:1, :]
     spread = sums_in[1:2, :]
     for h, at in chunks_of(plane_ref):
@@ -214,10 +212,9 @@
     direct = parts[0][...]
     for part in parts[1:]:
         direct = direct + part[...]
-    s_width = direct.shape[1]
     both = jnp.sum(jnp.sum(sums_ref[...], axis=0), axis=1, keepdims=True)
     loss_total, spread_total = both[0:1, :], -both[1:2, :]
-    _, spread_s, centre = spreads_of(stats_ref[...], t_width, s_width, total_rows)
+    spread_s, centre = stats_ref[2:3, :], stats_ref[3:4, :]
     pairs = total_rows * (total_rows - 1.0)
     correction = 2.0 * spread_total / (pairs * spread_s * spread_s)
     student = packed_ref[:, t_width:].astype(jnp.float32)
@@ -298,7 +295,7 @@
     out_shape = (
         [f32((rows, s_width))] * half
         + [f32((2, side, s_width + LANES)), f32((2, 2, side, LANES))]
-        + [f32(stats[0].shape), f32((2, LANES))]
+        + [f32((4, s_width)), f32((2, LANES))]
         + [jax.ShapeDtypeStruct((2, side, t_width + s_width), packed.dtype)]
     )
     *tiles, acc, norms, totals, early_sums, plane = call(
@@ -311,13 +308,13 @@
     returned = [shifted(x, "sub", -k) for k, x in enumerate(backs, 1)]
     given = [plane, line[half], totals, acc, norms]
     give, late_sums, visit_norms = call(
-        functools.partial(late_kernel, 1, t_width, total_rows),
+        functools.partial(late_kernel, 1, t_width),
         [f32((side, s_width)), f32((2, LANES)), f32((2, rows))],
         [*given, early_sums],
         pair_flops // 2,
     )
     keep, sums = call(
-        functools.partial(late_kernel, 0, t_width, total_rows),
+        functools.partial(late_kernel, 0, t_width),
         [f32((side, s_width)), f32((n_blk * n_sub, 2, LANES))],
         [*given, late_sums, visit_norms],
         pair_flops // 2,

time: 41.6 us -> 40.8 us (0.981)
  waiting for transfers between devices: 7.16 us -> 11.9 us
  starting transfers between devices: 17.9 us -> 13.4 us
  blocking collectives: 10.1 us -> 8.97 us
    ppermute x3, starting transfers between devices: 8.02 us -> 4.03 us  [shifted(): lax.ppermute(value, axis, [(i, (i + distance) % size) for i in range(size)])]
    ppermute x3, waiting for transfers between devices: 0.02 us -> 3.04 us  [shifted(): lax.ppermute(value, axis, [(i, (i + distance) % size) for i in range(size)])]
    ppermute x10, waiting for transfers between devices: 7.14 us -> 8.9 us  [exchange(): return lax.ppermute(value, axis, [(i, i ^ distance) for i in range(size)])]
    all_to_all x1, blocking collectives: 10.1 us -> 8.97 us  [to_all(): return lax.all_to_all(value, ('blk', 'sub'), 0, 0, tiled=True)]
    ppermute x10, starting transfers between devices: 9.88 us -> 9.42 us  [exchange(): return lax.ppermute(value, axis, [(i, i ^ distance) for i in range(size)])]
  transfers between devices with their start and end apart: 13 -> 13, of which waited for: 4 -> 6; matrix products, arithmetic and copies ran while one was open for 0% -> 0% of each run, Pallas kernels for 7% -> 8%
where the time goes in v17:
time: 40.8 us; the launch traced here: 40.6 us
  starting transfers between devices  13.4 us (33%)
  waiting for transfers between devices  11.9 us (29%)
  blocking collectives  8.97 us (22%)
  Pallas kernels  5.54 us (14%)
  between operations  0.69 us (2%)
    ppermute x10, starting transfers between devices, exchange(): return lax.ppermute(value, axis, [(i, i ^ distance) for i in range(size)])  9.42 us
    all_to_all x1, blocking collectives, to_all(): return lax.all_to_all(value, ('blk', 'sub'), 0, 0, tiled=True)  8.97 us
    ppermute x10, waiting for transfers between devices, exchange(): return lax.ppermute(value, axis, [(i, i ^ distance) for i in range(size)])  8.9 us
    pallas_call x7, Pallas kernels, call(): pl.pallas_call(kernel, out_shape=out_shape, in_specs=in_specs, out_specs=...  5.54 us
    ppermute x3, starting transfers between devices, shifted(): lax.ppermute(value, axis, [(i, (i + distance) % size) for i in range(size)])  4.03 us
    ppermute x3, waiting for transfers between devices, shifted(): lax.ppermute(value, axis, [(i, (i + distance) % size) for i in range(size)])  3.04 us
  transfers between devices with their start and end apart: 13, of which 6 were waited for; matrix products, arithmetic and copies ran while one was open for 0% of the time, Pallas kernels for 8%

profile of v17, /device:TPU:0, one launch (start us, length us, event | category | flops | bytes accessed | tf_op | source)
XLA Modules:
  0.0 40.6 jit_solution(11515490372427795075)
XLA Ops:
  0.6 1.0 %shard_map.41.packed_ref.refs_0_ = bf16[128,1408]{1,0:T(8,128)(2,1)S(1)} custom-call(bf16[128,1024]{1,0:T(8,128)(2,1)} %t_hbm.1, bf16[128,384]{1,0:T(8,128)(2,1)} %s_hbm.1), custom_call_target="tpu_custom_call" | custom-call | bytes 360448 | tf_op jit(solution)/shard_map/pallas_call | solution.py:229
  1.6 3.1 %collective-permute-start.1 = (bf16[128,1408]{1,0:T(8,128)(2,1)S(1)}, bf16[128,1408]{1,0:T(8,128)(2,1)S(1)}, u32[]{:S(2)}, u32[]{:S(2)}) collective-permute-start(bf16[128,1408]{1,0:T(8,128)(2,1)S(1)} %shard_map.41.packed_ref.refs_0_), channel_id=1, source_target_pairs={{0,1},{1,2},{2,3},{3,0},{4,5},{5,6},{6,7},{7,4},{8,9},{9,10},{10,1... | collective-permute-start | bytes 1081352 | tf_op jit(solution)/shard_map/ppermute | solution.py:24
  4.7 1.5 %collective-permute-start = (bf16[128,1408]{1,0:T(8,128)(2,1)S(1)}, bf16[128,1408]{1,0:T(8,128)(2,1)S(1)}, u32[]{:S(2)}, u32[]{:S(2)}) collective-permute-start(bf16[128,1408]{1,0:T(8,128)(2,1)S(1)} %shard_map.41.packed_ref.refs_0_), channel_id=1, source_target_pairs={{0,8},{4,12},{8,0},{12,4},{1,9},{5,13},{9,1},{13,5},{2,10},{6,14},... | collective-permute-start | bytes 1081352 | tf_op jit(solution)/shard_map/ppermute | solution.py:19
  6.2 0.2 shard_map.42
  6.4 1.6 %collective-permute-start.2 = (f32[1,1536]{1,0:T(1,128)S(1)}, f32[1,1536]{1,0:T(1,128)S(1)}, u32[]{:S(2)}, u32[]{:S(2)}) collective-permute-start(f32[1,1536]{1,0:T(1,128)S(1)} %shard_map.42), channel_id=1, source_target_pairs={{0,1},{1,0},{2,3},{3,2},{4,5},{5,4},{6,7},{7,6},{8,9},{9,8},{10,11... | collective-permute-start | bytes 18440 | tf_op jit(solution)/shard_map/ppermute | solution.py:19
  8.0 1.2 %collective-permute-start.3 = (f32[1,1536]{1,0:T(1,128)S(1)}, f32[1,1536]{1,0:T(1,128)S(1)}, u32[]{:S(2)}, u32[]{:S(2)}) collective-permute-start(f32[1,1536]{1,0:T(1,128)S(1)} %shard_map.42), channel_id=1, source_target_pairs={{0,2},{1,3},{2,0},{3,1},{4,6},{5,7},{6,4},{7,5},{8,10},{9,11},{10,... | collective-permute-start | bytes 18440 | tf_op jit(solution)/shard_map/ppermute | solution.py:19
  9.2 1.6 %collective-permute-start.4 = (f32[1,1536]{1,0:T(1,128)S(1)}, f32[1,1536]{1,0:T(1,128)S(1)}, u32[]{:S(2)}, u32[]{:S(2)}) collective-permute-start(f32[1,1536]{1,0:T(1,128)S(1)} %shard_map.42), channel_id=1, source_target_pairs={{0,3},{1,2},{2,1},{3,0},{4,7},{5,6},{6,5},{7,4},{8,11},{9,10},{10,... | collective-permute-start | bytes 18440 | tf_op jit(solution)/shard_map/ppermute | solution.py:19
  10.8 3.8 %collective-permute-done.2 = f32[1,1536]{1,0:T(1,128)S(1)} collective-permute-done((f32[1,1536]{1,0:T(1,128)S(1)}, f32[1,1536]{1,0:T(1,128)S(1)}, u32[]{:S(2)}, u32[]{:S(2)}) %collective-permute-start.2) | collective-permute-done | bytes 6176 | tf_op jit(solution)/shard_map/ppermute | solution.py:19
  14.6 1.1 %collective-permute-done.3 = f32[1,1536]{1,0:T(1,128)S(1)} collective-permute-done((f32[1,1536]{1,0:T(1,128)S(1)}, f32[1,1536]{1,0:T(1,128)S(1)}, u32[]{:S(2)}, u32[]{:S(2)}) %collective-permute-start.3) | collective-permute-done | bytes 6176 | tf_op jit(solution)/shard_map/ppermute | solution.py:19
  15.6 0.0 collective-permute-done.4
  15.6 0.0 collective-permute-done.1.refs_4_
  15.7 0.6 %collective-permute-start.9 = (bf16[128,1408]{1,0:T(8,128)(2,1)S(1)}, bf16[128,1408]{1,0:T(8,128)(2,1)S(1)}, u32[]{:S(2)}, u32[]{:S(2)}) collective-permute-start(bf16[128,1408]{1,0:T(8,128)(2,1)S(1)} %collective-permute-done.1.refs_4_), channel_id=1, source_target_pairs={{0,1},{1,2},{2,3},{3,0},{4,5},{5,6},{6,7},{7,4},{8,9},{9,10},{10,1... | collective-permute-start | bytes 1081352 | tf_op jit(solution)/shard_map/ppermute | solution.py:24
  16.3 0.0 collective-permute-done.refs_1_
  16.3 0.0 collective-permute-start.5
  16.3 0.5 %collective-permute-start.6 = (bf16[128,1408]{1,0:T(8,128)(2,1)S(1)}, bf16[128,1408]{1,0:T(8,128)(2,1)S(1)}, u32[]{:S(2)}, u32[]{:S(2)}) collective-permute-start(bf16[128,1408]{1,0:T(8,128)(2,1)S(1)} %collective-permute-done.refs_1_), channel_id=1, source_target_pairs={{0,4},{4,0},{8,12},{12,8},{1,5},{5,1},{9,13},{13,9},{2,6},{6,2},{1... | collective-permute-start | bytes 1081352 | tf_op jit(solution)/shard_map/ppermute | solution.py:19
  16.8 1.6 %collective-permute-start.7 = (f32[1,1536]{1,0:T(1,128)S(1)}, f32[1,1536]{1,0:T(1,128)S(1)}, u32[]{:S(2)}, u32[]{:S(2)}) collective-permute-start(f32[1,1536]{1,0:T(1,128)S(1)} %add_add_fusion), channel_id=1, source_target_pairs={{0,8},{4,12},{8,0},{12,4},{1,9},{5,13},{9,1},{13,5},{2,10},{6,14},... | collective-permute-start | bytes 18440 | tf_op jit(solution)/shard_map/ppermute | solution.py:19
  18.4 2.1 %collective-permute-done.7 = f32[1,1536]{1,0:T(1,128)S(1)} collective-permute-done((f32[1,1536]{1,0:T(1,128)S(1)}, f32[1,1536]{1,0:T(1,128)S(1)}, u32[]{:S(2)}, u32[]{:S(2)}) %collective-permute-start.7) | collective-permute-done | bytes 6176 | tf_op jit(solution)/shard_map/ppermute | solution.py:19
  20.5 0.1 collective-permute-start.8
  20.6 1.2 %collective-permute-done.8.refs_6_ = f32[1,1536]{1,0:T(1,128)S(1)} collective-permute-done((f32[1,1536]{1,0:T(1,128)S(1)}, f32[1,1536]{1,0:T(1,128)S(1)}, u32[]{:S(2)}, u32[]{:S(2)}) %collective-permute-start.8) | collective-permute-done | bytes 6176 | tf_op jit(solution)/shard_map/ppermute | solution.py:19
  21.8 0.0 collective-permute-done.6.refs_3_
  21.8 2.2 %shard_map.43 = (f32[128,384]{1,0:T(8,128)S(1)}, f32[128,384]{1,0:T(8,128)S(1)}, f32[2,256,512]{2,1,0:T(8,128)S(1)}, f32[2,2,256,128]{3,2,1,0:T(8,128)S(1)}, f32...) custom-call(bf16[128,1408]{1,0:T(8,128)(2,1)S(1)} %shard_map.41.packed_ref.refs_0_, ...), custom_call_target="tpu_custom_call" | custom-call | flops 570425344 | bytes 1814528 | tf_op jit(solution)/shard_map/pallas_call | solution.py:229
  24.0 3.0 %collective-permute-done.9.refs_1_ = bf16[128,1408]{1,0:T(8,128)(2,1)S(1)} collective-permute-done((bf16[128,1408]{1,0:T(8,128)(2,1)S(1)}, bf16[128,1408]{1,0:T(8,128)(2,1)S(1)}, u32[]{:S(2)}, u32[]{:S(2)}) %collective-permute-start.9) | collective-permute-done | bytes 360480 | tf_op jit(solution)/shard_map/ppermute | solution.py:24
  27.0 0.7 %shard_map.44 = (f32[256,384]{1,0:T(8,128)S(1)}, f32[2,128]{1,0:T(2,128)S(1)}, f32[2,128]{1,0:T(2,128)S(1)}) custom-call(bf16[2,256,1408]{2,1,0:T(8,128)(2,1)S(1)} %get-tuple-element.33.refs_0_, bf16[128,1408]{1,0:T(8,128)(2,1)S(1)} %collective-permute-done.9.refs_1_, f32[4,384]{1,0:T(4,128)S(1)} %get-tuple-element.32.refs_2_.stats_ref, ...), custom_call_target="tpu_custom_call" | custom-call | flops 142606336 | bytes 3382272 | tf_op jit(solution)/shard_map/pallas_call | solution.py:229
  27.7 0.1 collective-permute-start.10
  27.8 0.3 collective-permute-start.12
  28.1 0.6 %shard_map.45 = (f32[256,384]{1,0:T(8,128)S(1)}, f32[16,2,128]{2,1,0:T(2,128)S(1)}) custom-call(bf16[2,256,1408]{2,1,0:T(8,128)(2,1)S(1)} %get-tuple-element.33.refs_0_, bf16[128,1408]{1,0:T(8,128)(2,1)S(1)} %collective-permute-done.9.refs_1_, f32[4,384]{1,0:T(4,128)S(1)} %get-tuple-element.32.refs_2_.stats_ref, ...), custom_call_target="tpu_custom_call" | custom-call | flops 142606336 | bytes 3383296 | tf_op jit(solution)/shard_map/pallas_call | solution.py:229
  28.7 0.7 %collective-permute-done.10.got_ref = f32[256,384]{1,0:T(8,128)S(1)} collective-permute-done((f32[256,384]{1,0:T(8,128)S(1)}, f32[256,384]{1,0:T(8,128)S(1)}, u32[]{:S(2)}, u32[]{:S(2)}) %collective-permute-start.10) | collective-permute-done | bytes 393248 | tf_op jit(solution)/shard_map/ppermute | solution.py:19
  29.5 1.3 %collective-permute-start.11 = (f32[128,384]{1,0:T(8,128)S(1)}, f32[128,384]{1,0:T(8,128)S(1)}, u32[]{:S(2)}, u32[]{:S(2)}) collective-permute-start(f32[128,384]{1,0:T(8,128)S(1)} %get-tuple-element.44), channel_id=1, source_target_pairs={{0,8},{4,12},{8,0},{12,4},{1,9},{5,13},{9,1},{13,5},{2,10},{6,14},... | collective-permute-start | bytes 589832 | tf_op jit(solution)/shard_map/ppermute | solution.py:19
  30.8 9.0 %all_to_all.5.sums_ref = f32[16,2,128]{2,1,0:T(2,128)S(1)} all-to-all(f32[16,2,128]{2,1,0:T(2,128)S(1)} %get-tuple-element.39), channel_id=1, replica_groups=mesh['groups'=2,'blk'=4,'sub'=4] {'blk','sub'}, dimensions={0} | all-to-all | bytes 32768 | tf_op jit(solution)/shard_map/all_to_all | solution.py:250
  39.8 0.0 collective-permute-done.12.refs_3_
  39.8 0.0 collective-permute-done.11.refs_2_
  39.8 0.8 %shard_map.47 = (f32[128,384]{1,0:T(8,128)}, f32[1,128]{1,0:T(1,128)}) custom-call(bf16[128,1408]{1,0:T(8,128)(2,1)S(1)} %shard_map.41.packed_ref.refs_0_, f32[4,384]{1,0:T(4,128)S(1)} %get-tuple-element.32.refs_2_.stats_ref, f32[16,2,128]{2,1,0:T(2,128)S(1)} %all_to_all.5.sums_ref, f32[128,384]{1,0:T(8,128)S(1)} %get-tuple-element.40.refs_0_, ...), custom_call_target="tpu_custom_call" | custom-call | flops 393216 | bytes 1169408 | tf_op jit(solution)/shard_map/pallas_call | solution.py:229
  (4 shorter events, 0.1 us)
Async XLA Ops:
  1.6 14.0 %collective-permute-start.1 = (bf16[128,1408]{1,0:T(8,128)(2,1)S(1)}, bf16[128,1408]{1,0:T(8,128)(2,1)S(1)}, u32[]{:S(2)}, u32[]{:S(2)}) collective-permute-start(bf16[128,1408]{1,0:T(8,128)(2,1)S(1)} %shard_map.41.packed_ref.refs_0_), channel_id=1, source_target_pairs={{0,1},{1,2},{2,3},{3,0},{4,5},{5,6},{6,7},{7,4},{8,9},{9,10},{10,1... | collective-permute-start | bytes 1081352 | tf_op jit(solution)/shard_map/ppermute | solution.py:24
  4.7 11.6 %collective-permute-start = (bf16[128,1408]{1,0:T(8,128)(2,1)S(1)}, bf16[128,1408]{1,0:T(8,128)(2,1)S(1)}, u32[]{:S(2)}, u32[]{:S(2)}) collective-permute-start(bf16[128,1408]{1,0:T(8,128)(2,1)S(1)} %shard_map.41.packed_ref.refs_0_), channel_id=1, source_target_pairs={{0,8},{4,12},{8,0},{12,4},{1,9},{5,13},{9,1},{13,5},{2,10},{6,14},... | collective-permute-start | bytes 1081352 | tf_op jit(solution)/shard_map/ppermute | solution.py:19
  6.4 8.2 %collective-permute-start.2 = (f32[1,1536]{1,0:T(1,128)S(1)}, f32[1,1536]{1,0:T(1,128)S(1)}, u32[]{:S(2)}, u32[]{:S(2)}) collective-permute-start(f32[1,1536]{1,0:T(1,128)S(1)} %shard_map.42), channel_id=1, source_target_pairs={{0,1},{1,0},{2,3},{3,2},{4,5},{5,4},{6,7},{7,6},{8,9},{9,8},{10,11... | collective-permute-start | bytes 18440 | tf_op jit(solution)/shard_map/ppermute | solution.py:19
  8.0 7.7 %collective-permute-start.3 = (f32[1,1536]{1,0:T(1,128)S(1)}, f32[1,1536]{1,0:T(1,128)S(1)}, u32[]{:S(2)}, u32[]{:S(2)}) collective-permute-start(f32[1,1536]{1,0:T(1,128)S(1)} %shard_map.42), channel_id=1, source_target_pairs={{0,2},{1,3},{2,0},{3,1},{4,6},{5,7},{6,4},{7,5},{8,10},{9,11},{10,... | collective-permute-start | bytes 18440 | tf_op jit(solution)/shard_map/ppermute | solution.py:19
  9.2 6.4 %collective-permute-start.4 = (f32[1,1536]{1,0:T(1,128)S(1)}, f32[1,1536]{1,0:T(1,128)S(1)}, u32[]{:S(2)}, u32[]{:S(2)}) collective-permute-start(f32[1,1536]{1,0:T(1,128)S(1)} %shard_map.42), channel_id=1, source_target_pairs={{0,3},{1,2},{2,1},{3,0},{4,7},{5,6},{6,5},{7,4},{8,11},{9,10},{10,... | collective-permute-start | bytes 18440 | tf_op jit(solution)/shard_map/ppermute | solution.py:19
  15.7 11.4 %collective-permute-start.9 = (bf16[128,1408]{1,0:T(8,128)(2,1)S(1)}, bf16[128,1408]{1,0:T(8,128)(2,1)S(1)}, u32[]{:S(2)}, u32[]{:S(2)}) collective-permute-start(bf16[128,1408]{1,0:T(8,128)(2,1)S(1)} %collective-permute-done.1.refs_4_), channel_id=1, source_target_pairs={{0,1},{1,2},{2,3},{3,0},{4,5},{5,6},{6,7},{7,4},{8,9},{9,10},{10,1... | collective-permute-start | bytes 1081352 | tf_op jit(solution)/shard_map/ppermute | solution.py:24
  16.3 5.5 %collective-permute-start.5 = (bf16[128,1408]{1,0:T(8,128)(2,1)S(1)}, bf16[128,1408]{1,0:T(8,128)(2,1)S(1)}, u32[]{:S(2)}, u32[]{:S(2)}) collective-permute-start(bf16[128,1408]{1,0:T(8,128)(2,1)S(1)} %shard_map.41.packed_ref.refs_0_), channel_id=1, source_target_pairs={{0,4},{4,0},{8,12},{12,8},{1,5},{5,1},{9,13},{13,9},{2,6},{6,2},{1... | collective-permute-start | bytes 1081352 | tf_op jit(solution)/shard_map/ppermute | solution.py:19
  16.3 5.5 %collective-permute-start.6 = (bf16[128,1408]{1,0:T(8,128)(2,1)S(1)}, bf16[128,1408]{1,0:T(8,128)(2,1)S(1)}, u32[]{:S(2)}, u32[]{:S(2)}) collective-permute-start(bf16[128,1408]{1,0:T(8,128)(2,1)S(1)} %collective-permute-done.refs_1_), channel_id=1, source_target_pairs={{0,4},{4,0},{8,12},{12,8},{1,5},{5,1},{9,13},{13,9},{2,6},{6,2},{1... | collective-permute-start | bytes 1081352 | tf_op jit(solution)/shard_map/ppermute | solution.py:19
  16.8 3.7 %collective-permute-start.7 = (f32[1,1536]{1,0:T(1,128)S(1)}, f32[1,1536]{1,0:T(1,128)S(1)}, u32[]{:S(2)}, u32[]{:S(2)}) collective-permute-start(f32[1,1536]{1,0:T(1,128)S(1)} %add_add_fusion), channel_id=1, source_target_pairs={{0,8},{4,12},{8,0},{12,4},{1,9},{5,13},{9,1},{13,5},{2,10},{6,14},... | collective-permute-start | bytes 18440 | tf_op jit(solution)/shard_map/ppermute | solution.py:19
  20.5 1.2 %collective-permute-start.8 = (f32[1,1536]{1,0:T(1,128)S(1)}, f32[1,1536]{1,0:T(1,128)S(1)}, u32[]{:S(2)}, u32[]{:S(2)}) collective-permute-start(f32[1,1536]{1,0:T(1,128)S(1)} %add.15.refs_5_), channel_id=1, source_target_pairs={{0,4},{4,0},{8,12},{12,8},{1,5},{5,1},{9,13},{13,9},{2,6},{6,2},{1... | collective-permute-start | bytes 18440 | tf_op jit(solution)/shard_map/ppermute | solution.py:19
  27.7 1.8 %collective-permute-start.10 = (f32[256,384]{1,0:T(8,128)S(1)}, f32[256,384]{1,0:T(8,128)S(1)}, u32[]{:S(2)}, u32[]{:S(2)}) collective-permute-start(f32[256,384]{1,0:T(8,128)S(1)} %get-tuple-element.42), channel_id=1, source_target_pairs={{0,4},{4,0},{8,12},{12,8},{1,5},{5,1},{9,13},{13,9},{2,6},{6,2},{1... | collective-permute-start | bytes 1179656 | tf_op jit(solution)/shard_map/ppermute | solution.py:19
  27.8 12.0 %collective-permute-start.12 = (f32[128,384]{1,0:T(8,128)S(1)}, f32[128,384]{1,0:T(8,128)S(1)}, u32[]{:S(2)}, u32[]{:S(2)}) collective-permute-start(f32[128,384]{1,0:T(8,128)S(1)} %get-tuple-element.45), channel_id=1, source_target_pairs={{0,3},{1,0},{2,1},{3,2},{4,7},{5,4},{6,5},{7,6},{8,11},{9,8},{10,9... | collective-permute-start | bytes 589832 | tf_op jit(solution)/shard_map/ppermute | solution.py:24
  29.5 10.3 %collective-permute-start.11 = (f32[128,384]{1,0:T(8,128)S(1)}, f32[128,384]{1,0:T(8,128)S(1)}, u32[]{:S(2)}, u32[]{:S(2)}) collective-permute-start(f32[128,384]{1,0:T(8,128)S(1)} %get-tuple-element.44), channel_id=1, source_target_pairs={{0,8},{4,12},{8,0},{12,4},{1,9},{5,13},{9,1},{13,5},{2,10},{6,14},... | collective-permute-start | bytes 589832 | tf_op jit(solution)/shard_map/ppermute | solution.py:19

commit v18 on v17

--- a/solution.py
+++ b/solution.py
@@ -21,7 +21,7 @@
 
 def shifted(value, axis, distance):
     size = lax.axis_size(axis)
-    return lax.ppermute(value, axis, [(i, (i + distance) % size) for i in range(size)])
+    return lax.ppermute(value, axis, [(i, (i - distance) % size) for i in range(size)])
 
 
 def pack_kernel(t_hbm, s_hbm, packed_ref, sems):

time: 40.8 us -> 42.9 us (1.051)
  starting transfers between devices: 13.4 us -> 18.8 us
  waiting for transfers between devices: 11.9 us -> 6.72 us
  blocking collectives: 8.97 us -> 10.9 us
    ppermute x3, starting transfers between devices: 4.03 us -> 8.91 us  [shifted(): lax.ppermute(value, axis, [(i, (i - distance) % size) for i in range(size)])]
    ppermute x3, waiting for transfers between devices: 3.04 us -> 0.01 us  [shifted(): lax.ppermute(value, axis, [(i, (i - distance) % size) for i in range(size)])]
    ppermute x10, waiting for transfers between devices: 8.9 us -> 6.71 us  [exchange(): return lax.ppermute(value, axis, [(i, i ^ distance) for i in range(size)])]
    all_to_all x1, blocking collectives: 8.97 us -> 10.9 us  [to_all(): return lax.all_to_all(value, ('blk', 'sub'), 0, 0, tiled=True)]
    ppermute x10, starting transfers between devices: 9.42 us -> 9.88 us  [exchange(): return lax.ppermute(value, axis, [(i, i ^ distance) for i in range(size)])]
  transfers between devices with their start and end apart: 13 -> 13, of which waited for: 6 -> 6; matrix products, arithmetic and copies ran while one was open for 0% -> 0% of each run, Pallas kernels for 8% -> 7%
where the time goes in v18:
time: 42.9 us; the launch traced here: 42.7 us
  starting transfers between devices  18.8 us (44%)
  blocking collectives  10.9 us (25%)
  waiting for transfers between devices  6.72 us (16%)
  Pallas kernels  5.55 us (13%)
  between operations  0.7 us (2%)
    all_to_all x1, blocking collectives, to_all(): return lax.all_to_all(value, ('blk', 'sub'), 0, 0, tiled=True)  10.9 us
    ppermute x10, starting transfers between devices, exchange(): return lax.ppermute(value, axis, [(i, i ^ distance) for i in range(size)])  9.88 us
    ppermute x3, starting transfers between devices, shifted(): lax.ppermute(value, axis, [(i, (i - distance) % size) for i in range(size)])  8.91 us
    ppermute x10, waiting for transfers between devices, exchange(): return lax.ppermute(value, axis, [(i, i ^ distance) for i in range(size)])  6.71 us
    pallas_call x7, Pallas kernels, call(): pl.pallas_call(kernel, out_shape=out_shape, in_specs=in_specs, out_specs=...  5.55 us
  transfers between devices with their start and end apart: 13, of which 6 were waited for; matrix products, arithmetic and copies ran while one was open for 0% of the time, Pallas kernels for 7%

profile of v18, /device:TPU:0, one launch (start us, length us, event | category | flops | bytes accessed | tf_op | source)
XLA Modules:
  0.0 42.7 jit_solution(4868028275486172699)
XLA Ops:
  0.6 1.0 %shard_map.41.packed_ref.refs_0_ = bf16[128,1408]{1,0:T(8,128)(2,1)S(1)} custom-call(bf16[128,1024]{1,0:T(8,128)(2,1)} %t_hbm.1, bf16[128,384]{1,0:T(8,128)(2,1)} %s_hbm.1), custom_call_target="tpu_custom_call" | custom-call | bytes 360448 | tf_op jit(solution)/shard_map/pallas_call | solution.py:229
  1.6 5.1 %collective-permute-start.1 = (bf16[128,1408]{1,0:T(8,128)(2,1)S(1)}, bf16[128,1408]{1,0:T(8,128)(2,1)S(1)}, u32[]{:S(2)}, u32[]{:S(2)}) collective-permute-start(bf16[128,1408]{1,0:T(8,128)(2,1)S(1)} %shard_map.41.packed_ref.refs_0_), channel_id=1, source_target_pairs={{0,3},{1,0},{2,1},{3,2},{4,7},{5,4},{6,5},{7,6},{8,11},{9,8},{10,9... | collective-permute-start | bytes 1081352 | tf_op jit(solution)/shard_map/ppermute | solution.py:24
  6.7 1.5 %collective-permute-start = (bf16[128,1408]{1,0:T(8,128)(2,1)S(1)}, bf16[128,1408]{1,0:T(8,128)(2,1)S(1)}, u32[]{:S(2)}, u32[]{:S(2)}) collective-permute-start(bf16[128,1408]{1,0:T(8,128)(2,1)S(1)} %shard_map.41.packed_ref.refs_0_), channel_id=1, source_target_pairs={{0,8},{4,12},{8,0},{12,4},{1,9},{5,13},{9,1},{13,5},{2,10},{6,14},... | collective-permute-start | bytes 1081352 | tf_op jit(solution)/shard_map/ppermute | solution.py:19
  8.2 0.2 shard_map.42
  8.4 0.0 collective-permute-start.2
  8.4 1.0 %collective-permute-start.3 = (f32[1,1536]{1,0:T(1,128)S(1)}, f32[1,1536]{1,0:T(1,128)S(1)}, u32[]{:S(2)}, u32[]{:S(2)}) collective-permute-start(f32[1,1536]{1,0:T(1,128)S(1)} %shard_map.42), channel_id=1, source_target_pairs={{0,2},{1,3},{2,0},{3,1},{4,6},{5,7},{6,4},{7,5},{8,10},{9,11},{10,... | collective-permute-start | bytes 18440 | tf_op jit(solution)/shard_map/ppermute | solution.py:19
  9.4 3.4 %collective-permute-start.4 = (f32[1,1536]{1,0:T(1,128)S(1)}, f32[1,1536]{1,0:T(1,128)S(1)}, u32[]{:S(2)}, u32[]{:S(2)}) collective-permute-start(f32[1,1536]{1,0:T(1,128)S(1)} %shard_map.42), channel_id=1, source_target_pairs={{0,3},{1,2},{2,1},{3,0},{4,7},{5,6},{6,5},{7,4},{8,11},{9,10},{10,... | collective-permute-start | bytes 18440 | tf_op jit(solution)/shard_map/ppermute | solution.py:19
  12.8 1.9 %collective-permute-done.2 = f32[1,1536]{1,0:T(1,128)S(1)} collective-permute-done((f32[1,1536]{1,0:T(1,128)S(1)}, f32[1,1536]{1,0:T(1,128)S(1)}, u32[]{:S(2)}, u32[]{:S(2)}) %collective-permute-start.2) | collective-permute-done | bytes 6176 | tf_op jit(solution)/shard_map/ppermute | solution.py:19
  14.7 0.1 collective-permute-done.3
  14.8 0.9 %collective-permute-done.4 = f32[1,1536]{1,0:T(1,128)S(1)} collective-permute-done((f32[1,1536]{1,0:T(1,128)S(1)}, f32[1,1536]{1,0:T(1,128)S(1)}, u32[]{:S(2)}, u32[]{:S(2)}) %collective-permute-start.4) | collective-permute-done | bytes 6176 | tf_op jit(solution)/shard_map/ppermute | solution.py:19
  15.7 0.0 collective-permute-done.1.refs_4_
  15.7 3.4 %collective-permute-start.9 = (bf16[128,1408]{1,0:T(8,128)(2,1)S(1)}, bf16[128,1408]{1,0:T(8,128)(2,1)S(1)}, u32[]{:S(2)}, u32[]{:S(2)}) collective-permute-start(bf16[128,1408]{1,0:T(8,128)(2,1)S(1)} %collective-permute-done.1.refs_4_), channel_id=1, source_target_pairs={{0,3},{1,0},{2,1},{3,2},{4,7},{5,4},{6,5},{7,6},{8,11},{9,8},{10,9... | collective-permute-start | bytes 1081352 | tf_op jit(solution)/shard_map/ppermute | solution.py:24
  19.1 0.0 collective-permute-done.refs_1_
  19.2 0.0 collective-permute-start.5
  19.2 0.5 %collective-permute-start.6 = (bf16[128,1408]{1,0:T(8,128)(2,1)S(1)}, bf16[128,1408]{1,0:T(8,128)(2,1)S(1)}, u32[]{:S(2)}, u32[]{:S(2)}) collective-permute-start(bf16[128,1408]{1,0:T(8,128)(2,1)S(1)} %collective-permute-done.refs_1_), channel_id=1, source_target_pairs={{0,4},{4,0},{8,12},{12,8},{1,5},{5,1},{9,13},{13,9},{2,6},{6,2},{1... | collective-permute-start | bytes 1081352 | tf_op jit(solution)/shard_map/ppermute | solution.py:19
  19.7 1.6 %collective-permute-start.7 = (f32[1,1536]{1,0:T(1,128)S(1)}, f32[1,1536]{1,0:T(1,128)S(1)}, u32[]{:S(2)}, u32[]{:S(2)}) collective-permute-start(f32[1,1536]{1,0:T(1,128)S(1)} %add_add_fusion), channel_id=1, source_target_pairs={{0,8},{4,12},{8,0},{12,4},{1,9},{5,13},{9,1},{13,5},{2,10},{6,14},... | collective-permute-start | bytes 18440 | tf_op jit(solution)/shard_map/ppermute | solution.py:19
  21.3 2.1 %collective-permute-done.7 = f32[1,1536]{1,0:T(1,128)S(1)} collective-permute-done((f32[1,1536]{1,0:T(1,128)S(1)}, f32[1,1536]{1,0:T(1,128)S(1)}, u32[]{:S(2)}, u32[]{:S(2)}) %collective-permute-start.7) | collective-permute-done | bytes 6176 | tf_op jit(solution)/shard_map/ppermute | solution.py:19
  23.4 0.1 collective-permute-start.8
  23.5 1.2 %collective-permute-done.8.refs_6_ = f32[1,1536]{1,0:T(1,128)S(1)} collective-permute-done((f32[1,1536]{1,0:T(1,128)S(1)}, f32[1,1536]{1,0:T(1,128)S(1)}, u32[]{:S(2)}, u32[]{:S(2)}) %collective-permute-start.8) | collective-permute-done | bytes 6176 | tf_op jit(solution)/shard_map/ppermute | solution.py:19
  24.6 0.0 collective-permute-done.5.refs_2_
  24.6 0.0 collective-permute-done.6.refs_3_
  24.6 2.2 %shard_map.43 = (f32[128,384]{1,0:T(8,128)S(1)}, f32[128,384]{1,0:T(8,128)S(1)}, f32[2,256,512]{2,1,0:T(8,128)S(1)}, f32[2,2,256,128]{3,2,1,0:T(8,128)S(1)}, f32...) custom-call(bf16[128,1408]{1,0:T(8,128)(2,1)S(1)} %shard_map.41.packed_ref.refs_0_, ...), custom_call_target="tpu_custom_call" | custom-call | flops 570425344 | bytes 1814528 | tf_op jit(solution)/shard_map/pallas_call | solution.py:229
  26.9 0.7 %shard_map.44 = (f32[256,384]{1,0:T(8,128)S(1)}, f32[2,128]{1,0:T(2,128)S(1)}, f32[2,128]{1,0:T(2,128)S(1)}) custom-call(bf16[2,256,1408]{2,1,0:T(8,128)(2,1)S(1)} %get-tuple-element.33.refs_0_, bf16[128,1408]{1,0:T(8,128)(2,1)S(1)} %collective-permute-done.9.refs_1_, f32[4,384]{1,0:T(4,128)S(1)} %get-tuple-element.32.refs_2_.stats_ref, ...), custom_call_target="tpu_custom_call" | custom-call | flops 142606336 | bytes 3382272 | tf_op jit(solution)/shard_map/pallas_call | solution.py:229
  27.5 0.2 collective-permute-start.10
  27.8 0.4 collective-permute-start.12
  28.1 0.6 %shard_map.45 = (f32[256,384]{1,0:T(8,128)S(1)}, f32[16,2,128]{2,1,0:T(2,128)S(1)}) custom-call(bf16[2,256,1408]{2,1,0:T(8,128)(2,1)S(1)} %get-tuple-element.33.refs_0_, bf16[128,1408]{1,0:T(8,128)(2,1)S(1)} %collective-permute-done.9.refs_1_, f32[4,384]{1,0:T(4,128)S(1)} %get-tuple-element.32.refs_2_.stats_ref, ...), custom_call_target="tpu_custom_call" | custom-call | flops 142606336 | bytes 3383296 | tf_op jit(solution)/shard_map/pallas_call | solution.py:229
  28.8 0.5 %collective-permute-done.10.got_ref = f32[256,384]{1,0:T(8,128)S(1)} collective-permute-done((f32[256,384]{1,0:T(8,128)S(1)}, f32[256,384]{1,0:T(8,128)S(1)}, u32[]{:S(2)}, u32[]{:S(2)}) %collective-permute-start.10) | collective-permute-done | bytes 393248 | tf_op jit(solution)/shard_map/ppermute | solution.py:19
  29.4 1.6 %collective-permute-start.11 = (f32[128,384]{1,0:T(8,128)S(1)}, f32[128,384]{1,0:T(8,128)S(1)}, u32[]{:S(2)}, u32[]{:S(2)}) collective-permute-start(f32[128,384]{1,0:T(8,128)S(1)} %get-tuple-element.44), channel_id=1, source_target_pairs={{0,8},{4,12},{8,0},{12,4},{1,9},{5,13},{9,1},{13,5},{2,10},{6,14},... | collective-permute-start | bytes 589832 | tf_op jit(solution)/shard_map/ppermute | solution.py:19
  31.0 10.9 %all_to_all.5.sums_ref = f32[16,2,128]{2,1,0:T(2,128)S(1)} all-to-all(f32[16,2,128]{2,1,0:T(2,128)S(1)} %get-tuple-element.39), channel_id=1, replica_groups=mesh['groups'=2,'blk'=4,'sub'=4] {'blk','sub'}, dimensions={0} | all-to-all | bytes 32768 | tf_op jit(solution)/shard_map/all_to_all | solution.py:250
  41.9 0.0 collective-permute-done.12.refs_3_
  41.9 0.0 collective-permute-done.11.refs_2_
  41.9 0.8 %shard_map.47 = (f32[128,384]{1,0:T(8,128)}, f32[1,128]{1,0:T(1,128)}) custom-call(bf16[128,1408]{1,0:T(8,128)(2,1)S(1)} %shard_map.41.packed_ref.refs_0_, f32[4,384]{1,0:T(4,128)S(1)} %get-tuple-element.32.refs_2_.stats_ref, f32[16,2,128]{2,1,0:T(2,128)S(1)} %all_to_all.5.sums_ref, f32[128,384]{1,0:T(8,128)S(1)} %get-tuple-element.40.refs_0_, ...), custom_call_target="tpu_custom_call" | custom-call | flops 393216 | bytes 1169408 | tf_op jit(solution)/shard_map/pallas_call | solution.py:229
  (4 shorter events, 0.1 us)
Async XLA Ops:
  1.6 14.1 %collective-permute-start.1 = (bf16[128,1408]{1,0:T(8,128)(2,1)S(1)}, bf16[128,1408]{1,0:T(8,128)(2,1)S(1)}, u32[]{:S(2)}, u32[]{:S(2)}) collective-permute-start(bf16[128,1408]{1,0:T(8,128)(2,1)S(1)} %shard_map.41.packed_ref.refs_0_), channel_id=1, source_target_pairs={{0,3},{1,0},{2,1},{3,2},{4,7},{5,4},{6,5},{7,6},{8,11},{9,8},{10,9... | collective-permute-start | bytes 1081352 | tf_op jit(solution)/shard_map/ppermute | solution.py:24
  6.7 12.4 %collective-permute-start = (bf16[128,1408]{1,0:T(8,128)(2,1)S(1)}, bf16[128,1408]{1,0:T(8,128)(2,1)S(1)}, u32[]{:S(2)}, u32[]{:S(2)}) collective-permute-start(bf16[128,1408]{1,0:T(8,128)(2,1)S(1)} %shard_map.41.packed_ref.refs_0_), channel_id=1, source_target_pairs={{0,8},{4,12},{8,0},{12,4},{1,9},{5,13},{9,1},{13,5},{2,10},{6,14},... | collective-permute-start | bytes 1081352 | tf_op jit(solution)/shard_map/ppermute | solution.py:19
  8.4 6.3 %collective-permute-start.2 = (f32[1,1536]{1,0:T(1,128)S(1)}, f32[1,1536]{1,0:T(1,128)S(1)}, u32[]{:S(2)}, u32[]{:S(2)}) collective-permute-start(f32[1,1536]{1,0:T(1,128)S(1)} %shard_map.42), channel_id=1, source_target_pairs={{0,1},{1,0},{2,3},{3,2},{4,5},{5,4},{6,7},{7,6},{8,9},{9,8},{10,11... | collective-permute-start | bytes 18440 | tf_op jit(solution)/shard_map/ppermute | solution.py:19
  8.4 6.3 %collective-permute-start.3 = (f32[1,1536]{1,0:T(1,128)S(1)}, f32[1,1536]{1,0:T(1,128)S(1)}, u32[]{:S(2)}, u32[]{:S(2)}) collective-permute-start(f32[1,1536]{1,0:T(1,128)S(1)} %shard_map.42), channel_id=1, source_target_pairs={{0,2},{1,3},{2,0},{3,1},{4,6},{5,7},{6,4},{7,5},{8,10},{9,11},{10,... | collective-permute-start | bytes 18440 | tf_op jit(solution)/shard_map/ppermute | solution.py:19
  9.4 6.3 %collective-permute-start.4 = (f32[1,1536]{1,0:T(1,128)S(1)}, f32[1,1536]{1,0:T(1,128)S(1)}, u32[]{:S(2)}, u32[]{:S(2)}) collective-permute-start(f32[1,1536]{1,0:T(1,128)S(1)} %shard_map.42), channel_id=1, source_target_pairs={{0,3},{1,2},{2,1},{3,0},{4,7},{5,6},{6,5},{7,4},{8,11},{9,10},{10,... | collective-permute-start | bytes 18440 | tf_op jit(solution)/shard_map/ppermute | solution.py:19
  15.7 11.2 %collective-permute-start.9 = (bf16[128,1408]{1,0:T(8,128)(2,1)S(1)}, bf16[128,1408]{1,0:T(8,128)(2,1)S(1)}, u32[]{:S(2)}, u32[]{:S(2)}) collective-permute-start(bf16[128,1408]{1,0:T(8,128)(2,1)S(1)} %collective-permute-done.1.refs_4_), channel_id=1, source_target_pairs={{0,3},{1,0},{2,1},{3,2},{4,7},{5,4},{6,5},{7,6},{8,11},{9,8},{10,9... | collective-permute-start | bytes 1081352 | tf_op jit(solution)/shard_map/ppermute | solution.py:24
  19.2 5.5 %collective-permute-start.5 = (bf16[128,1408]{1,0:T(8,128)(2,1)S(1)}, bf16[128,1408]{1,0:T(8,128)(2,1)S(1)}, u32[]{:S(2)}, u32[]{:S(2)}) collective-permute-start(bf16[128,1408]{1,0:T(8,128)(2,1)S(1)} %shard_map.41.packed_ref.refs_0_), channel_id=1, source_target_pairs={{0,4},{4,0},{8,12},{12,8},{1,5},{5,1},{9,13},{13,9},{2,6},{6,2},{1... | collective-permute-start | bytes 1081352 | tf_op jit(solution)/shard_map/ppermute | solution.py:19
  19.2 5.5 %collective-permute-start.6 = (bf16[128,1408]{1,0:T(8,128)(2,1)S(1)}, bf16[128,1408]{1,0:T(8,128)(2,1)S(1)}, u32[]{:S(2)}, u32[]{:S(2)}) collective-permute-start(bf16[128,1408]{1,0:T(8,128)(2,1)S(1)} %collective-permute-done.refs_1_), channel_id=1, source_target_pairs={{0,4},{4,0},{8,12},{12,8},{1,5},{5,1},{9,13},{13,9},{2,6},{6,2},{1... | collective-permute-start | bytes 1081352 | tf_op jit(solution)/shard_map/ppermute | solution.py:19
  19.7 3.7 %collective-permute-start.7 = (f32[1,1536]{1,0:T(1,128)S(1)}, f32[1,1536]{1,0:T(1,128)S(1)}, u32[]{:S(2)}, u32[]{:S(2)}) collective-permute-start(f32[1,1536]{1,0:T(1,128)S(1)} %add_add_fusion), channel_id=1, source_target_pairs={{0,8},{4,12},{8,0},{12,4},{1,9},{5,13},{9,1},{13,5},{2,10},{6,14},... | collective-permute-start | bytes 18440 | tf_op jit(solution)/shard_map/ppermute | solution.py:19
  23.4 1.2 %collective-permute-start.8 = (f32[1,1536]{1,0:T(1,128)S(1)}, f32[1,1536]{1,0:T(1,128)S(1)}, u32[]{:S(2)}, u32[]{:S(2)}) collective-permute-start(f32[1,1536]{1,0:T(1,128)S(1)} %add.15.refs_5_), channel_id=1, source_target_pairs={{0,4},{4,0},{8,12},{12,8},{1,5},{5,1},{9,13},{13,9},{2,6},{6,2},{1... | collective-permute-start | bytes 18440 | tf_op jit(solution)/shard_map/ppermute | solution.py:19
  27.5 1.8 %collective-permute-start.10 = (f32[256,384]{1,0:T(8,128)S(1)}, f32[256,384]{1,0:T(8,128)S(1)}, u32[]{:S(2)}, u32[]{:S(2)}) collective-permute-start(f32[256,384]{1,0:T(8,128)S(1)} %get-tuple-element.42), channel_id=1, source_target_pairs={{0,4},{4,0},{8,12},{12,8},{1,5},{5,1},{9,13},{13,9},{2,6},{6,2},{1... | collective-permute-start | bytes 1179656 | tf_op jit(solution)/shard_map/ppermute | solution.py:19
  27.8 14.1 %collective-permute-start.12 = (f32[128,384]{1,0:T(8,128)S(1)}, f32[128,384]{1,0:T(8,128)S(1)}, u32[]{:S(2)}, u32[]{:S(2)}) collective-permute-start(f32[128,384]{1,0:T(8,128)S(1)} %get-tuple-element.45), channel_id=1, source_target_pairs={{0,1},{1,2},{2,3},{3,0},{4,5},{5,6},{6,7},{7,4},{8,9},{9,10},{10,1... | collective-permute-start | bytes 589832 | tf_op jit(solution)/shard_map/ppermute | solution.py:24
  29.4 12.5 %collective-permute-start.11 = (f32[128,384]{1,0:T(8,128)S(1)}, f32[128,384]{1,0:T(8,128)S(1)}, u32[]{:S(2)}, u32[]{:S(2)}) collective-permute-start(f32[128,384]{1,0:T(8,128)S(1)} %get-tuple-element.44), channel_id=1, source_target_pairs={{0,8},{4,12},{8,0},{12,4},{1,9},{5,13},{9,1},{13,5},{2,10},{6,14},... | collective-permute-start | bytes 589832 | tf_op jit(solution)/shard_map/ppermute | solution.py:19

commit v19 on v18

--- a/solution.py
+++ b/solution.py
@@ -21,7 +21,9 @@
 
 def shifted(value, axis, distance):
     size = lax.axis_size(axis)
-    return lax.ppermute(value, axis, [(i, (i - distance) % size) for i in range(size)])
+    places = [0, *range(1, size, 2), *reversed(range(2, size, 2))]
+    route = [(places[i], places[(i + distance) % size]) for i in range(size)]
+    return lax.ppermute(value, axis, route)
 
 
 def pack_kernel(t_hbm, s_hbm, packed_ref, sems):

time: 42.9 us -> 40.9 us (0.953)
  starting transfers between devices: 18.8 us -> 15 us
  waiting for transfers between devices: 6.72 us -> 9.27 us
  blocking collectives: 10.9 us -> 10.2 us
    ppermute x3, starting transfers between devices: 8.91 us -> 4.61 us  [shifted(): return lax.ppermute(value, axis, route)]
    ppermute x3, waiting for transfers between devices: 0.01 us -> 1.68 us  [shifted(): return lax.ppermute(value, axis, route)]
    ppermute x10, waiting for transfers between devices: 6.71 us -> 7.58 us  [exchange(): return lax.ppermute(value, axis, [(i, i ^ distance) for i in range(size)])]
    all_to_all x1, blocking collectives: 10.9 us -> 10.2 us  [to_all(): return lax.all_to_all(value, ('blk', 'sub'), 0, 0, tiled=True)]
    ppermute x10, starting transfers between devices: 9.88 us -> 10.4 us  [exchange(): return lax.ppermute(value, axis, [(i, i ^ distance) for i in range(size)])]
  transfers between devices with their start and end apart: 13 -> 13, of which waited for: 6 -> 6; matrix products, arithmetic and copies ran while one was open for 0% -> 0% of each run, Pallas kernels for 7% -> 8%
where the time goes in v19:
time: 40.9 us; the launch traced here: 40.7 us
  starting transfers between devices  15 us (37%)
  blocking collectives  10.2 us (25%)
  waiting for transfers between devices  9.27 us (23%)
  Pallas kernels  5.54 us (14%)
  between operations  0.69 us (2%)
    ppermute x10, starting transfers between devices, exchange(): return lax.ppermute(value, axis, [(i, i ^ distance) for i in range(size)])  10.4 us
    all_to_all x1, blocking collectives, to_all(): return lax.all_to_all(value, ('blk', 'sub'), 0, 0, tiled=True)  10.2 us
    ppermute x10, waiting for transfers between devices, exchange(): return lax.ppermute(value, axis, [(i, i ^ distance) for i in range(size)])  7.58 us
    pallas_call x7, Pallas kernels, call(): pl.pallas_call(kernel, out_shape=out_shape, in_specs=in_specs, out_specs=...  5.54 us
    ppermute x3, starting transfers between devices, shifted(): return lax.ppermute(value, axis, route)  4.61 us
    ppermute x3, waiting for transfers between devices, shifted(): return lax.ppermute(value, axis, route)  1.68 us
  transfers between devices with their start and end apart: 13, of which 6 were waited for; matrix products, arithmetic and copies ran while one was open for 0% of the time, Pallas kernels for 8%

profile of v19, /device:TPU:0, one launch (start us, length us, event | category | flops | bytes accessed | tf_op | source)
XLA Modules:
  0.0 40.7 jit_solution(11050414037497442025)
XLA Ops:
  0.6 1.0 %shard_map.41.packed_ref.refs_0_ = bf16[128,1408]{1,0:T(8,128)(2,1)S(1)} custom-call(bf16[128,1024]{1,0:T(8,128)(2,1)} %t_hbm.1, bf16[128,384]{1,0:T(8,128)(2,1)} %s_hbm.1), custom_call_target="tpu_custom_call" | custom-call | bytes 360448 | tf_op jit(solution)/shard_map/pallas_call | solution.py:231
  1.6 3.1 %collective-permute-start.1 = (bf16[128,1408]{1,0:T(8,128)(2,1)S(1)}, bf16[128,1408]{1,0:T(8,128)(2,1)S(1)}, u32[]{:S(2)}, u32[]{:S(2)}) collective-permute-start(bf16[128,1408]{1,0:T(8,128)(2,1)S(1)} %shard_map.41.packed_ref.refs_0_), channel_id=1, source_target_pairs={{0,1},{1,3},{3,2},{2,0},{4,5},{5,7},{7,6},{6,4},{8,9},{9,11},{11,1... | collective-permute-start | bytes 1081352 | tf_op jit(solution)/shard_map/ppermute | solution.py:26
  4.7 1.5 %collective-permute-start = (bf16[128,1408]{1,0:T(8,128)(2,1)S(1)}, bf16[128,1408]{1,0:T(8,128)(2,1)S(1)}, u32[]{:S(2)}, u32[]{:S(2)}) collective-permute-start(bf16[128,1408]{1,0:T(8,128)(2,1)S(1)} %shard_map.41.packed_ref.refs_0_), channel_id=1, source_target_pairs={{0,8},{4,12},{8,0},{12,4},{1,9},{5,13},{9,1},{13,5},{2,10},{6,14},... | collective-permute-start | bytes 1081352 | tf_op jit(solution)/shard_map/ppermute | solution.py:19
  6.2 0.2 shard_map.42
  6.4 2.6 %collective-permute-start.2 = (f32[1,1536]{1,0:T(1,128)S(1)}, f32[1,1536]{1,0:T(1,128)S(1)}, u32[]{:S(2)}, u32[]{:S(2)}) collective-permute-start(f32[1,1536]{1,0:T(1,128)S(1)} %shard_map.42), channel_id=1, source_target_pairs={{0,1},{1,0},{2,3},{3,2},{4,5},{5,4},{6,7},{7,6},{8,9},{9,8},{10,11... | collective-permute-start | bytes 18440 | tf_op jit(solution)/shard_map/ppermute | solution.py:19
  9.0 0.4 %collective-permute-start.3 = (f32[1,1536]{1,0:T(1,128)S(1)}, f32[1,1536]{1,0:T(1,128)S(1)}, u32[]{:S(2)}, u32[]{:S(2)}) collective-permute-start(f32[1,1536]{1,0:T(1,128)S(1)} %shard_map.42), channel_id=1, source_target_pairs={{0,2},{1,3},{2,0},{3,1},{4,6},{5,7},{6,4},{7,5},{8,10},{9,11},{10,... | collective-permute-start | bytes 18440 | tf_op jit(solution)/shard_map/ppermute | solution.py:19
  9.4 2.0 %collective-permute-start.4 = (f32[1,1536]{1,0:T(1,128)S(1)}, f32[1,1536]{1,0:T(1,128)S(1)}, u32[]{:S(2)}, u32[]{:S(2)}) collective-permute-start(f32[1,1536]{1,0:T(1,128)S(1)} %shard_map.42), channel_id=1, source_target_pairs={{0,3},{1,2},{2,1},{3,0},{4,7},{5,6},{6,5},{7,4},{8,11},{9,10},{10,... | collective-permute-start | bytes 18440 | tf_op jit(solution)/shard_map/ppermute | solution.py:19
  11.4 2.4 %collective-permute-done.2 = f32[1,1536]{1,0:T(1,128)S(1)} collective-permute-done((f32[1,1536]{1,0:T(1,128)S(1)}, f32[1,1536]{1,0:T(1,128)S(1)}, u32[]{:S(2)}, u32[]{:S(2)}) %collective-permute-start.2) | collective-permute-done | bytes 6176 | tf_op jit(solution)/shard_map/ppermute | solution.py:19
  13.8 0.6 %collective-permute-done.3 = f32[1,1536]{1,0:T(1,128)S(1)} collective-permute-done((f32[1,1536]{1,0:T(1,128)S(1)}, f32[1,1536]{1,0:T(1,128)S(1)}, u32[]{:S(2)}, u32[]{:S(2)}) %collective-permute-start.3) | collective-permute-done | bytes 6176 | tf_op jit(solution)/shard_map/ppermute | solution.py:19
  14.4 1.3 %collective-permute-done.4 = f32[1,1536]{1,0:T(1,128)S(1)} collective-permute-done((f32[1,1536]{1,0:T(1,128)S(1)}, f32[1,1536]{1,0:T(1,128)S(1)}, u32[]{:S(2)}, u32[]{:S(2)}) %collective-permute-start.4) | collective-permute-done | bytes 6176 | tf_op jit(solution)/shard_map/ppermute | solution.py:19
  15.7 0.0 collective-permute-done.1.refs_4_
  15.7 0.5 %collective-permute-start.9 = (bf16[128,1408]{1,0:T(8,128)(2,1)S(1)}, bf16[128,1408]{1,0:T(8,128)(2,1)S(1)}, u32[]{:S(2)}, u32[]{:S(2)}) collective-permute-start(bf16[128,1408]{1,0:T(8,128)(2,1)S(1)} %collective-permute-done.1.refs_4_), channel_id=1, source_target_pairs={{0,1},{1,3},{3,2},{2,0},{4,5},{5,7},{7,6},{6,4},{8,9},{9,11},{11,1... | collective-permute-start | bytes 1081352 | tf_op jit(solution)/shard_map/ppermute | solution.py:26
  16.2 0.0 collective-permute-done.refs_1_
  16.2 0.0 collective-permute-start.5
  16.2 0.5 %collective-permute-start.6 = (bf16[128,1408]{1,0:T(8,128)(2,1)S(1)}, bf16[128,1408]{1,0:T(8,128)(2,1)S(1)}, u32[]{:S(2)}, u32[]{:S(2)}) collective-permute-start(bf16[128,1408]{1,0:T(8,128)(2,1)S(1)} %collective-permute-done.refs_1_), channel_id=1, source_target_pairs={{0,4},{4,0},{8,12},{12,8},{1,5},{5,1},{9,13},{13,9},{2,6},{6,2},{1... | collective-permute-start | bytes 1081352 | tf_op jit(solution)/shard_map/ppermute | solution.py:19
  16.7 1.6 %collective-permute-start.7 = (f32[1,1536]{1,0:T(1,128)S(1)}, f32[1,1536]{1,0:T(1,128)S(1)}, u32[]{:S(2)}, u32[]{:S(2)}) collective-permute-start(f32[1,1536]{1,0:T(1,128)S(1)} %add_add_fusion), channel_id=1, source_target_pairs={{0,8},{4,12},{8,0},{12,4},{1,9},{5,13},{9,1},{13,5},{2,10},{6,14},... | collective-permute-start | bytes 18440 | tf_op jit(solution)/shard_map/ppermute | solution.py:19
  18.3 2.1 %collective-permute-done.7 = f32[1,1536]{1,0:T(1,128)S(1)} collective-permute-done((f32[1,1536]{1,0:T(1,128)S(1)}, f32[1,1536]{1,0:T(1,128)S(1)}, u32[]{:S(2)}, u32[]{:S(2)}) %collective-permute-start.7) | collective-permute-done | bytes 6176 | tf_op jit(solution)/shard_map/ppermute | solution.py:19
  20.4 0.1 collective-permute-start.8
  20.5 1.2 %collective-permute-done.8.refs_6_ = f32[1,1536]{1,0:T(1,128)S(1)} collective-permute-done((f32[1,1536]{1,0:T(1,128)S(1)}, f32[1,1536]{1,0:T(1,128)S(1)}, u32[]{:S(2)}, u32[]{:S(2)}) %collective-permute-start.8) | collective-permute-done | bytes 6176 | tf_op jit(solution)/shard_map/ppermute | solution.py:19
  21.7 0.0 collective-permute-done.5.refs_2_
  21.7 0.0 collective-permute-done.6.refs_3_
  21.7 2.2 %shard_map.43 = (f32[128,384]{1,0:T(8,128)S(1)}, f32[128,384]{1,0:T(8,128)S(1)}, f32[2,256,512]{2,1,0:T(8,128)S(1)}, f32[2,2,256,128]{3,2,1,0:T(8,128)S(1)}, f32...) custom-call(bf16[128,1408]{1,0:T(8,128)(2,1)S(1)} %shard_map.41.packed_ref.refs_0_, ...), custom_call_target="tpu_custom_call" | custom-call | flops 570425344 | bytes 1814528 | tf_op jit(solution)/shard_map/pallas_call | solution.py:231
  23.9 1.7 %collective-permute-done.9.refs_1_ = bf16[128,1408]{1,0:T(8,128)(2,1)S(1)} collective-permute-done((bf16[128,1408]{1,0:T(8,128)(2,1)S(1)}, bf16[128,1408]{1,0:T(8,128)(2,1)S(1)}, u32[]{:S(2)}, u32[]{:S(2)}) %collective-permute-start.9) | collective-permute-done | bytes 360480 | tf_op jit(solution)/shard_map/ppermute | solution.py:26
  25.6 0.7 %shard_map.44 = (f32[256,384]{1,0:T(8,128)S(1)}, f32[2,128]{1,0:T(2,128)S(1)}, f32[2,128]{1,0:T(2,128)S(1)}) custom-call(bf16[2,256,1408]{2,1,0:T(8,128)(2,1)S(1)} %get-tuple-element.33.refs_0_, bf16[128,1408]{1,0:T(8,128)(2,1)S(1)} %collective-permute-done.9.refs_1_, f32[4,384]{1,0:T(4,128)S(1)} %get-tuple-element.32.refs_2_.stats_ref, ...), custom_call_target="tpu_custom_call" | custom-call | flops 142606336 | bytes 3382272 | tf_op jit(solution)/shard_map/pallas_call | solution.py:231
  26.3 0.1 collective-permute-start.10
  26.3 1.0 %collective-permute-start.12 = (f32[128,384]{1,0:T(8,128)S(1)}, f32[128,384]{1,0:T(8,128)S(1)}, u32[]{:S(2)}, u32[]{:S(2)}) collective-permute-start(f32[128,384]{1,0:T(8,128)S(1)} %get-tuple-element.45), channel_id=1, source_target_pairs={{0,2},{1,0},{3,1},{2,3},{4,6},{5,4},{7,5},{6,7},{8,10},{9,8},{11,9... | collective-permute-start | bytes 589832 | tf_op jit(solution)/shard_map/ppermute | solution.py:26
  27.4 0.6 %shard_map.45 = (f32[256,384]{1,0:T(8,128)S(1)}, f32[16,2,128]{2,1,0:T(2,128)S(1)}) custom-call(bf16[2,256,1408]{2,1,0:T(8,128)(2,1)S(1)} %get-tuple-element.33.refs_0_, bf16[128,1408]{1,0:T(8,128)(2,1)S(1)} %collective-permute-done.9.refs_1_, f32[4,384]{1,0:T(4,128)S(1)} %get-tuple-element.32.refs_2_.stats_ref, ...), custom_call_target="tpu_custom_call" | custom-call | flops 142606336 | bytes 3383296 | tf_op jit(solution)/shard_map/pallas_call | solution.py:231
  28.0 0.0 collective-permute-done.10.got_ref
  28.1 1.6 %collective-permute-start.11 = (f32[128,384]{1,0:T(8,128)S(1)}, f32[128,384]{1,0:T(8,128)S(1)}, u32[]{:S(2)}, u32[]{:S(2)}) collective-permute-start(f32[128,384]{1,0:T(8,128)S(1)} %get-tuple-element.44), channel_id=1, source_target_pairs={{0,8},{4,12},{8,0},{12,4},{1,9},{5,13},{9,1},{13,5},{2,10},{6,14},... | collective-permute-start | bytes 589832 | tf_op jit(solution)/shard_map/ppermute | solution.py:19
  29.7 10.2 %all_to_all.5.sums_ref = f32[16,2,128]{2,1,0:T(2,128)S(1)} all-to-all(f32[16,2,128]{2,1,0:T(2,128)S(1)} %get-tuple-element.39), channel_id=1, replica_groups=mesh['groups'=2,'blk'=4,'sub'=4] {'blk','sub'}, dimensions={0} | all-to-all | bytes 32768 | tf_op jit(solution)/shard_map/all_to_all | solution.py:252
  39.9 0.0 collective-permute-done.11.refs_2_
  39.9 0.8 %shard_map.47 = (f32[128,384]{1,0:T(8,128)}, f32[1,128]{1,0:T(1,128)}) custom-call(bf16[128,1408]{1,0:T(8,128)(2,1)S(1)} %shard_map.41.packed_ref.refs_0_, f32[4,384]{1,0:T(4,128)S(1)} %get-tuple-element.32.refs_2_.stats_ref, f32[16,2,128]{2,1,0:T(2,128)S(1)} %all_to_all.5.sums_ref, f32[128,384]{1,0:T(8,128)S(1)} %get-tuple-element.40.refs_0_, ...), custom_call_target="tpu_custom_call" | custom-call | flops 393216 | bytes 1169408 | tf_op jit(solution)/shard_map/pallas_call | solution.py:231
  (4 shorter events, 0.1 us)
Async XLA Ops:
  1.6 14.1 %collective-permute-start.1 = (bf16[128,1408]{1,0:T(8,128)(2,1)S(1)}, bf16[128,1408]{1,0:T(8,128)(2,1)S(1)}, u32[]{:S(2)}, u32[]{:S(2)}) collective-permute-start(bf16[128,1408]{1,0:T(8,128)(2,1)S(1)} %shard_map.41.packed_ref.refs_0_), channel_id=1, source_target_pairs={{0,1},{1,3},{3,2},{2,0},{4,5},{5,7},{7,6},{6,4},{8,9},{9,11},{11,1... | collective-permute-start | bytes 1081352 | tf_op jit(solution)/shard_map/ppermute | solution.py:26
  4.7 11.5 %collective-permute-start = (bf16[128,1408]{1,0:T(8,128)(2,1)S(1)}, bf16[128,1408]{1,0:T(8,128)(2,1)S(1)}, u32[]{:S(2)}, u32[]{:S(2)}) collective-permute-start(bf16[128,1408]{1,0:T(8,128)(2,1)S(1)} %shard_map.41.packed_ref.refs_0_), channel_id=1, source_target_pairs={{0,8},{4,12},{8,0},{12,4},{1,9},{5,13},{9,1},{13,5},{2,10},{6,14},... | collective-permute-start | bytes 1081352 | tf_op jit(solution)/shard_map/ppermute | solution.py:19
  6.4 7.4 %collective-permute-start.2 = (f32[1,1536]{1,0:T(1,128)S(1)}, f32[1,1536]{1,0:T(1,128)S(1)}, u32[]{:S(2)}, u32[]{:S(2)}) collective-permute-start(f32[1,1536]{1,0:T(1,128)S(1)} %shard_map.42), channel_id=1, source_target_pairs={{0,1},{1,0},{2,3},{3,2},{4,5},{5,4},{6,7},{7,6},{8,9},{9,8},{10,11... | collective-permute-start | bytes 18440 | tf_op jit(solution)/shard_map/ppermute | solution.py:19
  9.0 5.5 %collective-permute-start.3 = (f32[1,1536]{1,0:T(1,128)S(1)}, f32[1,1536]{1,0:T(1,128)S(1)}, u32[]{:S(2)}, u32[]{:S(2)}) collective-permute-start(f32[1,1536]{1,0:T(1,128)S(1)} %shard_map.42), channel_id=1, source_target_pairs={{0,2},{1,3},{2,0},{3,1},{4,6},{5,7},{6,4},{7,5},{8,10},{9,11},{10,... | collective-permute-start | bytes 18440 | tf_op jit(solution)/shard_map/ppermute | solution.py:19
  9.4 6.3 %collective-permute-start.4 = (f32[1,1536]{1,0:T(1,128)S(1)}, f32[1,1536]{1,0:T(1,128)S(1)}, u32[]{:S(2)}, u32[]{:S(2)}) collective-permute-start(f32[1,1536]{1,0:T(1,128)S(1)} %shard_map.42), channel_id=1, source_target_pairs={{0,3},{1,2},{2,1},{3,0},{4,7},{5,6},{6,5},{7,4},{8,11},{9,10},{10,... | collective-permute-start | bytes 18440 | tf_op jit(solution)/shard_map/ppermute | solution.py:19
  15.7 9.9 %collective-permute-start.9 = (bf16[128,1408]{1,0:T(8,128)(2,1)S(1)}, bf16[128,1408]{1,0:T(8,128)(2,1)S(1)}, u32[]{:S(2)}, u32[]{:S(2)}) collective-permute-start(bf16[128,1408]{1,0:T(8,128)(2,1)S(1)} %collective-permute-done.1.refs_4_), channel_id=1, source_target_pairs={{0,1},{1,3},{3,2},{2,0},{4,5},{5,7},{7,6},{6,4},{8,9},{9,11},{11,1... | collective-permute-start | bytes 1081352 | tf_op jit(solution)/shard_map/ppermute | solution.py:26
  16.2 5.5 %collective-permute-start.5 = (bf16[128,1408]{1,0:T(8,128)(2,1)S(1)}, bf16[128,1408]{1,0:T(8,128)(2,1)S(1)}, u32[]{:S(2)}, u32[]{:S(2)}) collective-permute-start(bf16[128,1408]{1,0:T(8,128)(2,1)S(1)} %shard_map.41.packed_ref.refs_0_), channel_id=1, source_target_pairs={{0,4},{4,0},{8,12},{12,8},{1,5},{5,1},{9,13},{13,9},{2,6},{6,2},{1... | collective-permute-start | bytes 1081352 | tf_op jit(solution)/shard_map/ppermute | solution.py:19
  16.2 5.5 %collective-permute-start.6 = (bf16[128,1408]{1,0:T(8,128)(2,1)S(1)}, bf16[128,1408]{1,0:T(8,128)(2,1)S(1)}, u32[]{:S(2)}, u32[]{:S(2)}) collective-permute-start(bf16[128,1408]{1,0:T(8,128)(2,1)S(1)} %collective-permute-done.refs_1_), channel_id=1, source_target_pairs={{0,4},{4,0},{8,12},{12,8},{1,5},{5,1},{9,13},{13,9},{2,6},{6,2},{1... | collective-permute-start | bytes 1081352 | tf_op jit(solution)/shard_map/ppermute | solution.py:19
  16.7 3.7 %collective-permute-start.7 = (f32[1,1536]{1,0:T(1,128)S(1)}, f32[1,1536]{1,0:T(1,128)S(1)}, u32[]{:S(2)}, u32[]{:S(2)}) collective-permute-start(f32[1,1536]{1,0:T(1,128)S(1)} %add_add_fusion), channel_id=1, source_target_pairs={{0,8},{4,12},{8,0},{12,4},{1,9},{5,13},{9,1},{13,5},{2,10},{6,14},... | collective-permute-start | bytes 18440 | tf_op jit(solution)/shard_map/ppermute | solution.py:19
  20.4 1.2 %collective-permute-start.8 = (f32[1,1536]{1,0:T(1,128)S(1)}, f32[1,1536]{1,0:T(1,128)S(1)}, u32[]{:S(2)}, u32[]{:S(2)}) collective-permute-start(f32[1,1536]{1,0:T(1,128)S(1)} %add.15.refs_5_), channel_id=1, source_target_pairs={{0,4},{4,0},{8,12},{12,8},{1,5},{5,1},{9,13},{13,9},{2,6},{6,2},{1... | collective-permute-start | bytes 18440 | tf_op jit(solution)/shard_map/ppermute | solution.py:19
  26.3 1.8 %collective-permute-start.10 = (f32[256,384]{1,0:T(8,128)S(1)}, f32[256,384]{1,0:T(8,128)S(1)}, u32[]{:S(2)}, u32[]{:S(2)}) collective-permute-start(f32[256,384]{1,0:T(8,128)S(1)} %get-tuple-element.42), channel_id=1, source_target_pairs={{0,4},{4,0},{8,12},{12,8},{1,5},{5,1},{9,13},{13,9},{2,6},{6,2},{1... | collective-permute-start | bytes 1179656 | tf_op jit(solution)/shard_map/ppermute | solution.py:19
  26.3 13.6 %collective-permute-start.12 = (f32[128,384]{1,0:T(8,128)S(1)}, f32[128,384]{1,0:T(8,128)S(1)}, u32[]{:S(2)}, u32[]{:S(2)}) collective-permute-start(f32[128,384]{1,0:T(8,128)S(1)} %get-tuple-element.45), channel_id=1, source_target_pairs={{0,2},{1,0},{3,1},{2,3},{4,6},{5,4},{7,5},{6,7},{8,10},{9,8},{11,9... | collective-permute-start | bytes 589832 | tf_op jit(solution)/shard_map/ppermute | solution.py:26
  28.1 11.8 %collective-permute-start.11 = (f32[128,384]{1,0:T(8,128)S(1)}, f32[128,384]{1,0:T(8,128)S(1)}, u32[]{:S(2)}, u32[]{:S(2)}) collective-permute-start(f32[128,384]{1,0:T(8,128)S(1)} %get-tuple-element.44), channel_id=1, source_target_pairs={{0,8},{4,12},{8,0},{12,4},{1,9},{5,13},{9,1},{13,5},{2,10},{6,14},... | collective-permute-start | bytes 589832 | tf_op jit(solution)/shard_map/ppermute | solution.py:19

commit v20 on v17

--- a/solution.py
+++ b/solution.py
@@ -10,7 +10,7 @@
 FLOOR = 0.01
 EPSILON = 1e-06
 LANES = 128
-CHUNK = 256
+CHUNK = 128
 WHOLE = pl.BlockSpec(memory_space=pltpu.VMEM)
 
 

time: 40.8 us -> 41.3 us (1.012)
  waiting for transfers between devices: 11.9 us -> 10.5 us
  starting transfers between devices: 13.4 us -> 14.4 us
  Pallas kernels: 5.54 us -> 6.49 us
    pallas_call x7, Pallas kernels: 5.54 us -> 6.49 us  [call(): pl.pallas_call(kernel, out_shape=out_shape, in_specs=in_specs, out_specs=...]
    ppermute x10, waiting for transfers between devices: 8.9 us -> 8.18 us  [exchange(): return lax.ppermute(value, axis, [(i, i ^ distance) for i in range(size)])]
    ppermute x3, starting transfers between devices: 4.03 us -> 4.71 us  [shifted(): lax.ppermute(value, axis, [(i, (i + distance) % size) for i in range(size)])]
    ppermute x3, waiting for transfers between devices: 3.04 us -> 2.36 us  [shifted(): lax.ppermute(value, axis, [(i, (i + distance) % size) for i in range(size)])]
  transfers between devices with their start and end apart: 13 -> 13, of which waited for: 6 -> 5; matrix products, arithmetic and copies ran while one was open for 0% -> 0% of each run, Pallas kernels for 8% -> 9%
where the time goes in v20:
time: 41.3 us; the launch traced here: 41.1 us
  starting transfers between devices  14.4 us (35%)
  waiting for transfers between devices  10.5 us (25%)
  blocking collectives  8.97 us (22%)
  Pallas kernels  6.49 us (16%)
  between operations  0.71 us (2%)
    ppermute x10, starting transfers between devices, exchange(): return lax.ppermute(value, axis, [(i, i ^ distance) for i in range(size)])  9.66 us
    all_to_all x1, blocking collectives, to_all(): return lax.all_to_all(value, ('blk', 'sub'), 0, 0, tiled=True)  8.97 us
    ppermute x10, waiting for transfers between devices, exchange(): return lax.ppermute(value, axis, [(i, i ^ distance) for i in range(size)])  8.18 us
    pallas_call x7, Pallas kernels, call(): pl.pallas_call(kernel, out_shape=out_shape, in_specs=in_specs, out_specs=...  6.49 us
    ppermute x3, starting transfers between devices, shifted(): lax.ppermute(value, axis, [(i, (i + distance) % size) for i in range(size)])  4.71 us
    ppermute x3, waiting for transfers between devices, shifted(): lax.ppermute(value, axis, [(i, (i + distance) % size) for i in range(size)])  2.36 us
  transfers between devices with their start and end apart: 13, of which 5 were waited for; matrix products, arithmetic and copies ran while one was open for 0% of the time, Pallas kernels for 9%

profile of v20, /device:TPU:0, one launch (start us, length us, event | category | flops | bytes accessed | tf_op | source)
XLA Modules:
  0.0 41.1 jit_solution(8249133621678814278)
XLA Ops:
  0.6 1.0 %shard_map.41.packed_ref.refs_0_ = bf16[128,1408]{1,0:T(8,128)(2,1)S(1)} custom-call(bf16[128,1024]{1,0:T(8,128)(2,1)} %t_hbm.1, bf16[128,384]{1,0:T(8,128)(2,1)} %s_hbm.1), custom_call_target="tpu_custom_call" | custom-call | bytes 360448 | tf_op jit(solution)/shard_map/pallas_call | solution.py:229
  1.6 3.1 %collective-permute-start.1 = (bf16[128,1408]{1,0:T(8,128)(2,1)S(1)}, bf16[128,1408]{1,0:T(8,128)(2,1)S(1)}, u32[]{:S(2)}, u32[]{:S(2)}) collective-permute-start(bf16[128,1408]{1,0:T(8,128)(2,1)S(1)} %shard_map.41.packed_ref.refs_0_), channel_id=1, source_target_pairs={{0,1},{1,2},{2,3},{3,0},{4,5},{5,6},{6,7},{7,4},{8,9},{9,10},{10,1... | collective-permute-start | bytes 1081352 | tf_op jit(solution)/shard_map/ppermute | solution.py:24
  4.7 1.5 %collective-permute-start = (bf16[128,1408]{1,0:T(8,128)(2,1)S(1)}, bf16[128,1408]{1,0:T(8,128)(2,1)S(1)}, u32[]{:S(2)}, u32[]{:S(2)}) collective-permute-start(bf16[128,1408]{1,0:T(8,128)(2,1)S(1)} %shard_map.41.packed_ref.refs_0_), channel_id=1, source_target_pairs={{0,8},{4,12},{8,0},{12,4},{1,9},{5,13},{9,1},{13,5},{2,10},{6,14},... | collective-permute-start | bytes 1081352 | tf_op jit(solution)/shard_map/ppermute | solution.py:19
  6.2 0.2 shard_map.42
  6.4 1.6 %collective-permute-start.2 = (f32[1,1536]{1,0:T(1,128)S(1)}, f32[1,1536]{1,0:T(1,128)S(1)}, u32[]{:S(2)}, u32[]{:S(2)}) collective-permute-start(f32[1,1536]{1,0:T(1,128)S(1)} %shard_map.42), channel_id=1, source_target_pairs={{0,1},{1,0},{2,3},{3,2},{4,5},{5,4},{6,7},{7,6},{8,9},{9,8},{10,11... | collective-permute-start | bytes 18440 | tf_op jit(solution)/shard_map/ppermute | solution.py:19
  8.0 1.2 %collective-permute-start.3 = (f32[1,1536]{1,0:T(1,128)S(1)}, f32[1,1536]{1,0:T(1,128)S(1)}, u32[]{:S(2)}, u32[]{:S(2)}) collective-permute-start(f32[1,1536]{1,0:T(1,128)S(1)} %shard_map.42), channel_id=1, source_target_pairs={{0,2},{1,3},{2,0},{3,1},{4,6},{5,7},{6,4},{7,5},{8,10},{9,11},{10,... | collective-permute-start | bytes 18440 | tf_op jit(solution)/shard_map/ppermute | solution.py:19
  9.2 1.6 %collective-permute-start.4 = (f32[1,1536]{1,0:T(1,128)S(1)}, f32[1,1536]{1,0:T(1,128)S(1)}, u32[]{:S(2)}, u32[]{:S(2)}) collective-permute-start(f32[1,1536]{1,0:T(1,128)S(1)} %shard_map.42), channel_id=1, source_target_pairs={{0,3},{1,2},{2,1},{3,0},{4,7},{5,6},{6,5},{7,4},{8,11},{9,10},{10,... | collective-permute-start | bytes 18440 | tf_op jit(solution)/shard_map/ppermute | solution.py:19
  10.8 3.8 %collective-permute-done.2 = f32[1,1536]{1,0:T(1,128)S(1)} collective-permute-done((f32[1,1536]{1,0:T(1,128)S(1)}, f32[1,1536]{1,0:T(1,128)S(1)}, u32[]{:S(2)}, u32[]{:S(2)}) %collective-permute-start.2) | collective-permute-done | bytes 6176 | tf_op jit(solution)/shard_map/ppermute | solution.py:19
  14.6 1.1 %collective-permute-done.3 = f32[1,1536]{1,0:T(1,128)S(1)} collective-permute-done((f32[1,1536]{1,0:T(1,128)S(1)}, f32[1,1536]{1,0:T(1,128)S(1)}, u32[]{:S(2)}, u32[]{:S(2)}) %collective-permute-start.3) | collective-permute-done | bytes 6176 | tf_op jit(solution)/shard_map/ppermute | solution.py:19
  15.6 0.0 collective-permute-done.4
  15.6 0.0 collective-permute-done.1.refs_4_
  15.7 0.6 %collective-permute-start.9 = (bf16[128,1408]{1,0:T(8,128)(2,1)S(1)}, bf16[128,1408]{1,0:T(8,128)(2,1)S(1)}, u32[]{:S(2)}, u32[]{:S(2)}) collective-permute-start(bf16[128,1408]{1,0:T(8,128)(2,1)S(1)} %collective-permute-done.1.refs_4_), channel_id=1, source_target_pairs={{0,1},{1,2},{2,3},{3,0},{4,5},{5,6},{6,7},{7,4},{8,9},{9,10},{10,1... | collective-permute-start | bytes 1081352 | tf_op jit(solution)/shard_map/ppermute | solution.py:24
  16.3 0.0 collective-permute-done.refs_1_
  16.3 0.5 %collective-permute-start.6 = (bf16[128,1408]{1,0:T(8,128)(2,1)S(1)}, bf16[128,1408]{1,0:T(8,128)(2,1)S(1)}, u32[]{:S(2)}, u32[]{:S(2)}) collective-permute-start(bf16[128,1408]{1,0:T(8,128)(2,1)S(1)} %collective-permute-done.refs_1_), channel_id=1, source_target_pairs={{0,4},{4,0},{8,12},{12,8},{1,5},{5,1},{9,13},{13,9},{2,6},{6,2},{1... | collective-permute-start | bytes 1081352 | tf_op jit(solution)/shard_map/ppermute | solution.py:19
  16.8 1.6 %collective-permute-start.7 = (f32[1,1536]{1,0:T(1,128)S(1)}, f32[1,1536]{1,0:T(1,128)S(1)}, u32[]{:S(2)}, u32[]{:S(2)}) collective-permute-start(f32[1,1536]{1,0:T(1,128)S(1)} %add_add_fusion), channel_id=1, source_target_pairs={{0,8},{4,12},{8,0},{12,4},{1,9},{5,13},{9,1},{13,5},{2,10},{6,14},... | collective-permute-start | bytes 18440 | tf_op jit(solution)/shard_map/ppermute | solution.py:19
  18.4 2.1 %collective-permute-done.7 = f32[1,1536]{1,0:T(1,128)S(1)} collective-permute-done((f32[1,1536]{1,0:T(1,128)S(1)}, f32[1,1536]{1,0:T(1,128)S(1)}, u32[]{:S(2)}, u32[]{:S(2)}) %collective-permute-start.7) | collective-permute-done | bytes 6176 | tf_op jit(solution)/shard_map/ppermute | solution.py:19
  20.5 0.1 collective-permute-start.8
  20.6 1.2 %collective-permute-done.8.refs_6_ = f32[1,1536]{1,0:T(1,128)S(1)} collective-permute-done((f32[1,1536]{1,0:T(1,128)S(1)}, f32[1,1536]{1,0:T(1,128)S(1)}, u32[]{:S(2)}, u32[]{:S(2)}) %collective-permute-start.8) | collective-permute-done | bytes 6176 | tf_op jit(solution)/shard_map/ppermute | solution.py:19
  21.8 0.0 collective-permute-done.5.refs_2_
  21.8 0.0 collective-permute-done.6.refs_3_
  21.8 2.9 %shard_map.43 = (f32[128,384]{1,0:T(8,128)S(1)}, f32[128,384]{1,0:T(8,128)S(1)}, f32[2,256,512]{2,1,0:T(8,128)S(1)}, f32[2,2,256,128]{3,2,1,0:T(8,128)S(1)}, f32...) custom-call(bf16[128,1408]{1,0:T(8,128)(2,1)S(1)} %shard_map.41.packed_ref.refs_0_, ...), custom_call_target="tpu_custom_call" | custom-call | flops 570425344 | bytes 1814528 | tf_op jit(solution)/shard_map/pallas_call | solution.py:229
  24.7 2.4 %collective-permute-done.9.refs_1_ = bf16[128,1408]{1,0:T(8,128)(2,1)S(1)} collective-permute-done((bf16[128,1408]{1,0:T(8,128)(2,1)S(1)}, bf16[128,1408]{1,0:T(8,128)(2,1)S(1)}, u32[]{:S(2)}, u32[]{:S(2)}) %collective-permute-start.9) | collective-permute-done | bytes 360480 | tf_op jit(solution)/shard_map/ppermute | solution.py:24
  27.0 0.8 %shard_map.44 = (f32[256,384]{1,0:T(8,128)S(1)}, f32[2,128]{1,0:T(2,128)S(1)}, f32[2,128]{1,0:T(2,128)S(1)}) custom-call(bf16[2,256,1408]{2,1,0:T(8,128)(2,1)S(1)} %get-tuple-element.33.refs_0_, bf16[128,1408]{1,0:T(8,128)(2,1)S(1)} %collective-permute-done.9.refs_1_, f32[4,384]{1,0:T(4,128)S(1)} %get-tuple-element.32.refs_2_.stats_ref, ...), custom_call_target="tpu_custom_call" | custom-call | flops 142606336 | bytes 3382272 | tf_op jit(solution)/shard_map/pallas_call | solution.py:229
  27.8 0.1 collective-permute-start.10
  27.9 1.0 %collective-permute-start.12 = (f32[128,384]{1,0:T(8,128)S(1)}, f32[128,384]{1,0:T(8,128)S(1)}, u32[]{:S(2)}, u32[]{:S(2)}) collective-permute-start(f32[128,384]{1,0:T(8,128)S(1)} %get-tuple-element.45), channel_id=1, source_target_pairs={{0,3},{1,0},{2,1},{3,2},{4,7},{5,4},{6,5},{7,6},{8,11},{9,8},{10,9... | collective-permute-start | bytes 589832 | tf_op jit(solution)/shard_map/ppermute | solution.py:24
  28.9 0.8 %shard_map.45 = (f32[256,384]{1,0:T(8,128)S(1)}, f32[16,2,128]{2,1,0:T(2,128)S(1)}) custom-call(bf16[2,256,1408]{2,1,0:T(8,128)(2,1)S(1)} %get-tuple-element.33.refs_0_, bf16[128,1408]{1,0:T(8,128)(2,1)S(1)} %collective-permute-done.9.refs_1_, f32[4,384]{1,0:T(4,128)S(1)} %get-tuple-element.32.refs_2_.stats_ref, ...), custom_call_target="tpu_custom_call" | custom-call | flops 142606336 | bytes 3383296 | tf_op jit(solution)/shard_map/pallas_call | solution.py:229
  29.7 0.0 collective-permute-done.10.got_ref
  29.8 1.6 %collective-permute-start.11 = (f32[128,384]{1,0:T(8,128)S(1)}, f32[128,384]{1,0:T(8,128)S(1)}, u32[]{:S(2)}, u32[]{:S(2)}) collective-permute-start(f32[128,384]{1,0:T(8,128)S(1)} %get-tuple-element.44), channel_id=1, source_target_pairs={{0,8},{4,12},{8,0},{12,4},{1,9},{5,13},{9,1},{13,5},{2,10},{6,14},... | collective-permute-start | bytes 589832 | tf_op jit(solution)/shard_map/ppermute | solution.py:19
  31.3 9.0 %all_to_all.5.sums_ref = f32[16,2,128]{2,1,0:T(2,128)S(1)} all-to-all(f32[16,2,128]{2,1,0:T(2,128)S(1)} %get-tuple-element.39), channel_id=1, replica_groups=mesh['groups'=2,'blk'=4,'sub'=4] {'blk','sub'}, dimensions={0} | all-to-all | bytes 32768 | tf_op jit(solution)/shard_map/all_to_all | solution.py:250
  40.3 0.0 collective-permute-done.12.refs_3_
  40.3 0.0 collective-permute-done.11.refs_2_
  40.3 0.8 %shard_map.47 = (f32[128,384]{1,0:T(8,128)}, f32[1,128]{1,0:T(1,128)}) custom-call(bf16[128,1408]{1,0:T(8,128)(2,1)S(1)} %shard_map.41.packed_ref.refs_0_, f32[4,384]{1,0:T(4,128)S(1)} %get-tuple-element.32.refs_2_.stats_ref, f32[16,2,128]{2,1,0:T(2,128)S(1)} %all_to_all.5.sums_ref, f32[128,384]{1,0:T(8,128)S(1)} %get-tuple-element.40.refs_0_, ...), custom_call_target="tpu_custom_call" | custom-call | flops 393216 | bytes 1169408 | tf_op jit(solution)/shard_map/pallas_call | solution.py:229
  (4 shorter events, 0.1 us)
Async XLA Ops:
  1.6 14.0 %collective-permute-start.1 = (bf16[128,1408]{1,0:T(8,128)(2,1)S(1)}, bf16[128,1408]{1,0:T(8,128)(2,1)S(1)}, u32[]{:S(2)}, u32[]{:S(2)}) collective-permute-start(bf16[128,1408]{1,0:T(8,128)(2,1)S(1)} %shard_map.41.packed_ref.refs_0_), channel_id=1, source_target_pairs={{0,1},{1,2},{2,3},{3,0},{4,5},{5,6},{6,7},{7,4},{8,9},{9,10},{10,1... | collective-permute-start | bytes 1081352 | tf_op jit(solution)/shard_map/ppermute | solution.py:24
  4.7 11.6 %collective-permute-start = (bf16[128,1408]{1,0:T(8,128)(2,1)S(1)}, bf16[128,1408]{1,0:T(8,128)(2,1)S(1)}, u32[]{:S(2)}, u32[]{:S(2)}) collective-permute-start(bf16[128,1408]{1,0:T(8,128)(2,1)S(1)} %shard_map.41.packed_ref.refs_0_), channel_id=1, source_target_pairs={{0,8},{4,12},{8,0},{12,4},{1,9},{5,13},{9,1},{13,5},{2,10},{6,14},... | collective-permute-start | bytes 1081352 | tf_op jit(solution)/shard_map/ppermute | solution.py:19
  6.4 8.2 %collective-permute-start.2 = (f32[1,1536]{1,0:T(1,128)S(1)}, f32[1,1536]{1,0:T(1,128)S(1)}, u32[]{:S(2)}, u32[]{:S(2)}) collective-permute-start(f32[1,1536]{1,0:T(1,128)S(1)} %shard_map.42), channel_id=1, source_target_pairs={{0,1},{1,0},{2,3},{3,2},{4,5},{5,4},{6,7},{7,6},{8,9},{9,8},{10,11... | collective-permute-start | bytes 18440 | tf_op jit(solution)/shard_map/ppermute | solution.py:19
  8.0 7.7 %collective-permute-start.3 = (f32[1,1536]{1,0:T(1,128)S(1)}, f32[1,1536]{1,0:T(1,128)S(1)}, u32[]{:S(2)}, u32[]{:S(2)}) collective-permute-start(f32[1,1536]{1,0:T(1,128)S(1)} %shard_map.42), channel_id=1, source_target_pairs={{0,2},{1,3},{2,0},{3,1},{4,6},{5,7},{6,4},{7,5},{8,10},{9,11},{10,... | collective-permute-start | bytes 18440 | tf_op jit(solution)/shard_map/ppermute | solution.py:19
  9.2 6.4 %collective-permute-start.4 = (f32[1,1536]{1,0:T(1,128)S(1)}, f32[1,1536]{1,0:T(1,128)S(1)}, u32[]{:S(2)}, u32[]{:S(2)}) collective-permute-start(f32[1,1536]{1,0:T(1,128)S(1)} %shard_map.42), channel_id=1, source_target_pairs={{0,3},{1,2},{2,1},{3,0},{4,7},{5,6},{6,5},{7,4},{8,11},{9,10},{10,... | collective-permute-start | bytes 18440 | tf_op jit(solution)/shard_map/ppermute | solution.py:19
  15.7 11.4 %collective-permute-start.9 = (bf16[128,1408]{1,0:T(8,128)(2,1)S(1)}, bf16[128,1408]{1,0:T(8,128)(2,1)S(1)}, u32[]{:S(2)}, u32[]{:S(2)}) collective-permute-start(bf16[128,1408]{1,0:T(8,128)(2,1)S(1)} %collective-permute-done.1.refs_4_), channel_id=1, source_target_pairs={{0,1},{1,2},{2,3},{3,0},{4,5},{5,6},{6,7},{7,4},{8,9},{9,10},{10,1... | collective-permute-start | bytes 1081352 | tf_op jit(solution)/shard_map/ppermute | solution.py:24
  16.3 5.5 %collective-permute-start.5 = (bf16[128,1408]{1,0:T(8,128)(2,1)S(1)}, bf16[128,1408]{1,0:T(8,128)(2,1)S(1)}, u32[]{:S(2)}, u32[]{:S(2)}) collective-permute-start(bf16[128,1408]{1,0:T(8,128)(2,1)S(1)} %shard_map.41.packed_ref.refs_0_), channel_id=1, source_target_pairs={{0,4},{4,0},{8,12},{12,8},{1,5},{5,1},{9,13},{13,9},{2,6},{6,2},{1... | collective-permute-start | bytes 1081352 | tf_op jit(solution)/shard_map/ppermute | solution.py:19
  16.3 5.5 %collective-permute-start.6 = (bf16[128,1408]{1,0:T(8,128)(2,1)S(1)}, bf16[128,1408]{1,0:T(8,128)(2,1)S(1)}, u32[]{:S(2)}, u32[]{:S(2)}) collective-permute-start(bf16[128,1408]{1,0:T(8,128)(2,1)S(1)} %collective-permute-done.refs_1_), channel_id=1, source_target_pairs={{0,4},{4,0},{8,12},{12,8},{1,5},{5,1},{9,13},{13,9},{2,6},{6,2},{1... | collective-permute-start | bytes 1081352 | tf_op jit(solution)/shard_map/ppermute | solution.py:19
  16.8 3.7 %collective-permute-start.7 = (f32[1,1536]{1,0:T(1,128)S(1)}, f32[1,1536]{1,0:T(1,128)S(1)}, u32[]{:S(2)}, u32[]{:S(2)}) collective-permute-start(f32[1,1536]{1,0:T(1,128)S(1)} %add_add_fusion), channel_id=1, source_target_pairs={{0,8},{4,12},{8,0},{12,4},{1,9},{5,13},{9,1},{13,5},{2,10},{6,14},... | collective-permute-start | bytes 18440 | tf_op jit(solution)/shard_map/ppermute | solution.py:19
  20.5 1.2 %collective-permute-start.8 = (f32[1,1536]{1,0:T(1,128)S(1)}, f32[1,1536]{1,0:T(1,128)S(1)}, u32[]{:S(2)}, u32[]{:S(2)}) collective-permute-start(f32[1,1536]{1,0:T(1,128)S(1)} %add.15.refs_5_), channel_id=1, source_target_pairs={{0,4},{4,0},{8,12},{12,8},{1,5},{5,1},{9,13},{13,9},{2,6},{6,2},{1... | collective-permute-start | bytes 18440 | tf_op jit(solution)/shard_map/ppermute | solution.py:19
  27.8 1.9 %collective-permute-start.10 = (f32[256,384]{1,0:T(8,128)S(1)}, f32[256,384]{1,0:T(8,128)S(1)}, u32[]{:S(2)}, u32[]{:S(2)}) collective-permute-start(f32[256,384]{1,0:T(8,128)S(1)} %get-tuple-element.42), channel_id=1, source_target_pairs={{0,4},{4,0},{8,12},{12,8},{1,5},{5,1},{9,13},{13,9},{2,6},{6,2},{1... | collective-permute-start | bytes 1179656 | tf_op jit(solution)/shard_map/ppermute | solution.py:19
  27.9 12.4 %collective-permute-start.12 = (f32[128,384]{1,0:T(8,128)S(1)}, f32[128,384]{1,0:T(8,128)S(1)}, u32[]{:S(2)}, u32[]{:S(2)}) collective-permute-start(f32[128,384]{1,0:T(8,128)S(1)} %get-tuple-element.45), channel_id=1, source_target_pairs={{0,3},{1,0},{2,1},{3,2},{4,7},{5,4},{6,5},{7,6},{8,11},{9,8},{10,9... | collective-permute-start | bytes 589832 | tf_op jit(solution)/shard_map/ppermute | solution.py:24
  29.8 10.5 %collective-permute-start.11 = (f32[128,384]{1,0:T(8,128)S(1)}, f32[128,384]{1,0:T(8,128)S(1)}, u32[]{:S(2)}, u32[]{:S(2)}) collective-permute-start(f32[128,384]{1,0:T(8,128)S(1)} %get-tuple-element.44), channel_id=1, source_target_pairs={{0,8},{4,12},{8,0},{12,4},{1,9},{5,13},{9,1},{13,5},{2,10},{6,14},... | collective-permute-start | bytes 589832 | tf_op jit(solution)/shard_map/ppermute | solution.py:19

commit v21 on v17

--- a/solution.py
+++ b/solution.py
@@ -207,18 +207,12 @@
     out_refs[1][...] = keep_ref[rows : 2 * rows, :] + got_ref[rows : 2 * rows, :]
 
 
-def final_kernel(t_width, total_rows, packed_ref, stats_ref, sums_ref, *refs):
-    *parts, grad_ref, loss_ref = refs
-    direct = parts[0][...]
-    for part in parts[1:]:
-        direct = direct + part[...]
+def final_kernel(total_rows, stats_ref, sums_ref, factor_ref, loss_ref):
     both = jnp.sum(jnp.sum(sums_ref[...], axis=0), axis=1, keepdims=True)
     loss_total, spread_total = both[0:1, :], -both[1:2, :]
-    spread_s, centre = stats_ref[2:3, :], stats_ref[3:4, :]
+    spread_s = stats_ref[2:3, :]
     pairs = total_rows * (total_rows - 1.0)
-    correction = 2.0 * spread_total / (pairs * spread_s * spread_s)
-    student = packed_ref[:, t_width:].astype(jnp.float32)
-    grad_ref[...] = (2.0 / (total_rows - 1.0)) * direct + correction * (student - centre)
+    factor_ref[...] = 2.0 * spread_total / (pairs * spread_s * spread_s)
     loss_ref[...] = jnp.broadcast_to(loss_total / pairs, loss_ref.shape)
 
 
@@ -331,12 +325,15 @@
         distance *= 2
     all_sums = to_all(sums)
     parts = [own, keep, got] + returned
-    grad, loss = call(
-        functools.partial(final_kernel, t_width, total_rows),
-        [f32((rows, s_width)), f32((1, LANES))],
-        [packed, totals, all_sums] + parts,
+    factor, loss = call(
+        functools.partial(final_kernel, total_rows),
+        [f32((1, s_width)), f32((1, LANES))],
+        [totals, all_sums],
         8 * student.size,
     )
+    direct = functools.reduce(jnp.add, parts)
+    from_centre = packed[:, t_width:].astype(jnp.float32) - totals[3:4, :]
+    grad = (2.0 / (total_rows - 1.0)) * direct + factor * from_centre
     return grad, loss[0, :1]
 
 

time: 40.8 us -> 42.3 us (1.037)
  blocking collectives: 8.97 us -> 0 us
  waiting for transfers between devices: 11.9 us -> 17.8 us
  starting transfers between devices: 13.4 us -> 17 us
  other arithmetic: 0.02 us -> 0.8 us
    all_to_all x1 -> x0, blocking collectives: 8.97 us -> none  [to_all(): return lax.all_to_all(value, ('blk', 'sub'), 0, 0, tiled=True)]
    all_to_all x0 -> x1, waiting for transfers between devices: none -> 6.35 us  [to_all(): return lax.all_to_all(value, ('blk', 'sub'), 0, 0, tiled=True)]
    all_to_all x0 -> x1, starting transfers between devices: none -> 3.49 us  [to_all(): return lax.all_to_all(value, ('blk', 'sub'), 0, 0, tiled=True)]
    add x0 -> x1, other arithmetic: none -> 0.76 us  [per_device(): grad = 2.0 / (total_rows - 1.0) * direct + factor * from_centre]
    ppermute x10, waiting for transfers between devices: 8.9 us -> 8.46 us  [exchange(): return lax.ppermute(value, axis, [(i, i ^ distance) for i in range(size)])]
  transfers between devices with their start and end apart: 13 -> 14, of which waited for: 6 -> 7; matrix products, arithmetic and copies ran while one was open for 0% -> 0% of each run, Pallas kernels for 8% -> 10%
where the time goes in v21:
time: 42.3 us; the launch traced here: 42.1 us
  waiting for transfers between devices  17.8 us (42%)
  starting transfers between devices  17 us (40%)
  Pallas kernels  5.78 us (14%)
  other arithmetic  0.8 us (2%)
  between operations  0.7 us (2%)
    ppermute x10, starting transfers between devices, exchange(): return lax.ppermute(value, axis, [(i, i ^ distance) for i in range(size)])  9.42 us
    ppermute x10, waiting for transfers between devices, exchange(): return lax.ppermute(value, axis, [(i, i ^ distance) for i in range(size)])  8.46 us
    all_to_all x1, waiting for transfers between devices, to_all(): return lax.all_to_all(value, ('blk', 'sub'), 0, 0, tiled=True)  6.35 us
    pallas_call x7, Pallas kernels, call(): pl.pallas_call(kernel, out_shape=out_shape, in_specs=in_specs, out_specs=...  5.78 us
    ppermute x3, starting transfers between devices, shifted(): lax.ppermute(value, axis, [(i, (i + distance) % size) for i in range(size)])  4.05 us
    all_to_all x1, starting transfers between devices, to_all(): return lax.all_to_all(value, ('blk', 'sub'), 0, 0, tiled=True)  3.49 us
    ppermute x3, waiting for transfers between devices, shifted(): lax.ppermute(value, axis, [(i, (i + distance) % size) for i in range(size)])  3.02 us
  transfers between devices with their start and end apart: 14, of which 7 were waited for; matrix products, arithmetic and copies ran while one was open for 0% of the time, Pallas kernels for 10%

profile of v21, /device:TPU:0, one launch (start us, length us, event | category | flops | bytes accessed | tf_op | source)
XLA Modules:
  0.0 42.1 jit_solution(5298399512751909093)
XLA Ops:
  0.6 1.0 %shard_map.41.packed_ref.refs_0_ = bf16[128,1408]{1,0:T(8,128)(2,1)S(1)} custom-call(bf16[128,1024]{1,0:T(8,128)(2,1)} %t_hbm.1, bf16[128,384]{1,0:T(8,128)(2,1)} %s_hbm.1), custom_call_target="tpu_custom_call" | custom-call | bytes 360448 | tf_op jit(solution)/shard_map/pallas_call | solution.py:223
  1.6 3.1 %collective-permute-start.1 = (bf16[128,1408]{1,0:T(8,128)(2,1)S(1)}, bf16[128,1408]{1,0:T(8,128)(2,1)S(1)}, u32[]{:S(2)}, u32[]{:S(2)}) collective-permute-start(bf16[128,1408]{1,0:T(8,128)(2,1)S(1)} %shard_map.41.packed_ref.refs_0_), channel_id=1, source_target_pairs={{0,1},{1,2},{2,3},{3,0},{4,5},{5,6},{6,7},{7,4},{8,9},{9,10},{10,1... | collective-permute-start | bytes 1081352 | tf_op jit(solution)/shard_map/ppermute | solution.py:24
  4.7 1.5 %collective-permute-start = (bf16[128,1408]{1,0:T(8,128)(2,1)S(1)}, bf16[128,1408]{1,0:T(8,128)(2,1)S(1)}, u32[]{:S(2)}, u32[]{:S(2)}) collective-permute-start(bf16[128,1408]{1,0:T(8,128)(2,1)S(1)} %shard_map.41.packed_ref.refs_0_), channel_id=1, source_target_pairs={{0,8},{4,12},{8,0},{12,4},{1,9},{5,13},{9,1},{13,5},{2,10},{6,14},... | collective-permute-start | bytes 1081352 | tf_op jit(solution)/shard_map/ppermute | solution.py:19
  6.2 0.2 shard_map.42
  6.4 1.6 %collective-permute-start.2 = (f32[1,1536]{1,0:T(1,128)S(1)}, f32[1,1536]{1,0:T(1,128)S(1)}, u32[]{:S(2)}, u32[]{:S(2)}) collective-permute-start(f32[1,1536]{1,0:T(1,128)S(1)} %shard_map.42), channel_id=1, source_target_pairs={{0,1},{1,0},{2,3},{3,2},{4,5},{5,4},{6,7},{7,6},{8,9},{9,8},{10,11... | collective-permute-start | bytes 18440 | tf_op jit(solution)/shard_map/ppermute | solution.py:19
  8.0 1.2 %collective-permute-start.3 = (f32[1,1536]{1,0:T(1,128)S(1)}, f32[1,1536]{1,0:T(1,128)S(1)}, u32[]{:S(2)}, u32[]{:S(2)}) collective-permute-start(f32[1,1536]{1,0:T(1,128)S(1)} %shard_map.42), channel_id=1, source_target_pairs={{0,2},{1,3},{2,0},{3,1},{4,6},{5,7},{6,4},{7,5},{8,10},{9,11},{10,... | collective-permute-start | bytes 18440 | tf_op jit(solution)/shard_map/ppermute | solution.py:19
  9.2 1.6 %collective-permute-start.4 = (f32[1,1536]{1,0:T(1,128)S(1)}, f32[1,1536]{1,0:T(1,128)S(1)}, u32[]{:S(2)}, u32[]{:S(2)}) collective-permute-start(f32[1,1536]{1,0:T(1,128)S(1)} %shard_map.42), channel_id=1, source_target_pairs={{0,3},{1,2},{2,1},{3,0},{4,7},{5,6},{6,5},{7,4},{8,11},{9,10},{10,... | collective-permute-start | bytes 18440 | tf_op jit(solution)/shard_map/ppermute | solution.py:19
  10.8 3.8 %collective-permute-done.2 = f32[1,1536]{1,0:T(1,128)S(1)} collective-permute-done((f32[1,1536]{1,0:T(1,128)S(1)}, f32[1,1536]{1,0:T(1,128)S(1)}, u32[]{:S(2)}, u32[]{:S(2)}) %collective-permute-start.2) | collective-permute-done | bytes 6176 | tf_op jit(solution)/shard_map/ppermute | solution.py:19
  14.6 1.1 %collective-permute-done.3 = f32[1,1536]{1,0:T(1,128)S(1)} collective-permute-done((f32[1,1536]{1,0:T(1,128)S(1)}, f32[1,1536]{1,0:T(1,128)S(1)}, u32[]{:S(2)}, u32[]{:S(2)}) %collective-permute-start.3) | collective-permute-done | bytes 6176 | tf_op jit(solution)/shard_map/ppermute | solution.py:19
  15.6 0.0 collective-permute-done.4
  15.6 0.0 collective-permute-done.1.refs_4_
  15.7 0.6 %collective-permute-start.9 = (bf16[128,1408]{1,0:T(8,128)(2,1)S(1)}, bf16[128,1408]{1,0:T(8,128)(2,1)S(1)}, u32[]{:S(2)}, u32[]{:S(2)}) collective-permute-start(bf16[128,1408]{1,0:T(8,128)(2,1)S(1)} %collective-permute-done.1.refs_4_), channel_id=1, source_target_pairs={{0,1},{1,2},{2,3},{3,0},{4,5},{5,6},{6,7},{7,4},{8,9},{9,10},{10,1... | collective-permute-start | bytes 1081352 | tf_op jit(solution)/shard_map/ppermute | solution.py:24
  16.3 0.0 collective-permute-done.refs_1_
  16.3 0.5 %collective-permute-start.6 = (bf16[128,1408]{1,0:T(8,128)(2,1)S(1)}, bf16[128,1408]{1,0:T(8,128)(2,1)S(1)}, u32[]{:S(2)}, u32[]{:S(2)}) collective-permute-start(bf16[128,1408]{1,0:T(8,128)(2,1)S(1)} %collective-permute-done.refs_1_), channel_id=1, source_target_pairs={{0,4},{4,0},{8,12},{12,8},{1,5},{5,1},{9,13},{13,9},{2,6},{6,2},{1... | collective-permute-start | bytes 1081352 | tf_op jit(solution)/shard_map/ppermute | solution.py:19
  16.8 1.6 %collective-permute-start.7 = (f32[1,1536]{1,0:T(1,128)S(1)}, f32[1,1536]{1,0:T(1,128)S(1)}, u32[]{:S(2)}, u32[]{:S(2)}) collective-permute-start(f32[1,1536]{1,0:T(1,128)S(1)} %add_add_fusion), channel_id=1, source_target_pairs={{0,8},{4,12},{8,0},{12,4},{1,9},{5,13},{9,1},{13,5},{2,10},{6,14},... | collective-permute-start | bytes 18440 | tf_op jit(solution)/shard_map/ppermute | solution.py:19
  18.4 2.1 %collective-permute-done.7 = f32[1,1536]{1,0:T(1,128)S(1)} collective-permute-done((f32[1,1536]{1,0:T(1,128)S(1)}, f32[1,1536]{1,0:T(1,128)S(1)}, u32[]{:S(2)}, u32[]{:S(2)}) %collective-permute-start.7) | collective-permute-done | bytes 6176 | tf_op jit(solution)/shard_map/ppermute | solution.py:19
  20.5 0.1 collective-permute-start.8
  20.6 1.2 %collective-permute-done.8.refs_6_ = f32[1,1536]{1,0:T(1,128)S(1)} collective-permute-done((f32[1,1536]{1,0:T(1,128)S(1)}, f32[1,1536]{1,0:T(1,128)S(1)}, u32[]{:S(2)}, u32[]{:S(2)}) %collective-permute-start.8) | collective-permute-done | bytes 6176 | tf_op jit(solution)/shard_map/ppermute | solution.py:19
  21.8 0.0 collective-permute-done.5.refs_2_
  21.8 0.0 collective-permute-done.6.refs_3_
  21.8 2.2 %shard_map.43 = (f32[128,384]{1,0:T(8,128)S(1)}, f32[128,384]{1,0:T(8,128)S(1)}, f32[2,256,512]{2,1,0:T(8,128)S(1)}, f32[2,2,256,128]{3,2,1,0:T(8,128)S(1)}, f32...) custom-call(bf16[128,1408]{1,0:T(8,128)(2,1)S(1)} %shard_map.41.packed_ref.refs_0_, ...), custom_call_target="tpu_custom_call" | custom-call | flops 570425344 | bytes 1814528 | tf_op jit(solution)/shard_map/pallas_call | solution.py:223
  24.0 3.0 %collective-permute-done.9.refs_1_ = bf16[128,1408]{1,0:T(8,128)(2,1)S(1)} collective-permute-done((bf16[128,1408]{1,0:T(8,128)(2,1)S(1)}, bf16[128,1408]{1,0:T(8,128)(2,1)S(1)}, u32[]{:S(2)}, u32[]{:S(2)}) %collective-permute-start.9) | collective-permute-done | bytes 360480 | tf_op jit(solution)/shard_map/ppermute | solution.py:24
  27.0 0.7 %shard_map.44 = (f32[256,384]{1,0:T(8,128)S(1)}, f32[2,128]{1,0:T(2,128)S(1)}, f32[2,128]{1,0:T(2,128)S(1)}) custom-call(bf16[2,256,1408]{2,1,0:T(8,128)(2,1)S(1)} %get-tuple-element.33.refs_0_, bf16[128,1408]{1,0:T(8,128)(2,1)S(1)} %collective-permute-done.9.refs_1_, f32[4,384]{1,0:T(4,128)S(1)} %get-tuple-element.34.refs_2_.stats_ref, ...), custom_call_target="tpu_custom_call" | custom-call | flops 142606336 | bytes 3382272 | tf_op jit(solution)/shard_map/pallas_call | solution.py:223
  27.7 0.1 collective-permute-start.10
  27.8 0.3 collective-permute-start.12
  28.1 1.1 %shard_map.45 = (f32[256,384]{1,0:T(8,128)S(1)}, f32[16,2,128]{2,1,0:T(2,128)}) custom-call(bf16[2,256,1408]{2,1,0:T(8,128)(2,1)S(1)} %get-tuple-element.33.refs_0_, bf16[128,1408]{1,0:T(8,128)(2,1)S(1)} %collective-permute-done.9.refs_1_, f32[4,384]{1,0:T(4,128)S(1)} %get-tuple-element.34.refs_2_.stats_ref, f32[2,256,512]{2,1,0:T(8,128)S(1)} %get-tuple-element.35.refs_3_, ...), custom_call_target="tpu_custom_call" | custom-call | flops 142606336 | bytes 3383296 | tf_op jit(solution)/shard_map/pallas_call | solution.py:223
  29.2 0.3 collective-permute-done.10.got_ref
  29.5 1.3 %collective-permute-start.11 = (f32[128,384]{1,0:T(8,128)S(1)}, f32[128,384]{1,0:T(8,128)S(1)}, u32[]{:S(2)}, u32[]{:S(2)}) collective-permute-start(f32[128,384]{1,0:T(8,128)S(1)} %get-tuple-element.43), channel_id=1, source_target_pairs={{0,8},{4,12},{8,0},{12,4},{1,9},{5,13},{9,1},{13,5},{2,10},{6,14},... | collective-permute-start | bytes 589832 | tf_op jit(solution)/shard_map/ppermute | solution.py:19
  30.8 3.5 %all-to-all-start = ((f32[16,2,128]{2,1,0:T(2,128)}), f32[16,2,128]{2,1,0:T(2,128)S(1)}, u32[]{:S(2)}, u32[]{:S(2)}) async-start(f32[16,2,128]{2,1,0:T(2,128)} %get-tuple-element.45), calls=%async_computation | async-start | bytes 32768 | tf_op jit(solution)/shard_map/all_to_all | solution.py:244
  34.3 6.4 %all-to-all-done.sums_ref = f32[16,2,128]{2,1,0:T(2,128)S(1)} async-done(((f32[16,2,128]{2,1,0:T(2,128)}), f32[16,2,128]{2,1,0:T(2,128)S(1)}, u32[]{:S(2)}, u32[]{:S(2)}) %all-to-all-start) | async-done | bytes 16416 | tf_op jit(solution)/shard_map/all_to_all | solution.py:244
  40.7 0.6 %shard_map.47 = (f32[1,384]{1,0:T(1,128)S(1)}, f32[1,128]{1,0:T(1,128)}) custom-call(f32[4,384]{1,0:T(4,128)S(1)} %get-tuple-element.34.refs_2_.stats_ref, f32[16,2,128]{2,1,0:T(2,128)S(1)} %all-to-all-done.sums_ref), custom_call_target="tpu_custom_call" | custom-call | flops 393216 | bytes 22528 | tf_op jit(solution)/shard_map/pallas_call | solution.py:223
  41.3 0.8 %multiply_add_fusion = f32[128,384]{1,0:T(8,128)} fusion(f32[128,384]{1,0:T(8,128)S(1)} %collective-permute-done.12, f32[128,384]{1,0:T(8,128)S(1)} %collective-permute-done.11, f32[128,384]{1,0:T(8,128)S(1)} %get-tuple-element.32, f32[128,384]{1,0:T(8,128)S(1)} %get-tuple-element.42, bf16[128,1408]{1,0:T(8,128)(2,1)S(1)} %shard_map.41.packed_ref.refs_0_, ...), kind=kLoop, calls=%fused_computation | loop fusion | flops 393216 | bytes 1084416 | tf_op jit(solution)/shard_map/add | solution.py:336
  (8 shorter events, 0.1 us)
Async XLA Ops:
  1.6 14.0 %collective-permute-start.1 = (bf16[128,1408]{1,0:T(8,128)(2,1)S(1)}, bf16[128,1408]{1,0:T(8,128)(2,1)S(1)}, u32[]{:S(2)}, u32[]{:S(2)}) collective-permute-start(bf16[128,1408]{1,0:T(8,128)(2,1)S(1)} %shard_map.41.packed_ref.refs_0_), channel_id=1, source_target_pairs={{0,1},{1,2},{2,3},{3,0},{4,5},{5,6},{6,7},{7,4},{8,9},{9,10},{10,1... | collective-permute-start | bytes 1081352 | tf_op jit(solution)/shard_map/ppermute | solution.py:24
  4.7 11.6 %collective-permute-start = (bf16[128,1408]{1,0:T(8,128)(2,1)S(1)}, bf16[128,1408]{1,0:T(8,128)(2,1)S(1)}, u32[]{:S(2)}, u32[]{:S(2)}) collective-permute-start(bf16[128,1408]{1,0:T(8,128)(2,1)S(1)} %shard_map.41.packed_ref.refs_0_), channel_id=1, source_target_pairs={{0,8},{4,12},{8,0},{12,4},{1,9},{5,13},{9,1},{13,5},{2,10},{6,14},... | collective-permute-start | bytes 1081352 | tf_op jit(solution)/shard_map/ppermute | solution.py:19
  6.4 8.2 %collective-permute-start.2 = (f32[1,1536]{1,0:T(1,128)S(1)}, f32[1,1536]{1,0:T(1,128)S(1)}, u32[]{:S(2)}, u32[]{:S(2)}) collective-permute-start(f32[1,1536]{1,0:T(1,128)S(1)} %shard_map.42), channel_id=1, source_target_pairs={{0,1},{1,0},{2,3},{3,2},{4,5},{5,4},{6,7},{7,6},{8,9},{9,8},{10,11... | collective-permute-start | bytes 18440 | tf_op jit(solution)/shard_map/ppermute | solution.py:19
  8.0 7.7 %collective-permute-start.3 = (f32[1,1536]{1,0:T(1,128)S(1)}, f32[1,1536]{1,0:T(1,128)S(1)}, u32[]{:S(2)}, u32[]{:S(2)}) collective-permute-start(f32[1,1536]{1,0:T(1,128)S(1)} %shard_map.42), channel_id=1, source_target_pairs={{0,2},{1,3},{2,0},{3,1},{4,6},{5,7},{6,4},{7,5},{8,10},{9,11},{10,... | collective-permute-start | bytes 18440 | tf_op jit(solution)/shard_map/ppermute | solution.py:19
  9.2 6.4 %collective-permute-start.4 = (f32[1,1536]{1,0:T(1,128)S(1)}, f32[1,1536]{1,0:T(1,128)S(1)}, u32[]{:S(2)}, u32[]{:S(2)}) collective-permute-start(f32[1,1536]{1,0:T(1,128)S(1)} %shard_map.42), channel_id=1, source_target_pairs={{0,3},{1,2},{2,1},{3,0},{4,7},{5,6},{6,5},{7,4},{8,11},{9,10},{10,... | collective-permute-start | bytes 18440 | tf_op jit(solution)/shard_map/ppermute | solution.py:19
  15.7 11.4 %collective-permute-start.9 = (bf16[128,1408]{1,0:T(8,128)(2,1)S(1)}, bf16[128,1408]{1,0:T(8,128)(2,1)S(1)}, u32[]{:S(2)}, u32[]{:S(2)}) collective-permute-start(bf16[128,1408]{1,0:T(8,128)(2,1)S(1)} %collective-permute-done.1.refs_4_), channel_id=1, source_target_pairs={{0,1},{1,2},{2,3},{3,0},{4,5},{5,6},{6,7},{7,4},{8,9},{9,10},{10,1... | collective-permute-start | bytes 1081352 | tf_op jit(solution)/shard_map/ppermute | solution.py:24
  16.3 5.5 %collective-permute-start.5 = (bf16[128,1408]{1,0:T(8,128)(2,1)S(1)}, bf16[128,1408]{1,0:T(8,128)(2,1)S(1)}, u32[]{:S(2)}, u32[]{:S(2)}) collective-permute-start(bf16[128,1408]{1,0:T(8,128)(2,1)S(1)} %shard_map.41.packed_ref.refs_0_), channel_id=1, source_target_pairs={{0,4},{4,0},{8,12},{12,8},{1,5},{5,1},{9,13},{13,9},{2,6},{6,2},{1... | collective-permute-start | bytes 1081352 | tf_op jit(solution)/shard_map/ppermute | solution.py:19
  16.3 5.5 %collective-permute-start.6 = (bf16[128,1408]{1,0:T(8,128)(2,1)S(1)}, bf16[128,1408]{1,0:T(8,128)(2,1)S(1)}, u32[]{:S(2)}, u32[]{:S(2)}) collective-permute-start(bf16[128,1408]{1,0:T(8,128)(2,1)S(1)} %collective-permute-done.refs_1_), channel_id=1, source_target_pairs={{0,4},{4,0},{8,12},{12,8},{1,5},{5,1},{9,13},{13,9},{2,6},{6,2},{1... | collective-permute-start | bytes 1081352 | tf_op jit(solution)/shard_map/ppermute | solution.py:19
  16.8 3.7 %collective-permute-start.7 = (f32[1,1536]{1,0:T(1,128)S(1)}, f32[1,1536]{1,0:T(1,128)S(1)}, u32[]{:S(2)}, u32[]{:S(2)}) collective-permute-start(f32[1,1536]{1,0:T(1,128)S(1)} %add_add_fusion), channel_id=1, source_target_pairs={{0,8},{4,12},{8,0},{12,4},{1,9},{5,13},{9,1},{13,5},{2,10},{6,14},... | collective-permute-start | bytes 18440 | tf_op jit(solution)/shard_map/ppermute | solution.py:19
  20.5 1.2 %collective-permute-start.8 = (f32[1,1536]{1,0:T(1,128)S(1)}, f32[1,1536]{1,0:T(1,128)S(1)}, u32[]{:S(2)}, u32[]{:S(2)}) collective-permute-start(f32[1,1536]{1,0:T(1,128)S(1)} %add.27.refs_5_), channel_id=1, source_target_pairs={{0,4},{4,0},{8,12},{12,8},{1,5},{5,1},{9,13},{13,9},{2,6},{6,2},{1... | collective-permute-start | bytes 18440 | tf_op jit(solution)/shard_map/ppermute | solution.py:19
  27.7 1.8 %collective-permute-start.10 = (f32[256,384]{1,0:T(8,128)S(1)}, f32[256,384]{1,0:T(8,128)S(1)}, u32[]{:S(2)}, u32[]{:S(2)}) collective-permute-start(f32[256,384]{1,0:T(8,128)S(1)} %get-tuple-element.41), channel_id=1, source_target_pairs={{0,4},{4,0},{8,12},{12,8},{1,5},{5,1},{9,13},{13,9},{2,6},{6,2},{1... | collective-permute-start | bytes 1179656 | tf_op jit(solution)/shard_map/ppermute | solution.py:19
  27.8 13.6 %collective-permute-start.12 = (f32[128,384]{1,0:T(8,128)S(1)}, f32[128,384]{1,0:T(8,128)S(1)}, u32[]{:S(2)}, u32[]{:S(2)}) collective-permute-start(f32[128,384]{1,0:T(8,128)S(1)} %get-tuple-element.44), channel_id=1, source_target_pairs={{0,3},{1,0},{2,1},{3,2},{4,7},{5,4},{6,5},{7,6},{8,11},{9,8},{10,9... | collective-permute-start | bytes 589832 | tf_op jit(solution)/shard_map/ppermute | solution.py:24
  29.5 11.8 %collective-permute-start.11 = (f32[128,384]{1,0:T(8,128)S(1)}, f32[128,384]{1,0:T(8,128)S(1)}, u32[]{:S(2)}, u32[]{:S(2)}) collective-permute-start(f32[128,384]{1,0:T(8,128)S(1)} %get-tuple-element.43), channel_id=1, source_target_pairs={{0,8},{4,12},{8,0},{12,4},{1,9},{5,13},{9,1},{13,5},{2,10},{6,14},... | collective-permute-start | bytes 589832 | tf_op jit(solution)/shard_map/ppermute | solution.py:19
  30.8 9.9 %all-to-all-start = ((f32[16,2,128]{2,1,0:T(2,128)}), f32[16,2,128]{2,1,0:T(2,128)S(1)}, u32[]{:S(2)}, u32[]{:S(2)}) async-start(f32[16,2,128]{2,1,0:T(2,128)} %get-tuple-element.45), calls=%async_computation | async-start | bytes 32768 | tf_op jit(solution)/shard_map/all_to_all | solution.py:244

commit v22 on v17

--- a/solution.py
+++ b/solution.py
@@ -277,19 +277,24 @@
         4 * packed.size,
     )
     line = [packed, shifted(packed, "sub", 1)]
+    other_stats = exchange(stats, "blk", 1)
+    packed, other_stats = lax.optimization_barrier((packed, other_stats))
+    stats = stats + other_stats
     tz = [exchange(stats, "sub", d) for d in range(1, n_sub)]
     line[1], *tz = lax.optimization_barrier((line[1], *tz))
     for _ in range(half - 1):
         line.append(shifted(line[-1], "sub", 1))
     stats = functools.reduce(jnp.add, [stats] + tz)
     tiles = [packed]
-    for distance in halvings("blk"):
+    distances = halvings("blk")
+    for distance in distances:
         if distance == 1:
             *tiles, line[1] = lax.optimization_barrier((*tiles, line[1]))
+        elif distance == 2:
+            stats = [stats, exchange(stats, "blk", distance)]
         else:
             stats = stats + exchange(stats, "blk", distance)
         tiles = tiles + [exchange(x, "blk", distance) for x in tiles]
-    stats = [stats, exchange(stats, "blk", 1)]
 
     pair_flops = 2 * rows * rows * n_blk * (t_width + 3 * s_width)
     out_shape = (

time: 40.8 us -> 42.3 us (1.037)
  waiting for transfers between devices: 11.9 us -> 13.6 us
    ppermute x3, waiting for transfers between devices: 3.04 us -> 4.87 us  [shifted(): lax.ppermute(value, axis, [(i, (i + distance) % size) for i in range(size)])]
    ppermute x3, starting transfers between devices: 4.03 us -> 3.32 us  [shifted(): lax.ppermute(value, axis, [(i, (i + distance) % size) for i in range(size)])]
    ppermute x10, starting transfers between devices: 9.42 us -> 9.97 us  [exchange(): return lax.ppermute(value, axis, [(i, i ^ distance) for i in range(size)])]
  transfers between devices with their start and end apart: 13 -> 13, of which waited for: 6 -> 5; matrix products, arithmetic and copies ran while one was open for 0% -> 0% of each run, Pallas kernels for 8% -> 7%
where the time goes in v22:
time: 42.3 us; the launch traced here: 42.1 us
  waiting for transfers between devices  13.6 us (32%)
  starting transfers between devices  13.3 us (31%)
  blocking collectives  8.97 us (21%)
  Pallas kernels  5.55 us (13%)
  between operations  0.69 us (2%)
    ppermute x10, starting transfers between devices, exchange(): return lax.ppermute(value, axis, [(i, i ^ distance) for i in range(size)])  9.97 us
    all_to_all x1, blocking collectives, to_all(): return lax.all_to_all(value, ('blk', 'sub'), 0, 0, tiled=True)  8.97 us
    ppermute x10, waiting for transfers between devices, exchange(): return lax.ppermute(value, axis, [(i, i ^ distance) for i in range(size)])  8.7 us
    pallas_call x7, Pallas kernels, call(): pl.pallas_call(kernel, out_shape=out_shape, in_specs=in_specs, out_specs=...  5.55 us
    ppermute x3, waiting for transfers between devices, shifted(): lax.ppermute(value, axis, [(i, (i + distance) % size) for i in range(size)])  4.87 us
    ppermute x3, starting transfers between devices, shifted(): lax.ppermute(value, axis, [(i, (i + distance) % size) for i in range(size)])  3.32 us
  transfers between devices with their start and end apart: 13, of which 5 were waited for; matrix products, arithmetic and copies ran while one was open for 0% of the time, Pallas kernels for 7%

profile of v22, /device:TPU:0, one launch (start us, length us, event | category | flops | bytes accessed | tf_op | source)
XLA Modules:
  0.0 42.1 jit_solution(951592233547955632)
XLA Ops:
  0.6 1.0 %shard_map.41.packed_ref.refs_0_ = bf16[128,1408]{1,0:T(8,128)(2,1)S(1)} custom-call(bf16[128,1024]{1,0:T(8,128)(2,1)} %t_hbm.1, bf16[128,384]{1,0:T(8,128)(2,1)} %s_hbm.1), custom_call_target="tpu_custom_call" | custom-call | bytes 360448 | tf_op jit(solution)/shard_map/pallas_call | solution.py:229
  1.6 0.2 shard_map.42
  1.8 0.5 %collective-permute-start = (f32[1,1536]{1,0:T(1,128)S(1)}, f32[1,1536]{1,0:T(1,128)S(1)}, u32[]{:S(2)}, u32[]{:S(2)}) collective-permute-start(f32[1,1536]{1,0:T(1,128)S(1)} %shard_map.42), channel_id=1, source_target_pairs={{0,4},{4,0},{8,12},{12,8},{1,5},{5,1},{9,13},{13,9},{2,6},{6,2},{1... | collective-permute-start | bytes 18440 | tf_op jit(solution)/shard_map/ppermute | solution.py:19
  2.2 2.6 %collective-permute-start.2 = (bf16[128,1408]{1,0:T(8,128)(2,1)S(1)}, bf16[128,1408]{1,0:T(8,128)(2,1)S(1)}, u32[]{:S(2)}, u32[]{:S(2)}) collective-permute-start(bf16[128,1408]{1,0:T(8,128)(2,1)S(1)} %shard_map.41.packed_ref.refs_0_), channel_id=1, source_target_pairs={{0,1},{1,2},{2,3},{3,0},{4,5},{5,6},{6,7},{7,4},{8,9},{9,10},{10,1... | collective-permute-start | bytes 1081352 | tf_op jit(solution)/shard_map/ppermute | solution.py:24
  4.9 0.0 collective-permute-done
  4.9 1.5 %collective-permute-start.1 = (bf16[128,1408]{1,0:T(8,128)(2,1)S(1)}, bf16[128,1408]{1,0:T(8,128)(2,1)S(1)}, u32[]{:S(2)}, u32[]{:S(2)}) collective-permute-start(bf16[128,1408]{1,0:T(8,128)(2,1)S(1)} %shard_map.41.packed_ref.refs_0_), channel_id=1, source_target_pairs={{0,8},{4,12},{8,0},{12,4},{1,9},{5,13},{9,1},{13,5},{2,10},{6,14},... | collective-permute-start | bytes 1081352 | tf_op jit(solution)/shard_map/ppermute | solution.py:19
  6.4 1.6 %collective-permute-start.3 = (f32[1,1536]{1,0:T(1,128)S(1)}, f32[1,1536]{1,0:T(1,128)S(1)}, u32[]{:S(2)}, u32[]{:S(2)}) collective-permute-start(f32[1,1536]{1,0:T(1,128)S(1)} %add.12), channel_id=1, source_target_pairs={{0,1},{1,0},{2,3},{3,2},{4,5},{5,4},{6,7},{7,6},{8,9},{9,8},{10,11... | collective-permute-start | bytes 18440 | tf_op jit(solution)/shard_map/ppermute | solution.py:19
  8.1 2.1 %collective-permute-start.4 = (f32[1,1536]{1,0:T(1,128)S(1)}, f32[1,1536]{1,0:T(1,128)S(1)}, u32[]{:S(2)}, u32[]{:S(2)}) collective-permute-start(f32[1,1536]{1,0:T(1,128)S(1)} %add.12), channel_id=1, source_target_pairs={{0,2},{1,3},{2,0},{3,1},{4,6},{5,7},{6,4},{7,5},{8,10},{9,11},{10,... | collective-permute-start | bytes 18440 | tf_op jit(solution)/shard_map/ppermute | solution.py:19
  10.2 0.7 %collective-permute-start.5 = (f32[1,1536]{1,0:T(1,128)S(1)}, f32[1,1536]{1,0:T(1,128)S(1)}, u32[]{:S(2)}, u32[]{:S(2)}) collective-permute-start(f32[1,1536]{1,0:T(1,128)S(1)} %add.12), channel_id=1, source_target_pairs={{0,3},{1,2},{2,1},{3,0},{4,7},{5,6},{6,5},{7,4},{8,11},{9,10},{10,... | collective-permute-start | bytes 18440 | tf_op jit(solution)/shard_map/ppermute | solution.py:19
  10.9 5.1 %collective-permute-done.3 = f32[1,1536]{1,0:T(1,128)S(1)} collective-permute-done((f32[1,1536]{1,0:T(1,128)S(1)}, f32[1,1536]{1,0:T(1,128)S(1)}, u32[]{:S(2)}, u32[]{:S(2)}) %collective-permute-start.3) | collective-permute-done | bytes 6176 | tf_op jit(solution)/shard_map/ppermute | solution.py:19
  16.0 0.4 collective-permute-done.4
  16.4 0.0 collective-permute-done.5
  16.4 0.0 collective-permute-done.2.refs_4_
  16.4 0.6 %collective-permute-start.9 = (bf16[128,1408]{1,0:T(8,128)(2,1)S(1)}, bf16[128,1408]{1,0:T(8,128)(2,1)S(1)}, u32[]{:S(2)}, u32[]{:S(2)}) collective-permute-start(bf16[128,1408]{1,0:T(8,128)(2,1)S(1)} %collective-permute-done.2.refs_4_), channel_id=1, source_target_pairs={{0,1},{1,2},{2,3},{3,0},{4,5},{5,6},{6,7},{7,4},{8,9},{9,10},{10,1... | collective-permute-start | bytes 1081352 | tf_op jit(solution)/shard_map/ppermute | solution.py:24
  17.1 0.0 collective-permute-done.1.refs_1_
  17.1 0.0 collective-permute-start.6
  17.1 0.5 %collective-permute-start.7 = (bf16[128,1408]{1,0:T(8,128)(2,1)S(1)}, bf16[128,1408]{1,0:T(8,128)(2,1)S(1)}, u32[]{:S(2)}, u32[]{:S(2)}) collective-permute-start(bf16[128,1408]{1,0:T(8,128)(2,1)S(1)} %collective-permute-done.1.refs_1_), channel_id=1, source_target_pairs={{0,4},{4,0},{8,12},{12,8},{1,5},{5,1},{9,13},{13,9},{2,6},{6,2},{1... | collective-permute-start | bytes 1081352 | tf_op jit(solution)/shard_map/ppermute | solution.py:19
  17.6 1.6 %collective-permute-start.8 = (f32[1,1536]{1,0:T(1,128)S(1)}, f32[1,1536]{1,0:T(1,128)S(1)}, u32[]{:S(2)}, u32[]{:S(2)}) collective-permute-start(f32[1,1536]{1,0:T(1,128)S(1)} %add_add_fusion.refs_5_), channel_id=1, source_target_pairs={{0,8},{4,12},{8,0},{12,4},{1,9},{5,13},{9,1},{13,5},{2,10},{6,14},... | collective-permute-start | bytes 18440 | tf_op jit(solution)/shard_map/ppermute | solution.py:19
  19.2 2.1 %collective-permute-done.8.refs_6_ = f32[1,1536]{1,0:T(1,128)S(1)} collective-permute-done((f32[1,1536]{1,0:T(1,128)S(1)}, f32[1,1536]{1,0:T(1,128)S(1)}, u32[]{:S(2)}, u32[]{:S(2)}) %collective-permute-start.8) | collective-permute-done | bytes 6176 | tf_op jit(solution)/shard_map/ppermute | solution.py:19
  21.3 0.0 collective-permute-done.6.refs_2_
  21.3 2.2 %shard_map.43 = (f32[128,384]{1,0:T(8,128)S(1)}, f32[128,384]{1,0:T(8,128)S(1)}, f32[2,256,512]{2,1,0:T(8,128)S(1)}, f32[2,2,256,128]{3,2,1,0:T(8,128)S(1)}, f32...) custom-call(bf16[128,1408]{1,0:T(8,128)(2,1)S(1)} %shard_map.41.packed_ref.refs_0_, ...), custom_call_target="tpu_custom_call" | custom-call | flops 570425344 | bytes 1814528 | tf_op jit(solution)/shard_map/pallas_call | solution.py:229
  23.5 4.9 %collective-permute-done.9.refs_1_ = bf16[128,1408]{1,0:T(8,128)(2,1)S(1)} collective-permute-done((bf16[128,1408]{1,0:T(8,128)(2,1)S(1)}, bf16[128,1408]{1,0:T(8,128)(2,1)S(1)}, u32[]{:S(2)}, u32[]{:S(2)}) %collective-permute-start.9) | collective-permute-done | bytes 360480 | tf_op jit(solution)/shard_map/ppermute | solution.py:24
  28.4 0.7 %shard_map.44 = (f32[256,384]{1,0:T(8,128)S(1)}, f32[2,128]{1,0:T(2,128)S(1)}, f32[2,128]{1,0:T(2,128)S(1)}) custom-call(bf16[2,256,1408]{2,1,0:T(8,128)(2,1)S(1)} %get-tuple-element.37.refs_0_, bf16[128,1408]{1,0:T(8,128)(2,1)S(1)} %collective-permute-done.9.refs_1_, f32[4,384]{1,0:T(4,128)S(1)} %get-tuple-element.36.refs_2_.stats_ref, ...), custom_call_target="tpu_custom_call" | custom-call | flops 142606336 | bytes 3382272 | tf_op jit(solution)/shard_map/pallas_call | solution.py:229
  29.1 0.1 collective-permute-start.10
  29.1 0.1 collective-permute-start.12
  29.2 0.7 %shard_map.45 = (f32[256,384]{1,0:T(8,128)S(1)}, f32[16,2,128]{2,1,0:T(2,128)S(1)}) custom-call(bf16[2,256,1408]{2,1,0:T(8,128)(2,1)S(1)} %get-tuple-element.37.refs_0_, bf16[128,1408]{1,0:T(8,128)(2,1)S(1)} %collective-permute-done.9.refs_1_, f32[4,384]{1,0:T(4,128)S(1)} %get-tuple-element.36.refs_2_.stats_ref, ...), custom_call_target="tpu_custom_call" | custom-call | flops 142606336 | bytes 3383296 | tf_op jit(solution)/shard_map/pallas_call | solution.py:229
  29.9 1.0 %collective-permute-done.10.got_ref = f32[256,384]{1,0:T(8,128)S(1)} collective-permute-done((f32[256,384]{1,0:T(8,128)S(1)}, f32[256,384]{1,0:T(8,128)S(1)}, u32[]{:S(2)}, u32[]{:S(2)}) %collective-permute-start.10) | collective-permute-done | bytes 393248 | tf_op jit(solution)/shard_map/ppermute | solution.py:19
  30.9 1.4 %collective-permute-start.11 = (f32[128,384]{1,0:T(8,128)S(1)}, f32[128,384]{1,0:T(8,128)S(1)}, u32[]{:S(2)}, u32[]{:S(2)}) collective-permute-start(f32[128,384]{1,0:T(8,128)S(1)} %get-tuple-element.48), channel_id=1, source_target_pairs={{0,8},{4,12},{8,0},{12,4},{1,9},{5,13},{9,1},{13,5},{2,10},{6,14},... | collective-permute-start | bytes 589832 | tf_op jit(solution)/shard_map/ppermute | solution.py:19
  32.3 9.0 %all_to_all.5.sums_ref = f32[16,2,128]{2,1,0:T(2,128)S(1)} all-to-all(f32[16,2,128]{2,1,0:T(2,128)S(1)} %get-tuple-element.43), channel_id=1, replica_groups=mesh['groups'=2,'blk'=4,'sub'=4] {'blk','sub'}, dimensions={0} | all-to-all | bytes 32768 | tf_op jit(solution)/shard_map/all_to_all | solution.py:250
  41.3 0.0 collective-permute-done.12.refs_3_
  41.3 0.0 collective-permute-done.11.refs_2_
  41.3 0.8 %shard_map.47 = (f32[128,384]{1,0:T(8,128)}, f32[1,128]{1,0:T(1,128)}) custom-call(bf16[128,1408]{1,0:T(8,128)(2,1)S(1)} %shard_map.41.packed_ref.refs_0_, f32[4,384]{1,0:T(4,128)S(1)} %get-tuple-element.36.refs_2_.stats_ref, f32[16,2,128]{2,1,0:T(2,128)S(1)} %all_to_all.5.sums_ref, f32[128,384]{1,0:T(8,128)S(1)} %get-tuple-element.44.refs_0_, ...), custom_call_target="tpu_custom_call" | custom-call | flops 393216 | bytes 1169408 | tf_op jit(solution)/shard_map/pallas_call | solution.py:229
  (4 shorter events, 0.1 us)
Async XLA Ops:
  1.8 3.1 %collective-permute-start = (f32[1,1536]{1,0:T(1,128)S(1)}, f32[1,1536]{1,0:T(1,128)S(1)}, u32[]{:S(2)}, u32[]{:S(2)}) collective-permute-start(f32[1,1536]{1,0:T(1,128)S(1)} %shard_map.42), channel_id=1, source_target_pairs={{0,4},{4,0},{8,12},{12,8},{1,5},{5,1},{9,13},{13,9},{2,6},{6,2},{1... | collective-permute-start | bytes 18440 | tf_op jit(solution)/shard_map/ppermute | solution.py:19
  2.2 14.2 %collective-permute-start.2 = (bf16[128,1408]{1,0:T(8,128)(2,1)S(1)}, bf16[128,1408]{1,0:T(8,128)(2,1)S(1)}, u32[]{:S(2)}, u32[]{:S(2)}) collective-permute-start(bf16[128,1408]{1,0:T(8,128)(2,1)S(1)} %shard_map.41.packed_ref.refs_0_), channel_id=1, source_target_pairs={{0,1},{1,2},{2,3},{3,0},{4,5},{5,6},{6,7},{7,4},{8,9},{9,10},{10,1... | collective-permute-start | bytes 1081352 | tf_op jit(solution)/shard_map/ppermute | solution.py:24
  4.9 12.2 %collective-permute-start.1 = (bf16[128,1408]{1,0:T(8,128)(2,1)S(1)}, bf16[128,1408]{1,0:T(8,128)(2,1)S(1)}, u32[]{:S(2)}, u32[]{:S(2)}) collective-permute-start(bf16[128,1408]{1,0:T(8,128)(2,1)S(1)} %shard_map.41.packed_ref.refs_0_), channel_id=1, source_target_pairs={{0,8},{4,12},{8,0},{12,4},{1,9},{5,13},{9,1},{13,5},{2,10},{6,14},... | collective-permute-start | bytes 1081352 | tf_op jit(solution)/shard_map/ppermute | solution.py:19
  6.4 9.6 %collective-permute-start.3 = (f32[1,1536]{1,0:T(1,128)S(1)}, f32[1,1536]{1,0:T(1,128)S(1)}, u32[]{:S(2)}, u32[]{:S(2)}) collective-permute-start(f32[1,1536]{1,0:T(1,128)S(1)} %add.12), channel_id=1, source_target_pairs={{0,1},{1,0},{2,3},{3,2},{4,5},{5,4},{6,7},{7,6},{8,9},{9,8},{10,11... | collective-permute-start | bytes 18440 | tf_op jit(solution)/shard_map/ppermute | solution.py:19
  8.1 8.4 %collective-permute-start.4 = (f32[1,1536]{1,0:T(1,128)S(1)}, f32[1,1536]{1,0:T(1,128)S(1)}, u32[]{:S(2)}, u32[]{:S(2)}) collective-permute-start(f32[1,1536]{1,0:T(1,128)S(1)} %add.12), channel_id=1, source_target_pairs={{0,2},{1,3},{2,0},{3,1},{4,6},{5,7},{6,4},{7,5},{8,10},{9,11},{10,... | collective-permute-start | bytes 18440 | tf_op jit(solution)/shard_map/ppermute | solution.py:19
  10.2 6.3 %collective-permute-start.5 = (f32[1,1536]{1,0:T(1,128)S(1)}, f32[1,1536]{1,0:T(1,128)S(1)}, u32[]{:S(2)}, u32[]{:S(2)}) collective-permute-start(f32[1,1536]{1,0:T(1,128)S(1)} %add.12), channel_id=1, source_target_pairs={{0,3},{1,2},{2,1},{3,0},{4,7},{5,6},{6,5},{7,4},{8,11},{9,10},{10,... | collective-permute-start | bytes 18440 | tf_op jit(solution)/shard_map/ppermute | solution.py:19
  16.4 12.0 %collective-permute-start.9 = (bf16[128,1408]{1,0:T(8,128)(2,1)S(1)}, bf16[128,1408]{1,0:T(8,128)(2,1)S(1)}, u32[]{:S(2)}, u32[]{:S(2)}) collective-permute-start(bf16[128,1408]{1,0:T(8,128)(2,1)S(1)} %collective-permute-done.2.refs_4_), channel_id=1, source_target_pairs={{0,1},{1,2},{2,3},{3,0},{4,5},{5,6},{6,7},{7,4},{8,9},{9,10},{10,1... | collective-permute-start | bytes 1081352 | tf_op jit(solution)/shard_map/ppermute | solution.py:24
  17.1 4.2 %collective-permute-start.6 = (bf16[128,1408]{1,0:T(8,128)(2,1)S(1)}, bf16[128,1408]{1,0:T(8,128)(2,1)S(1)}, u32[]{:S(2)}, u32[]{:S(2)}) collective-permute-start(bf16[128,1408]{1,0:T(8,128)(2,1)S(1)} %shard_map.41.packed_ref.refs_0_), channel_id=1, source_target_pairs={{0,4},{4,0},{8,12},{12,8},{1,5},{5,1},{9,13},{13,9},{2,6},{6,2},{1... | collective-permute-start | bytes 1081352 | tf_op jit(solution)/shard_map/ppermute | solution.py:19
  17.1 4.2 %collective-permute-start.7 = (bf16[128,1408]{1,0:T(8,128)(2,1)S(1)}, bf16[128,1408]{1,0:T(8,128)(2,1)S(1)}, u32[]{:S(2)}, u32[]{:S(2)}) collective-permute-start(bf16[128,1408]{1,0:T(8,128)(2,1)S(1)} %collective-permute-done.1.refs_1_), channel_id=1, source_target_pairs={{0,4},{4,0},{8,12},{12,8},{1,5},{5,1},{9,13},{13,9},{2,6},{6,2},{1... | collective-permute-start | bytes 1081352 | tf_op jit(solution)/shard_map/ppermute | solution.py:19
  17.6 3.7 %collective-permute-start.8 = (f32[1,1536]{1,0:T(1,128)S(1)}, f32[1,1536]{1,0:T(1,128)S(1)}, u32[]{:S(2)}, u32[]{:S(2)}) collective-permute-start(f32[1,1536]{1,0:T(1,128)S(1)} %add_add_fusion.refs_5_), channel_id=1, source_target_pairs={{0,8},{4,12},{8,0},{12,4},{1,9},{5,13},{9,1},{13,5},{2,10},{6,14},... | collective-permute-start | bytes 18440 | tf_op jit(solution)/shard_map/ppermute | solution.py:19
  29.1 1.8 %collective-permute-start.10 = (f32[256,384]{1,0:T(8,128)S(1)}, f32[256,384]{1,0:T(8,128)S(1)}, u32[]{:S(2)}, u32[]{:S(2)}) collective-permute-start(f32[256,384]{1,0:T(8,128)S(1)} %get-tuple-element.46), channel_id=1, source_target_pairs={{0,4},{4,0},{8,12},{12,8},{1,5},{5,1},{9,13},{13,9},{2,6},{6,2},{1... | collective-permute-start | bytes 1179656 | tf_op jit(solution)/shard_map/ppermute | solution.py:19
  29.1 12.1 %collective-permute-start.12 = (f32[128,384]{1,0:T(8,128)S(1)}, f32[128,384]{1,0:T(8,128)S(1)}, u32[]{:S(2)}, u32[]{:S(2)}) collective-permute-start(f32[128,384]{1,0:T(8,128)S(1)} %get-tuple-element.49), channel_id=1, source_target_pairs={{0,3},{1,0},{2,1},{3,2},{4,7},{5,4},{6,5},{7,6},{8,11},{9,8},{10,9... | collective-permute-start | bytes 589832 | tf_op jit(solution)/shard_map/ppermute | solution.py:24
  30.9 10.4 %collective-permute-start.11 = (f32[128,384]{1,0:T(8,128)S(1)}, f32[128,384]{1,0:T(8,128)S(1)}, u32[]{:S(2)}, u32[]{:S(2)}) collective-permute-start(f32[128,384]{1,0:T(8,128)S(1)} %get-tuple-element.48), channel_id=1, source_target_pairs={{0,8},{4,12},{8,0},{12,4},{1,9},{5,13},{9,1},{13,5},{2,10},{6,14},... | collective-permute-start | bytes 589832 | tf_op jit(solution)/shard_map/ppermute | solution.py:19

commit v23 on v17

--- a/solution.py
+++ b/solution.py
@@ -247,7 +247,7 @@
 
 
 def to_all(value):
-    return lax.all_to_all(value, ("blk", "sub"), 0, 0, tiled=True)
+    return lax.all_to_all(value, ("sub", "blk"), 0, 0, tiled=True)
 
 
 def per_device(teacher, student):

time: 40.8 us -> 40.9 us (level)
  no operation moved by 1% of the time
where the time goes in v23:
time: 40.9 us; the launch traced here: 40.7 us
  starting transfers between devices  13.4 us (33%)
  waiting for transfers between devices  11.9 us (29%)
  blocking collectives  9.06 us (22%)
  Pallas kernels  5.54 us (14%)
  between operations  0.69 us (2%)
    ppermute x10, starting transfers between devices, exchange(): return lax.ppermute(value, axis, [(i, i ^ distance) for i in range(size)])  9.42 us
    all_to_all x1, blocking collectives, to_all(): return lax.all_to_all(value, ('sub', 'blk'), 0, 0, tiled=True)  9.06 us
    ppermute x10, waiting for transfers between devices, exchange(): return lax.ppermute(value, axis, [(i, i ^ distance) for i in range(size)])  8.9 us
    pallas_call x7, Pallas kernels, call(): pl.pallas_call(kernel, out_shape=out_shape, in_specs=in_specs, out_specs=...  5.54 us
    ppermute x3, starting transfers between devices, shifted(): lax.ppermute(value, axis, [(i, (i + distance) % size) for i in range(size)])  4.03 us
    ppermute x3, waiting for transfers between devices, shifted(): lax.ppermute(value, axis, [(i, (i + distance) % size) for i in range(size)])  3.04 us
  transfers between devices with their start and end apart: 13, of which 6 were waited for; matrix products, arithmetic and copies ran while one was open for 0% of the time, Pallas kernels for 8%

profile of v23, /device:TPU:0, one launch (start us, length us, event | category | flops | bytes accessed | tf_op | source)
XLA Modules:
  0.0 40.7 jit_solution(14231943618607943219)
XLA Ops:
  0.6 1.0 %shard_map.41.packed_ref.refs_0_ = bf16[128,1408]{1,0:T(8,128)(2,1)S(1)} custom-call(bf16[128,1024]{1,0:T(8,128)(2,1)} %t_hbm.1, bf16[128,384]{1,0:T(8,128)(2,1)} %s_hbm.1), custom_call_target="tpu_custom_call" | custom-call | bytes 360448 | tf_op jit(solution)/shard_map/pallas_call | solution.py:229
  1.6 3.1 %collective-permute-start.1 = (bf16[128,1408]{1,0:T(8,128)(2,1)S(1)}, bf16[128,1408]{1,0:T(8,128)(2,1)S(1)}, u32[]{:S(2)}, u32[]{:S(2)}) collective-permute-start(bf16[128,1408]{1,0:T(8,128)(2,1)S(1)} %shard_map.41.packed_ref.refs_0_), channel_id=1, source_target_pairs={{0,1},{1,2},{2,3},{3,0},{4,5},{5,6},{6,7},{7,4},{8,9},{9,10},{10,1... | collective-permute-start | bytes 1081352 | tf_op jit(solution)/shard_map/ppermute | solution.py:24
  4.7 1.5 %collective-permute-start = (bf16[128,1408]{1,0:T(8,128)(2,1)S(1)}, bf16[128,1408]{1,0:T(8,128)(2,1)S(1)}, u32[]{:S(2)}, u32[]{:S(2)}) collective-permute-start(bf16[128,1408]{1,0:T(8,128)(2,1)S(1)} %shard_map.41.packed_ref.refs_0_), channel_id=1, source_target_pairs={{0,8},{4,12},{8,0},{12,4},{1,9},{5,13},{9,1},{13,5},{2,10},{6,14},... | collective-permute-start | bytes 1081352 | tf_op jit(solution)/shard_map/ppermute | solution.py:19
  6.2 0.2 shard_map.42
  6.4 1.6 %collective-permute-start.2 = (f32[1,1536]{1,0:T(1,128)S(1)}, f32[1,1536]{1,0:T(1,128)S(1)}, u32[]{:S(2)}, u32[]{:S(2)}) collective-permute-start(f32[1,1536]{1,0:T(1,128)S(1)} %shard_map.42), channel_id=1, source_target_pairs={{0,1},{1,0},{2,3},{3,2},{4,5},{5,4},{6,7},{7,6},{8,9},{9,8},{10,11... | collective-permute-start | bytes 18440 | tf_op jit(solution)/shard_map/ppermute | solution.py:19
  8.0 1.2 %collective-permute-start.3 = (f32[1,1536]{1,0:T(1,128)S(1)}, f32[1,1536]{1,0:T(1,128)S(1)}, u32[]{:S(2)}, u32[]{:S(2)}) collective-permute-start(f32[1,1536]{1,0:T(1,128)S(1)} %shard_map.42), channel_id=1, source_target_pairs={{0,2},{1,3},{2,0},{3,1},{4,6},{5,7},{6,4},{7,5},{8,10},{9,11},{10,... | collective-permute-start | bytes 18440 | tf_op jit(solution)/shard_map/ppermute | solution.py:19
  9.2 1.6 %collective-permute-start.4 = (f32[1,1536]{1,0:T(1,128)S(1)}, f32[1,1536]{1,0:T(1,128)S(1)}, u32[]{:S(2)}, u32[]{:S(2)}) collective-permute-start(f32[1,1536]{1,0:T(1,128)S(1)} %shard_map.42), channel_id=1, source_target_pairs={{0,3},{1,2},{2,1},{3,0},{4,7},{5,6},{6,5},{7,4},{8,11},{9,10},{10,... | collective-permute-start | bytes 18440 | tf_op jit(solution)/shard_map/ppermute | solution.py:19
  10.8 3.8 %collective-permute-done.2 = f32[1,1536]{1,0:T(1,128)S(1)} collective-permute-done((f32[1,1536]{1,0:T(1,128)S(1)}, f32[1,1536]{1,0:T(1,128)S(1)}, u32[]{:S(2)}, u32[]{:S(2)}) %collective-permute-start.2) | collective-permute-done | bytes 6176 | tf_op jit(solution)/shard_map/ppermute | solution.py:19
  14.6 1.1 %collective-permute-done.3 = f32[1,1536]{1,0:T(1,128)S(1)} collective-permute-done((f32[1,1536]{1,0:T(1,128)S(1)}, f32[1,1536]{1,0:T(1,128)S(1)}, u32[]{:S(2)}, u32[]{:S(2)}) %collective-permute-start.3) | collective-permute-done | bytes 6176 | tf_op jit(solution)/shard_map/ppermute | solution.py:19
  15.6 0.0 collective-permute-done.4
  15.6 0.0 collective-permute-done.1.refs_4_
  15.7 0.6 %collective-permute-start.9 = (bf16[128,1408]{1,0:T(8,128)(2,1)S(1)}, bf16[128,1408]{1,0:T(8,128)(2,1)S(1)}, u32[]{:S(2)}, u32[]{:S(2)}) collective-permute-start(bf16[128,1408]{1,0:T(8,128)(2,1)S(1)} %collective-permute-done.1.refs_4_), channel_id=1, source_target_pairs={{0,1},{1,2},{2,3},{3,0},{4,5},{5,6},{6,7},{7,4},{8,9},{9,10},{10,1... | collective-permute-start | bytes 1081352 | tf_op jit(solution)/shard_map/ppermute | solution.py:24
  16.3 0.0 collective-permute-done.refs_1_
  16.3 0.0 collective-permute-start.5
  16.3 0.5 %collective-permute-start.6 = (bf16[128,1408]{1,0:T(8,128)(2,1)S(1)}, bf16[128,1408]{1,0:T(8,128)(2,1)S(1)}, u32[]{:S(2)}, u32[]{:S(2)}) collective-permute-start(bf16[128,1408]{1,0:T(8,128)(2,1)S(1)} %collective-permute-done.refs_1_), channel_id=1, source_target_pairs={{0,4},{4,0},{8,12},{12,8},{1,5},{5,1},{9,13},{13,9},{2,6},{6,2},{1... | collective-permute-start | bytes 1081352 | tf_op jit(solution)/shard_map/ppermute | solution.py:19
  16.8 1.6 %collective-permute-start.7 = (f32[1,1536]{1,0:T(1,128)S(1)}, f32[1,1536]{1,0:T(1,128)S(1)}, u32[]{:S(2)}, u32[]{:S(2)}) collective-permute-start(f32[1,1536]{1,0:T(1,128)S(1)} %add_add_fusion), channel_id=1, source_target_pairs={{0,8},{4,12},{8,0},{12,4},{1,9},{5,13},{9,1},{13,5},{2,10},{6,14},... | collective-permute-start | bytes 18440 | tf_op jit(solution)/shard_map/ppermute | solution.py:19
  18.4 2.1 %collective-permute-done.7 = f32[1,1536]{1,0:T(1,128)S(1)} collective-permute-done((f32[1,1536]{1,0:T(1,128)S(1)}, f32[1,1536]{1,0:T(1,128)S(1)}, u32[]{:S(2)}, u32[]{:S(2)}) %collective-permute-start.7) | collective-permute-done | bytes 6176 | tf_op jit(solution)/shard_map/ppermute | solution.py:19
  20.5 0.1 collective-permute-start.8
  20.6 1.2 %collective-permute-done.8.refs_6_ = f32[1,1536]{1,0:T(1,128)S(1)} collective-permute-done((f32[1,1536]{1,0:T(1,128)S(1)}, f32[1,1536]{1,0:T(1,128)S(1)}, u32[]{:S(2)}, u32[]{:S(2)}) %collective-permute-start.8) | collective-permute-done | bytes 6176 | tf_op jit(solution)/shard_map/ppermute | solution.py:19
  21.8 0.0 collective-permute-done.5.refs_2_
  21.8 0.0 collective-permute-done.6.refs_3_
  21.8 2.2 %shard_map.43 = (f32[128,384]{1,0:T(8,128)S(1)}, f32[128,384]{1,0:T(8,128)S(1)}, f32[2,256,512]{2,1,0:T(8,128)S(1)}, f32[2,2,256,128]{3,2,1,0:T(8,128)S(1)}, f32...) custom-call(bf16[128,1408]{1,0:T(8,128)(2,1)S(1)} %shard_map.41.packed_ref.refs_0_, ...), custom_call_target="tpu_custom_call" | custom-call | flops 570425344 | bytes 1814528 | tf_op jit(solution)/shard_map/pallas_call | solution.py:229
  24.0 3.0 %collective-permute-done.9.refs_1_ = bf16[128,1408]{1,0:T(8,128)(2,1)S(1)} collective-permute-done((bf16[128,1408]{1,0:T(8,128)(2,1)S(1)}, bf16[128,1408]{1,0:T(8,128)(2,1)S(1)}, u32[]{:S(2)}, u32[]{:S(2)}) %collective-permute-start.9) | collective-permute-done | bytes 360480 | tf_op jit(solution)/shard_map/ppermute | solution.py:24
  27.0 0.7 %shard_map.44 = (f32[256,384]{1,0:T(8,128)S(1)}, f32[2,128]{1,0:T(2,128)S(1)}, f32[2,128]{1,0:T(2,128)S(1)}) custom-call(bf16[2,256,1408]{2,1,0:T(8,128)(2,1)S(1)} %get-tuple-element.33.refs_0_, bf16[128,1408]{1,0:T(8,128)(2,1)S(1)} %collective-permute-done.9.refs_1_, f32[4,384]{1,0:T(4,128)S(1)} %get-tuple-element.32.refs_2_.stats_ref, ...), custom_call_target="tpu_custom_call" | custom-call | flops 142606336 | bytes 3382272 | tf_op jit(solution)/shard_map/pallas_call | solution.py:229
  27.7 0.1 collective-permute-start.10
  27.8 0.3 collective-permute-start.12
  28.1 0.6 %shard_map.45 = (f32[256,384]{1,0:T(8,128)S(1)}, f32[16,2,128]{2,1,0:T(2,128)S(1)}) custom-call(bf16[2,256,1408]{2,1,0:T(8,128)(2,1)S(1)} %get-tuple-element.33.refs_0_, bf16[128,1408]{1,0:T(8,128)(2,1)S(1)} %collective-permute-done.9.refs_1_, f32[4,384]{1,0:T(4,128)S(1)} %get-tuple-element.32.refs_2_.stats_ref, ...), custom_call_target="tpu_custom_call" | custom-call | flops 142606336 | bytes 3383296 | tf_op jit(solution)/shard_map/pallas_call | solution.py:229
  28.7 0.7 %collective-permute-done.10.got_ref = f32[256,384]{1,0:T(8,128)S(1)} collective-permute-done((f32[256,384]{1,0:T(8,128)S(1)}, f32[256,384]{1,0:T(8,128)S(1)}, u32[]{:S(2)}, u32[]{:S(2)}) %collective-permute-start.10) | collective-permute-done | bytes 393248 | tf_op jit(solution)/shard_map/ppermute | solution.py:19
  29.5 1.3 %collective-permute-start.11 = (f32[128,384]{1,0:T(8,128)S(1)}, f32[128,384]{1,0:T(8,128)S(1)}, u32[]{:S(2)}, u32[]{:S(2)}) collective-permute-start(f32[128,384]{1,0:T(8,128)S(1)} %get-tuple-element.44), channel_id=1, source_target_pairs={{0,8},{4,12},{8,0},{12,4},{1,9},{5,13},{9,1},{13,5},{2,10},{6,14},... | collective-permute-start | bytes 589832 | tf_op jit(solution)/shard_map/ppermute | solution.py:19
  30.8 9.1 %all_to_all.5.sums_ref = f32[16,2,128]{2,1,0:T(2,128)S(1)} all-to-all(f32[16,2,128]{2,1,0:T(2,128)S(1)} %get-tuple-element.39), channel_id=1, replica_groups=mesh['groups'=2,'blk'=4,'sub'=4] {'sub','blk'}, dimensions={0} | all-to-all | bytes 32768 | tf_op jit(solution)/shard_map/all_to_all | solution.py:250
  39.9 0.0 collective-permute-done.11.refs_2_
  39.9 0.8 %shard_map.47 = (f32[128,384]{1,0:T(8,128)}, f32[1,128]{1,0:T(1,128)}) custom-call(bf16[128,1408]{1,0:T(8,128)(2,1)S(1)} %shard_map.41.packed_ref.refs_0_, f32[4,384]{1,0:T(4,128)S(1)} %get-tuple-element.32.refs_2_.stats_ref, f32[16,2,128]{2,1,0:T(2,128)S(1)} %all_to_all.5.sums_ref, f32[128,384]{1,0:T(8,128)S(1)} %get-tuple-element.40.refs_0_, ...), custom_call_target="tpu_custom_call" | custom-call | flops 393216 | bytes 1169408 | tf_op jit(solution)/shard_map/pallas_call | solution.py:229
  (4 shorter events, 0.1 us)
Async XLA Ops:
  1.6 14.0 %collective-permute-start.1 = (bf16[128,1408]{1,0:T(8,128)(2,1)S(1)}, bf16[128,1408]{1,0:T(8,128)(2,1)S(1)}, u32[]{:S(2)}, u32[]{:S(2)}) collective-permute-start(bf16[128,1408]{1,0:T(8,128)(2,1)S(1)} %shard_map.41.packed_ref.refs_0_), channel_id=1, source_target_pairs={{0,1},{1,2},{2,3},{3,0},{4,5},{5,6},{6,7},{7,4},{8,9},{9,10},{10,1... | collective-permute-start | bytes 1081352 | tf_op jit(solution)/shard_map/ppermute | solution.py:24
  4.7 11.6 %collective-permute-start = (bf16[128,1408]{1,0:T(8,128)(2,1)S(1)}, bf16[128,1408]{1,0:T(8,128)(2,1)S(1)}, u32[]{:S(2)}, u32[]{:S(2)}) collective-permute-start(bf16[128,1408]{1,0:T(8,128)(2,1)S(1)} %shard_map.41.packed_ref.refs_0_), channel_id=1, source_target_pairs={{0,8},{4,12},{8,0},{12,4},{1,9},{5,13},{9,1},{13,5},{2,10},{6,14},... | collective-permute-start | bytes 1081352 | tf_op jit(solution)/shard_map/ppermute | solution.py:19
  6.4 8.2 %collective-permute-start.2 = (f32[1,1536]{1,0:T(1,128)S(1)}, f32[1,1536]{1,0:T(1,128)S(1)}, u32[]{:S(2)}, u32[]{:S(2)}) collective-permute-start(f32[1,1536]{1,0:T(1,128)S(1)} %shard_map.42), channel_id=1, source_target_pairs={{0,1},{1,0},{2,3},{3,2},{4,5},{5,4},{6,7},{7,6},{8,9},{9,8},{10,11... | collective-permute-start | bytes 18440 | tf_op jit(solution)/shard_map/ppermute | solution.py:19
  8.0 7.7 %collective-permute-start.3 = (f32[1,1536]{1,0:T(1,128)S(1)}, f32[1,1536]{1,0:T(1,128)S(1)}, u32[]{:S(2)}, u32[]{:S(2)}) collective-permute-start(f32[1,1536]{1,0:T(1,128)S(1)} %shard_map.42), channel_id=1, source_target_pairs={{0,2},{1,3},{2,0},{3,1},{4,6},{5,7},{6,4},{7,5},{8,10},{9,11},{10,... | collective-permute-start | bytes 18440 | tf_op jit(solution)/shard_map/ppermute | solution.py:19
  9.2 6.4 %collective-permute-start.4 = (f32[1,1536]{1,0:T(1,128)S(1)}, f32[1,1536]{1,0:T(1,128)S(1)}, u32[]{:S(2)}, u32[]{:S(2)}) collective-permute-start(f32[1,1536]{1,0:T(1,128)S(1)} %shard_map.42), channel_id=1, source_target_pairs={{0,3},{1,2},{2,1},{3,0},{4,7},{5,6},{6,5},{7,4},{8,11},{9,10},{10,... | collective-permute-start | bytes 18440 | tf_op jit(solution)/shard_map/ppermute | solution.py:19
  15.7 11.4 %collective-permute-start.9 = (bf16[128,1408]{1,0:T(8,128)(2,1)S(1)}, bf16[128,1408]{1,0:T(8,128)(2,1)S(1)}, u32[]{:S(2)}, u32[]{:S(2)}) collective-permute-start(bf16[128,1408]{1,0:T(8,128)(2,1)S(1)} %collective-permute-done.1.refs_4_), channel_id=1, source_target_pairs={{0,1},{1,2},{2,3},{3,0},{4,5},{5,6},{6,7},{7,4},{8,9},{9,10},{10,1... | collective-permute-start | bytes 1081352 | tf_op jit(solution)/shard_map/ppermute | solution.py:24
  16.3 5.5 %collective-permute-start.5 = (bf16[128,1408]{1,0:T(8,128)(2,1)S(1)}, bf16[128,1408]{1,0:T(8,128)(2,1)S(1)}, u32[]{:S(2)}, u32[]{:S(2)}) collective-permute-start(bf16[128,1408]{1,0:T(8,128)(2,1)S(1)} %shard_map.41.packed_ref.refs_0_), channel_id=1, source_target_pairs={{0,4},{4,0},{8,12},{12,8},{1,5},{5,1},{9,13},{13,9},{2,6},{6,2},{1... | collective-permute-start | bytes 1081352 | tf_op jit(solution)/shard_map/ppermute | solution.py:19
  16.3 5.5 %collective-permute-start.6 = (bf16[128,1408]{1,0:T(8,128)(2,1)S(1)}, bf16[128,1408]{1,0:T(8,128)(2,1)S(1)}, u32[]{:S(2)}, u32[]{:S(2)}) collective-permute-start(bf16[128,1408]{1,0:T(8,128)(2,1)S(1)} %collective-permute-done.refs_1_), channel_id=1, source_target_pairs={{0,4},{4,0},{8,12},{12,8},{1,5},{5,1},{9,13},{13,9},{2,6},{6,2},{1... | collective-permute-start | bytes 1081352 | tf_op jit(solution)/shard_map/ppermute | solution.py:19
  16.8 3.7 %collective-permute-start.7 = (f32[1,1536]{1,0:T(1,128)S(1)}, f32[1,1536]{1,0:T(1,128)S(1)}, u32[]{:S(2)}, u32[]{:S(2)}) collective-permute-start(f32[1,1536]{1,0:T(1,128)S(1)} %add_add_fusion), channel_id=1, source_target_pairs={{0,8},{4,12},{8,0},{12,4},{1,9},{5,13},{9,1},{13,5},{2,10},{6,14},... | collective-permute-start | bytes 18440 | tf_op jit(solution)/shard_map/ppermute | solution.py:19
  20.5 1.2 %collective-permute-start.8 = (f32[1,1536]{1,0:T(1,128)S(1)}, f32[1,1536]{1,0:T(1,128)S(1)}, u32[]{:S(2)}, u32[]{:S(2)}) collective-permute-start(f32[1,1536]{1,0:T(1,128)S(1)} %add.15.refs_5_), channel_id=1, source_target_pairs={{0,4},{4,0},{8,12},{12,8},{1,5},{5,1},{9,13},{13,9},{2,6},{6,2},{1... | collective-permute-start | bytes 18440 | tf_op jit(solution)/shard_map/ppermute | solution.py:19
  27.7 1.8 %collective-permute-start.10 = (f32[256,384]{1,0:T(8,128)S(1)}, f32[256,384]{1,0:T(8,128)S(1)}, u32[]{:S(2)}, u32[]{:S(2)}) collective-permute-start(f32[256,384]{1,0:T(8,128)S(1)} %get-tuple-element.42), channel_id=1, source_target_pairs={{0,4},{4,0},{8,12},{12,8},{1,5},{5,1},{9,13},{13,9},{2,6},{6,2},{1... | collective-permute-start | bytes 1179656 | tf_op jit(solution)/shard_map/ppermute | solution.py:19
  27.8 12.1 %collective-permute-start.12 = (f32[128,384]{1,0:T(8,128)S(1)}, f32[128,384]{1,0:T(8,128)S(1)}, u32[]{:S(2)}, u32[]{:S(2)}) collective-permute-start(f32[128,384]{1,0:T(8,128)S(1)} %get-tuple-element.45), channel_id=1, source_target_pairs={{0,3},{1,0},{2,1},{3,2},{4,7},{5,4},{6,5},{7,6},{8,11},{9,8},{10,9... | collective-permute-start | bytes 589832 | tf_op jit(solution)/shard_map/ppermute | solution.py:24
  29.5 10.4 %collective-permute-start.11 = (f32[128,384]{1,0:T(8,128)S(1)}, f32[128,384]{1,0:T(8,128)S(1)}, u32[]{:S(2)}, u32[]{:S(2)}) collective-permute-start(f32[128,384]{1,0:T(8,128)S(1)} %get-tuple-element.44), channel_id=1, source_target_pairs={{0,8},{4,12},{8,0},{12,4},{1,9},{5,13},{9,1},{13,5},{2,10},{6,14},... | collective-permute-start | bytes 589832 | tf_op jit(solution)/shard_map/ppermute | solution.py:19

commit v24 on v17

--- a/solution.py
+++ b/solution.py
@@ -177,11 +177,11 @@
 
 def late_kernel(side, t_width, *refs):
     if side:
-        plane_ref, ref, stats_ref, acc_ref, norm_ref, sums_in, out_ref, sums_ref, visit_ref = refs
+        plane_ref, ref, stats_ref, acc_ref, norm_ref, sums_in, *out_refs, sums_ref, visit_ref = refs
         v = visiting(ref, t_width)
         visit_ref[0:1, :], visit_ref[1:2, :] = v[2:]
     else:
-        plane_ref, ref, stats_ref, acc_ref, norm_ref, sums_in, visit_ref, out_ref, sums_ref = refs
+        plane_ref, ref, stats_ref, acc_ref, norm_ref, sums_in, visit_ref, *out_refs, sums_ref = refs
         v = (ref[:, :t_width], ref[:, t_width:], visit_ref[0:1, :], visit_ref[1:2, :])
     inv_t, inv_s = stats_ref[0:1, :LANES], stats_ref[1:2, :LANES]
     loss = sums_in[0:1, :]
@@ -195,16 +195,25 @@
         loss = loss + loss_part
         spread = spread + spread_part
         back = jnp.dot(weights, with_ones(v[1]), preferred_element_type=jnp.float32)
-        out_ref[at, :] = direct_of(cs, acc_ref[h, at, :] + back)
+        direct = direct_of(cs, acc_ref[h, at, :] + back)
+        share = out_refs[0].shape[0]
+        step = min(share, at.size)
+        for begin in range(at.start, at.start + at.size, step):
+            to_ref, to = out_refs[begin // share], begin % share
+            to_ref[to : to + step, :] = direct[begin - at.start : begin - at.start + step]
     for i in range(1 if side else sums_ref.shape[0]):
         at = sums_ref if side else sums_ref.at[i]
         at[0:1, :] = loss
         at[1:2, :] = spread
 
 
-def halve_kernel(rows, keep_ref, got_ref, *out_refs):
-    out_refs[0][...] = keep_ref[:rows, :] + got_ref[:rows, :]
-    out_refs[1][...] = keep_ref[rows : 2 * rows, :] + got_ref[rows : 2 * rows, :]
+def halve_kernel(keep_ref, *refs):
+    *got_refs, first_ref, second_ref = refs
+    rows = first_ref.shape[0]
+    if len(got_refs) == 1:
+        got_refs = [got_refs[0].at[:rows, :], got_refs[0].at[rows:, :]]
+    first_ref[...] = keep_ref[:rows, :] + got_refs[0][...]
+    second_ref[...] = keep_ref[rows:, :] + got_refs[1][...]
 
 
 def final_kernel(t_width, total_rows, packed_ref, stats_ref, sums_ref, *refs):
@@ -307,9 +316,9 @@
     own, backs = tiles[0], tiles[1:]
     returned = [shifted(x, "sub", -k) for k, x in enumerate(backs, 1)]
     given = [plane, line[half], totals, acc, norms]
-    give, late_sums, visit_norms = call(
+    *give, late_sums, visit_norms = call(
         functools.partial(late_kernel, 1, t_width),
-        [f32((side, s_width)), f32((2, LANES)), f32((2, rows))],
+        [f32((side // 2, s_width))] * 2 + [f32((2, LANES)), f32((2, rows))],
         [*given, early_sums],
         pair_flops // 2,
     )
@@ -319,18 +328,16 @@
         [*given, late_sums, visit_norms],
         pair_flops // 2,
     )
-    got = exchange(give, "blk", 1)
+    got = [exchange(x, "blk", 1) for x in give]
     tiles, distance = n_blk // 2, 2
     while tiles > 1:
         tiles //= 2
         out_shape = [f32((rows * tiles, s_width))] * 2
-        keep, give = call(
-            functools.partial(halve_kernel, rows * tiles), out_shape, (keep, got), 2 * keep.size
-        )
-        got = exchange(give, "blk", distance)
+        keep, give = call(halve_kernel, out_shape, (keep, *got), 2 * keep.size)
+        got = [exchange(give, "blk", distance)]
         distance *= 2
     all_sums = to_all(sums)
-    parts = [own, keep, got] + returned
+    parts = [own, keep] + got + returned
     grad, loss = call(
         functools.partial(final_kernel, t_width, total_rows),
         [f32((rows, s_width)), f32((1, LANES))],

time: 40.8 us -> 41.1 us (level)
    ppermute x10 -> x11, starting transfers between devices: 9.42 us -> 9.91 us  [exchange(): return lax.ppermute(value, axis, [(i, i ^ distance) for i in range(size)])]
    ppermute x10 -> x11, waiting for transfers between devices: 8.9 us -> 8.55 us  [exchange(): return lax.ppermute(value, axis, [(i, i ^ distance) for i in range(size)])]
  transfers between devices with their start and end apart: 13 -> 14, of which waited for: 6 -> 7; matrix products, arithmetic and copies ran while one was open for 0% -> 0% of each run, Pallas kernels for 8% -> 8%
where the time goes in v24:
time: 41.1 us; the launch traced here: 41 us
  starting transfers between devices  13.8 us (34%)
  waiting for transfers between devices  11.6 us (28%)
  blocking collectives  9.32 us (23%)
  Pallas kernels  5.53 us (13%)
  between operations  0.69 us (2%)
    ppermute x11, starting transfers between devices, exchange(): return lax.ppermute(value, axis, [(i, i ^ distance) for i in range(size)])  9.91 us
    all_to_all x1, blocking collectives, to_all(): return lax.all_to_all(value, ('blk', 'sub'), 0, 0, tiled=True)  9.32 us
    ppermute x11, waiting for transfers between devices, exchange(): return lax.ppermute(value, axis, [(i, i ^ distance) for i in range(size)])  8.55 us
    pallas_call x7, Pallas kernels, call(): pl.pallas_call(kernel, out_shape=out_shape, in_specs=in_specs, out_specs=...  5.53 us
    ppermute x3, starting transfers between devices, shifted(): lax.ppermute(value, axis, [(i, (i + distance) % size) for i in range(size)])  3.88 us
    ppermute x3, waiting for transfers between devices, shifted(): lax.ppermute(value, axis, [(i, (i + distance) % size) for i in range(size)])  3.04 us
  transfers between devices with their start and end apart: 14, of which 7 were waited for; matrix products, arithmetic and copies ran while one was open for 0% of the time, Pallas kernels for 8%

profile of v24, /device:TPU:0, one launch (start us, length us, event | category | flops | bytes accessed | tf_op | source)
XLA Modules:
  0.0 41.0 jit_solution(12556295551744041974)
XLA Ops:
  0.6 1.0 %shard_map.41.packed_ref.refs_0_ = bf16[128,1408]{1,0:T(8,128)(2,1)S(1)} custom-call(bf16[128,1024]{1,0:T(8,128)(2,1)} %t_hbm.1, bf16[128,384]{1,0:T(8,128)(2,1)} %s_hbm.1), custom_call_target="tpu_custom_call" | custom-call | bytes 360448 | tf_op jit(solution)/shard_map/pallas_call | solution.py:238
  1.6 3.1 %collective-permute-start.1 = (bf16[128,1408]{1,0:T(8,128)(2,1)S(1)}, bf16[128,1408]{1,0:T(8,128)(2,1)S(1)}, u32[]{:S(2)}, u32[]{:S(2)}) collective-permute-start(bf16[128,1408]{1,0:T(8,128)(2,1)S(1)} %shard_map.41.packed_ref.refs_0_), channel_id=1, source_target_pairs={{0,1},{1,2},{2,3},{3,0},{4,5},{5,6},{6,7},{7,4},{8,9},{9,10},{10,1... | collective-permute-start | bytes 1081352 | tf_op jit(solution)/shard_map/ppermute | solution.py:24
  4.7 1.5 %collective-permute-start = (bf16[128,1408]{1,0:T(8,128)(2,1)S(1)}, bf16[128,1408]{1,0:T(8,128)(2,1)S(1)}, u32[]{:S(2)}, u32[]{:S(2)}) collective-permute-start(bf16[128,1408]{1,0:T(8,128)(2,1)S(1)} %shard_map.41.packed_ref.refs_0_), channel_id=1, source_target_pairs={{0,8},{4,12},{8,0},{12,4},{1,9},{5,13},{9,1},{13,5},{2,10},{6,14},... | collective-permute-start | bytes 1081352 | tf_op jit(solution)/shard_map/ppermute | solution.py:19
  6.2 0.2 shard_map.42
  6.4 1.6 %collective-permute-start.2 = (f32[1,1536]{1,0:T(1,128)S(1)}, f32[1,1536]{1,0:T(1,128)S(1)}, u32[]{:S(2)}, u32[]{:S(2)}) collective-permute-start(f32[1,1536]{1,0:T(1,128)S(1)} %shard_map.42), channel_id=1, source_target_pairs={{0,1},{1,0},{2,3},{3,2},{4,5},{5,4},{6,7},{7,6},{8,9},{9,8},{10,11... | collective-permute-start | bytes 18440 | tf_op jit(solution)/shard_map/ppermute | solution.py:19
  8.0 1.2 %collective-permute-start.3 = (f32[1,1536]{1,0:T(1,128)S(1)}, f32[1,1536]{1,0:T(1,128)S(1)}, u32[]{:S(2)}, u32[]{:S(2)}) collective-permute-start(f32[1,1536]{1,0:T(1,128)S(1)} %shard_map.42), channel_id=1, source_target_pairs={{0,2},{1,3},{2,0},{3,1},{4,6},{5,7},{6,4},{7,5},{8,10},{9,11},{10,... | collective-permute-start | bytes 18440 | tf_op jit(solution)/shard_map/ppermute | solution.py:19
  9.2 1.6 %collective-permute-start.4 = (f32[1,1536]{1,0:T(1,128)S(1)}, f32[1,1536]{1,0:T(1,128)S(1)}, u32[]{:S(2)}, u32[]{:S(2)}) collective-permute-start(f32[1,1536]{1,0:T(1,128)S(1)} %shard_map.42), channel_id=1, source_target_pairs={{0,3},{1,2},{2,1},{3,0},{4,7},{5,6},{6,5},{7,4},{8,11},{9,10},{10,... | collective-permute-start | bytes 18440 | tf_op jit(solution)/shard_map/ppermute | solution.py:19
  10.8 3.8 %collective-permute-done.2 = f32[1,1536]{1,0:T(1,128)S(1)} collective-permute-done((f32[1,1536]{1,0:T(1,128)S(1)}, f32[1,1536]{1,0:T(1,128)S(1)}, u32[]{:S(2)}, u32[]{:S(2)}) %collective-permute-start.2) | collective-permute-done | bytes 6176 | tf_op jit(solution)/shard_map/ppermute | solution.py:19
  14.6 1.1 %collective-permute-done.3 = f32[1,1536]{1,0:T(1,128)S(1)} collective-permute-done((f32[1,1536]{1,0:T(1,128)S(1)}, f32[1,1536]{1,0:T(1,128)S(1)}, u32[]{:S(2)}, u32[]{:S(2)}) %collective-permute-start.3) | collective-permute-done | bytes 6176 | tf_op jit(solution)/shard_map/ppermute | solution.py:19
  15.6 0.0 collective-permute-done.4
  15.6 0.0 collective-permute-done.1.refs_4_
  15.7 0.6 %collective-permute-start.9 = (bf16[128,1408]{1,0:T(8,128)(2,1)S(1)}, bf16[128,1408]{1,0:T(8,128)(2,1)S(1)}, u32[]{:S(2)}, u32[]{:S(2)}) collective-permute-start(bf16[128,1408]{1,0:T(8,128)(2,1)S(1)} %collective-permute-done.1.refs_4_), channel_id=1, source_target_pairs={{0,1},{1,2},{2,3},{3,0},{4,5},{5,6},{6,7},{7,4},{8,9},{9,10},{10,1... | collective-permute-start | bytes 1081352 | tf_op jit(solution)/shard_map/ppermute | solution.py:24
  16.3 0.0 collective-permute-done.refs_1_
  16.3 0.0 collective-permute-start.5
  16.3 0.5 %collective-permute-start.6 = (bf16[128,1408]{1,0:T(8,128)(2,1)S(1)}, bf16[128,1408]{1,0:T(8,128)(2,1)S(1)}, u32[]{:S(2)}, u32[]{:S(2)}) collective-permute-start(bf16[128,1408]{1,0:T(8,128)(2,1)S(1)} %collective-permute-done.refs_1_), channel_id=1, source_target_pairs={{0,4},{4,0},{8,12},{12,8},{1,5},{5,1},{9,13},{13,9},{2,6},{6,2},{1... | collective-permute-start | bytes 1081352 | tf_op jit(solution)/shard_map/ppermute | solution.py:19
  16.8 1.6 %collective-permute-start.7 = (f32[1,1536]{1,0:T(1,128)S(1)}, f32[1,1536]{1,0:T(1,128)S(1)}, u32[]{:S(2)}, u32[]{:S(2)}) collective-permute-start(f32[1,1536]{1,0:T(1,128)S(1)} %add_add_fusion), channel_id=1, source_target_pairs={{0,8},{4,12},{8,0},{12,4},{1,9},{5,13},{9,1},{13,5},{2,10},{6,14},... | collective-permute-start | bytes 18440 | tf_op jit(solution)/shard_map/ppermute | solution.py:19
  18.4 2.1 %collective-permute-done.7 = f32[1,1536]{1,0:T(1,128)S(1)} collective-permute-done((f32[1,1536]{1,0:T(1,128)S(1)}, f32[1,1536]{1,0:T(1,128)S(1)}, u32[]{:S(2)}, u32[]{:S(2)}) %collective-permute-start.7) | collective-permute-done | bytes 6176 | tf_op jit(solution)/shard_map/ppermute | solution.py:19
  20.5 0.1 collective-permute-start.8
  20.6 1.2 %collective-permute-done.8.refs_6_ = f32[1,1536]{1,0:T(1,128)S(1)} collective-permute-done((f32[1,1536]{1,0:T(1,128)S(1)}, f32[1,1536]{1,0:T(1,128)S(1)}, u32[]{:S(2)}, u32[]{:S(2)}) %collective-permute-start.8) | collective-permute-done | bytes 6176 | tf_op jit(solution)/shard_map/ppermute | solution.py:19
  21.8 0.0 collective-permute-done.5.refs_2_
  21.8 2.2 %shard_map.43 = (f32[128,384]{1,0:T(8,128)S(1)}, f32[128,384]{1,0:T(8,128)S(1)}, f32[2,256,512]{2,1,0:T(8,128)S(1)}, f32[2,2,256,128]{3,2,1,0:T(8,128)S(1)}, f32...) custom-call(bf16[128,1408]{1,0:T(8,128)(2,1)S(1)} %shard_map.41.packed_ref.refs_0_, ...), custom_call_target="tpu_custom_call" | custom-call | flops 570425344 | bytes 1814528 | tf_op jit(solution)/shard_map/pallas_call | solution.py:238
  24.0 3.0 %collective-permute-done.9.refs_1_ = bf16[128,1408]{1,0:T(8,128)(2,1)S(1)} collective-permute-done((bf16[128,1408]{1,0:T(8,128)(2,1)S(1)}, bf16[128,1408]{1,0:T(8,128)(2,1)S(1)}, u32[]{:S(2)}, u32[]{:S(2)}) %collective-permute-start.9) | collective-permute-done | bytes 360480 | tf_op jit(solution)/shard_map/ppermute | solution.py:24
  27.0 0.7 %shard_map.44 = (f32[128,384]{1,0:T(8,128)S(1)}, f32[128,384]{1,0:T(8,128)S(1)}, f32[2,128]{1,0:T(2,128)S(1)}, f32[2,128]{1,0:T(2,128)S(1)}) custom-call(bf16[2,256,1408]{2,1,0:T(8,128)(2,1)S(1)} %get-tuple-element.34.refs_0_, bf16[128,1408]{1,0:T(8,128)(2,1)S(1)} %collective-permute-done.9.refs_1_, f32[4,384]{1,0:T(4,128)S(1)} %get-tuple-element.33.refs_2_.stats_ref, ...), custom_call_target="tpu_custom_call" | custom-call | flops 142606336 | bytes 3382272 | tf_op jit(solution)/shard_map/pallas_call | solution.py:238
  27.7 0.1 collective-permute-start.10
  27.8 0.5 %collective-permute-start.11 = (f32[128,384]{1,0:T(8,128)S(1)}, f32[128,384]{1,0:T(8,128)S(1)}, u32[]{:S(2)}, u32[]{:S(2)}) collective-permute-start(f32[128,384]{1,0:T(8,128)S(1)} %get-tuple-element.44), channel_id=1, source_target_pairs={{0,4},{4,0},{8,12},{12,8},{1,5},{5,1},{9,13},{13,9},{2,6},{6,2},{1... | collective-permute-start | bytes 589832 | tf_op jit(solution)/shard_map/ppermute | solution.py:19
  28.3 0.2 collective-permute-start.13
  28.4 0.6 %shard_map.45 = (f32[256,384]{1,0:T(8,128)S(1)}, f32[16,2,128]{2,1,0:T(2,128)S(1)}) custom-call(bf16[2,256,1408]{2,1,0:T(8,128)(2,1)S(1)} %get-tuple-element.34.refs_0_, bf16[128,1408]{1,0:T(8,128)(2,1)S(1)} %collective-permute-done.9.refs_1_, f32[4,384]{1,0:T(4,128)S(1)} %get-tuple-element.33.refs_2_.stats_ref, ...), custom_call_target="tpu_custom_call" | custom-call | flops 142606336 | bytes 3383296 | tf_op jit(solution)/shard_map/pallas_call | solution.py:238
  29.1 0.1 collective-permute-done.10.refs_0_
  29.2 0.3 collective-permute-done.11.refs_1_
  29.5 1.3 %collective-permute-start.12 = (f32[128,384]{1,0:T(8,128)S(1)}, f32[128,384]{1,0:T(8,128)S(1)}, u32[]{:S(2)}, u32[]{:S(2)}) collective-permute-start(f32[128,384]{1,0:T(8,128)S(1)} %get-tuple-element.46), channel_id=1, source_target_pairs={{0,8},{4,12},{8,0},{12,4},{1,9},{5,13},{9,1},{13,5},{2,10},{6,14},... | collective-permute-start | bytes 589832 | tf_op jit(solution)/shard_map/ppermute | solution.py:19
  30.8 9.3 %all_to_all.5.sums_ref = f32[16,2,128]{2,1,0:T(2,128)S(1)} all-to-all(f32[16,2,128]{2,1,0:T(2,128)S(1)} %get-tuple-element.40), channel_id=1, replica_groups=mesh['groups'=2,'blk'=4,'sub'=4] {'blk','sub'}, dimensions={0} | all-to-all | bytes 32768 | tf_op jit(solution)/shard_map/all_to_all | solution.py:259
  40.1 0.8 %shard_map.47 = (f32[128,384]{1,0:T(8,128)}, f32[1,128]{1,0:T(1,128)}) custom-call(bf16[128,1408]{1,0:T(8,128)(2,1)S(1)} %shard_map.41.packed_ref.refs_0_, f32[4,384]{1,0:T(4,128)S(1)} %get-tuple-element.33.refs_2_.stats_ref, f32[16,2,128]{2,1,0:T(2,128)S(1)} %all_to_all.5.sums_ref, f32[128,384]{1,0:T(8,128)S(1)} %get-tuple-element.41.refs_0_, ...), custom_call_target="tpu_custom_call" | custom-call | flops 393216 | bytes 1169408 | tf_op jit(solution)/shard_map/pallas_call | solution.py:238
  (6 shorter events, 0.1 us)
Async XLA Ops:
  1.6 14.0 %collective-permute-start.1 = (bf16[128,1408]{1,0:T(8,128)(2,1)S(1)}, bf16[128,1408]{1,0:T(8,128)(2,1)S(1)}, u32[]{:S(2)}, u32[]{:S(2)}) collective-permute-start(bf16[128,1408]{1,0:T(8,128)(2,1)S(1)} %shard_map.41.packed_ref.refs_0_), channel_id=1, source_target_pairs={{0,1},{1,2},{2,3},{3,0},{4,5},{5,6},{6,7},{7,4},{8,9},{9,10},{10,1... | collective-permute-start | bytes 1081352 | tf_op jit(solution)/shard_map/ppermute | solution.py:24
  4.7 11.6 %collective-permute-start = (bf16[128,1408]{1,0:T(8,128)(2,1)S(1)}, bf16[128,1408]{1,0:T(8,128)(2,1)S(1)}, u32[]{:S(2)}, u32[]{:S(2)}) collective-permute-start(bf16[128,1408]{1,0:T(8,128)(2,1)S(1)} %shard_map.41.packed_ref.refs_0_), channel_id=1, source_target_pairs={{0,8},{4,12},{8,0},{12,4},{1,9},{5,13},{9,1},{13,5},{2,10},{6,14},... | collective-permute-start | bytes 1081352 | tf_op jit(solution)/shard_map/ppermute | solution.py:19
  6.4 8.2 %collective-permute-start.2 = (f32[1,1536]{1,0:T(1,128)S(1)}, f32[1,1536]{1,0:T(1,128)S(1)}, u32[]{:S(2)}, u32[]{:S(2)}) collective-permute-start(f32[1,1536]{1,0:T(1,128)S(1)} %shard_map.42), channel_id=1, source_target_pairs={{0,1},{1,0},{2,3},{3,2},{4,5},{5,4},{6,7},{7,6},{8,9},{9,8},{10,11... | collective-permute-start | bytes 18440 | tf_op jit(solution)/shard_map/ppermute | solution.py:19
  8.0 7.7 %collective-permute-start.3 = (f32[1,1536]{1,0:T(1,128)S(1)}, f32[1,1536]{1,0:T(1,128)S(1)}, u32[]{:S(2)}, u32[]{:S(2)}) collective-permute-start(f32[1,1536]{1,0:T(1,128)S(1)} %shard_map.42), channel_id=1, source_target_pairs={{0,2},{1,3},{2,0},{3,1},{4,6},{5,7},{6,4},{7,5},{8,10},{9,11},{10,... | collective-permute-start | bytes 18440 | tf_op jit(solution)/shard_map/ppermute | solution.py:19
  9.2 6.4 %collective-permute-start.4 = (f32[1,1536]{1,0:T(1,128)S(1)}, f32[1,1536]{1,0:T(1,128)S(1)}, u32[]{:S(2)}, u32[]{:S(2)}) collective-permute-start(f32[1,1536]{1,0:T(1,128)S(1)} %shard_map.42), channel_id=1, source_target_pairs={{0,3},{1,2},{2,1},{3,0},{4,7},{5,6},{6,5},{7,4},{8,11},{9,10},{10,... | collective-permute-start | bytes 18440 | tf_op jit(solution)/shard_map/ppermute | solution.py:19
  15.7 11.4 %collective-permute-start.9 = (bf16[128,1408]{1,0:T(8,128)(2,1)S(1)}, bf16[128,1408]{1,0:T(8,128)(2,1)S(1)}, u32[]{:S(2)}, u32[]{:S(2)}) collective-permute-start(bf16[128,1408]{1,0:T(8,128)(2,1)S(1)} %collective-permute-done.1.refs_4_), channel_id=1, source_target_pairs={{0,1},{1,2},{2,3},{3,0},{4,5},{5,6},{6,7},{7,4},{8,9},{9,10},{10,1... | collective-permute-start | bytes 1081352 | tf_op jit(solution)/shard_map/ppermute | solution.py:24
  16.3 5.5 %collective-permute-start.5 = (bf16[128,1408]{1,0:T(8,128)(2,1)S(1)}, bf16[128,1408]{1,0:T(8,128)(2,1)S(1)}, u32[]{:S(2)}, u32[]{:S(2)}) collective-permute-start(bf16[128,1408]{1,0:T(8,128)(2,1)S(1)} %shard_map.41.packed_ref.refs_0_), channel_id=1, source_target_pairs={{0,4},{4,0},{8,12},{12,8},{1,5},{5,1},{9,13},{13,9},{2,6},{6,2},{1... | collective-permute-start | bytes 1081352 | tf_op jit(solution)/shard_map/ppermute | solution.py:19
  16.3 5.5 %collective-permute-start.6 = (bf16[128,1408]{1,0:T(8,128)(2,1)S(1)}, bf16[128,1408]{1,0:T(8,128)(2,1)S(1)}, u32[]{:S(2)}, u32[]{:S(2)}) collective-permute-start(bf16[128,1408]{1,0:T(8,128)(2,1)S(1)} %collective-permute-done.refs_1_), channel_id=1, source_target_pairs={{0,4},{4,0},{8,12},{12,8},{1,5},{5,1},{9,13},{13,9},{2,6},{6,2},{1... | collective-permute-start | bytes 1081352 | tf_op jit(solution)/shard_map/ppermute | solution.py:19
  16.8 3.7 %collective-permute-start.7 = (f32[1,1536]{1,0:T(1,128)S(1)}, f32[1,1536]{1,0:T(1,128)S(1)}, u32[]{:S(2)}, u32[]{:S(2)}) collective-permute-start(f32[1,1536]{1,0:T(1,128)S(1)} %add_add_fusion), channel_id=1, source_target_pairs={{0,8},{4,12},{8,0},{12,4},{1,9},{5,13},{9,1},{13,5},{2,10},{6,14},... | collective-permute-start | bytes 18440 | tf_op jit(solution)/shard_map/ppermute | solution.py:19
  20.5 1.2 %collective-permute-start.8 = (f32[1,1536]{1,0:T(1,128)S(1)}, f32[1,1536]{1,0:T(1,128)S(1)}, u32[]{:S(2)}, u32[]{:S(2)}) collective-permute-start(f32[1,1536]{1,0:T(1,128)S(1)} %add.15.refs_5_), channel_id=1, source_target_pairs={{0,4},{4,0},{8,12},{12,8},{1,5},{5,1},{9,13},{13,9},{2,6},{6,2},{1... | collective-permute-start | bytes 18440 | tf_op jit(solution)/shard_map/ppermute | solution.py:19
  27.7 1.5 %collective-permute-start.10 = (f32[128,384]{1,0:T(8,128)S(1)}, f32[128,384]{1,0:T(8,128)S(1)}, u32[]{:S(2)}, u32[]{:S(2)}) collective-permute-start(f32[128,384]{1,0:T(8,128)S(1)} %get-tuple-element.43), channel_id=1, source_target_pairs={{0,4},{4,0},{8,12},{12,8},{1,5},{5,1},{9,13},{13,9},{2,6},{6,2},{1... | collective-permute-start | bytes 589832 | tf_op jit(solution)/shard_map/ppermute | solution.py:19
  27.8 1.7 %collective-permute-start.11 = (f32[128,384]{1,0:T(8,128)S(1)}, f32[128,384]{1,0:T(8,128)S(1)}, u32[]{:S(2)}, u32[]{:S(2)}) collective-permute-start(f32[128,384]{1,0:T(8,128)S(1)} %get-tuple-element.44), channel_id=1, source_target_pairs={{0,4},{4,0},{8,12},{12,8},{1,5},{5,1},{9,13},{13,9},{2,6},{6,2},{1... | collective-permute-start | bytes 589832 | tf_op jit(solution)/shard_map/ppermute | solution.py:19
  28.3 11.9 %collective-permute-start.13 = (f32[128,384]{1,0:T(8,128)S(1)}, f32[128,384]{1,0:T(8,128)S(1)}, u32[]{:S(2)}, u32[]{:S(2)}) collective-permute-start(f32[128,384]{1,0:T(8,128)S(1)} %get-tuple-element.47), channel_id=1, source_target_pairs={{0,3},{1,0},{2,1},{3,2},{4,7},{5,4},{6,5},{7,6},{8,11},{9,8},{10,9... | collective-permute-start | bytes 589832 | tf_op jit(solution)/shard_map/ppermute | solution.py:24
  29.5 10.6 %collective-permute-start.12 = (f32[128,384]{1,0:T(8,128)S(1)}, f32[128,384]{1,0:T(8,128)S(1)}, u32[]{:S(2)}, u32[]{:S(2)}) collective-permute-start(f32[128,384]{1,0:T(8,128)S(1)} %get-tuple-element.46), channel_id=1, source_target_pairs={{0,8},{4,12},{8,0},{12,4},{1,9},{5,13},{9,1},{13,5},{2,10},{6,14},... | collective-permute-start | bytes 589832 | tf_op jit(solution)/shard_map/ppermute | solution.py:19

commit v25 on v17

--- a/solution.py
+++ b/solution.py
@@ -196,10 +196,14 @@
         spread = spread + spread_part
         back = jnp.dot(weights, with_ones(v[1]), preferred_element_type=jnp.float32)
         out_ref[at, :] = direct_of(cs, acc_ref[h, at, :] + back)
-    for i in range(1 if side else sums_ref.shape[0]):
-        at = sums_ref if side else sums_ref.at[i]
-        at[0:1, :] = loss
-        at[1:2, :] = spread
+    if side:
+        sums_ref[0:1, :] = loss
+        sums_ref[1:2, :] = spread
+    else:
+        middle = LANES // 2
+        folded = [row[:, :middle] + row[:, middle:] for row in (loss, spread)]
+        row = jnp.concatenate(folded, axis=1)
+        sums_ref[...] = jnp.broadcast_to(row[None], sums_ref.shape)
 
 
 def halve_kernel(rows, keep_ref, got_ref, *out_refs):
@@ -212,8 +216,9 @@
     direct = parts[0][...]
     for part in parts[1:]:
         direct = direct + part[...]
-    both = jnp.sum(jnp.sum(sums_ref[...], axis=0), axis=1, keepdims=True)
-    loss_total, spread_total = both[0:1, :], -both[1:2, :]
+    both = jnp.sum(sums_ref[...], axis=0)
+    loss_total = jnp.sum(both[:, : LANES // 2], axis=1, keepdims=True)
+    spread_total = -jnp.sum(both[:, LANES // 2 :], axis=1, keepdims=True)
     spread_s, centre = stats_ref[2:3, :], stats_ref[3:4, :]
     pairs = total_rows * (total_rows - 1.0)
     correction = 2.0 * spread_total / (pairs * spread_s * spread_s)
@@ -315,7 +320,7 @@
     )
     keep, sums = call(
         functools.partial(late_kernel, 0, t_width),
-        [f32((side, s_width)), f32((n_blk * n_sub, 2, LANES))],
+        [f32((side, s_width)), f32((n_blk * n_sub, 1, LANES))],
         [*given, late_sums, visit_norms],
         pair_flops // 2,
     )

time: 40.8 us -> 40.8 us (level)
  no operation moved by 1% of the time
where the time goes in v25:
time: 40.8 us; the launch traced here: 40.6 us
  starting transfers between devices  13.5 us (33%)
  waiting for transfers between devices  11.8 us (29%)
  blocking collectives  8.91 us (22%)
  Pallas kernels  5.68 us (14%)
  between operations  0.69 us (2%)
    ppermute x10, starting transfers between devices, exchange(): return lax.ppermute(value, axis, [(i, i ^ distance) for i in range(size)])  9.42 us
    all_to_all x1, blocking collectives, to_all(): return lax.all_to_all(value, ('blk', 'sub'), 0, 0, tiled=True)  8.91 us
    ppermute x10, waiting for transfers between devices, exchange(): return lax.ppermute(value, axis, [(i, i ^ distance) for i in range(size)])  8.83 us
    pallas_call x7, Pallas kernels, call(): pl.pallas_call(kernel, out_shape=out_shape, in_specs=in_specs, out_specs=...  5.68 us
    ppermute x3, starting transfers between devices, shifted(): lax.ppermute(value, axis, [(i, (i + distance) % size) for i in range(size)])  4.09 us
    ppermute x3, waiting for transfers between devices, shifted(): lax.ppermute(value, axis, [(i, (i + distance) % size) for i in range(size)])  2.98 us
  transfers between devices with their start and end apart: 13, of which 6 were waited for; matrix products, arithmetic and copies ran while one was open for 0% of the time, Pallas kernels for 8%

profile of v25, /device:TPU:0, one launch (start us, length us, event | category | flops | bytes accessed | tf_op | source)
XLA Modules:
  0.0 40.6 jit_solution(15685128444705042418)
XLA Ops:
  0.6 1.0 %shard_map.41.packed_ref.refs_0_ = bf16[128,1408]{1,0:T(8,128)(2,1)S(1)} custom-call(bf16[128,1024]{1,0:T(8,128)(2,1)} %t_hbm.1, bf16[128,384]{1,0:T(8,128)(2,1)} %s_hbm.1), custom_call_target="tpu_custom_call" | custom-call | bytes 360448 | tf_op jit(solution)/shard_map/pallas_call | solution.py:234
  1.6 3.1 %collective-permute-start.1 = (bf16[128,1408]{1,0:T(8,128)(2,1)S(1)}, bf16[128,1408]{1,0:T(8,128)(2,1)S(1)}, u32[]{:S(2)}, u32[]{:S(2)}) collective-permute-start(bf16[128,1408]{1,0:T(8,128)(2,1)S(1)} %shard_map.41.packed_ref.refs_0_), channel_id=1, source_target_pairs={{0,1},{1,2},{2,3},{3,0},{4,5},{5,6},{6,7},{7,4},{8,9},{9,10},{10,1... | collective-permute-start | bytes 1081352 | tf_op jit(solution)/shard_map/ppermute | solution.py:24
  4.7 1.5 %collective-permute-start = (bf16[128,1408]{1,0:T(8,128)(2,1)S(1)}, bf16[128,1408]{1,0:T(8,128)(2,1)S(1)}, u32[]{:S(2)}, u32[]{:S(2)}) collective-permute-start(bf16[128,1408]{1,0:T(8,128)(2,1)S(1)} %shard_map.41.packed_ref.refs_0_), channel_id=1, source_target_pairs={{0,8},{4,12},{8,0},{12,4},{1,9},{5,13},{9,1},{13,5},{2,10},{6,14},... | collective-permute-start | bytes 1081352 | tf_op jit(solution)/shard_map/ppermute | solution.py:19
  6.2 0.2 shard_map.42
  6.4 1.6 %collective-permute-start.2 = (f32[1,1536]{1,0:T(1,128)S(1)}, f32[1,1536]{1,0:T(1,128)S(1)}, u32[]{:S(2)}, u32[]{:S(2)}) collective-permute-start(f32[1,1536]{1,0:T(1,128)S(1)} %shard_map.42), channel_id=1, source_target_pairs={{0,1},{1,0},{2,3},{3,2},{4,5},{5,4},{6,7},{7,6},{8,9},{9,8},{10,11... | collective-permute-start | bytes 18440 | tf_op jit(solution)/shard_map/ppermute | solution.py:19
  8.0 1.2 %collective-permute-start.3 = (f32[1,1536]{1,0:T(1,128)S(1)}, f32[1,1536]{1,0:T(1,128)S(1)}, u32[]{:S(2)}, u32[]{:S(2)}) collective-permute-start(f32[1,1536]{1,0:T(1,128)S(1)} %shard_map.42), channel_id=1, source_target_pairs={{0,2},{1,3},{2,0},{3,1},{4,6},{5,7},{6,4},{7,5},{8,10},{9,11},{10,... | collective-permute-start | bytes 18440 | tf_op jit(solution)/shard_map/ppermute | solution.py:19
  9.2 1.6 %collective-permute-start.4 = (f32[1,1536]{1,0:T(1,128)S(1)}, f32[1,1536]{1,0:T(1,128)S(1)}, u32[]{:S(2)}, u32[]{:S(2)}) collective-permute-start(f32[1,1536]{1,0:T(1,128)S(1)} %shard_map.42), channel_id=1, source_target_pairs={{0,3},{1,2},{2,1},{3,0},{4,7},{5,6},{6,5},{7,4},{8,11},{9,10},{10,... | collective-permute-start | bytes 18440 | tf_op jit(solution)/shard_map/ppermute | solution.py:19
  10.8 3.8 %collective-permute-done.2 = f32[1,1536]{1,0:T(1,128)S(1)} collective-permute-done((f32[1,1536]{1,0:T(1,128)S(1)}, f32[1,1536]{1,0:T(1,128)S(1)}, u32[]{:S(2)}, u32[]{:S(2)}) %collective-permute-start.2) | collective-permute-done | bytes 6176 | tf_op jit(solution)/shard_map/ppermute | solution.py:19
  14.6 1.1 %collective-permute-done.3 = f32[1,1536]{1,0:T(1,128)S(1)} collective-permute-done((f32[1,1536]{1,0:T(1,128)S(1)}, f32[1,1536]{1,0:T(1,128)S(1)}, u32[]{:S(2)}, u32[]{:S(2)}) %collective-permute-start.3) | collective-permute-done | bytes 6176 | tf_op jit(solution)/shard_map/ppermute | solution.py:19
  15.6 0.0 collective-permute-done.4
  15.6 0.0 collective-permute-done.1.refs_4_
  15.7 0.6 %collective-permute-start.9 = (bf16[128,1408]{1,0:T(8,128)(2,1)S(1)}, bf16[128,1408]{1,0:T(8,128)(2,1)S(1)}, u32[]{:S(2)}, u32[]{:S(2)}) collective-permute-start(bf16[128,1408]{1,0:T(8,128)(2,1)S(1)} %collective-permute-done.1.refs_4_), channel_id=1, source_target_pairs={{0,1},{1,2},{2,3},{3,0},{4,5},{5,6},{6,7},{7,4},{8,9},{9,10},{10,1... | collective-permute-start | bytes 1081352 | tf_op jit(solution)/shard_map/ppermute | solution.py:24
  16.3 0.0 collective-permute-done.refs_1_
  16.3 0.0 collective-permute-start.5
  16.3 0.5 %collective-permute-start.6 = (bf16[128,1408]{1,0:T(8,128)(2,1)S(1)}, bf16[128,1408]{1,0:T(8,128)(2,1)S(1)}, u32[]{:S(2)}, u32[]{:S(2)}) collective-permute-start(bf16[128,1408]{1,0:T(8,128)(2,1)S(1)} %collective-permute-done.refs_1_), channel_id=1, source_target_pairs={{0,4},{4,0},{8,12},{12,8},{1,5},{5,1},{9,13},{13,9},{2,6},{6,2},{1... | collective-permute-start | bytes 1081352 | tf_op jit(solution)/shard_map/ppermute | solution.py:19
  16.8 1.6 %collective-permute-start.7 = (f32[1,1536]{1,0:T(1,128)S(1)}, f32[1,1536]{1,0:T(1,128)S(1)}, u32[]{:S(2)}, u32[]{:S(2)}) collective-permute-start(f32[1,1536]{1,0:T(1,128)S(1)} %add_add_fusion), channel_id=1, source_target_pairs={{0,8},{4,12},{8,0},{12,4},{1,9},{5,13},{9,1},{13,5},{2,10},{6,14},... | collective-permute-start | bytes 18440 | tf_op jit(solution)/shard_map/ppermute | solution.py:19
  18.4 2.1 %collective-permute-done.7 = f32[1,1536]{1,0:T(1,128)S(1)} collective-permute-done((f32[1,1536]{1,0:T(1,128)S(1)}, f32[1,1536]{1,0:T(1,128)S(1)}, u32[]{:S(2)}, u32[]{:S(2)}) %collective-permute-start.7) | collective-permute-done | bytes 6176 | tf_op jit(solution)/shard_map/ppermute | solution.py:19
  20.5 0.1 collective-permute-start.8
  20.6 1.2 %collective-permute-done.8.refs_6_ = f32[1,1536]{1,0:T(1,128)S(1)} collective-permute-done((f32[1,1536]{1,0:T(1,128)S(1)}, f32[1,1536]{1,0:T(1,128)S(1)}, u32[]{:S(2)}, u32[]{:S(2)}) %collective-permute-start.8) | collective-permute-done | bytes 6176 | tf_op jit(solution)/shard_map/ppermute | solution.py:19
  21.8 0.0 collective-permute-done.5.refs_2_
  21.8 0.0 collective-permute-done.6.refs_3_
  21.8 2.3 %shard_map.43 = (f32[128,384]{1,0:T(8,128)S(1)}, f32[128,384]{1,0:T(8,128)S(1)}, f32[2,256,512]{2,1,0:T(8,128)S(1)}, f32[2,2,256,128]{3,2,1,0:T(8,128)S(1)}, f32...) custom-call(bf16[128,1408]{1,0:T(8,128)(2,1)S(1)} %shard_map.41.packed_ref.refs_0_, ...), custom_call_target="tpu_custom_call" | custom-call | flops 570425344 | bytes 1814528 | tf_op jit(solution)/shard_map/pallas_call | solution.py:234
  24.1 3.0 %collective-permute-done.9.refs_1_ = bf16[128,1408]{1,0:T(8,128)(2,1)S(1)} collective-permute-done((bf16[128,1408]{1,0:T(8,128)(2,1)S(1)}, bf16[128,1408]{1,0:T(8,128)(2,1)S(1)}, u32[]{:S(2)}, u32[]{:S(2)}) %collective-permute-start.9) | collective-permute-done | bytes 360480 | tf_op jit(solution)/shard_map/ppermute | solution.py:24
  27.0 0.7 %shard_map.44 = (f32[256,384]{1,0:T(8,128)S(1)}, f32[2,128]{1,0:T(2,128)S(1)}, f32[2,128]{1,0:T(2,128)S(1)}) custom-call(bf16[2,256,1408]{2,1,0:T(8,128)(2,1)S(1)} %get-tuple-element.33.refs_0_, bf16[128,1408]{1,0:T(8,128)(2,1)S(1)} %collective-permute-done.9.refs_1_, f32[4,384]{1,0:T(4,128)S(1)} %get-tuple-element.32.refs_2_.stats_ref, ...), custom_call_target="tpu_custom_call" | custom-call | flops 142606336 | bytes 3382272 | tf_op jit(solution)/shard_map/pallas_call | solution.py:234
  27.7 0.1 collective-permute-start.10
  27.8 0.4 collective-permute-start.12
  28.2 0.7 %shard_map.45 = (f32[256,384]{1,0:T(8,128)S(1)}, f32[16,1,128]{2,1,0:T(1,128)S(1)}) custom-call(bf16[2,256,1408]{2,1,0:T(8,128)(2,1)S(1)} %get-tuple-element.33.refs_0_, bf16[128,1408]{1,0:T(8,128)(2,1)S(1)} %collective-permute-done.9.refs_1_, f32[4,384]{1,0:T(4,128)S(1)} %get-tuple-element.32.refs_2_.stats_ref, ...), custom_call_target="tpu_custom_call" | custom-call | flops 142606336 | bytes 3383296 | tf_op jit(solution)/shard_map/pallas_call | solution.py:234
  28.8 0.7 %collective-permute-done.10.got_ref = f32[256,384]{1,0:T(8,128)S(1)} collective-permute-done((f32[256,384]{1,0:T(8,128)S(1)}, f32[256,384]{1,0:T(8,128)S(1)}, u32[]{:S(2)}, u32[]{:S(2)}) %collective-permute-start.10) | collective-permute-done | bytes 393248 | tf_op jit(solution)/shard_map/ppermute | solution.py:19
  29.5 1.3 %collective-permute-start.11 = (f32[128,384]{1,0:T(8,128)S(1)}, f32[128,384]{1,0:T(8,128)S(1)}, u32[]{:S(2)}, u32[]{:S(2)}) collective-permute-start(f32[128,384]{1,0:T(8,128)S(1)} %get-tuple-element.44), channel_id=1, source_target_pairs={{0,8},{4,12},{8,0},{12,4},{1,9},{5,13},{9,1},{13,5},{2,10},{6,14},... | collective-permute-start | bytes 589832 | tf_op jit(solution)/shard_map/ppermute | solution.py:19
  30.8 8.9 %all_to_all.5.sums_ref = f32[16,1,128]{2,1,0:T(1,128)S(1)} all-to-all(f32[16,1,128]{2,1,0:T(1,128)S(1)} %get-tuple-element.39), channel_id=1, replica_groups=mesh['groups'=2,'blk'=4,'sub'=4] {'blk','sub'}, dimensions={0} | all-to-all | bytes 16384 | tf_op jit(solution)/shard_map/all_to_all | solution.py:255
  39.7 0.0 collective-permute-done.12.refs_3_
  39.8 0.9 %shard_map.47 = (f32[128,384]{1,0:T(8,128)}, f32[1,128]{1,0:T(1,128)}) custom-call(bf16[128,1408]{1,0:T(8,128)(2,1)S(1)} %shard_map.41.packed_ref.refs_0_, f32[4,384]{1,0:T(4,128)S(1)} %get-tuple-element.32.refs_2_.stats_ref, f32[16,1,128]{2,1,0:T(1,128)S(1)} %all_to_all.5.sums_ref, f32[128,384]{1,0:T(8,128)S(1)} %get-tuple-element.40.refs_0_, ...), custom_call_target="tpu_custom_call" | custom-call | flops 393216 | bytes 1161216 | tf_op jit(solution)/shard_map/pallas_call | solution.py:234
  (4 shorter events, 0.1 us)
Async XLA Ops:
  1.6 14.0 %collective-permute-start.1 = (bf16[128,1408]{1,0:T(8,128)(2,1)S(1)}, bf16[128,1408]{1,0:T(8,128)(2,1)S(1)}, u32[]{:S(2)}, u32[]{:S(2)}) collective-permute-start(bf16[128,1408]{1,0:T(8,128)(2,1)S(1)} %shard_map.41.packed_ref.refs_0_), channel_id=1, source_target_pairs={{0,1},{1,2},{2,3},{3,0},{4,5},{5,6},{6,7},{7,4},{8,9},{9,10},{10,1... | collective-permute-start | bytes 1081352 | tf_op jit(solution)/shard_map/ppermute | solution.py:24
  4.7 11.6 %collective-permute-start = (bf16[128,1408]{1,0:T(8,128)(2,1)S(1)}, bf16[128,1408]{1,0:T(8,128)(2,1)S(1)}, u32[]{:S(2)}, u32[]{:S(2)}) collective-permute-start(bf16[128,1408]{1,0:T(8,128)(2,1)S(1)} %shard_map.41.packed_ref.refs_0_), channel_id=1, source_target_pairs={{0,8},{4,12},{8,0},{12,4},{1,9},{5,13},{9,1},{13,5},{2,10},{6,14},... | collective-permute-start | bytes 1081352 | tf_op jit(solution)/shard_map/ppermute | solution.py:19
  6.4 8.2 %collective-permute-start.2 = (f32[1,1536]{1,0:T(1,128)S(1)}, f32[1,1536]{1,0:T(1,128)S(1)}, u32[]{:S(2)}, u32[]{:S(2)}) collective-permute-start(f32[1,1536]{1,0:T(1,128)S(1)} %shard_map.42), channel_id=1, source_target_pairs={{0,1},{1,0},{2,3},{3,2},{4,5},{5,4},{6,7},{7,6},{8,9},{9,8},{10,11... | collective-permute-start | bytes 18440 | tf_op jit(solution)/shard_map/ppermute | solution.py:19
  8.0 7.7 %collective-permute-start.3 = (f32[1,1536]{1,0:T(1,128)S(1)}, f32[1,1536]{1,0:T(1,128)S(1)}, u32[]{:S(2)}, u32[]{:S(2)}) collective-permute-start(f32[1,1536]{1,0:T(1,128)S(1)} %shard_map.42), channel_id=1, source_target_pairs={{0,2},{1,3},{2,0},{3,1},{4,6},{5,7},{6,4},{7,5},{8,10},{9,11},{10,... | collective-permute-start | bytes 18440 | tf_op jit(solution)/shard_map/ppermute | solution.py:19
  9.2 6.4 %collective-permute-start.4 = (f32[1,1536]{1,0:T(1,128)S(1)}, f32[1,1536]{1,0:T(1,128)S(1)}, u32[]{:S(2)}, u32[]{:S(2)}) collective-permute-start(f32[1,1536]{1,0:T(1,128)S(1)} %shard_map.42), channel_id=1, source_target_pairs={{0,3},{1,2},{2,1},{3,0},{4,7},{5,6},{6,5},{7,4},{8,11},{9,10},{10,... | collective-permute-start | bytes 18440 | tf_op jit(solution)/shard_map/ppermute | solution.py:19
  15.7 11.4 %collective-permute-start.9 = (bf16[128,1408]{1,0:T(8,128)(2,1)S(1)}, bf16[128,1408]{1,0:T(8,128)(2,1)S(1)}, u32[]{:S(2)}, u32[]{:S(2)}) collective-permute-start(bf16[128,1408]{1,0:T(8,128)(2,1)S(1)} %collective-permute-done.1.refs_4_), channel_id=1, source_target_pairs={{0,1},{1,2},{2,3},{3,0},{4,5},{5,6},{6,7},{7,4},{8,9},{9,10},{10,1... | collective-permute-start | bytes 1081352 | tf_op jit(solution)/shard_map/ppermute | solution.py:24
  16.3 5.5 %collective-permute-start.5 = (bf16[128,1408]{1,0:T(8,128)(2,1)S(1)}, bf16[128,1408]{1,0:T(8,128)(2,1)S(1)}, u32[]{:S(2)}, u32[]{:S(2)}) collective-permute-start(bf16[128,1408]{1,0:T(8,128)(2,1)S(1)} %shard_map.41.packed_ref.refs_0_), channel_id=1, source_target_pairs={{0,4},{4,0},{8,12},{12,8},{1,5},{5,1},{9,13},{13,9},{2,6},{6,2},{1... | collective-permute-start | bytes 1081352 | tf_op jit(solution)/shard_map/ppermute | solution.py:19
  16.3 5.5 %collective-permute-start.6 = (bf16[128,1408]{1,0:T(8,128)(2,1)S(1)}, bf16[128,1408]{1,0:T(8,128)(2,1)S(1)}, u32[]{:S(2)}, u32[]{:S(2)}) collective-permute-start(bf16[128,1408]{1,0:T(8,128)(2,1)S(1)} %collective-permute-done.refs_1_), channel_id=1, source_target_pairs={{0,4},{4,0},{8,12},{12,8},{1,5},{5,1},{9,13},{13,9},{2,6},{6,2},{1... | collective-permute-start | bytes 1081352 | tf_op jit(solution)/shard_map/ppermute | solution.py:19
  16.8 3.7 %collective-permute-start.7 = (f32[1,1536]{1,0:T(1,128)S(1)}, f32[1,1536]{1,0:T(1,128)S(1)}, u32[]{:S(2)}, u32[]{:S(2)}) collective-permute-start(f32[1,1536]{1,0:T(1,128)S(1)} %add_add_fusion), channel_id=1, source_target_pairs={{0,8},{4,12},{8,0},{12,4},{1,9},{5,13},{9,1},{13,5},{2,10},{6,14},... | collective-permute-start | bytes 18440 | tf_op jit(solution)/shard_map/ppermute | solution.py:19
  20.5 1.2 %collective-permute-start.8 = (f32[1,1536]{1,0:T(1,128)S(1)}, f32[1,1536]{1,0:T(1,128)S(1)}, u32[]{:S(2)}, u32[]{:S(2)}) collective-permute-start(f32[1,1536]{1,0:T(1,128)S(1)} %add.15.refs_5_), channel_id=1, source_target_pairs={{0,4},{4,0},{8,12},{12,8},{1,5},{5,1},{9,13},{13,9},{2,6},{6,2},{1... | collective-permute-start | bytes 18440 | tf_op jit(solution)/shard_map/ppermute | solution.py:19
  27.7 1.8 %collective-permute-start.10 = (f32[256,384]{1,0:T(8,128)S(1)}, f32[256,384]{1,0:T(8,128)S(1)}, u32[]{:S(2)}, u32[]{:S(2)}) collective-permute-start(f32[256,384]{1,0:T(8,128)S(1)} %get-tuple-element.42), channel_id=1, source_target_pairs={{0,4},{4,0},{8,12},{12,8},{1,5},{5,1},{9,13},{13,9},{2,6},{6,2},{1... | collective-permute-start | bytes 1179656 | tf_op jit(solution)/shard_map/ppermute | solution.py:19
  27.8 12.0 %collective-permute-start.12 = (f32[128,384]{1,0:T(8,128)S(1)}, f32[128,384]{1,0:T(8,128)S(1)}, u32[]{:S(2)}, u32[]{:S(2)}) collective-permute-start(f32[128,384]{1,0:T(8,128)S(1)} %get-tuple-element.45), channel_id=1, source_target_pairs={{0,3},{1,0},{2,1},{3,2},{4,7},{5,4},{6,5},{7,6},{8,11},{9,8},{10,9... | collective-permute-start | bytes 589832 | tf_op jit(solution)/shard_map/ppermute | solution.py:24
  29.5 10.2 %collective-permute-start.11 = (f32[128,384]{1,0:T(8,128)S(1)}, f32[128,384]{1,0:T(8,128)S(1)}, u32[]{:S(2)}, u32[]{:S(2)}) collective-permute-start(f32[128,384]{1,0:T(8,128)S(1)} %get-tuple-element.44), channel_id=1, source_target_pairs={{0,8},{4,12},{8,0},{12,4},{1,9},{5,13},{9,1},{13,5},{2,10},{6,14},... | collective-permute-start | bytes 589832 | tf_op jit(solution)/shard_map/ppermute | solution.py:19

commit v26 on v25

--- a/solution.py
+++ b/solution.py
@@ -21,7 +21,9 @@
 
 def shifted(value, axis, distance):
     size = lax.axis_size(axis)
-    return lax.ppermute(value, axis, [(i, (i + distance) % size) for i in range(size)])
+    places = [0, *range(1, size, 2), *reversed(range(2, size, 2))]
+    route = [(places[i], places[(i + distance) % size]) for i in range(size)]
+    return lax.ppermute(value, axis, route)
 
 
 def pack_kernel(t_hbm, s_hbm, packed_ref, sems):

time: 40.8 us -> 40.9 us (level)
  waiting for transfers between devices: 11.8 us -> 9.19 us
  starting transfers between devices: 13.5 us -> 15 us
  blocking collectives: 8.91 us -> 10.2 us
    ppermute x3, waiting for transfers between devices: 2.98 us -> 1.62 us  [shifted(): return lax.ppermute(value, axis, route)]
    all_to_all x1, blocking collectives: 8.91 us -> 10.2 us  [to_all(): return lax.all_to_all(value, ('blk', 'sub'), 0, 0, tiled=True)]
    ppermute x10, waiting for transfers between devices: 8.83 us -> 7.57 us  [exchange(): return lax.ppermute(value, axis, [(i, i ^ distance) for i in range(size)])]
    ppermute x10, starting transfers between devices: 9.42 us -> 10.4 us  [exchange(): return lax.ppermute(value, axis, [(i, i ^ distance) for i in range(size)])]
    ppermute x3, starting transfers between devices: 4.09 us -> 4.61 us  [shifted(): return lax.ppermute(value, axis, route)]
where the time goes in v26:
time: 40.9 us; the launch traced here: 40.8 us
  starting transfers between devices  15 us (37%)
  blocking collectives  10.2 us (25%)
  waiting for transfers between devices  9.19 us (22%)
  Pallas kernels  5.69 us (14%)
  between operations  0.7 us (2%)
    ppermute x10, starting transfers between devices, exchange(): return lax.ppermute(value, axis, [(i, i ^ distance) for i in range(size)])  10.4 us
    all_to_all x1, blocking collectives, to_all(): return lax.all_to_all(value, ('blk', 'sub'), 0, 0, tiled=True)  10.2 us
    ppermute x10, waiting for transfers between devices, exchange(): return lax.ppermute(value, axis, [(i, i ^ distance) for i in range(size)])  7.57 us
    pallas_call x7, Pallas kernels, call(): pl.pallas_call(kernel, out_shape=out_shape, in_specs=in_specs, out_specs=...  5.69 us
    ppermute x3, starting transfers between devices, shifted(): return lax.ppermute(value, axis, route)  4.61 us
    ppermute x3, waiting for transfers between devices, shifted(): return lax.ppermute(value, axis, route)  1.62 us
  transfers between devices with their start and end apart: 13, of which 6 were waited for; matrix products, arithmetic and copies ran while one was open for 0% of the time, Pallas kernels for 8%

profile of v26, /device:TPU:0, one launch (start us, length us, event | category | flops | bytes accessed | tf_op | source)
XLA Modules:
  0.0 40.8 jit_solution(18230544965986077546)
XLA Ops:
  0.6 1.0 %shard_map.41.packed_ref.refs_0_ = bf16[128,1408]{1,0:T(8,128)(2,1)S(1)} custom-call(bf16[128,1024]{1,0:T(8,128)(2,1)} %t_hbm.1, bf16[128,384]{1,0:T(8,128)(2,1)} %s_hbm.1), custom_call_target="tpu_custom_call" | custom-call | bytes 360448 | tf_op jit(solution)/shard_map/pallas_call | solution.py:236
  1.6 3.1 %collective-permute-start.1 = (bf16[128,1408]{1,0:T(8,128)(2,1)S(1)}, bf16[128,1408]{1,0:T(8,128)(2,1)S(1)}, u32[]{:S(2)}, u32[]{:S(2)}) collective-permute-start(bf16[128,1408]{1,0:T(8,128)(2,1)S(1)} %shard_map.41.packed_ref.refs_0_), channel_id=1, source_target_pairs={{0,1},{1,3},{3,2},{2,0},{4,5},{5,7},{7,6},{6,4},{8,9},{9,11},{11,1... | collective-permute-start | bytes 1081352 | tf_op jit(solution)/shard_map/ppermute | solution.py:26
  4.7 1.5 %collective-permute-start = (bf16[128,1408]{1,0:T(8,128)(2,1)S(1)}, bf16[128,1408]{1,0:T(8,128)(2,1)S(1)}, u32[]{:S(2)}, u32[]{:S(2)}) collective-permute-start(bf16[128,1408]{1,0:T(8,128)(2,1)S(1)} %shard_map.41.packed_ref.refs_0_), channel_id=1, source_target_pairs={{0,8},{4,12},{8,0},{12,4},{1,9},{5,13},{9,1},{13,5},{2,10},{6,14},... | collective-permute-start | bytes 1081352 | tf_op jit(solution)/shard_map/ppermute | solution.py:19
  6.2 0.2 shard_map.42
  6.4 2.6 %collective-permute-start.2 = (f32[1,1536]{1,0:T(1,128)S(1)}, f32[1,1536]{1,0:T(1,128)S(1)}, u32[]{:S(2)}, u32[]{:S(2)}) collective-permute-start(f32[1,1536]{1,0:T(1,128)S(1)} %shard_map.42), channel_id=1, source_target_pairs={{0,1},{1,0},{2,3},{3,2},{4,5},{5,4},{6,7},{7,6},{8,9},{9,8},{10,11... | collective-permute-start | bytes 18440 | tf_op jit(solution)/shard_map/ppermute | solution.py:19
  9.0 0.4 %collective-permute-start.3 = (f32[1,1536]{1,0:T(1,128)S(1)}, f32[1,1536]{1,0:T(1,128)S(1)}, u32[]{:S(2)}, u32[]{:S(2)}) collective-permute-start(f32[1,1536]{1,0:T(1,128)S(1)} %shard_map.42), channel_id=1, source_target_pairs={{0,2},{1,3},{2,0},{3,1},{4,6},{5,7},{6,4},{7,5},{8,10},{9,11},{10,... | collective-permute-start | bytes 18440 | tf_op jit(solution)/shard_map/ppermute | solution.py:19
  9.4 2.0 %collective-permute-start.4 = (f32[1,1536]{1,0:T(1,128)S(1)}, f32[1,1536]{1,0:T(1,128)S(1)}, u32[]{:S(2)}, u32[]{:S(2)}) collective-permute-start(f32[1,1536]{1,0:T(1,128)S(1)} %shard_map.42), channel_id=1, source_target_pairs={{0,3},{1,2},{2,1},{3,0},{4,7},{5,6},{6,5},{7,4},{8,11},{9,10},{10,... | collective-permute-start | bytes 18440 | tf_op jit(solution)/shard_map/ppermute | solution.py:19
  11.4 2.4 %collective-permute-done.2 = f32[1,1536]{1,0:T(1,128)S(1)} collective-permute-done((f32[1,1536]{1,0:T(1,128)S(1)}, f32[1,1536]{1,0:T(1,128)S(1)}, u32[]{:S(2)}, u32[]{:S(2)}) %collective-permute-start.2) | collective-permute-done | bytes 6176 | tf_op jit(solution)/shard_map/ppermute | solution.py:19
  13.8 0.6 %collective-permute-done.3 = f32[1,1536]{1,0:T(1,128)S(1)} collective-permute-done((f32[1,1536]{1,0:T(1,128)S(1)}, f32[1,1536]{1,0:T(1,128)S(1)}, u32[]{:S(2)}, u32[]{:S(2)}) %collective-permute-start.3) | collective-permute-done | bytes 6176 | tf_op jit(solution)/shard_map/ppermute | solution.py:19
  14.4 1.3 %collective-permute-done.4 = f32[1,1536]{1,0:T(1,128)S(1)} collective-permute-done((f32[1,1536]{1,0:T(1,128)S(1)}, f32[1,1536]{1,0:T(1,128)S(1)}, u32[]{:S(2)}, u32[]{:S(2)}) %collective-permute-start.4) | collective-permute-done | bytes 6176 | tf_op jit(solution)/shard_map/ppermute | solution.py:19
  15.7 0.0 collective-permute-done.1.refs_4_
  15.7 0.5 %collective-permute-start.9 = (bf16[128,1408]{1,0:T(8,128)(2,1)S(1)}, bf16[128,1408]{1,0:T(8,128)(2,1)S(1)}, u32[]{:S(2)}, u32[]{:S(2)}) collective-permute-start(bf16[128,1408]{1,0:T(8,128)(2,1)S(1)} %collective-permute-done.1.refs_4_), channel_id=1, source_target_pairs={{0,1},{1,3},{3,2},{2,0},{4,5},{5,7},{7,6},{6,4},{8,9},{9,11},{11,1... | collective-permute-start | bytes 1081352 | tf_op jit(solution)/shard_map/ppermute | solution.py:26
  16.2 0.0 collective-permute-done.refs_1_
  16.2 0.0 collective-permute-start.5
  16.2 0.5 %collective-permute-start.6 = (bf16[128,1408]{1,0:T(8,128)(2,1)S(1)}, bf16[128,1408]{1,0:T(8,128)(2,1)S(1)}, u32[]{:S(2)}, u32[]{:S(2)}) collective-permute-start(bf16[128,1408]{1,0:T(8,128)(2,1)S(1)} %collective-permute-done.refs_1_), channel_id=1, source_target_pairs={{0,4},{4,0},{8,12},{12,8},{1,5},{5,1},{9,13},{13,9},{2,6},{6,2},{1... | collective-permute-start | bytes 1081352 | tf_op jit(solution)/shard_map/ppermute | solution.py:19
  16.7 1.6 %collective-permute-start.7 = (f32[1,1536]{1,0:T(1,128)S(1)}, f32[1,1536]{1,0:T(1,128)S(1)}, u32[]{:S(2)}, u32[]{:S(2)}) collective-permute-start(f32[1,1536]{1,0:T(1,128)S(1)} %add_add_fusion), channel_id=1, source_target_pairs={{0,8},{4,12},{8,0},{12,4},{1,9},{5,13},{9,1},{13,5},{2,10},{6,14},... | collective-permute-start | bytes 18440 | tf_op jit(solution)/shard_map/ppermute | solution.py:19
  18.3 2.1 %collective-permute-done.7 = f32[1,1536]{1,0:T(1,128)S(1)} collective-permute-done((f32[1,1536]{1,0:T(1,128)S(1)}, f32[1,1536]{1,0:T(1,128)S(1)}, u32[]{:S(2)}, u32[]{:S(2)}) %collective-permute-start.7) | collective-permute-done | bytes 6176 | tf_op jit(solution)/shard_map/ppermute | solution.py:19
  20.4 0.1 collective-permute-start.8
  20.5 1.2 %collective-permute-done.8.refs_6_ = f32[1,1536]{1,0:T(1,128)S(1)} collective-permute-done((f32[1,1536]{1,0:T(1,128)S(1)}, f32[1,1536]{1,0:T(1,128)S(1)}, u32[]{:S(2)}, u32[]{:S(2)}) %collective-permute-start.8) | collective-permute-done | bytes 6176 | tf_op jit(solution)/shard_map/ppermute | solution.py:19
  21.7 0.0 collective-permute-done.5.refs_2_
  21.7 2.3 %shard_map.43 = (f32[128,384]{1,0:T(8,128)S(1)}, f32[128,384]{1,0:T(8,128)S(1)}, f32[2,256,512]{2,1,0:T(8,128)S(1)}, f32[2,2,256,128]{3,2,1,0:T(8,128)S(1)}, f32...) custom-call(bf16[128,1408]{1,0:T(8,128)(2,1)S(1)} %shard_map.41.packed_ref.refs_0_, ...), custom_call_target="tpu_custom_call" | custom-call | flops 570425344 | bytes 1814528 | tf_op jit(solution)/shard_map/pallas_call | solution.py:236
  24.0 1.6 %collective-permute-done.9.refs_1_ = bf16[128,1408]{1,0:T(8,128)(2,1)S(1)} collective-permute-done((bf16[128,1408]{1,0:T(8,128)(2,1)S(1)}, bf16[128,1408]{1,0:T(8,128)(2,1)S(1)}, u32[]{:S(2)}, u32[]{:S(2)}) %collective-permute-start.9) | collective-permute-done | bytes 360480 | tf_op jit(solution)/shard_map/ppermute | solution.py:26
  25.6 0.7 %shard_map.44 = (f32[256,384]{1,0:T(8,128)S(1)}, f32[2,128]{1,0:T(2,128)S(1)}, f32[2,128]{1,0:T(2,128)S(1)}) custom-call(bf16[2,256,1408]{2,1,0:T(8,128)(2,1)S(1)} %get-tuple-element.33.refs_0_, bf16[128,1408]{1,0:T(8,128)(2,1)S(1)} %collective-permute-done.9.refs_1_, f32[4,384]{1,0:T(4,128)S(1)} %get-tuple-element.32.refs_2_.stats_ref, ...), custom_call_target="tpu_custom_call" | custom-call | flops 142606336 | bytes 3382272 | tf_op jit(solution)/shard_map/pallas_call | solution.py:236
  26.3 0.1 collective-permute-start.10
  26.3 1.0 %collective-permute-start.12 = (f32[128,384]{1,0:T(8,128)S(1)}, f32[128,384]{1,0:T(8,128)S(1)}, u32[]{:S(2)}, u32[]{:S(2)}) collective-permute-start(f32[128,384]{1,0:T(8,128)S(1)} %get-tuple-element.45), channel_id=1, source_target_pairs={{0,2},{1,0},{3,1},{2,3},{4,6},{5,4},{7,5},{6,7},{8,10},{9,8},{11,9... | collective-permute-start | bytes 589832 | tf_op jit(solution)/shard_map/ppermute | solution.py:26
  27.4 0.7 %shard_map.45 = (f32[256,384]{1,0:T(8,128)S(1)}, f32[16,1,128]{2,1,0:T(1,128)S(1)}) custom-call(bf16[2,256,1408]{2,1,0:T(8,128)(2,1)S(1)} %get-tuple-element.33.refs_0_, bf16[128,1408]{1,0:T(8,128)(2,1)S(1)} %collective-permute-done.9.refs_1_, f32[4,384]{1,0:T(4,128)S(1)} %get-tuple-element.32.refs_2_.stats_ref, ...), custom_call_target="tpu_custom_call" | custom-call | flops 142606336 | bytes 3383296 | tf_op jit(solution)/shard_map/pallas_call | solution.py:236
  28.0 0.0 collective-permute-done.10.got_ref
  28.1 1.6 %collective-permute-start.11 = (f32[128,384]{1,0:T(8,128)S(1)}, f32[128,384]{1,0:T(8,128)S(1)}, u32[]{:S(2)}, u32[]{:S(2)}) collective-permute-start(f32[128,384]{1,0:T(8,128)S(1)} %get-tuple-element.44), channel_id=1, source_target_pairs={{0,8},{4,12},{8,0},{12,4},{1,9},{5,13},{9,1},{13,5},{2,10},{6,14},... | collective-permute-start | bytes 589832 | tf_op jit(solution)/shard_map/ppermute | solution.py:19
  29.7 10.2 %all_to_all.5.sums_ref = f32[16,1,128]{2,1,0:T(1,128)S(1)} all-to-all(f32[16,1,128]{2,1,0:T(1,128)S(1)} %get-tuple-element.39), channel_id=1, replica_groups=mesh['groups'=2,'blk'=4,'sub'=4] {'blk','sub'}, dimensions={0} | all-to-all | bytes 16384 | tf_op jit(solution)/shard_map/all_to_all | solution.py:257
  39.9 0.0 collective-permute-done.12.refs_3_
  39.9 0.0 collective-permute-done.11.refs_2_
  39.9 0.9 %shard_map.47 = (f32[128,384]{1,0:T(8,128)}, f32[1,128]{1,0:T(1,128)}) custom-call(bf16[128,1408]{1,0:T(8,128)(2,1)S(1)} %shard_map.41.packed_ref.refs_0_, f32[4,384]{1,0:T(4,128)S(1)} %get-tuple-element.32.refs_2_.stats_ref, f32[16,1,128]{2,1,0:T(1,128)S(1)} %all_to_all.5.sums_ref, f32[128,384]{1,0:T(8,128)S(1)} %get-tuple-element.40.refs_0_, ...), custom_call_target="tpu_custom_call" | custom-call | flops 393216 | bytes 1161216 | tf_op jit(solution)/shard_map/pallas_call | solution.py:236
  (4 shorter events, 0.1 us)
Async XLA Ops:
  1.6 14.1 %collective-permute-start.1 = (bf16[128,1408]{1,0:T(8,128)(2,1)S(1)}, bf16[128,1408]{1,0:T(8,128)(2,1)S(1)}, u32[]{:S(2)}, u32[]{:S(2)}) collective-permute-start(bf16[128,1408]{1,0:T(8,128)(2,1)S(1)} %shard_map.41.packed_ref.refs_0_), channel_id=1, source_target_pairs={{0,1},{1,3},{3,2},{2,0},{4,5},{5,7},{7,6},{6,4},{8,9},{9,11},{11,1... | collective-permute-start | bytes 1081352 | tf_op jit(solution)/shard_map/ppermute | solution.py:26
  4.7 11.5 %collective-permute-start = (bf16[128,1408]{1,0:T(8,128)(2,1)S(1)}, bf16[128,1408]{1,0:T(8,128)(2,1)S(1)}, u32[]{:S(2)}, u32[]{:S(2)}) collective-permute-start(bf16[128,1408]{1,0:T(8,128)(2,1)S(1)} %shard_map.41.packed_ref.refs_0_), channel_id=1, source_target_pairs={{0,8},{4,12},{8,0},{12,4},{1,9},{5,13},{9,1},{13,5},{2,10},{6,14},... | collective-permute-start | bytes 1081352 | tf_op jit(solution)/shard_map/ppermute | solution.py:19
  6.4 7.4 %collective-permute-start.2 = (f32[1,1536]{1,0:T(1,128)S(1)}, f32[1,1536]{1,0:T(1,128)S(1)}, u32[]{:S(2)}, u32[]{:S(2)}) collective-permute-start(f32[1,1536]{1,0:T(1,128)S(1)} %shard_map.42), channel_id=1, source_target_pairs={{0,1},{1,0},{2,3},{3,2},{4,5},{5,4},{6,7},{7,6},{8,9},{9,8},{10,11... | collective-permute-start | bytes 18440 | tf_op jit(solution)/shard_map/ppermute | solution.py:19
  9.0 5.5 %collective-permute-start.3 = (f32[1,1536]{1,0:T(1,128)S(1)}, f32[1,1536]{1,0:T(1,128)S(1)}, u32[]{:S(2)}, u32[]{:S(2)}) collective-permute-start(f32[1,1536]{1,0:T(1,128)S(1)} %shard_map.42), channel_id=1, source_target_pairs={{0,2},{1,3},{2,0},{3,1},{4,6},{5,7},{6,4},{7,5},{8,10},{9,11},{10,... | collective-permute-start | bytes 18440 | tf_op jit(solution)/shard_map/ppermute | solution.py:19
  9.4 6.3 %collective-permute-start.4 = (f32[1,1536]{1,0:T(1,128)S(1)}, f32[1,1536]{1,0:T(1,128)S(1)}, u32[]{:S(2)}, u32[]{:S(2)}) collective-permute-start(f32[1,1536]{1,0:T(1,128)S(1)} %shard_map.42), channel_id=1, source_target_pairs={{0,3},{1,2},{2,1},{3,0},{4,7},{5,6},{6,5},{7,4},{8,11},{9,10},{10,... | collective-permute-start | bytes 18440 | tf_op jit(solution)/shard_map/ppermute | solution.py:19
  15.7 9.9 %collective-permute-start.9 = (bf16[128,1408]{1,0:T(8,128)(2,1)S(1)}, bf16[128,1408]{1,0:T(8,128)(2,1)S(1)}, u32[]{:S(2)}, u32[]{:S(2)}) collective-permute-start(bf16[128,1408]{1,0:T(8,128)(2,1)S(1)} %collective-permute-done.1.refs_4_), channel_id=1, source_target_pairs={{0,1},{1,3},{3,2},{2,0},{4,5},{5,7},{7,6},{6,4},{8,9},{9,11},{11,1... | collective-permute-start | bytes 1081352 | tf_op jit(solution)/shard_map/ppermute | solution.py:26
  16.2 5.5 %collective-permute-start.5 = (bf16[128,1408]{1,0:T(8,128)(2,1)S(1)}, bf16[128,1408]{1,0:T(8,128)(2,1)S(1)}, u32[]{:S(2)}, u32[]{:S(2)}) collective-permute-start(bf16[128,1408]{1,0:T(8,128)(2,1)S(1)} %shard_map.41.packed_ref.refs_0_), channel_id=1, source_target_pairs={{0,4},{4,0},{8,12},{12,8},{1,5},{5,1},{9,13},{13,9},{2,6},{6,2},{1... | collective-permute-start | bytes 1081352 | tf_op jit(solution)/shard_map/ppermute | solution.py:19
  16.2 5.5 %collective-permute-start.6 = (bf16[128,1408]{1,0:T(8,128)(2,1)S(1)}, bf16[128,1408]{1,0:T(8,128)(2,1)S(1)}, u32[]{:S(2)}, u32[]{:S(2)}) collective-permute-start(bf16[128,1408]{1,0:T(8,128)(2,1)S(1)} %collective-permute-done.refs_1_), channel_id=1, source_target_pairs={{0,4},{4,0},{8,12},{12,8},{1,5},{5,1},{9,13},{13,9},{2,6},{6,2},{1... | collective-permute-start | bytes 1081352 | tf_op jit(solution)/shard_map/ppermute | solution.py:19
  16.7 3.7 %collective-permute-start.7 = (f32[1,1536]{1,0:T(1,128)S(1)}, f32[1,1536]{1,0:T(1,128)S(1)}, u32[]{:S(2)}, u32[]{:S(2)}) collective-permute-start(f32[1,1536]{1,0:T(1,128)S(1)} %add_add_fusion), channel_id=1, source_target_pairs={{0,8},{4,12},{8,0},{12,4},{1,9},{5,13},{9,1},{13,5},{2,10},{6,14},... | collective-permute-start | bytes 18440 | tf_op jit(solution)/shard_map/ppermute | solution.py:19
  20.4 1.2 %collective-permute-start.8 = (f32[1,1536]{1,0:T(1,128)S(1)}, f32[1,1536]{1,0:T(1,128)S(1)}, u32[]{:S(2)}, u32[]{:S(2)}) collective-permute-start(f32[1,1536]{1,0:T(1,128)S(1)} %add.15.refs_5_), channel_id=1, source_target_pairs={{0,4},{4,0},{8,12},{12,8},{1,5},{5,1},{9,13},{13,9},{2,6},{6,2},{1... | collective-permute-start | bytes 18440 | tf_op jit(solution)/shard_map/ppermute | solution.py:19
  26.3 1.8 %collective-permute-start.10 = (f32[256,384]{1,0:T(8,128)S(1)}, f32[256,384]{1,0:T(8,128)S(1)}, u32[]{:S(2)}, u32[]{:S(2)}) collective-permute-start(f32[256,384]{1,0:T(8,128)S(1)} %get-tuple-element.42), channel_id=1, source_target_pairs={{0,4},{4,0},{8,12},{12,8},{1,5},{5,1},{9,13},{13,9},{2,6},{6,2},{1... | collective-permute-start | bytes 1179656 | tf_op jit(solution)/shard_map/ppermute | solution.py:19
  26.3 13.5 %collective-permute-start.12 = (f32[128,384]{1,0:T(8,128)S(1)}, f32[128,384]{1,0:T(8,128)S(1)}, u32[]{:S(2)}, u32[]{:S(2)}) collective-permute-start(f32[128,384]{1,0:T(8,128)S(1)} %get-tuple-element.45), channel_id=1, source_target_pairs={{0,2},{1,0},{3,1},{2,3},{4,6},{5,4},{7,5},{6,7},{8,10},{9,8},{11,9... | collective-permute-start | bytes 589832 | tf_op jit(solution)/shard_map/ppermute | solution.py:26
  28.1 11.8 %collective-permute-start.11 = (f32[128,384]{1,0:T(8,128)S(1)}, f32[128,384]{1,0:T(8,128)S(1)}, u32[]{:S(2)}, u32[]{:S(2)}) collective-permute-start(f32[128,384]{1,0:T(8,128)S(1)} %get-tuple-element.44), channel_id=1, source_target_pairs={{0,8},{4,12},{8,0},{12,4},{1,9},{5,13},{9,1},{13,5},{2,10},{6,14},... | collective-permute-start | bytes 589832 | tf_op jit(solution)/shard_map/ppermute | solution.py:19

commit v27 on v25

--- a/solution.py
+++ b/solution.py
@@ -36,7 +36,8 @@
         copy.wait()
 
 
-def stats_kernel(t_width, packed_ref, stats_ref):
+def stats_kernel(t_width, packed_ref, *refs):
+    *given, stats_ref = refs
     value = packed_ref[...].astype(jnp.float32)
     squares = jnp.sum(value * value, axis=0, keepdims=True)
     square_t = jnp.sum(squares[:, :t_width], axis=1, keepdims=True)
@@ -45,6 +46,8 @@
     width = value.shape[1]
     stats_ref[:, :width] = jnp.sum(value, axis=0, keepdims=True)
     stats_ref[:, width:] = jnp.where(lane == 0, square_t, jnp.where(lane == 1, square_s, 0.0))
+    for ref in given:
+        stats_ref[...] = stats_ref[...] + ref[...]
 
 
 def spreads_of(stats, t_width, s_width, total_rows):
@@ -282,11 +285,16 @@
         4 * packed.size,
     )
     line = [packed, shifted(packed, "sub", 1)]
-    tz = [exchange(stats, "sub", d) for d in range(1, n_sub)]
+    tz = [shifted(stats, "sub", d) for d in range(2, n_sub)]
     line[1], *tz = lax.optimization_barrier((line[1], *tz))
     for _ in range(half - 1):
         line.append(shifted(line[-1], "sub", 1))
-    stats = functools.reduce(jnp.add, [stats] + tz)
+    stats = call(
+        functools.partial(stats_kernel, t_width),
+        f32(stats.shape),
+        (line[1], stats, *tz),
+        4 * packed.size,
+    )
     tiles = [packed]
     for distance in halvings("blk"):
         if distance == 1:

time: 40.8 us -> 42.3 us (1.037)
  waiting for transfers between devices: 11.8 us -> 13.7 us
  starting transfers between devices: 13.5 us -> 13 us
    ppermute x3 -> x5, waiting for transfers between devices: 2.98 us -> 9.43 us  [shifted(): lax.ppermute(value, axis, [(i, (i + distance) % size) for i in range(size)])]
    ppermute x10 -> x7, waiting for transfers between devices: 8.83 us -> 4.25 us  [exchange(): return lax.ppermute(value, axis, [(i, i ^ distance) for i in range(size)])]
    ppermute x10 -> x7, starting transfers between devices: 9.42 us -> 5.33 us  [exchange(): return lax.ppermute(value, axis, [(i, i ^ distance) for i in range(size)])]
    ppermute x3 -> x5, starting transfers between devices: 4.09 us -> 7.64 us  [shifted(): lax.ppermute(value, axis, [(i, (i + distance) % size) for i in range(size)])]
    pallas_call x7 -> x8, Pallas kernels: 5.68 us -> 5.89 us  [call(): pl.pallas_call(kernel, out_shape=out_shape, in_specs=in_specs, out_specs=...]
  transfers between devices with their start and end apart: 13 -> 12, of which waited for: 6 -> 5; matrix products, arithmetic and copies ran while one was open for 0% -> 0% of each run, Pallas kernels for 8% -> 8%
where the time goes in v27:
time: 42.3 us; the launch traced here: 42.2 us
  waiting for transfers between devices  13.7 us (32%)
  starting transfers between devices  13 us (31%)
  blocking collectives  8.91 us (21%)
  Pallas kernels  5.89 us (14%)
  between operations  0.71 us (2%)
    ppermute x5, waiting for transfers between devices, shifted(): lax.ppermute(value, axis, [(i, (i + distance) % size) for i in range(size)])  9.43 us
    all_to_all x1, blocking collectives, to_all(): return lax.all_to_all(value, ('blk', 'sub'), 0, 0, tiled=True)  8.91 us
    ppermute x5, starting transfers between devices, shifted(): lax.ppermute(value, axis, [(i, (i + distance) % size) for i in range(size)])  7.64 us
    pallas_call x8, Pallas kernels, call(): pl.pallas_call(kernel, out_shape=out_shape, in_specs=in_specs, out_specs=...  5.89 us
    ppermute x7, starting transfers between devices, exchange(): return lax.ppermute(value, axis, [(i, i ^ distance) for i in range(size)])  5.33 us
    ppermute x7, waiting for transfers between devices, exchange(): return lax.ppermute(value, axis, [(i, i ^ distance) for i in range(size)])  4.25 us
  transfers between devices with their start and end apart: 12, of which 5 were waited for; matrix products, arithmetic and copies ran while one was open for 0% of the time, Pallas kernels for 8%

profile of v27, /device:TPU:0, one launch (start us, length us, event | category | flops | bytes accessed | tf_op | source)
XLA Modules:
  0.0 42.2 jit_solution(1777295801945791267)
XLA Ops:
  0.6 1.0 %shard_map.41.packed_ref.refs_0_ = bf16[128,1408]{1,0:T(8,128)(2,1)S(1)} custom-call(bf16[128,1024]{1,0:T(8,128)(2,1)} %t_hbm.1, bf16[128,384]{1,0:T(8,128)(2,1)} %s_hbm.1), custom_call_target="tpu_custom_call" | custom-call | bytes 360448 | tf_op jit(solution)/shard_map/pallas_call | solution.py:237
  1.6 3.1 %collective-permute-start.1 = (bf16[128,1408]{1,0:T(8,128)(2,1)S(1)}, bf16[128,1408]{1,0:T(8,128)(2,1)S(1)}, u32[]{:S(2)}, u32[]{:S(2)}) collective-permute-start(bf16[128,1408]{1,0:T(8,128)(2,1)S(1)} %shard_map.41.packed_ref.refs_0_), channel_id=1, source_target_pairs={{0,1},{1,2},{2,3},{3,0},{4,5},{5,6},{6,7},{7,4},{8,9},{9,10},{10,1... | collective-permute-start | bytes 1081352 | tf_op jit(solution)/shard_map/ppermute | solution.py:24
  4.7 1.5 %collective-permute-start = (bf16[128,1408]{1,0:T(8,128)(2,1)S(1)}, bf16[128,1408]{1,0:T(8,128)(2,1)S(1)}, u32[]{:S(2)}, u32[]{:S(2)}) collective-permute-start(bf16[128,1408]{1,0:T(8,128)(2,1)S(1)} %shard_map.41.packed_ref.refs_0_), channel_id=1, source_target_pairs={{0,8},{4,12},{8,0},{12,4},{1,9},{5,13},{9,1},{13,5},{2,10},{6,14},... | collective-permute-start | bytes 1081352 | tf_op jit(solution)/shard_map/ppermute | solution.py:19
  6.2 0.2 shard_map.42.refs_0_
  6.4 2.6 %collective-permute-start.2 = (f32[1,1536]{1,0:T(1,128)S(1)}, f32[1,1536]{1,0:T(1,128)S(1)}, u32[]{:S(2)}, u32[]{:S(2)}) collective-permute-start(f32[1,1536]{1,0:T(1,128)S(1)} %shard_map.42.refs_0_), channel_id=1, source_target_pairs={{0,2},{1,3},{2,0},{3,1},{4,6},{5,7},{6,4},{7,5},{8,10},{9,11},{10,... | collective-permute-start | bytes 18440 | tf_op jit(solution)/shard_map/ppermute | solution.py:24
  9.0 1.3 %collective-permute-start.3 = (f32[1,1536]{1,0:T(1,128)S(1)}, f32[1,1536]{1,0:T(1,128)S(1)}, u32[]{:S(2)}, u32[]{:S(2)}) collective-permute-start(f32[1,1536]{1,0:T(1,128)S(1)} %shard_map.42.refs_0_), channel_id=1, source_target_pairs={{0,3},{1,0},{2,1},{3,2},{4,7},{5,4},{6,5},{7,6},{8,11},{9,8},{10,9... | collective-permute-start | bytes 18440 | tf_op jit(solution)/shard_map/ppermute | solution.py:24
  10.3 5.2 %collective-permute-done.2.refs_1_ = f32[1,1536]{1,0:T(1,128)S(1)} collective-permute-done((f32[1,1536]{1,0:T(1,128)S(1)}, f32[1,1536]{1,0:T(1,128)S(1)}, u32[]{:S(2)}, u32[]{:S(2)}) %collective-permute-start.2) | collective-permute-done | bytes 6176 | tf_op jit(solution)/shard_map/ppermute | solution.py:24
  15.5 0.0 collective-permute-done.3.refs_2_
  15.5 0.0 collective-permute-done.1.packed_ref.refs_4_
  15.5 0.0 collective-permute-done.refs_1_
  15.5 0.1 collective-permute-start.4
  15.6 0.5 %collective-permute-start.5 = (bf16[128,1408]{1,0:T(8,128)(2,1)S(1)}, bf16[128,1408]{1,0:T(8,128)(2,1)S(1)}, u32[]{:S(2)}, u32[]{:S(2)}) collective-permute-start(bf16[128,1408]{1,0:T(8,128)(2,1)S(1)} %collective-permute-done.refs_1_), channel_id=1, source_target_pairs={{0,4},{4,0},{8,12},{12,8},{1,5},{5,1},{9,13},{13,9},{2,6},{6,2},{1... | collective-permute-start | bytes 1081352 | tf_op jit(solution)/shard_map/ppermute | solution.py:19
  16.1 0.6 %collective-permute-start.8 = (bf16[128,1408]{1,0:T(8,128)(2,1)S(1)}, bf16[128,1408]{1,0:T(8,128)(2,1)S(1)}, u32[]{:S(2)}, u32[]{:S(2)}) collective-permute-start(bf16[128,1408]{1,0:T(8,128)(2,1)S(1)} %collective-permute-done.1.packed_ref.refs_4_), channel_id=1, source_target_pairs={{0,1},{1,2},{2,3},{3,0},{4,5},{5,6},{6,7},{7,4},{8,9},{9,10},{10,1... | collective-permute-start | bytes 1081352 | tf_op jit(solution)/shard_map/ppermute | solution.py:24
  16.7 0.2 shard_map.43
  16.9 1.5 %collective-permute-start.6 = (f32[1,1536]{1,0:T(1,128)S(1)}, f32[1,1536]{1,0:T(1,128)S(1)}, u32[]{:S(2)}, u32[]{:S(2)}) collective-permute-start(f32[1,1536]{1,0:T(1,128)S(1)} %shard_map.43), channel_id=1, source_target_pairs={{0,8},{4,12},{8,0},{12,4},{1,9},{5,13},{9,1},{13,5},{2,10},{6,14},... | collective-permute-start | bytes 18440 | tf_op jit(solution)/shard_map/ppermute | solution.py:19
  18.4 2.1 %collective-permute-done.6 = f32[1,1536]{1,0:T(1,128)S(1)} collective-permute-done((f32[1,1536]{1,0:T(1,128)S(1)}, f32[1,1536]{1,0:T(1,128)S(1)}, u32[]{:S(2)}, u32[]{:S(2)}) %collective-permute-start.6) | collective-permute-done | bytes 6176 | tf_op jit(solution)/shard_map/ppermute | solution.py:19
  20.5 0.1 collective-permute-start.7
  20.6 1.2 %collective-permute-done.7.refs_6_ = f32[1,1536]{1,0:T(1,128)S(1)} collective-permute-done((f32[1,1536]{1,0:T(1,128)S(1)}, f32[1,1536]{1,0:T(1,128)S(1)}, u32[]{:S(2)}, u32[]{:S(2)}) %collective-permute-start.7) | collective-permute-done | bytes 6176 | tf_op jit(solution)/shard_map/ppermute | solution.py:19
  21.7 0.0 collective-permute-done.4.refs_2_
  21.7 0.0 collective-permute-done.5.refs_3_
  21.7 2.3 %shard_map.44 = (f32[128,384]{1,0:T(8,128)S(1)}, f32[128,384]{1,0:T(8,128)S(1)}, f32[2,256,512]{2,1,0:T(8,128)S(1)}, f32[2,2,256,128]{3,2,1,0:T(8,128)S(1)}, f32...) custom-call(bf16[128,1408]{1,0:T(8,128)(2,1)S(1)} %shard_map.41.packed_ref.refs_0_, ...), custom_call_target="tpu_custom_call" | custom-call | flops 570425344 | bytes 1814528 | tf_op jit(solution)/shard_map/pallas_call | solution.py:237
  24.0 4.2 %collective-permute-done.8.refs_1_ = bf16[128,1408]{1,0:T(8,128)(2,1)S(1)} collective-permute-done((bf16[128,1408]{1,0:T(8,128)(2,1)S(1)}, bf16[128,1408]{1,0:T(8,128)(2,1)S(1)}, u32[]{:S(2)}, u32[]{:S(2)}) %collective-permute-start.8) | collective-permute-done | bytes 360480 | tf_op jit(solution)/shard_map/ppermute | solution.py:24
  28.3 0.7 %shard_map.45 = (f32[256,384]{1,0:T(8,128)S(1)}, f32[2,128]{1,0:T(2,128)S(1)}, f32[2,128]{1,0:T(2,128)S(1)}) custom-call(bf16[2,256,1408]{2,1,0:T(8,128)(2,1)S(1)} %get-tuple-element.31.refs_0_, bf16[128,1408]{1,0:T(8,128)(2,1)S(1)} %collective-permute-done.8.refs_1_, f32[4,384]{1,0:T(4,128)S(1)} %get-tuple-element.30.refs_2_.stats_ref, ...), custom_call_target="tpu_custom_call" | custom-call | flops 142606336 | bytes 3382272 | tf_op jit(solution)/shard_map/pallas_call | solution.py:237
  29.0 0.1 collective-permute-start.9
  29.0 0.1 collective-permute-start.11
  29.1 0.7 %shard_map.46 = (f32[256,384]{1,0:T(8,128)S(1)}, f32[16,1,128]{2,1,0:T(1,128)S(1)}) custom-call(bf16[2,256,1408]{2,1,0:T(8,128)(2,1)S(1)} %get-tuple-element.31.refs_0_, bf16[128,1408]{1,0:T(8,128)(2,1)S(1)} %collective-permute-done.8.refs_1_, f32[4,384]{1,0:T(4,128)S(1)} %get-tuple-element.30.refs_2_.stats_ref, ...), custom_call_target="tpu_custom_call" | custom-call | flops 142606336 | bytes 3383296 | tf_op jit(solution)/shard_map/pallas_call | solution.py:237
  29.8 1.0 %collective-permute-done.9.got_ref = f32[256,384]{1,0:T(8,128)S(1)} collective-permute-done((f32[256,384]{1,0:T(8,128)S(1)}, f32[256,384]{1,0:T(8,128)S(1)}, u32[]{:S(2)}, u32[]{:S(2)}) %collective-permute-start.9) | collective-permute-done | bytes 393248 | tf_op jit(solution)/shard_map/ppermute | solution.py:19
  30.8 1.6 %collective-permute-start.10 = (f32[128,384]{1,0:T(8,128)S(1)}, f32[128,384]{1,0:T(8,128)S(1)}, u32[]{:S(2)}, u32[]{:S(2)}) collective-permute-start(f32[128,384]{1,0:T(8,128)S(1)} %get-tuple-element.42), channel_id=1, source_target_pairs={{0,8},{4,12},{8,0},{12,4},{1,9},{5,13},{9,1},{13,5},{2,10},{6,14},... | collective-permute-start | bytes 589832 | tf_op jit(solution)/shard_map/ppermute | solution.py:19
  32.4 8.9 %all_to_all.5.sums_ref = f32[16,1,128]{2,1,0:T(1,128)S(1)} all-to-all(f32[16,1,128]{2,1,0:T(1,128)S(1)} %get-tuple-element.37), channel_id=1, replica_groups=mesh['groups'=2,'blk'=4,'sub'=4] {'blk','sub'}, dimensions={0} | all-to-all | bytes 16384 | tf_op jit(solution)/shard_map/all_to_all | solution.py:258
  41.3 0.0 collective-permute-done.11.refs_3_
  41.3 0.0 collective-permute-done.10.refs_2_
  41.3 0.9 %shard_map.48 = (f32[128,384]{1,0:T(8,128)}, f32[1,128]{1,0:T(1,128)}) custom-call(bf16[128,1408]{1,0:T(8,128)(2,1)S(1)} %shard_map.41.packed_ref.refs_0_, f32[4,384]{1,0:T(4,128)S(1)} %get-tuple-element.30.refs_2_.stats_ref, f32[16,1,128]{2,1,0:T(1,128)S(1)} %all_to_all.5.sums_ref, f32[128,384]{1,0:T(8,128)S(1)} %get-tuple-element.38.refs_0_, ...), custom_call_target="tpu_custom_call" | custom-call | flops 393216 | bytes 1161216 | tf_op jit(solution)/shard_map/pallas_call | solution.py:237
  (2 shorter events, 0.0 us)
Async XLA Ops:
  1.6 13.9 %collective-permute-start.1 = (bf16[128,1408]{1,0:T(8,128)(2,1)S(1)}, bf16[128,1408]{1,0:T(8,128)(2,1)S(1)}, u32[]{:S(2)}, u32[]{:S(2)}) collective-permute-start(bf16[128,1408]{1,0:T(8,128)(2,1)S(1)} %shard_map.41.packed_ref.refs_0_), channel_id=1, source_target_pairs={{0,1},{1,2},{2,3},{3,0},{4,5},{5,6},{6,7},{7,4},{8,9},{9,10},{10,1... | collective-permute-start | bytes 1081352 | tf_op jit(solution)/shard_map/ppermute | solution.py:24
  4.7 10.8 %collective-permute-start = (bf16[128,1408]{1,0:T(8,128)(2,1)S(1)}, bf16[128,1408]{1,0:T(8,128)(2,1)S(1)}, u32[]{:S(2)}, u32[]{:S(2)}) collective-permute-start(bf16[128,1408]{1,0:T(8,128)(2,1)S(1)} %shard_map.41.packed_ref.refs_0_), channel_id=1, source_target_pairs={{0,8},{4,12},{8,0},{12,4},{1,9},{5,13},{9,1},{13,5},{2,10},{6,14},... | collective-permute-start | bytes 1081352 | tf_op jit(solution)/shard_map/ppermute | solution.py:19
  6.4 9.1 %collective-permute-start.2 = (f32[1,1536]{1,0:T(1,128)S(1)}, f32[1,1536]{1,0:T(1,128)S(1)}, u32[]{:S(2)}, u32[]{:S(2)}) collective-permute-start(f32[1,1536]{1,0:T(1,128)S(1)} %shard_map.42.refs_0_), channel_id=1, source_target_pairs={{0,2},{1,3},{2,0},{3,1},{4,6},{5,7},{6,4},{7,5},{8,10},{9,11},{10,... | collective-permute-start | bytes 18440 | tf_op jit(solution)/shard_map/ppermute | solution.py:24
  9.0 6.5 %collective-permute-start.3 = (f32[1,1536]{1,0:T(1,128)S(1)}, f32[1,1536]{1,0:T(1,128)S(1)}, u32[]{:S(2)}, u32[]{:S(2)}) collective-permute-start(f32[1,1536]{1,0:T(1,128)S(1)} %shard_map.42.refs_0_), channel_id=1, source_target_pairs={{0,3},{1,0},{2,1},{3,2},{4,7},{5,4},{6,5},{7,6},{8,11},{9,8},{10,9... | collective-permute-start | bytes 18440 | tf_op jit(solution)/shard_map/ppermute | solution.py:24
  15.5 6.2 %collective-permute-start.4 = (bf16[128,1408]{1,0:T(8,128)(2,1)S(1)}, bf16[128,1408]{1,0:T(8,128)(2,1)S(1)}, u32[]{:S(2)}, u32[]{:S(2)}) collective-permute-start(bf16[128,1408]{1,0:T(8,128)(2,1)S(1)} %shard_map.41.packed_ref.refs_0_), channel_id=1, source_target_pairs={{0,4},{4,0},{8,12},{12,8},{1,5},{5,1},{9,13},{13,9},{2,6},{6,2},{1... | collective-permute-start | bytes 1081352 | tf_op jit(solution)/shard_map/ppermute | solution.py:19
  15.6 6.1 %collective-permute-start.5 = (bf16[128,1408]{1,0:T(8,128)(2,1)S(1)}, bf16[128,1408]{1,0:T(8,128)(2,1)S(1)}, u32[]{:S(2)}, u32[]{:S(2)}) collective-permute-start(bf16[128,1408]{1,0:T(8,128)(2,1)S(1)} %collective-permute-done.refs_1_), channel_id=1, source_target_pairs={{0,4},{4,0},{8,12},{12,8},{1,5},{5,1},{9,13},{13,9},{2,6},{6,2},{1... | collective-permute-start | bytes 1081352 | tf_op jit(solution)/shard_map/ppermute | solution.py:19
  16.1 12.2 %collective-permute-start.8 = (bf16[128,1408]{1,0:T(8,128)(2,1)S(1)}, bf16[128,1408]{1,0:T(8,128)(2,1)S(1)}, u32[]{:S(2)}, u32[]{:S(2)}) collective-permute-start(bf16[128,1408]{1,0:T(8,128)(2,1)S(1)} %collective-permute-done.1.packed_ref.refs_4_), channel_id=1, source_target_pairs={{0,1},{1,2},{2,3},{3,0},{4,5},{5,6},{6,7},{7,4},{8,9},{9,10},{10,1... | collective-permute-start | bytes 1081352 | tf_op jit(solution)/shard_map/ppermute | solution.py:24
  16.9 3.6 %collective-permute-start.6 = (f32[1,1536]{1,0:T(1,128)S(1)}, f32[1,1536]{1,0:T(1,128)S(1)}, u32[]{:S(2)}, u32[]{:S(2)}) collective-permute-start(f32[1,1536]{1,0:T(1,128)S(1)} %shard_map.43), channel_id=1, source_target_pairs={{0,8},{4,12},{8,0},{12,4},{1,9},{5,13},{9,1},{13,5},{2,10},{6,14},... | collective-permute-start | bytes 18440 | tf_op jit(solution)/shard_map/ppermute | solution.py:19
  20.5 1.2 %collective-permute-start.7 = (f32[1,1536]{1,0:T(1,128)S(1)}, f32[1,1536]{1,0:T(1,128)S(1)}, u32[]{:S(2)}, u32[]{:S(2)}) collective-permute-start(f32[1,1536]{1,0:T(1,128)S(1)} %add.3.refs_5_), channel_id=1, source_target_pairs={{0,4},{4,0},{8,12},{12,8},{1,5},{5,1},{9,13},{13,9},{2,6},{6,2},{1... | collective-permute-start | bytes 18440 | tf_op jit(solution)/shard_map/ppermute | solution.py:19
  29.0 1.8 %collective-permute-start.9 = (f32[256,384]{1,0:T(8,128)S(1)}, f32[256,384]{1,0:T(8,128)S(1)}, u32[]{:S(2)}, u32[]{:S(2)}) collective-permute-start(f32[256,384]{1,0:T(8,128)S(1)} %get-tuple-element.40), channel_id=1, source_target_pairs={{0,4},{4,0},{8,12},{12,8},{1,5},{5,1},{9,13},{13,9},{2,6},{6,2},{1... | collective-permute-start | bytes 1179656 | tf_op jit(solution)/shard_map/ppermute | solution.py:19
  29.0 12.3 %collective-permute-start.11 = (f32[128,384]{1,0:T(8,128)S(1)}, f32[128,384]{1,0:T(8,128)S(1)}, u32[]{:S(2)}, u32[]{:S(2)}) collective-permute-start(f32[128,384]{1,0:T(8,128)S(1)} %get-tuple-element.43), channel_id=1, source_target_pairs={{0,3},{1,0},{2,1},{3,2},{4,7},{5,4},{6,5},{7,6},{8,11},{9,8},{10,9... | collective-permute-start | bytes 589832 | tf_op jit(solution)/shard_map/ppermute | solution.py:24
  30.8 10.5 %collective-permute-start.10 = (f32[128,384]{1,0:T(8,128)S(1)}, f32[128,384]{1,0:T(8,128)S(1)}, u32[]{:S(2)}, u32[]{:S(2)}) collective-permute-start(f32[128,384]{1,0:T(8,128)S(1)} %get-tuple-element.42), channel_id=1, source_target_pairs={{0,8},{4,12},{8,0},{12,4},{1,9},{5,13},{9,1},{13,5},{2,10},{6,14},... | collective-permute-start | bytes 589832 | tf_op jit(solution)/shard_map/ppermute | solution.py:19
